TPU v7x, 32 devices: a whole 2x2x4 slice. The times are simulated.
32 devices in a mesh: seq: 32 (over z, y, x, core).
Axes of the slice: x: 2, y: 2, z: 4, core: 2. Of those that a mesh axis runs over, the one named last changes fastest.
Arguments:
- tokens: bfloat16 [8192, 2048], P('seq'), may hold values from -6 to 6
- starts: int32 [8192], P('seq'), may hold values from 0 to 1, as said below
- cotangent: bfloat16 [8192, 2048], P('seq'), may hold values from -6 to 6
- norm_gain: bfloat16 [2048], P('seq'), may hold values from 0.5 to 1.5
- gate_branch: bfloat16 [2048, 2560], P('seq'), may hold values from -0.125 to 0.125
- input_branch: bfloat16 [2048, 2560], P('seq'), may hold values from -0.125 to 0.125
- conv_weight: bfloat16 [4, 2560], P(None, 'seq'), may hold values from -3 to 3
- conv_bias: bfloat16 [2560], P('seq'), may hold values from -3 to 3
- decay_gate: bfloat16 [2560, 160], P('seq'), may hold values from -0.5 to 0.5
- decay_bias: bfloat16 [2560], P('seq'), may hold values from -3 to 3
- input_gate: bfloat16 [2560, 160], P('seq'), may hold values from -0.5 to 0.5
- input_bias: bfloat16 [2560], P('seq'), may hold values from -3 to 3
- decay_param: bfloat16 [2560], P('seq'), may hold values from -14 to -2.5, as said below
- out_proj: bfloat16 [2560, 2048], P('seq'), may hold values from -0.5 to 0.5
- mlp_gain: bfloat16 [2048], P('seq'), may hold values from 0.5 to 1.5
- mlp_gate: bfloat16 [2048, 6144], P('seq'), may hold values from -0.125 to 0.125
- mlp_up: bfloat16 [2048, 6144], P('seq'), may hold values from -0.125 to 0.125
- mlp_down: bfloat16 [6144, 2048], P('seq'), may hold values from -0.15625 to 0.15625
Outputs:
- block_out: bfloat16 [8192, 2048], P('seq')
- grad_tokens: float32 [8192, 2048], P('seq')
- grad_norm_gain: float32 [2048], P('seq')
- grad_gate_branch: float32 [2048, 2560], P('seq')
- grad_input_branch: float32 [2048, 2560], P('seq')
- grad_conv_weight: float32 [4, 2560], P(None, 'seq')
- grad_conv_bias: float32 [2560], P('seq')
- grad_decay_gate: float32 [2560, 160], P('seq')
- grad_decay_bias: float32 [2560], P('seq')
- grad_input_gate: float32 [2560, 160], P('seq')
- grad_input_bias: float32 [2560], P('seq')
- grad_decay_param: float32 [2560], P('seq')
- grad_out_proj: float32 [2560, 2048], P('seq')
- grad_mlp_gain: float32 [2048], P('seq')
- grad_mlp_gate: float32 [2048, 6144], P('seq')
- grad_mlp_up: float32 [2048, 6144], P('seq')
- grad_mlp_down: float32 [6144, 2048], P('seq')
Inputs may be any that keep to these rules, and one draw needn't show every extreme that they name: starts marks five sequences: position 0 is a start, two more starts lie in the first 256 positions and two in the last 256, so one sequence covers every position from 256 to 7935. `decay_param`: softplus of it is a channel's decay rate per step.
All inputs are finite; a program needn't handle non-finite values.
Results may differ from a plain program's by a relative error of at most 0.0071.
The roundings to bfloat16 on the way count: a program that leaves them out, or rounds other values in their place, can miss the bound.
Values may be sent and summed in bfloat16 or wider, within the bound.
A program may use at most 576 MiB of HBM per device.

v0:
```python
import jax
import jax.numpy as jnp
from jax import lax
from jax.sharding import PartitionSpec as P

H = 16
CW = 4


epsilon = 1e-06
rate_scale = 8.0


def passed_along(block, axis, distance):
    devices = range(lax.axis_size(axis))
    route = [(i - distance, i) for i in devices if i - distance in devices]
    return lax.ppermute(block, axis, route)


def prefix(value, axis, combine, identity, reverse):
    peers, place = (lax.axis_size(axis), lax.axis_index(axis))
    everything = jax.tree.map(lambda part: lax.all_gather(part, axis), value)
    start = jax.tree.map(
        lambda part, zero: jnp.broadcast_to(jnp.asarray(zero, part.dtype), part.shape),
        value,
        identity,
    )

    def hop(k, before):
        at = peers - 1 - k if reverse else k
        reached = at > place if reverse else at < place
        new = combine(before, jax.tree.map(lambda part: part[at], everything))
        return jax.tree.map(lambda a, b: jnp.where(reached, a, b), new, before)

    return lax.fori_loop(0, peers, hop, start)


def gelu_tanh(values):
    return jax.nn.gelu(values, approximate=True)


def rms_norm(values, scales):
    return values * lax.rsqrt(jnp.mean(values * values, axis=-1, keepdims=True) + epsilon) * scales


def combine(earlier_part, later_part):
    return (earlier_part[0] * later_part[0], later_part[0] * earlier_part[1] + later_part[1])


def heads_product(values, weight):
    row_count, lru_width = values.shape
    shaped = values.reshape(row_count, H, lru_width // H)
    blocks = weight.reshape(H, lru_width // H, lru_width // H)
    return jnp.einsum("thi,hij->thj", shaped, blocks, preferred_element_type=jnp.float32).reshape(
        row_count, lru_width
    )


def heads_back(grads_low, weight):
    row_count, lru_width = grads_low.shape
    shaped = grads_low.reshape(row_count, H, lru_width // H)
    blocks = weight.reshape(H, lru_width // H, lru_width // H)
    return jnp.einsum("thj,hij->thi", shaped, blocks, preferred_element_type=jnp.float32).reshape(
        row_count, lru_width
    )


def heads_grad(values, grads_low):
    row_count, lru_width = values.shape
    left_side = values.reshape(row_count, H, lru_width // H)
    right_side = grads_low.reshape(row_count, H, lru_width // H)
    return jnp.einsum(
        "thi,thj->hij", left_side, right_side, preferred_element_type=jnp.float32
    ).reshape(lru_width, lru_width // H)


def lru_terms(decay_pre, input_pre, conv_out, decay_param, flag_rows):
    log_decay = -rate_scale * jax.nn.sigmoid(decay_pre) * jax.nn.softplus(decay_param)
    keep_rows = 1.0 - flag_rows[:, None]
    coefficient = jnp.exp(log_decay) * keep_rows
    scale_in = flag_rows[:, None] + keep_rows * jnp.sqrt(-jnp.expm1(2.0 * log_decay))
    drive_term = scale_in * jax.nn.sigmoid(input_pre) * conv_out
    return (coefficient, drive_term)


def build_masks(flag_rows):
    row_count = flag_rows.shape[0]
    running = jnp.ones((row_count,), jnp.float32)
    masks = [running]
    for offset in range(1, CW):
        earlier_flags = jnp.concatenate(
            [jnp.zeros((offset - 1,), jnp.float32), flag_rows[: row_count - (offset - 1)]]
        )
        running = running * (1.0 - earlier_flags)
        masks.append(running)
    return masks


def send_mask(flag_rows):
    tail_keep = 1.0 - flag_rows[flag_rows.shape[0] - (CW - 1) :]
    after_rows = jnp.cumprod(tail_keep[::-1])[::-1]
    return jnp.concatenate([after_rows[1:], jnp.ones((1,), jnp.float32)])


def conv_local(padded, weight, bias, masks):
    row_count = masks[0].shape[0]
    conv_total = bias + jnp.zeros((row_count, padded.shape[1]), jnp.float32)
    for offset in range(CW):
        lead = CW - 1 - offset
        conv_total = conv_total + weight[offset] * (
            padded[lead : lead + row_count] * masks[offset][:, None]
        )
    return conv_total


def mlp_act(gate_values, up_values):
    return gelu_tanh(gate_values) * up_values


def body(
    tokens,
    starts,
    cotangent,
    norm_gain,
    gate_branch,
    input_branch,
    conv_weight,
    conv_bias,
    decay_gate,
    decay_bias,
    input_gate,
    input_bias,
    decay_param,
    out_proj,
    mlp_gain,
    mlp_gate,
    mlp_up,
    mlp_down,
):
    (
        whole_norm_gain,
        whole_gate_branch,
        whole_input_branch,
        whole_conv_weight,
        whole_conv_bias,
        whole_decay_gate,
        whole_decay_bias,
        whole_input_gate,
        whole_input_bias,
        whole_decay_param,
        whole_out_proj,
    ) = (
        lax.all_gather(norm_gain, "seq", axis=0, tiled=True),
        lax.all_gather(gate_branch, "seq", axis=0, tiled=True),
        lax.all_gather(input_branch, "seq", axis=0, tiled=True),
        lax.all_gather(conv_weight, "seq", axis=1, tiled=True),
        lax.all_gather(conv_bias, "seq", axis=0, tiled=True),
        lax.all_gather(decay_gate, "seq", axis=0, tiled=True),
        lax.all_gather(decay_bias, "seq", axis=0, tiled=True),
        lax.all_gather(input_gate, "seq", axis=0, tiled=True),
        lax.all_gather(input_bias, "seq", axis=0, tiled=True),
        lax.all_gather(decay_param, "seq", axis=0, tiled=True),
        lax.all_gather(out_proj, "seq", axis=0, tiled=True),
    )
    flag_rows = starts.astype(jnp.float32)
    row_count = tokens.shape[0]
    values = tokens.astype(jnp.float32)
    normed = rms_norm(values, whole_norm_gain.astype(jnp.float32)).astype(jnp.bfloat16)
    gate_pre = jnp.dot(normed, whole_gate_branch, preferred_element_type=jnp.float32)
    gate_act = gelu_tanh(gate_pre)
    conv_input = jnp.dot(normed, whole_input_branch, preferred_element_type=jnp.float32).astype(
        jnp.bfloat16
    )
    lru_width = conv_input.shape[1]
    alive_rows = send_mask(flag_rows)
    masks = build_masks(flag_rows)
    outgoing = conv_input[row_count - (CW - 1) :] * alive_rows[:, None].astype(jnp.bfloat16)
    incoming = passed_along(outgoing, "seq", 1)
    padded = jnp.concatenate([incoming, conv_input], axis=0).astype(jnp.float32)
    conv_out = conv_local(
        padded, whole_conv_weight.astype(jnp.float32), whole_conv_bias.astype(jnp.float32), masks
    )
    conv_low = conv_out.astype(jnp.bfloat16)
    decay_pre = heads_product(conv_low, whole_decay_gate) + whole_decay_bias.astype(jnp.float32)
    input_pre = heads_product(conv_low, whole_input_gate) + whole_input_bias.astype(jnp.float32)
    param_full = whole_decay_param.astype(jnp.float32)
    coefficient, drive_term = lru_terms(decay_pre, input_pre, conv_out, param_full, flag_rows)
    cumulative, local_state = lax.associative_scan(combine, (coefficient, drive_term), axis=0)
    entering = prefix(
        (cumulative[-1], local_state[-1]),
        "seq",
        combine,
        (jnp.ones_like(cumulative[-1]), jnp.zeros_like(local_state[-1])),
        False,
    )
    incoming_state = entering[1]
    states = local_state + cumulative * incoming_state[None, :]
    mixed_rows = (states * gate_act).astype(jnp.bfloat16)
    middle = values + jnp.dot(mixed_rows, whole_out_proj, preferred_element_type=jnp.float32)
    whole_mlp_gain, whole_mlp_gate, whole_mlp_up, whole_mlp_down = (
        lax.all_gather(mlp_gain, "seq", axis=0, tiled=True),
        lax.all_gather(mlp_gate, "seq", axis=0, tiled=True),
        lax.all_gather(mlp_up, "seq", axis=0, tiled=True),
        lax.all_gather(mlp_down, "seq", axis=0, tiled=True),
    )
    gain_two = whole_mlp_gain.astype(jnp.float32)
    normed_two = rms_norm(middle, gain_two).astype(jnp.bfloat16)
    gate_mlp = jnp.dot(normed_two, whole_mlp_gate, preferred_element_type=jnp.float32)
    up_mlp = jnp.dot(normed_two, whole_mlp_up, preferred_element_type=jnp.float32)
    hidden = mlp_act(gate_mlp, up_mlp).astype(jnp.bfloat16)
    result = middle + jnp.dot(hidden, whole_mlp_down, preferred_element_type=jnp.float32)
    block_out = result.astype(jnp.bfloat16)
    back_mlp_gain, back_mlp_gate, back_mlp_up, back_mlp_down = (
        lax.all_gather(mlp_gain, "seq", axis=0, tiled=True),
        lax.all_gather(mlp_gate, "seq", axis=0, tiled=True),
        lax.all_gather(mlp_up, "seq", axis=0, tiled=True),
        lax.all_gather(mlp_down, "seq", axis=0, tiled=True),
    )
    grad_mlp_down = jnp.einsum("tf,td->fd", hidden, cotangent, preferred_element_type=jnp.float32)
    grad_hidden = jnp.einsum(
        "td,fd->tf", cotangent, back_mlp_down, preferred_element_type=jnp.float32
    )
    unused_act, pull_act = jax.vjp(mlp_act, gate_mlp, up_mlp)
    grad_gate_full, grad_up_full = pull_act(grad_hidden)
    grad_gate_low = grad_gate_full.astype(jnp.bfloat16)
    grad_up_low = grad_up_full.astype(jnp.bfloat16)
    grad_mlp_gate = jnp.einsum(
        "td,tf->df", normed_two, grad_gate_low, preferred_element_type=jnp.float32
    )
    grad_mlp_up = jnp.einsum(
        "td,tf->df", normed_two, grad_up_low, preferred_element_type=jnp.float32
    )
    grad_normed_two = jnp.einsum(
        "tf,df->td", grad_gate_low, back_mlp_gate, preferred_element_type=jnp.float32
    ) + jnp.einsum("tf,df->td", grad_up_low, back_mlp_up, preferred_element_type=jnp.float32)
    unused_norm, pull_norm = jax.vjp(rms_norm, middle, back_mlp_gain.astype(jnp.float32))
    grad_middle_norm, grad_mlp_gain = pull_norm(grad_normed_two)
    mlp_sums = (
        lax.psum_scatter(grad_mlp_gain, "seq", scatter_dimension=0, tiled=True),
        lax.psum_scatter(grad_mlp_gate, "seq", scatter_dimension=0, tiled=True),
        lax.psum_scatter(grad_mlp_up, "seq", scatter_dimension=0, tiled=True),
        lax.psum_scatter(grad_mlp_down, "seq", scatter_dimension=0, tiled=True),
    )
    grad_middle = cotangent.astype(jnp.float32) + grad_middle_norm
    grad_branch = grad_middle.astype(jnp.bfloat16)
    (
        back_norm_gain,
        back_gate_branch,
        back_input_branch,
        back_conv_weight,
        back_conv_bias,
        back_decay_gate,
        back_decay_bias,
        back_input_gate,
        back_input_bias,
        back_decay_param,
        back_out_proj,
    ) = (
        lax.all_gather(norm_gain, "seq", axis=0, tiled=True),
        lax.all_gather(gate_branch, "seq", axis=0, tiled=True),
        lax.all_gather(input_branch, "seq", axis=0, tiled=True),
        lax.all_gather(conv_weight, "seq", axis=1, tiled=True),
        lax.all_gather(conv_bias, "seq", axis=0, tiled=True),
        lax.all_gather(decay_gate, "seq", axis=0, tiled=True),
        lax.all_gather(decay_bias, "seq", axis=0, tiled=True),
        lax.all_gather(input_gate, "seq", axis=0, tiled=True),
        lax.all_gather(input_bias, "seq", axis=0, tiled=True),
        lax.all_gather(decay_param, "seq", axis=0, tiled=True),
        lax.all_gather(out_proj, "seq", axis=0, tiled=True),
    )
    grad_out_proj = jnp.einsum(
        "tr,td->rd", mixed_rows, grad_branch, preferred_element_type=jnp.float32
    )
    grad_mixed = jnp.einsum(
        "td,rd->tr", grad_branch, back_out_proj, preferred_element_type=jnp.float32
    )
    grad_states = grad_mixed * gate_act
    unused_gelu, pull_gelu = jax.vjp(gelu_tanh, gate_pre)
    grad_gate_pre = pull_gelu(grad_mixed * states)[0].astype(jnp.bfloat16)
    shifted_coef = jnp.concatenate([coefficient[1:], jnp.ones((1, lru_width), jnp.float32)], axis=0)
    back_cumulative, back_local = lax.associative_scan(
        combine, (shifted_coef[::-1], grad_states[::-1]), axis=0
    )
    back_cumulative = back_cumulative[::-1]
    back_local = back_local[::-1]
    leaving = prefix(
        (coefficient[0] * back_cumulative[0], coefficient[0] * back_local[0]),
        "seq",
        combine,
        (jnp.ones_like(back_local[0]), jnp.zeros_like(back_local[0])),
        True,
    )
    incoming_adjoint = leaving[1]
    adjoint = back_local + back_cumulative * incoming_adjoint[None, :]
    previous = jnp.concatenate([incoming_state[None, :], states[:-1]], axis=0)

    def terms_only(decay_values, input_values, conv_values, param_values):
        return lru_terms(decay_values, input_values, conv_values, param_values, flag_rows)

    unused_terms, pull_terms = jax.vjp(
        terms_only, decay_pre, input_pre, conv_out, back_decay_param.astype(jnp.float32)
    )
    grad_decay_full, grad_input_full, grad_conv_direct, grad_decay_param = pull_terms(
        (adjoint * previous, adjoint)
    )
    grad_decay_bias = jnp.sum(grad_decay_full, axis=0)
    grad_input_bias = jnp.sum(grad_input_full, axis=0)
    grad_decay_low = grad_decay_full.astype(jnp.bfloat16)
    grad_input_low = grad_input_full.astype(jnp.bfloat16)
    grad_decay_gate = heads_grad(conv_low, grad_decay_low)
    grad_input_gate = heads_grad(conv_low, grad_input_low)
    grad_conv_out = (
        grad_conv_direct
        + heads_back(grad_decay_low, back_decay_gate)
        + heads_back(grad_input_low, back_input_gate)
    )

    def conv_only(padded_values, weight_values, bias_values):
        return conv_local(padded_values, weight_values, bias_values, masks)

    unused_conv, pull_conv = jax.vjp(
        conv_only, padded, back_conv_weight.astype(jnp.float32), back_conv_bias.astype(jnp.float32)
    )
    grad_padded, grad_conv_weight, grad_conv_bias = pull_conv(grad_conv_out)
    returned_rows = passed_along(grad_padded[: CW - 1], "seq", -1)
    addition = jnp.concatenate(
        [
            jnp.zeros((row_count - (CW - 1), lru_width), jnp.float32),
            returned_rows * alive_rows[:, None],
        ],
        axis=0,
    )
    grad_conv_input = (grad_padded[CW - 1 :] + addition).astype(jnp.bfloat16)
    grad_input_branch = jnp.einsum(
        "td,tr->dr", normed, grad_conv_input, preferred_element_type=jnp.float32
    )
    grad_gate_branch = jnp.einsum(
        "td,tr->dr", normed, grad_gate_pre, preferred_element_type=jnp.float32
    )
    grad_normed = jnp.einsum(
        "tr,dr->td", grad_conv_input, back_input_branch, preferred_element_type=jnp.float32
    ) + jnp.einsum("tr,dr->td", grad_gate_pre, back_gate_branch, preferred_element_type=jnp.float32)
    unused_first, pull_first = jax.vjp(rms_norm, values, back_norm_gain.astype(jnp.float32))
    grad_values_norm, grad_norm_gain = pull_first(grad_normed)
    grad_tokens = grad_middle + grad_values_norm
    rec_sums = (
        lax.psum_scatter(grad_norm_gain, "seq", scatter_dimension=0, tiled=True),
        lax.psum_scatter(grad_gate_branch, "seq", scatter_dimension=0, tiled=True),
        lax.psum_scatter(grad_input_branch, "seq", scatter_dimension=0, tiled=True),
        lax.psum_scatter(grad_conv_weight, "seq", scatter_dimension=1, tiled=True),
        lax.psum_scatter(grad_conv_bias, "seq", scatter_dimension=0, tiled=True),
        lax.psum_scatter(grad_decay_gate, "seq", scatter_dimension=0, tiled=True),
        lax.psum_scatter(grad_decay_bias, "seq", scatter_dimension=0, tiled=True),
        lax.psum_scatter(grad_input_gate, "seq", scatter_dimension=0, tiled=True),
        lax.psum_scatter(grad_input_bias, "seq", scatter_dimension=0, tiled=True),
        lax.psum_scatter(grad_decay_param, "seq", scatter_dimension=0, tiled=True),
        lax.psum_scatter(grad_out_proj, "seq", scatter_dimension=0, tiled=True),
    )
    return (
        block_out,
        grad_tokens,
        rec_sums[0],
        rec_sums[1],
        rec_sums[2],
        rec_sums[3],
        rec_sums[4],
        rec_sums[5],
        rec_sums[6],
        rec_sums[7],
        rec_sums[8],
        rec_sums[9],
        rec_sums[10],
        mlp_sums[0],
        mlp_sums[1],
        mlp_sums[2],
        mlp_sums[3],
    )


def solution(mesh):
    in_specs = (
        P("seq", None),
        P("seq"),
        P("seq", None),
        P("seq"),
        P("seq", None),
        P("seq", None),
        P(None, "seq"),
        P("seq"),
        P("seq", None),
        P("seq"),
        P("seq", None),
        P("seq"),
        P("seq"),
        P("seq", None),
        P("seq"),
        P("seq", None),
        P("seq", None),
        P("seq", None),
    )
    out_specs = (
        P("seq", None),
        P("seq", None),
        P("seq"),
        P("seq", None),
        P("seq", None),
        P(None, "seq"),
        P("seq"),
        P("seq", None),
        P("seq"),
        P("seq", None),
        P("seq"),
        P("seq"),
        P("seq", None),
        P("seq"),
        P("seq", None),
        P("seq", None),
        P("seq", None),
    )
    return jax.shard_map(body, mesh=mesh, in_specs=in_specs, out_specs=out_specs, check_vma=False)
```

profile of v0, /device:TPU:0, one launch (start us, length us, event | category | flops | bytes accessed | tf_op | source)
XLA Modules:
  0.0 3586.0 jit_solution(16548466024227957304)
XLA Ops:
  12.9 43.0 %all-reduce.89 = (bf16[2560]{0:T(1024)(128)(2,1)S(1)}, bf16[2048]{0:T(1024)(128)(2,1)S(1)}, bf16[2560]{0:T(1024)(128)(2,1)S(1)}, bf16[2560]{0:T(1024)(128)(2,1)S...) all-reduce(bf16[2560]{0:T(1024)(128)(2,1)S(1)} %dynamic-update-slic, ...), channel_id=1, replica_groups=mesh['seq'=32] {'seq'}, use_global_device_ids=true, to_apply=%add.79 | all-reduce | flops 14336 | bytes 57344
  56.4 40.9 %all-gather = bf16[32,80,4]{1,2,0:T(4,128)(2,1)S(1)} all-gather(bf16[1,80,4]{1,2,0:T(4,128)(2,1)S(1)} %bitcast.122), channel_id=1, replica_groups=mesh['seq'=32] {'seq'}, dimensions={0}, use_global_device_ids=true | all-gather | bytes 21120 | tf_op jit(solution)/shard_map/all_gather | solution.py:156
  98.5 41.5 %all_gather.75 = bf16[2560,160]{1,0:T(8,128)(2,1)S(1)} all-gather(bf16[80,160]{1,0:T(8,128)(2,1)S(1)} %copy-done.119), channel_id=1, replica_groups=mesh['seq'=32] {'seq'}, dimensions={0}, use_global_device_ids=true | all-gather | bytes 844800 | tf_op jit(solution)/shard_map/all_gather | solution.py:158
  140.0 49.1 %all_gather.78 = bf16[2560,160]{1,0:T(8,128)(2,1)} all-gather(bf16[80,160]{1,0:T(8,128)(2,1)S(1)} %copy-done.120), channel_id=1, replica_groups=mesh['seq'=32] {'seq'}, dimensions={0}, use_global_device_ids=true | all-gather | bytes 844800 | tf_op jit(solution)/shard_map/all_gather | solution.py:160
  377.1 9.3 pad.239
  387.3 41.8 %all-gather.2 = f32[32,1,2560]{2,1,0:T(1,128)S(1)} all-gather(f32[1,1,2560]{2,1,0:T(1,128)S(1)} %add_bitcast_fusion), channel_id=1, replica_groups=mesh['seq'=32] {'seq'}, dimensions={0}, use_global_device_ids=true | all-gather | bytes 337920 | tf_op jit(solution)/shard_map/all_gather | solution.py:22
  431.6 9.2 pad.254
  446.3 38.4 %all-gather.1 = f32[32,1,2560]{2,1,0:T(1,128)S(1)} all-gather(f32[1,1,2560]{2,1,0:T(1,128)S(1)} %add_bitcast_fusion.1), channel_id=1, replica_groups=mesh['seq'=32] {'seq'}, dimensions={0}, use_global_device_ids=true | all-gather | bytes 337920 | tf_op jit(solution)/shard_map/all_gather | solution.py:22
  484.8 10.8 slice.655
  495.6 10.9 slice.662
  517.2 12.8 multiply_convert_fusion.2
  530.0 8.4 multiply_reduce_fusion.7
  538.7 15.3 fusion.97
  554.0 51.1 %all-gather.20.cloned.1.call-done = bf16[2048,6144]{1,0:T(8,128)(2,1)} async-done(((bf16[64,6144]{1,0:T(8,128)(2,1)}), bf16[2048,6144]{1,0:T(8,128)(2,1)}) %all-gather.20.cloned.1.call-update) | async-done | bytes 25165840 | tf_op jit(solution)/shard_map/all_gather | solution.py:203
  605.1 14.2 fusion.98
  619.3 141.3 %all-gather.22.cloned.1.call-done = bf16[6144,2048]{1,0:T(8,128)(2,1)} async-done(((bf16[192,2048]{1,0:T(8,128)(2,1)}), bf16[6144,2048]{1,0:T(8,128)(2,1)}) %all-gather.22.cloned.1.call-update) | async-done | bytes 25165840 | tf_op jit(solution)/shard_map/all_gather | solution.py:204
  760.6 21.9 multiply_convert_fusion
  782.6 13.5 fusion.99
  796.1 15.3 multiply_reduce_fusion.5
  814.6 9.5 fusion.32
  830.5 10.7 slice.657
  841.2 10.7 slice.659
  937.7 9.1 pad.287
  960.4 9.1 pad.271
  969.6 10.8 slice.715
  991.2 9.4 pad.286
  1007.1 39.4 %all-gather.4 = f32[32,1,2560]{2,1,0:T(1,128)S(1)} all-gather(f32[1,1,2560]{2,1,0:T(1,128)S(1)} %get-tuple-element.354), channel_id=1, replica_groups=mesh['seq'=32] {'seq'}, dimensions={0}, use_global_device_ids=true | all-gather | bytes 337920 | tf_op jit(solution)/shard_map/all_gather | solution.py:22
  1046.5 37.5 %all-gather.3 = f32[32,1,2560]{2,1,0:T(1,128)S(1)} all-gather(f32[1,1,2560]{2,1,0:T(1,128)S(1)} %get-tuple-element.355), channel_id=1, replica_groups=mesh['seq'=32] {'seq'}, dimensions={0}, use_global_device_ids=true | all-gather | bytes 337920 | tf_op jit(solution)/shard_map/all_gather | solution.py:22
  1087.9 13.1 rev.14
  1101.1 21.0 rev.13
  1151.5 9.4 multiply_reduce_fusion.4
  1170.1 10.3 fusion.37
  1182.1 8.9 fusion.77
  1198.5 8.8 fusion.43
  1208.6 21.4 fusion.103
  1230.0 21.4 fusion.104
  1252.6 21.5 fusion.105
  1280.7 13.1 fusion.20
  1293.9 8.7 fusion.24
  1302.6 40.6 %all-reduce.88 = (f32[2048]{0:T(1024)S(1)}, f32[2560]{0:T(1024)S(1)}, f32[2560]{0:T(1024)S(1)}, f32[2560]{0:T(1024)S(1)}, f32[2560]{0:T(1024)S(1)}, /*index=5*/f32[2048]{0:T(1024)S(1)}) all-reduce(f32[2048]{0:T(1024)S(1)} %get-tuple-element.289, f32[2560]{0:T(1024)S(1)} %copy-done.97, ...), channel_id=2, replica_groups=mesh['seq'=32] {'seq'}, use_global_device_ids=true, to_apply=%region_10.11.clone | all-reduce | flops 14336 | bytes 114688
  1351.5 81.0 %reduce-scatter.16.cloned.1.call-done = f32[80,160]{1,0:T(8,128)} async-done(((f32[2560,160]{1,0:T(8,128)}), f32[80,160]{1,0:T(8,128)}) %reduce-scatter.16.cloned.1.call-update) | async-done | bytes 51216 | tf_op jit(solution)/shard_map/reduce_scatter | solution.py:352
  1432.5 136.4 %reduce-scatter.18.cloned.1.call-done = f32[80,160]{1,0:T(8,128)} async-done(((f32[2560,160]{1,0:T(8,128)}), f32[80,160]{1,0:T(8,128)}) %reduce-scatter.18.cloned.1.call-update) | async-done | bytes 51216 | tf_op jit(solution)/shard_map/reduce_scatter | solution.py:354
  1568.9 224.2 %reduce-scatter.20.cloned.1.call-done = f32[80,2048]{1,0:T(8,128)} async-done(((f32[2560,2048]{1,0:T(8,128)}), f32[80,2048]{1,0:T(8,128)}) %reduce-scatter.20.cloned.1.call-update) | async-done | bytes 655376 | tf_op jit(solution)/shard_map/reduce_scatter | solution.py:357
  1793.1 232.6 %reduce-scatter.12.cloned.1.call-done = f32[64,2560]{1,0:T(8,128)} async-done(((f32[2048,2560]{1,0:T(8,128)}), f32[64,2560]{1,0:T(8,128)}) %reduce-scatter.12.cloned.1.call-update) | async-done | bytes 655376 | tf_op jit(solution)/shard_map/reduce_scatter | solution.py:348
  2025.7 232.4 %reduce-scatter.14.cloned.1.call-done = f32[64,2560]{1,0:T(8,128)} async-done(((f32[2048,2560]{1,0:T(8,128)}), f32[64,2560]{1,0:T(8,128)}) %reduce-scatter.14.cloned.1.call-update) | async-done | bytes 655376 | tf_op jit(solution)/shard_map/reduce_scatter | solution.py:349
  2258.1 444.0 %reduce-scatter.22.cloned.1.call-done = f32[64,6144]{1,0:T(8,128)} async-done(((f32[2048,6144]{1,0:T(8,128)}), f32[64,6144]{1,0:T(8,128)}) %reduce-scatter.22.cloned.1.call-update) | async-done | bytes 1572880 | tf_op jit(solution)/shard_map/reduce_scatter | solution.py:240
  2702.2 438.6 %reduce-scatter.24.cloned.1.call-done = f32[64,6144]{1,0:T(8,128)} async-done(((f32[2048,6144]{1,0:T(8,128)}), f32[64,6144]{1,0:T(8,128)}) %reduce-scatter.24.cloned.1.call-update) | async-done | bytes 1572880 | tf_op jit(solution)/shard_map/reduce_scatter | solution.py:241
  3140.8 438.6 %reduce-scatter.26.cloned.1.call-done = f32[192,2048]{1,0:T(8,128)} async-done(((f32[6144,2048]{1,0:T(8,128)}), f32[192,2048]{1,0:T(8,128)}) %reduce-scatter.26.cloned.1.call-update) | async-done | bytes 1572880 | tf_op jit(solution)/shard_map/reduce_scatter | solution.py:242
  (799 shorter events, 413.4 us)
Async XLA Ops:
  7.3 48.6 %copy-start.139 = (s32[256]{0:T(256)S(1)}, s32[256]{0:T(256)}, u32[]{:S(2)}) copy-start(s32[256]{0:T(256)} %param.23) | copy-start | bytes 3076
  7.3 49.1 %copy-start.140 = (bf16[4,80]{1,0:T(4,128)(2,1)S(1)}, bf16[4,80]{1,0:T(4,128)(2,1)}, u32[]{:S(2)}) copy-start(bf16[4,80]{1,0:T(4,128)(2,1)} %param.28) | copy-start | bytes 1924
  7.3 90.2 %copy-start.6 = (bf16[256,2048]{1,0:T(8,128)(2,1)S(1)}, bf16[256,2048]{1,0:T(8,128)(2,1)}, u32[]{:S(2)}) copy-start(bf16[256,2048]{1,0:T(8,128)(2,1)} %param.22) | copy-start | bytes 3145732
  7.3 91.2 %copy-start.119 = (bf16[80,160]{1,0:T(8,128)(2,1)S(1)}, bf16[80,160]{1,0:T(8,128)(2,1)}, u32[]{:S(2)}) copy-start(bf16[80,160]{1,0:T(8,128)(2,1)} %param.30) | copy-start | bytes 76804
  7.3 181.8 %all-gather.12.cloned.1.call-start = ((), (), s32[]{:S(2)}) async-start(), calls=%async_computation.9 | async-start | bytes 10813440 | tf_op jit(solution)/shard_map/all_gather | solution.py:155
  8.0 509.2 %all-gather.14.cloned.1.call-start = ((), (), s32[]{:S(2)}) async-start(), calls=%async_computation.10 | async-start | bytes 10813440 | tf_op jit(solution)/shard_map/all_gather | solution.py:154
  8.8 521.2 %all-gather.16.cloned.1.call-start = ((), (), s32[]{:S(2)}) async-start(), calls=%async_computation.11 | async-start | bytes 10813440 | tf_op jit(solution)/shard_map/all_gather | solution.py:163
  9.5 130.5 %copy-start.120 = (bf16[80,160]{1,0:T(8,128)(2,1)S(1)}, bf16[80,160]{1,0:T(8,128)(2,1)}, u32[]{:S(2)}) copy-start(bf16[80,160]{1,0:T(8,128)(2,1)} %param.32) | copy-start | bytes 76804
  9.5 529.2 %all-gather.18.cloned.1.call-start = ((), (), s32[]{:S(2)}) async-start(), calls=%async_computation.12 | async-start | bytes 25952256 | tf_op jit(solution)/shard_map/all_gather | solution.py:202
  10.1 595.0 %all-gather.20.cloned.1.call-start = ((), (), s32[]{:S(2)}) async-start(), calls=%async_computation.13 | async-start | bytes 25952256 | tf_op jit(solution)/shard_map/all_gather | solution.py:203
  10.7 749.9 %all-gather.22.cloned.1.call-start = ((), (), s32[]{:S(2)}) async-start(), calls=%async_computation.14 | async-start | bytes 25952256 | tf_op jit(solution)/shard_map/all_gather | solution.py:204
  11.3 1338.9 %reduce-scatter.28.cloned.1.call-start = ((), (), s32[]{:S(2)}) async-start(), calls=%async_computation.23 | async-start | bytes 1351680
  55.9 140.1 %copy-start.130 = (bf16[2560]{0:T(1024)(128)(2,1)}, bf16[2560]{0:T(1024)(128)(2,1)S(1)}, u32[]{:S(2)}) copy-start(bf16[2560]{0:T(1024)(128)(2,1)S(1)} %get-tuple-element.322) | copy-start | bytes 15364
  55.9 461.3 %copy-start.58 = (f32[2048]{0:T(1024)}, f32[2048]{0:T(1024)S(1)}, u32[]{:S(2)}) copy-start(f32[2048]{0:T(1024)S(1)} %convert_element_type.91) | copy-start | bytes 24580
  55.9 164.0 %copy-start.128 = (f32[256]{0:T(256)}, f32[256]{0:T(256)S(1)}, u32[]{:S(2)}) copy-start(f32[256]{0:T(256)S(1)} %convert_element_type.88) | copy-start | bytes 3076
  56.4 139.6 %copy-start.147 = (f32[2]{0:T(128)}, f32[2]{0:T(128)S(1)}, u32[]{:S(2)}) copy-start(f32[2]{0:T(128)S(1)} %slice.564) | copy-start | bytes 28
  97.8 98.3 %copy-start.136 = (f32[256]{0:T(256)}, f32[256]{0:T(256)S(1)}, u32[]{:S(2)}) copy-start(f32[256]{0:T(256)S(1)} %fusion.27) | copy-start | bytes 3076
  97.8 419.4 %copy-start.86 = (f32[256]{0:T(256)}, f32[256]{0:T(256)S(1)}, u32[]{:S(2)}) copy-start(f32[256]{0:T(256)S(1)} %fusion.70) | copy-start | bytes 3076
  97.9 104.2 %copy-start.132 = (f32[256]{0:T(256)}, f32[256]{0:T(256)S(1)}, u32[]{:S(2)}) copy-start(f32[256]{0:T(256)S(1)} %get-tuple-element.337) | copy-start | bytes 3076
  97.9 104.3 %copy-start.134 = (f32[256]{0:T(256)}, f32[256]{0:T(256)S(1)}, u32[]{:S(2)}) copy-start(f32[256]{0:T(256)S(1)} %get-tuple-element.338) | copy-start | bytes 3076
  97.9 122.0 %copy-start.93 = (f32[256]{0:T(256)}, f32[256]{0:T(256)S(1)}, u32[]{:S(2)}) copy-start(f32[256]{0:T(256)S(1)} %get-tuple-element.426) | copy-start | bytes 3076
  98.5 121.4 %copy-start.69 = (f32[2560]{0:T(1024)}, f32[2560]{0:T(1024)S(1)}, u32[]{:S(2)}) copy-start(f32[2560]{0:T(1024)S(1)} %get-tuple-element.425) | copy-start | bytes 30724
  140.0 67.2 %copy-start.19 = (bf16[2560,160]{1,0:T(8,128)(2,1)}, bf16[2560,160]{1,0:T(8,128)(2,1)S(1)}, u32[]{:S(2)}) copy-start(bf16[2560,160]{1,0:T(8,128)(2,1)S(1)} %all_gather.75) | copy-start | bytes 2457604
  197.2 3.2 collective-permute-start
  377.1 54.5 %copy-start.30 = (f32[256,2560]{1,0:T(8,128)}, f32[256,2560]{1,0:T(8,128)S(1)}, u32[]{:S(2)}) copy-start(f32[256,2560]{1,0:T(8,128)S(1)} %pad.238) | copy-start | bytes 7864324
  377.1 52.0 %copy-start.125 = (f32[1,2560]{1,0:T(1,128)S(1)}, f32[1,2560]{1,0:T(1,128)}, u32[]{:S(2)}) copy-start(f32[1,2560]{1,0:T(1,128)} %slice.770) | copy-start | bytes 30724
  445.3 39.5 %copy-start.31 = (f32[256,2560]{1,0:T(8,128)}, f32[256,2560]{1,0:T(8,128)S(1)}, u32[]{:S(2)}) copy-start(f32[256,2560]{1,0:T(8,128)S(1)} %pad.255) | copy-start | bytes 7864324
  495.6 21.6 copy-start.7
  538.4 273.0 %copy-start.37 = (f32[256,2048]{1,0:T(8,128)}, f32[256,2048]{1,0:T(8,128)S(1)}, u32[]{:S(2)}) copy-start(f32[256,2048]{1,0:T(8,128)S(1)} %get-tuple-element.429) | copy-start | bytes 6291460
  538.7 66.4 %copy-start.16 = (bf16[256,2048]{1,0:T(8,128)(2,1)}, bf16[256,2048]{1,0:T(8,128)(2,1)S(1)}, u32[]{:S(2)}) copy-start(bf16[256,2048]{1,0:T(8,128)(2,1)S(1)} %multiply_convert_fusion.3) | copy-start | bytes 3145732
  1005.3 78.8 %copy-start.64 = (f32[2560]{0:T(1024)S(1)}, f32[2560]{0:T(1024)}, u32[]{:S(2)}) copy-start(f32[2560]{0:T(1024)} %custom-call.1) | copy-start | bytes 30724
  1005.3 82.7 %copy-start.34 = (f32[256,2560]{1,0:T(8,128)S(1)}, f32[256,2560]{1,0:T(8,128)}, u32[]{:S(2)}) copy-start(f32[256,2560]{1,0:T(8,128)} %add.656) | copy-start | bytes 7864324
  1101.1 21.1 copy-start.63
  1101.1 21.1 copy-start.68
  1101.1 21.1 copy-start.70
  1101.1 21.1 copy-start.94
  1101.1 21.1 copy-start.129
  1162.6 269.9 %reduce-scatter.16.cloned.1.call-start = ((), (), s32[]{:S(2)}) async-start(), calls=%async_computation.17 | async-start | bytes 2703360 | tf_op jit(solution)/shard_map/reduce_scatter | solution.py:352
  1165.2 403.8 %reduce-scatter.18.cloned.1.call-start = ((), (), s32[]{:S(2)}) async-start(), calls=%async_computation.18 | async-start | bytes 2703360 | tf_op jit(solution)/shard_map/reduce_scatter | solution.py:354
  1168.5 624.6 %reduce-scatter.20.cloned.1.call-start = ((), (), s32[]{:S(2)}) async-start(), calls=%async_computation.19 | async-start | bytes 21626880 | tf_op jit(solution)/shard_map/reduce_scatter | solution.py:357
  1180.5 845.2 %reduce-scatter.12.cloned.1.call-start = ((), (), s32[]{:S(2)}) async-start(), calls=%async_computation.15 | async-start | bytes 21626880 | tf_op jit(solution)/shard_map/reduce_scatter | solution.py:348
  1191.0 1067.1 %reduce-scatter.14.cloned.1.call-start = ((), (), s32[]{:S(2)}) async-start(), calls=%async_computation.16 | async-start | bytes 21626880 | tf_op jit(solution)/shard_map/reduce_scatter | solution.py:349
  1194.6 3.1 collective-permute-start.1
  1207.4 1494.8 %reduce-scatter.22.cloned.1.call-start = ((), (), s32[]{:S(2)}) async-start(), calls=%async_computation.20 | async-start | bytes 51904512 | tf_op jit(solution)/shard_map/reduce_scatter | solution.py:240
  1230.0 1910.8 %reduce-scatter.24.cloned.1.call-start = ((), (), s32[]{:S(2)}) async-start(), calls=%async_computation.21 | async-start | bytes 51904512 | tf_op jit(solution)/shard_map/reduce_scatter | solution.py:241
  1251.4 2327.9 %reduce-scatter.26.cloned.1.call-start = ((), (), s32[]{:S(2)}) async-start(), calls=%async_computation.22 | async-start | bytes 51904512 | tf_op jit(solution)/shard_map/reduce_scatter | solution.py:242
  1293.8 52.8 %copy-start.137 = (f32[256]{0:T(256)S(1)}, f32[256]{0:T(256)}, u32[]{:S(2)}) copy-start(f32[256]{0:T(256)} %copy-done.136) | copy-start | bytes 3076
  1293.8 52.8 %copy-start.15 = (f32[256,2048]{1,0:T(8,128)S(1)}, f32[256,2048]{1,0:T(8,128)}, u32[]{:S(2)}) copy-start(f32[256,2048]{1,0:T(8,128)} %copy-done.13) | copy-start | bytes 6291460
  (118 other events, 586.6 us)
Sparse Core Ops, SparseCore 0:
  11.0 91.3 all-gather.11
  105.2 94.1 all-gather.13
  202.2 87.2 all-gather.15
  292.3 156.1 all-gather.17
  451.2 153.8 all-gather.19
  607.8 152.7 all-gather.21
  1162.7 132.9 reduce-scatter.27
  1298.6 133.8 reduce-scatter.15
  1435.5 133.4 reduce-scatter.17
  1571.8 221.2 reduce-scatter.19
  1796.1 229.5 reduce-scatter.11
  2028.5 229.5 reduce-scatter.13
  2266.3 435.8 reduce-scatter.21
  2710.1 430.5 reduce-scatter.23
  3148.7 430.5 reduce-scatter.25
where the time goes:
time: 3600 us; the launch traced here: 3590 us
  waiting for transfers between devices  2430 us (68%)
  local copies, waits for them, and re-layouts  402 us (11%)
  blocking collectives  372 us (10%)
  matrix products  253 us (7%)
  other arithmetic  111 us (3%)
    reduce_scatter x1, waiting for transfers between devices, body(): lax.psum_scatter(grad_mlp_gate, 'seq', scatter_dimension=0, tiled=True)  444 us
    reduce_scatter x1, waiting for transfers between devices, body(): lax.psum_scatter(grad_mlp_up, 'seq', scatter_dimension=0, tiled=True)  439 us
    reduce_scatter x1, waiting for transfers between devices, body(): lax.psum_scatter(grad_mlp_down, 'seq', scatter_dimension=0, tiled=True)  439 us
    reduce_scatter x1, waiting for transfers between devices, body(): lax.psum_scatter(grad_gate_branch, 'seq', scatter_dimension=0, tiled=True)  233 us
    reduce_scatter x1, waiting for transfers between devices, body(): lax.psum_scatter(grad_input_branch, 'seq', scatter_dimension=0, tiled=True)  232 us
    reduce_scatter x1, waiting for transfers between devices, body(): lax.psum_scatter(grad_out_proj, 'seq', scatter_dimension=0, tiled=True)  224 us
    all_gather x4, blocking collectives, prefix(): everything = jax.tree.map(lambda part: lax.all_gather(part, axis), value)  157 us
    all_gather x1, waiting for transfers between devices, body(): lax.all_gather(mlp_down, 'seq', axis=0, tiled=True)  141 us
  transfers between devices with their start and end apart: 17, of which 12 were waited for; matrix products, arithmetic and copies ran while one was open for 12% of the time, Pallas kernels for 0%

commit v1 on v0

--- a/solution.py
+++ b/solution.py
@@ -1,6 +1,10 @@
+import functools
+
 import jax
 import jax.numpy as jnp
 from jax import lax
+from jax.experimental import pallas as pl
+from jax.experimental.pallas import tpu as pltpu
 from jax.sharding import PartitionSpec as P
 
 H = 16
@@ -117,7 +121,7 @@
     return gelu_tanh(gate_values) * up_values
 
 
-def body(
+def token_split_body(
     tokens,
     starts,
     cotangent,
@@ -377,6 +381,777 @@
     )
 
 
+CHIPS = 4
+MESH = pl.DeviceIdType.MESH
+
+
+def place():
+    me = lax.axis_index("seq")
+    core = lax.rem(me, 2)
+    x = lax.rem(lax.div(me, 2), 2)
+    y = lax.rem(lax.div(me, 4), 2)
+    return me, lax.div(me, 8), 2 * y + x, core, x, y
+
+
+def column_groups(n):
+    return [[8 * z + 2 * p + c for c in range(2) for z in range(n // 8)] for p in range(CHIPS)]
+
+
+def line_groups(n):
+    return [[8 * z + r for z in range(n // 8)] for r in range(8)]
+
+
+def greet(devices):
+    barrier = pltpu.get_barrier_semaphore()
+    for device in devices:
+        pl.semaphore_signal(barrier, inc=1, device_id=(device,), device_id_type=MESH)
+    pl.semaphore_wait(barrier, len(devices))
+
+
+def remote(source, target, send_sem, recv_sem, device):
+    return pltpu.make_async_remote_copy(
+        src_ref=source,
+        dst_ref=target,
+        send_sem=send_sem,
+        recv_sem=recv_sem,
+        device_id=(device,),
+        device_id_type=MESH,
+    )
+
+
+def comm_params(collective_id, vmem_mib=None):
+    return pltpu.CompilerParams(
+        collective_id=collective_id,
+        has_side_effects=True,
+        vmem_limit_bytes=None if vmem_mib is None else vmem_mib * 2**20,
+    )
+
+
+ANY = pl.BlockSpec(memory_space=pl.ANY)
+VMEM = pl.BlockSpec(memory_space=pltpu.VMEM)
+
+
+def plane_gather_kernel(x_ref, o_ref, send, recv, local):
+    me, z, p, c, x, y = place()
+    x_dev, y_dev = me + 2 - 4 * x, me + 4 - 8 * y
+    p_x, p_y = p + 1 - 2 * x, p + 2 - 4 * y
+    greet((x_dev, y_dev))
+    half = x_ref.shape[0] // 2
+    to_x = remote(x_ref, o_ref.at[p], send.at[0], recv.at[0], x_dev)
+    to_y = remote(x_ref, o_ref.at[p], send.at[1], recv.at[1], y_dev)
+    to_x.start()
+    to_y.start()
+    own = pltpu.make_async_copy(x_ref, o_ref.at[p], local)
+    own.start()
+    to_x.wait_recv()
+    first = o_ref.at[p_x, pl.ds(0, half)]
+    on_y = remote(first, first, send.at[2], recv.at[2], y_dev)
+    on_y.start()
+    to_y.wait_recv()
+    second = o_ref.at[p_y, pl.ds(half, half)]
+    on_x = remote(second, second, send.at[3], recv.at[3], x_dev)
+    on_x.start()
+    to_x.wait_send()
+    to_y.wait_send()
+    on_y.wait()
+    on_x.wait()
+    own.wait()
+
+
+def plane_gather(block, collective_id):
+    return pl.pallas_call(
+        plane_gather_kernel,
+        out_shape=jax.ShapeDtypeStruct((CHIPS,) + block.shape, block.dtype),
+        in_specs=[ANY],
+        out_specs=ANY,
+        scratch_shapes=[
+            pltpu.SemaphoreType.DMA((4,)),
+            pltpu.SemaphoreType.DMA((4,)),
+            pltpu.SemaphoreType.DMA,
+        ],
+        compiler_params=comm_params(collective_id),
+        name="plane_gather",
+    )(block)
+
+
+def plane_swap_kernel(count, *refs):
+    ins, outs = refs[:count], refs[count : 2 * count]
+    send, recv, local = refs[2 * count :]
+    me, z, p, c, x, y = place()
+    x_dev, y_dev = me + 2 - 4 * x, me + 4 - 8 * y
+    d_dev = y_dev + 2 - 4 * x
+    p_x, p_y, p_d = p + 1 - 2 * x, p + 2 - 4 * y, 3 - p
+    peers = ((x_dev, p_x), (y_dev, p_y), (d_dev, p_d))
+    greet([device for device, unused in peers])
+    copies = []
+    for k in range(count):
+        for j, (device, chip) in enumerate(peers):
+            copies.append(remote(ins[k].at[chip], outs[k].at[p], send.at[k, j], recv.at[k, j], device))
+        copies.append(pltpu.make_async_copy(ins[k].at[p], outs[k].at[p], local.at[k]))
+    for copy in copies:
+        copy.start()
+    for copy in copies:
+        copy.wait()
+
+
+def plane_swap(arrays, collective_id):
+    count = len(arrays)
+    return pl.pallas_call(
+        functools.partial(plane_swap_kernel, count),
+        out_shape=[jax.ShapeDtypeStruct(a.shape, a.dtype) for a in arrays],
+        in_specs=[ANY] * count,
+        out_specs=[ANY] * count,
+        scratch_shapes=[
+            pltpu.SemaphoreType.DMA((count, 3)),
+            pltpu.SemaphoreType.DMA((count, 3)),
+            pltpu.SemaphoreType.DMA((count,)),
+        ],
+        compiler_params=comm_params(collective_id),
+        name="plane_swap",
+    )(*arrays)
+
+
+def plane_sum_kernel(part, out, own, from_x, from_y, diag_x, diag_y, on_x, on_y, send, recv, local):
+    me, z, p, c, x, y = place()
+    x_dev, y_dev = me + 2 - 4 * x, me + 4 - 8 * y
+    p_x, p_y, p_d = p + 1 - 2 * x, p + 2 - 4 * y, 3 - p
+    greet((x_dev, y_dev))
+    rows = part.shape[1]
+    half = rows // 2
+    low, high = pl.ds(0, half), pl.ds(half, half)
+    copies = [
+        remote(part.at[p_d, low], diag_x, send.at[0], recv.at[0], x_dev),
+        remote(part.at[p_d, high], diag_y, send.at[1], recv.at[1], y_dev),
+        remote(part.at[p_x, low], from_x.at[low], send.at[2], recv.at[2], x_dev),
+        remote(part.at[p_y, high], from_y.at[high], send.at[3], recv.at[3], y_dev),
+    ]
+    for copy in copies:
+        copy.start()
+    locals_ = [
+        pltpu.make_async_copy(part.at[p_y, low], on_y, local.at[0]),
+        pltpu.make_async_copy(part.at[p_x, high], on_x, local.at[1]),
+        pltpu.make_async_copy(part.at[p], own, local.at[2]),
+    ]
+    for copy in locals_:
+        copy.start()
+
+    def add_into(target, addend):
+        @pl.loop(0, half // 16)
+        def add_rows(i):
+            at = pl.ds(pl.multiple_of(i * 16, 16), 16)
+            target[at, :] = (
+                target[at, :].astype(jnp.float32) + addend[at, :].astype(jnp.float32)
+            ).astype(target.dtype)
+
+    locals_[0].wait()
+    copies[0].wait_recv()
+    add_into(on_y, diag_x)
+    to_y = remote(on_y, from_y.at[low], send.at[4], recv.at[4], y_dev)
+    to_y.start()
+    locals_[1].wait()
+    copies[1].wait_recv()
+    add_into(on_x, diag_y)
+    to_x = remote(on_x, from_x.at[high], send.at[5], recv.at[5], x_dev)
+    to_x.start()
+    locals_[2].wait()
+    copies[2].wait_recv()
+    copies[3].wait_recv()
+    to_y.wait()
+    to_x.wait()
+    for copy in copies:
+        copy.wait_send()
+
+    @pl.loop(0, rows // 16)
+    def sum_rows(i):
+        at = pl.ds(pl.multiple_of(i * 16, 16), 16)
+        out[at, :] = (
+            own[at, :].astype(jnp.float32)
+            + from_x[at, :].astype(jnp.float32)
+            + from_y[at, :].astype(jnp.float32)
+        )
+
+
+def plane_sum(parts, collective_id):
+    unused, rows, columns = parts.shape
+    whole, part = (rows, columns), (rows // 2, columns)
+    return pl.pallas_call(
+        plane_sum_kernel,
+        out_shape=jax.ShapeDtypeStruct(whole, jnp.float32),
+        in_specs=[ANY],
+        out_specs=VMEM,
+        scratch_shapes=[
+            pltpu.VMEM(whole, parts.dtype),
+            pltpu.VMEM(whole, parts.dtype),
+            pltpu.VMEM(whole, parts.dtype),
+            pltpu.VMEM(part, parts.dtype),
+            pltpu.VMEM(part, parts.dtype),
+            pltpu.VMEM(part, parts.dtype),
+            pltpu.VMEM(part, parts.dtype),
+            pltpu.SemaphoreType.DMA((6,)),
+            pltpu.SemaphoreType.DMA((6,)),
+            pltpu.SemaphoreType.DMA((3,)),
+        ],
+        compiler_params=comm_params(collective_id, 32),
+        name="plane_sum",
+    )(parts)
+
+
+def small_gather_kernel(planes, x_ref, o_ref, send, recv):
+    me, z, p, c, x, y = place()
+    r = lax.rem(me, 8)
+    base = me - r
+    near = [base + lax.rem(r + d, 8) for d in range(1, 8)]
+    far = [8 * lax.rem(z + d, planes) + r for d in range(1, planes)]
+    greet(near + far)
+    o_ref[z, r] = x_ref[...]
+    copies = [
+        remote(x_ref, o_ref.at[z, r], send.at[d], recv.at[d], device) for d, device in enumerate(near)
+    ]
+    for copy in copies:
+        copy.start()
+    for copy in copies:
+        copy.wait()
+    copies = [
+        remote(o_ref.at[z], o_ref.at[z], send.at[7 + d], recv.at[7 + d], device)
+        for d, device in enumerate(far)
+    ]
+    for copy in copies:
+        copy.start()
+    for copy in copies:
+        copy.wait()
+
+
+def small_gather(block, collective_id):
+    planes = lax.axis_size("seq") // 8
+    return pl.pallas_call(
+        functools.partial(small_gather_kernel, planes),
+        out_shape=jax.ShapeDtypeStruct((planes, 8) + block.shape, block.dtype),
+        in_specs=[VMEM],
+        out_specs=VMEM,
+        scratch_shapes=[
+            pltpu.SemaphoreType.DMA((6 + planes,)),
+            pltpu.SemaphoreType.DMA((6 + planes,)),
+        ],
+        compiler_params=comm_params(collective_id),
+        name="small_gather",
+    )(block)
+
+
+def small_sum_kernel(planes, x_ref, o_ref, lines, line, near_parts, send, recv):
+    me, z, p, c, x, y = place()
+    r = lax.rem(me, 8)
+    base = me - r
+    near = [(lax.rem(r + d, 8), base + lax.rem(r + d, 8)) for d in range(1, 8)]
+    far = [(lax.rem(z + d, planes), 8 * lax.rem(z + d, planes) + r) for d in range(1, planes)]
+    greet([device for unused, device in near + far])
+    copies = [
+        remote(x_ref.at[there], lines.at[d], send.at[d], recv.at[d], device)
+        for d, (there, device) in enumerate(far)
+    ]
+    for copy in copies:
+        copy.start()
+    for copy in copies:
+        copy.wait()
+    line[...] = x_ref[z] + sum(lines[d] for d in range(planes - 1))
+    copies = [
+        remote(
+            line.at[there], near_parts.at[d], send.at[planes - 1 + d], recv.at[planes - 1 + d], device
+        )
+        for d, (there, device) in enumerate(near)
+    ]
+    for copy in copies:
+        copy.start()
+    for copy in copies:
+        copy.wait()
+    o_ref[...] = line[r] + sum(near_parts[d] for d in range(7))
+
+
+def small_sum(parts, collective_id):
+    planes, unused, rows, lanes = parts.shape
+    return pl.pallas_call(
+        functools.partial(small_sum_kernel, planes),
+        out_shape=jax.ShapeDtypeStruct((rows, lanes), jnp.float32),
+        in_specs=[VMEM],
+        out_specs=VMEM,
+        scratch_shapes=[
+            pltpu.VMEM((planes - 1, 8, rows, lanes), jnp.float32),
+            pltpu.VMEM((8, rows, lanes), jnp.float32),
+            pltpu.VMEM((7, rows, lanes), jnp.float32),
+            pltpu.SemaphoreType.DMA((6 + planes,)),
+            pltpu.SemaphoreType.DMA((6 + planes,)),
+        ],
+        compiler_params=comm_params(collective_id),
+        name="small_sum",
+    )(parts)
+
+
+def carry_kernel(planes, reverse, x_ref, o_ref, everyone, before, send, recv):
+    me, z, p, c, x, y = place()
+    count = 2 * planes
+    q = 2 * z + c
+    peers = []
+    for d in range(1, count):
+        other = lax.rem(q + d, count)
+        peers.append(8 * lax.div(other, 2) + 2 * p + lax.rem(other, 2))
+    greet(peers)
+    everyone[q] = x_ref[...]
+    copies = [
+        remote(x_ref, everyone.at[q], send.at[d], recv.at[d], device) for d, device in enumerate(peers)
+    ]
+    for copy in copies:
+        copy.start()
+    for copy in copies:
+        copy.wait()
+    carried = jnp.zeros((1, x_ref.shape[1]), jnp.float32)
+    order = [(k, j, e) for k in range(planes) for j in range(CHIPS) for e in range(2)]
+    for k, j, e in reversed(order) if reverse else order:
+        before[8 * k + 2 * j + e : 8 * k + 2 * j + e + 1, :] = carried
+        part = everyone.at[2 * k + e]
+        carried = part[j : j + 1, :] * carried + part[CHIPS + j : CHIPS + j + 1, :]
+    for j in range(CHIPS):
+        o_ref[j : j + 1, :] = before[pl.ds(8 * z + 2 * j + c, 1), :]
+
+
+def carry_in(product, last, reverse, collective_id):
+    planes = lax.axis_size("seq") // 8
+    channels = product.shape[1]
+    return pl.pallas_call(
+        functools.partial(carry_kernel, planes, reverse),
+        out_shape=jax.ShapeDtypeStruct((CHIPS, channels), jnp.float32),
+        in_specs=[VMEM],
+        out_specs=VMEM,
+        scratch_shapes=[
+            pltpu.VMEM((2 * planes, 2 * CHIPS, channels), jnp.float32),
+            pltpu.VMEM((8 * planes, channels), jnp.float32),
+            pltpu.SemaphoreType.DMA((2 * planes - 1,)),
+            pltpu.SemaphoreType.DMA((2 * planes - 1,)),
+        ],
+        compiler_params=comm_params(collective_id),
+        name="carry_in",
+    )(jnp.concatenate([product, last], axis=0))
+
+
+def scan_kernel(reverse, coef_ref, drive_ref, cumulative_ref, local_ref):
+    rows, channels = coef_ref.shape[1:]
+    row = lax.broadcasted_iota(jnp.int32, (8, channels), 0)
+
+    def shifted(values, step, fill):
+        if reverse:
+            return jnp.where(row < 8 - step, pltpu.roll(values, 8 - step, 0), fill)
+        return jnp.where(row >= step, pltpu.roll(values, step, 0), fill)
+
+    def tile(i, carry):
+        i = rows // 8 - 1 - i if reverse else i
+        at = pl.ds(pl.multiple_of(i * 8, 8), 8)
+        a, b = coef_ref[0, at, :], drive_ref[0, at, :]
+        for step in (1, 2, 4):
+            b = a * shifted(b, step, 0.0) + b
+            a = a * shifted(a, step, 1.0)
+        before_a, before_b = carry
+        b = a * before_b + b
+        a = a * before_a
+        cumulative_ref[0, at, :] = a
+        local_ref[0, at, :] = b
+        last = slice(0, 1) if reverse else slice(7, 8)
+        return a[last, :], b[last, :]
+
+    lax.fori_loop(
+        0,
+        rows // 8,
+        tile,
+        (jnp.ones((1, channels), jnp.float32), jnp.zeros((1, channels), jnp.float32)),
+    )
+
+
+def block_scan(coefficient, drive, reverse):
+    blocks, rows, channels = coefficient.shape
+    spec = pl.BlockSpec((1, rows, channels), lambda b: (b, 0, 0))
+    return pl.pallas_call(
+        functools.partial(scan_kernel, reverse),
+        grid=(blocks,),
+        out_shape=[jax.ShapeDtypeStruct(coefficient.shape, jnp.float32)] * 2,
+        in_specs=[spec, spec],
+        out_specs=[spec, spec],
+        compiler_params=pltpu.CompilerParams(vmem_limit_bytes=24 * 2**20),
+        name="block_scan",
+    )(coefficient, drive)
+
+
+def regrouped(values, axis, n):
+    shape = values.shape
+    split = shape[:axis] + (n // 2, 2, shape[axis] // n) + shape[axis + 1 :]
+    return jnp.moveaxis(values.reshape(split), axis + 1, axis).reshape(shape)
+
+
+def regrouped_back(values, axis, n):
+    shape = values.shape
+    split = shape[:axis] + (2, n // 2, shape[axis] // n) + shape[axis + 1 :]
+    return jnp.moveaxis(values.reshape(split), axis, axis + 1).reshape(shape)
+
+
+def by_chip(weight, planes):
+    rows, columns = weight.shape
+    split = weight.reshape(rows, planes, CHIPS, 2, columns // (planes * 8))
+    return split.transpose(2, 0, 3, 1, 4).reshape(CHIPS, rows, columns // CHIPS)
+
+
+def from_chips(parts, planes):
+    unused, rows, columns = parts.shape
+    split = parts.reshape(CHIPS, rows, 2, planes, columns // (planes * 2))
+    return split.transpose(1, 3, 0, 2, 4).reshape(rows, CHIPS * columns)
+
+
+def behind(value, *earlier):
+    return lax.optimization_barrier((value, *earlier))[0]
+
+
+def plane_body(
+    tokens,
+    starts,
+    cotangent,
+    norm_gain,
+    gate_branch,
+    input_branch,
+    conv_weight,
+    conv_bias,
+    decay_gate,
+    decay_bias,
+    input_gate,
+    input_bias,
+    decay_param,
+    out_proj,
+    mlp_gain,
+    mlp_gate,
+    mlp_up,
+    mlp_down,
+):
+    f32, bf16 = jnp.float32, jnp.bfloat16
+    n = lax.axis_size("seq")
+    planes = n // 8
+    me, z, p, c, x, y = place()
+    groups = column_groups(n)
+    rows, width = tokens.shape
+    rows_d, lru_width = gate_branch.shape
+    head = decay_gate.shape[1]
+    rows_r, rows_f = out_proj.shape[0], mlp_down.shape[0]
+    channels = lru_width // CHIPS
+    units = mlp_gate.shape[1] // CHIPS
+    half_units = units // 2
+
+    def column_gather(block):
+        return lax.all_gather(block, "seq", axis=0, tiled=True, axis_index_groups=groups)
+
+    def line_sum(parts):
+        return lax.psum_scatter(
+            parts, "seq", scatter_dimension=0, tiled=True, axis_index_groups=line_groups(n)
+        )
+
+    sibling = [(d, d + 1 - 2 * (d % 2)) for d in range(n)]
+
+    def halves(values, axis):
+        half = values.shape[axis] // 2
+        return (
+            lax.dynamic_slice_in_dim(values, c * half, half, axis),
+            lax.dynamic_slice_in_dim(values, (1 - c) * half, half, axis),
+        )
+
+    def plane_permuted(block):
+        whole = lax.dynamic_update_slice_in_dim(
+            jnp.zeros((CHIPS * rows, block.shape[1]), block.dtype), block, p * rows, 0
+        )
+        p_x, p_y, p_d = p + 1 - 2 * x, p + 2 - 4 * y, 3 - p
+        for chip, flip in ((p_x, (1, 0)), (p_y, (0, 1)), (p_d, (1, 1))):
+            route = [
+                (d, d + flip[0] * (2 - 4 * (d // 2 % 2)) + flip[1] * (4 - 8 * (d // 4 % 2))) for d in range(n)
+            ]
+            part = lax.ppermute(block, "seq", route)
+            whole = lax.dynamic_update_slice_in_dim(whole, part, chip * rows, 0)
+        return whole
+
+    def exchanged(values):
+        return lax.ppermute(values, "seq", sibling)
+
+    def product(left, right):
+        return jnp.dot(left, right, preferred_element_type=f32)
+
+    def product_t(left, right):
+        return jnp.einsum("tk,nk->tn", left, right, preferred_element_type=f32)
+
+    def weight_grad(left, right):
+        return jnp.einsum("ta,tb->ab", left, right, preferred_element_type=f32)
+
+    lanes = 128
+
+    def row(values):
+        return jnp.pad(values.astype(f32), (0, lanes - values.shape[0]))[None]
+
+    small = jnp.concatenate(
+        [
+            row(norm_gain),
+            row(mlp_gain),
+            starts.astype(f32).reshape(rows // lanes, lanes),
+            *[row(conv_weight[k]) for k in range(CW)],
+            row(conv_bias),
+            row(decay_bias),
+            row(input_bias),
+            row(decay_param),
+            jnp.zeros((4, lanes), f32),
+        ],
+        axis=0,
+    )
+    weights_in = jnp.concatenate([by_chip(gate_branch, planes), by_chip(input_branch, planes)], axis=2)
+    (swapped_in,) = plane_swap([weights_in], 2)
+    small = small_gather(behind(small, swapped_in), 1)
+    flags = 2 + rows // lanes
+    gain_one = regrouped(small[:, :, 0, :rows_d].reshape(width), 0, n)
+    gain_two = regrouped(small[:, :, 1, :rows_d].reshape(width), 0, n)
+    all_flags = small[:, :, 2:flags].reshape(n * rows)
+    vectors = lax.dynamic_slice_in_dim(
+        small.reshape(planes, CHIPS, 2, 16, lanes), p, 1, axis=1
+    )[:, 0, :, flags : flags + CW + 4, :rows_r]
+    vectors = vectors.transpose(2, 1, 0, 3).reshape(CW + 4, channels)
+    taps = vectors[:CW]
+    bias_conv, bias_decay, bias_input, param = (vectors[CW + k] for k in range(4))
+
+    running = jnp.ones((n * rows,), f32)
+    masks_all = [running]
+    for offset in range(1, CW):
+        earlier = jnp.concatenate([jnp.zeros((offset - 1,), f32), all_flags[: n * rows - (offset - 1)]])
+        running = running * (1.0 - earlier)
+        masks_all.append(running)
+    masks_all = jnp.stack(masks_all).reshape(CW, planes, CHIPS, 2, rows)
+
+    def own_blocks(values):
+        return lax.dynamic_slice(
+            values,
+            (0, z, 0, c, 0),
+            (values.shape[0], 1, CHIPS, 1, values.shape[4]),
+        )[:, 0, :, 0]
+
+    masks = own_blocks(masks_all)
+    after = masks_all[..., : CW - 1].reshape(CW, n, CW - 1)
+    after = jnp.concatenate([after[:, 1:], jnp.zeros((CW, 1, CW - 1), f32)], axis=1)
+    after = own_blocks(after.reshape(CW, planes, CHIPS, 2, CW - 1))
+    flag_rows = own_blocks(all_flags.reshape(1, planes, CHIPS, 2, rows))[0]
+
+    gate_parts, up_parts = by_chip(mlp_gate, planes), by_chip(mlp_up, planes)
+    mlp_pieces = [
+        jnp.concatenate([w[:, :, k * half_units : (k + 1) * half_units] for w in (gate_parts, up_parts)], axis=2)
+        for k in range(2)
+    ]
+    whole_in = column_gather(swapped_in.reshape(CHIPS * rows_d, 2 * channels))
+    rec_rows = column_gather(
+        jnp.concatenate([regrouped(out_proj, 1, n), decay_gate, input_gate], axis=1)
+    )
+    whole_out, gates = rec_rows[:, :width], rec_rows[:, width:]
+    gates = gates.reshape(2, planes, rows_r, 2, 2, rows_r)
+    diagonal = jnp.eye(planes, dtype=bf16)[None, :, None, None, :, None]
+    decay_blocks, input_blocks = (
+        (gates[:, :, :, k, :, None, :] * diagonal).reshape(channels, channels) for k in range(2)
+    )
+
+    values = regrouped(tokens, 1, n).astype(f32)
+    cot = regrouped(cotangent, 1, n)
+    normed = rms_norm(values, gain_one).astype(bf16)
+    normed_all = plane_gather(normed, 3).reshape(CHIPS * rows, width)
+    swapped_mlp = plane_swap(behind(tuple(mlp_pieces), normed_all), 4)
+    whole_down = column_gather(regrouped(mlp_down, 1, n))
+    whole_mlp = [column_gather(part.reshape(CHIPS * rows_d, 2 * half_units)) for part in swapped_mlp]
+    cot_all = plane_permuted(behind(cot, swapped_mlp[0]))
+
+    gate_pre = product(normed_all, whole_in[:, :channels])
+    gate_act = gelu_tanh(gate_pre)
+    conv_input = product(normed_all, whole_in[:, channels:]).astype(bf16)
+    blocks = conv_input.reshape(CHIPS, rows, channels)
+    tails = blocks[:, rows - (CW - 1) :]
+    from_sibling = lax.ppermute(tails, "seq", sibling)
+    from_below = lax.ppermute(
+        tails[CHIPS - 1 :], "seq", [(d, d + 7) for d in range(n - 8) if d % 2 == 1]
+    )
+    before_rows = jnp.where(
+        c == 1, from_sibling, jnp.concatenate([from_below, from_sibling[: CHIPS - 1]], axis=0)
+    )
+    padded = jnp.concatenate([before_rows, blocks], axis=1).astype(f32)
+
+    conv_out = bias_conv + jnp.zeros((CHIPS, rows, channels), f32)
+    for offset in range(CW):
+        lead = CW - 1 - offset
+        conv_out = conv_out + taps[offset] * (padded[:, lead : lead + rows] * masks[offset][:, :, None])
+    conv_out = conv_out.reshape(CHIPS * rows, channels)
+    conv_low = conv_out.astype(bf16)
+    decay_pre = product(conv_low, decay_blocks) + bias_decay
+    input_pre = product(conv_low, input_blocks) + bias_input
+    flat_flags = flag_rows.reshape(CHIPS * rows)
+    coefficient, drive = lru_terms(decay_pre, input_pre, conv_out, param, flat_flags)
+    cube = (CHIPS, rows, channels)
+    cumulative, local_state = block_scan(coefficient.reshape(cube), drive.reshape(cube), False)
+    entering = carry_in(cumulative[:, -1], local_state[:, -1], False, 6)
+    states = local_state + cumulative * entering[:, None, :]
+    flat_states = states.reshape(CHIPS * rows, channels)
+    mixed = (flat_states * gate_act).astype(bf16)
+    branch_parts = product(mixed, whole_out).reshape(CHIPS, rows, width)
+    middle = values + plane_sum(branch_parts, 7)
+    normed_two = rms_norm(middle, gain_two).astype(bf16)
+    two_all = plane_gather(normed_two, 8).reshape(CHIPS * rows, width)
+
+    cot_other = exchanged(cot_all)
+    two_own, two_other = halves(two_all, 1)
+    two_other = exchanged(two_other)
+    grad_hidden = product_t(cot_all, whole_down)
+    hiddens, grads_low, piece_grads = [], [], []
+    two_now = two_all
+    for k in range(2):
+        weights = whole_mlp[k]
+        gate_mlp = product(two_now, weights[:, :half_units])
+        up_mlp = product(two_now, weights[:, half_units:])
+        hidden, pull_act = jax.vjp(mlp_act, gate_mlp, up_mlp)
+        hiddens.append(hidden.astype(bf16))
+        grad_gate, grad_up = pull_act(grad_hidden[:, k * half_units : (k + 1) * half_units])
+        low = jnp.concatenate([grad_gate.astype(bf16), grad_up.astype(bf16)], axis=1)
+        grads_low.append(low)
+        piece_grads.append((weight_grad(two_own, low) + weight_grad(two_other, exchanged(low))).astype(bf16))
+        two_now = behind(two_now, piece_grads[-1])
+    hidden = jnp.concatenate(hiddens, axis=1)
+    two_parts = product_t(grads_low[0], whole_mlp[0]) + product_t(grads_low[1], whole_mlp[1])
+    two_parts = behind(two_parts.astype(bf16), piece_grads[1])
+    piece_grads = [line_sum(part) for part in piece_grads]
+    grad_normed_two = plane_sum(two_parts.reshape(CHIPS, rows, width), 9)
+    unused_norm, pull_norm = jax.vjp(rms_norm, middle, gain_two)
+    grad_middle_norm, grad_mlp_gain = pull_norm(grad_normed_two)
+    grad_middle = cot.astype(f32) + grad_middle_norm
+    hidden_own, hidden_other = halves(behind(hidden, grad_normed_two), 1)
+    down_grad = (weight_grad(hidden_own, cot_all) + weight_grad(exchanged(hidden_other), cot_other)).astype(bf16)
+    grad_mlp_down = line_sum(down_grad)
+    grad_branch = plane_gather(behind(grad_middle.astype(bf16), down_grad), 10).reshape(CHIPS * rows, width)
+    grad_branch = behind(grad_branch, piece_grads[0])
+
+    grad_out_proj = weight_grad(mixed, grad_branch)
+    grad_mixed = product_t(grad_branch, whole_out)
+    grad_states = grad_mixed * gate_act
+    unused_gelu, pull_gelu = jax.vjp(gelu_tanh, gate_pre)
+    grad_gate_pre = pull_gelu(grad_mixed * flat_states)[0].astype(bf16)
+    coef_cube = coefficient.reshape(cube)
+    shifted_coef = jnp.concatenate([coef_cube[:, 1:], jnp.ones((CHIPS, 1, channels), f32)], axis=1)
+    back_cumulative, back_local = block_scan(shifted_coef, grad_states.reshape(cube), True)
+    back_cumulative, back_local = lax.optimization_barrier((back_cumulative, back_local, piece_grads[1]))[:2]
+    leaving = carry_in(
+        coef_cube[:, 0] * back_cumulative[:, 0], coef_cube[:, 0] * back_local[:, 0], True, 12
+    )
+    adjoint = (back_local + back_cumulative * leaving[:, None, :]).reshape(CHIPS * rows, channels)
+    previous = jnp.concatenate([entering[:, None, :], states[:, :-1]], axis=1).reshape(
+        CHIPS * rows, channels
+    )
+
+    def terms_only(decay_values, input_values, conv_values, param_values):
+        return lru_terms(decay_values, input_values, conv_values, param_values, flat_flags)
+
+    unused_terms, pull_terms = jax.vjp(terms_only, decay_pre, input_pre, conv_out, param)
+    grad_decay_full, grad_input_full, grad_conv_direct, grad_param = pull_terms(
+        (adjoint * previous, adjoint)
+    )
+    grad_decay_low, grad_input_low = grad_decay_full.astype(bf16), grad_input_full.astype(bf16)
+
+    def diagonal_blocks(left, right):
+        full = weight_grad(left, right).reshape(2, planes, rows_r, 2, planes, rows_r)
+        same = jnp.eye(planes, dtype=f32)[None, :, None, None, :, None]
+        return jnp.sum(full * same, axis=4).reshape(channels, head)
+
+    row_parts, row_parts_other = halves(
+        jnp.concatenate(
+            [
+                grad_out_proj,
+                diagonal_blocks(conv_low, grad_decay_low),
+                diagonal_blocks(conv_low, grad_input_low),
+            ],
+            axis=1,
+        ),
+        0,
+    )
+    rec_row_grads = line_sum((row_parts + exchanged(row_parts_other)).astype(bf16))
+    grad_conv_out = (
+        grad_conv_direct
+        + product_t(grad_decay_low, decay_blocks)
+        + product_t(grad_input_low, input_blocks)
+    ).reshape(cube)
+    heads_rows = grad_conv_out[:, : CW - 1]
+    from_sibling = lax.ppermute(heads_rows, "seq", sibling)
+    from_above = lax.ppermute(heads_rows[:1], "seq", [(d, d - 7) for d in range(8, n) if d % 2 == 0])
+    after_rows = jnp.where(c == 0, from_sibling, jnp.concatenate([from_sibling[1:], from_above], axis=0))
+    extended = jnp.concatenate([grad_conv_out, after_rows], axis=1)
+    grad_conv_input = jnp.zeros(cube, f32)
+    grad_taps = []
+    for offset in range(CW):
+        lead = CW - 1 - offset
+        keep = jnp.concatenate([masks[offset], after[offset]], axis=1)[:, :, None]
+        grad_conv_input = grad_conv_input + taps[offset] * (extended * keep)[:, offset : offset + rows]
+        grad_taps.append(
+            jnp.sum(grad_conv_out * (padded[:, lead : lead + rows] * masks[offset][:, :, None]), axis=(0, 1))
+        )
+    grad_conv_low = grad_conv_input.reshape(CHIPS * rows, channels).astype(bf16)
+    in_low = jnp.concatenate([grad_gate_pre, grad_conv_low], axis=1)
+    normed_own, normed_other = halves(normed_all, 1)
+    in_grads = weight_grad(normed_own, in_low) + weight_grad(exchanged(normed_other), exchanged(in_low))
+    in_grads = line_sum(in_grads.astype(bf16))
+    normed_parts = product_t(in_low, whole_in).astype(bf16).reshape(CHIPS, rows, width)
+    grad_normed = plane_sum(behind(normed_parts, grad_mlp_down), 13)
+    down_parts = product(hidden, whole_down).astype(bf16).reshape(CHIPS, rows, width)
+    block_out = (middle + plane_sum(behind(down_parts, grad_normed), 11)).astype(bf16)
+    unused_first, pull_first = jax.vjp(rms_norm, values, gain_one)
+    grad_values_norm, grad_norm_gain = pull_first(grad_normed)
+    grad_tokens = grad_middle + grad_values_norm
+
+    mlp_out = plane_swap([part.reshape(CHIPS, rows_d, part.shape[1]) for part in piece_grads], 14)
+    grad_mlp_gate, grad_mlp_up = (
+        from_chips(
+            jnp.concatenate([part[:, :, k * half_units : (k + 1) * half_units] for part in mlp_out], axis=2),
+            planes,
+        ).astype(f32)
+        for k in range(2)
+    )
+    (in_out,) = plane_swap([in_grads.reshape(CHIPS, rows_d, 2 * channels)], 16)
+    grad_gate_branch = from_chips(in_out[:, :, :channels], planes).astype(f32)
+    grad_input_branch = from_chips(in_out[:, :, channels:], planes).astype(f32)
+
+    sums = jnp.stack(
+        [
+            *grad_taps,
+            jnp.sum(grad_conv_out, axis=(0, 1)),
+            jnp.sum(grad_decay_full, axis=0),
+            jnp.sum(grad_input_full, axis=0),
+            grad_param,
+        ]
+    )
+    vector_parts = sums.reshape(CW + 4, 2, planes, rows_r).transpose(2, 1, 0, 3)
+    vector_parts = jnp.pad(vector_parts, ((0, 0), (0, 0), (0, 0), (0, lanes - rows_r)))
+    here = (jnp.arange(CHIPS) == p).astype(f32)[None, :, None, None, None]
+    vector_parts = (vector_parts[:, None] * here).reshape(planes, 8, CW + 4, lanes)
+    gain_parts = jnp.stack([grad_norm_gain, grad_mlp_gain]).reshape(2, 2, planes, CHIPS, rows_d)
+    gain_parts = gain_parts.transpose(2, 3, 1, 0, 4).reshape(planes, 8, 2, rows_d)
+    gain_parts = jnp.pad(gain_parts, ((0, 0), (0, 0), (0, 6), (0, lanes - rows_d)))
+    small_grads = small_sum(jnp.concatenate([vector_parts, gain_parts], axis=2), 15)
+    vector_grads = small_grads[: CW + 4, :rows_r]
+    gain_grads = small_grads[CW + 4 :, :rows_d]
+    return (
+        regrouped_back(block_out, 1, n),
+        regrouped_back(grad_tokens, 1, n),
+        gain_grads[0],
+        grad_gate_branch,
+        grad_input_branch,
+        vector_grads[:CW],
+        vector_grads[CW],
+        rec_row_grads[:, width : width + head].astype(f32),
+        vector_grads[CW + 1],
+        rec_row_grads[:, width + head :].astype(f32),
+        vector_grads[CW + 2],
+        vector_grads[CW + 3],
+        regrouped_back(rec_row_grads[:, :width].astype(f32), 1, n),
+        gain_grads[1],
+        grad_mlp_gate,
+        grad_mlp_up,
+        regrouped_back(grad_mlp_down.astype(f32), 1, n),
+    )
+
+
 def solution(mesh):
     in_specs = (
         P("seq", None),
@@ -417,4 +1192,5 @@
         P("seq", None),
         P("seq", None),
     )
+    body = plane_body if mesh.shape["seq"] == 2 * H else token_split_body
     return jax.shard_map(body, mesh=mesh, in_specs=in_specs, out_specs=out_specs, check_vma=False)

time: 3600 us -> 935 us (0.26)
  waiting for transfers between devices: 2430 us -> 30.1 us
  Pallas kernels: 0 us -> 432 us
  blocking collectives: 372 us -> 0 us
  local copies, waits for them, and re-layouts: 402 us -> 175 us
  matrix products: 253 us -> 194 us
  other arithmetic: 111 us -> 70.4 us
    reduce_scatter x8 -> x5, waiting for transfers between devices: 2230 us -> 0.02 us  [line_sum(): lax.psum_scatter(parts, 'seq', scatter_dimension=0, tiled=True, axis_inde...]
    pallas_call x0 -> x17, Pallas kernels: none -> 432 us  [the longest x4 182 us: plane_sum(): pl.pallas_call(plane_sum_kernel, out_shape=jax.ShapeDtypeStruct(whole, jn...]
    all_gather x7 -> x0, blocking collectives: 289 us -> none  [the longest x4 157 us: prefix(): everything = jax.tree.map(lambda part: lax.all_gather(part, axis), value)]
    slice x114 -> x33, local copies, waits for them, and re-layouts: 233 us -> 13.9 us  [the longest x2 3.97 us: plane_body(): part[:, :, k * half_units:(k + 1) * half_units]]
    all_gather x6 -> x5, waiting for transfers between devices: 192 us -> 0.06 us  [column_gather(): lax.all_gather(block, 'seq', axis=0, tiled=True, axis_index_groups=groups)]
    pad x56 -> x1, local copies, waits for them, and re-layouts: 86.2 us -> 0.01 us  [plane_body(): jnp.pad(vector_parts, ((0, 0), (0, 0), (0, 0), (0, lanes - rows_r)))]
    unnamed x2 -> x0, blocking collectives: 83.6 us -> none
    dot_general x24 -> x28, matrix products: 253 us -> 194 us  [the longest x10 67.2 us: product(): return jnp.dot(left, right, preferred_element_type=f32)]
  transfers between devices with their start and end apart: 17 -> 25, of which waited for: 12 -> 2; matrix products, arithmetic and copies ran while one was open for 12% -> 43% of each run, Pallas kernels for 0% -> 45%
where the time goes in v1:
time: 935 us; the launch traced here: 929 us
  Pallas kernels  432 us (46%)
  matrix products  194 us (21%)
  local copies, waits for them, and re-layouts  175 us (19%)
  other arithmetic  70.4 us (8%)
  waiting for transfers between devices  30.1 us (3%)
  between operations  17.1 us (2%)
  starting transfers between devices  10.9 us (1%)
    pallas_call x4, Pallas kernels, plane_sum(): pl.pallas_call(plane_sum_kernel, out_shape=jax.ShapeDtypeStruct(whole, jn...  182 us
    pallas_call x3, Pallas kernels, plane_gather(): pl.pallas_call(plane_gather_kernel, out_shape=jax.ShapeDtypeStruct((CHIPS...  113 us
    dot_general x10, matrix products, product(): return jnp.dot(left, right, preferred_element_type=f32)  67.2 us
    dot_general x7, matrix products, product_t(): return jnp.einsum('tk,nk->tn', left, right, preferred_element_type=f32)  64.9 us
    pallas_call x4, Pallas kernels, plane_swap(): pl.pallas_call(functools.partial(plane_swap_kernel, count), out_shape=[ja...  62.4 us
    dot_general x11, matrix products, weight_grad(): return jnp.einsum('ta,tb->ab', left, right, preferred_element_type=f32)  62.2 us
    unnamed x279, local copies, waits for them, and re-layouts  37.7 us
    pallas_call x2, Pallas kernels, carry_in(): pl.pallas_call(functools.partial(carry_kernel, planes, reverse), out_shap...  31.9 us
  transfers between devices with their start and end apart: 25, of which 2 were waited for; matrix products, arithmetic and copies ran while one was open for 43% of the time, Pallas kernels for 45%

profile of v1, /device:TPU:0, one launch (start us, length us, event | category | flops | bytes accessed | tf_op | source)
XLA Modules:
  0.0 929.5 jit_solution(2875751362716593215)
XLA Ops:
  14.6 12.3 %plane_swap.4 = bf16[4,64,1280]{2,1,0:T(8,128)(2,1)} custom-call(bf16[4,64,1280]{2,1,0:T(8,128)(2,1)} %pad_maximum_fusion.8.refs_0_), custom_call_target="tpu_custom_call" | custom-call | tf_op jit(solution)/shard_map/plane_swap/pallas_call | solution.py:499
  28.8 18.5 %small_gather.1 = f32[4,8,16,128]{3,2,1,0:T(8,128)} custom-call(f32[16,128]{1,0:T(8,128)} %concatenate.92.x_ref), custom_call_target="tpu_custom_call" | custom-call | tf_op jit(solution)/shard_map/small_gather/pallas_call | solution.py:626
  55.2 37.7 %plane_gather.3 = bf16[4,256,2048]{2,1,0:T(8,128)(2,1)} custom-call(bf16[256,2048]{1,0:T(8,128)(2,1)} %multiply_convert_fusion.5.x_ref), custom_call_target="tpu_custom_call" | custom-call | tf_op jit(solution)/shard_map/plane_gather/pallas_call | solution.py:462
  104.7 19.1 %plane_swap.5 = (bf16[4,64,1536]{2,1,0:T(8,128)(2,1)}, bf16[4,64,1536]{2,1,0:T(8,128)(2,1)}) custom-call(bf16[4,64,1536]{2,1,0:T(8,128)(2,1)} %get-tuple-element.41.refs_0_, bf16[4,64,1536]{2,1,0:T(8,128)(2,1)} %get-tuple-element.42.refs_1_), custom_call_target="tpu_custom_call" | custom-call | tf_op jit(solution)/shard_map/plane_swap/pallas_call | solution.py:499
  139.7 13.1 %collective-permute-done.2 = bf16[256,2048]{0,1:T(8,128)(2,1)} collective-permute-done((bf16[256,2048]{0,1:T(8,128)(2,1)S(1)}, bf16[256,2048]{0,1:T(8,128)(2,1)}, u32[]{:S(2)}, u32[]{:S(2)}) %collective-permute-start.2) | collective-permute-done | bytes 1048608 | tf_op jit(solution)/shard_map/ppermute | solution.py:867
  155.2 16.7 %collective-permute-done.3 = bf16[256,2048]{0,1:T(8,128)(2,1)S(1)} collective-permute-done((bf16[256,2048]{0,1:T(8,128)(2,1)S(1)}, bf16[256,2048]{0,1:T(8,128)(2,1)S(1)}, u32[]{:S(2)}, u32[]{:S(2)}) %collective-permute-start.3) | collective-permute-done | bytes 1048608 | tf_op jit(solution)/shard_map/ppermute | solution.py:867
  177.3 6.5 fusion.68
  195.2 4.7 bitcast_multiply_fusion.5
  208.1 19.1 %carry_in.2 = f32[4,640]{1,0:T(4,128)} custom-call(f32[8,640]{1,0:T(8,128)} %pad_maximum_fusion.10.x_ref), custom_call_target="tpu_custom_call" | custom-call | tf_op jit(solution)/shard_map/carry_in/pallas_call | solution.py:718
  230.9 8.0 fusion.55
  242.3 71.9 %plane_sum.4 = f32[256,2048]{1,0:T(8,128)S(1)} custom-call(f32[4,256,2048]{2,1,0:T(8,128)S(1)} %bitcast.279), custom_call_target="tpu_custom_call" | custom-call | tf_op jit(solution)/shard_map/plane_sum/pallas_call | solution.py:577
  317.0 37.8 %plane_gather.4 = bf16[4,256,2048]{2,1,0:T(8,128)(2,1)} custom-call(bf16[256,2048]{1,0:T(8,128)(2,1)} %multiply_convert_fusion.4.x_ref), custom_call_target="tpu_custom_call" | custom-call | tf_op jit(solution)/shard_map/plane_gather/pallas_call | solution.py:462
  354.8 8.3 fusion.18
  363.1 11.8 %fusion.108 = f32[1024,1536]{0,1:T(8,128)} fusion(bf16[1536,2048]{1,0:T(8,128)(2,1)} %all-gather.12.cloned.1.call-done, bf16[1024,2048]{0,1:T(8,128)(2,1)} %constant_dynamic-update-slice_fusion.8), kind=kOutput, calls=%fused_computation.280 | convolution fusion | flops 6442450944 | bytes 16777216 | tf_op jit(solution)/shard_map/tk,nk->tn/dot_general | solution.py:878
  375.0 8.6 fusion.6
  389.8 6.0 fusion.66
  395.8 7.8 add_convert_fusion.3
  403.7 6.6 fusion.14
  410.4 8.5 fusion.13
  432.4 7.8 add_convert_fusion.2
  440.3 12.7 %fusion.95 = f32[1024,2048]{1,0:T(8,128)} fusion(bf16[2048,1536]{1,0:T(8,128)(2,1)} %all-gather.10.cloned.1.call-done, bf16[1024,768]{0,1:T(8,128)(2,1)} %copy-done.53, bf16[1024,768]{0,1:T(8,128)(2,1)} %copy-done.52), kind=kOutput, calls=%fused_computation.270 | convolution fusion | flops 6448742400 | bytes 17825792 | tf_op jit(solution)/shard_map/tk,nk->tn/dot_general | solution.py:878
  454.9 12.2 %add_convert_fusion = bf16[1024,2048]{1,0:T(8,128)(2,1)S(1)} fusion(f32[1024,2048]{1,0:T(8,128)} %fusion.95, bf16[2048,1536]{1,0:T(8,128)(2,1)} %all-gather.14.cloned.1.call-done, bf16[1024,768]{0,1:T(8,128)(2,1)S(1)} %copy-done.59, bf16[1024,768]{0,1:T(8,128)(2,1)S(1)} %copy-done.56), kind=kOutput, calls=%fused_computation | convolution fusion | flops 6452936704 | bytes 22020096 | tf_op jit(solution)/shard_map/tk,nk->tn/dot_general | solution.py:878
  467.1 36.9 %plane_sum.5 = f32[256,2048]{1,0:T(8,128)S(1)} custom-call(bf16[4,256,2048]{2,1,0:T(8,128)(2,1)S(1)} %bitcast.282), custom_call_target="tpu_custom_call" | custom-call | tf_op jit(solution)/shard_map/plane_sum/pallas_call | solution.py:577
  514.7 6.0 fusion.106
  520.7 7.2 add_convert_fusion.1
  527.9 37.3 %plane_gather.5 = bf16[4,256,2048]{2,1,0:T(8,128)(2,1)} custom-call(bf16[256,2048]{1,0:T(8,128)(2,1)} %fusion.94.x_ref), custom_call_target="tpu_custom_call" | custom-call | tf_op jit(solution)/shard_map/plane_gather/pallas_call | solution.py:462
  566.6 7.6 fusion.107
  574.2 7.7 fusion.28
  594.5 12.8 %carry_in.3 = f32[4,640]{1,0:T(4,128)} custom-call(f32[8,640]{1,0:T(8,128)} %pad_maximum_fusion.11.x_ref), custom_call_target="tpu_custom_call" | custom-call | tf_op jit(solution)/shard_map/carry_in/pallas_call | solution.py:718
  613.2 8.1 convert_bitcast_fusion
  638.1 7.8 concatenate.119
  657.3 7.3 multiply_reduce_fusion.3
  670.6 6.5 fusion.36
  681.4 4.3 add_convert_fusion.5
  685.8 11.4 %convolution_convert_fusion = bf16[1024,2048]{1,0:T(8,128)(2,1)} fusion(bf16[1536,2048]{1,0:T(8,128)(2,1)} %all-gather.12.cloned.1.call-done, bf16[1024,768]{0,1:T(8,128)(2,1)} %get-tuple-element.117, bf16[1024,768]{0,1:T(8,128)(2,1)} %get-tuple-element.118), kind=kOutput, calls=%fused_computation.14 | convolution fusion | flops 6450839552 | bytes 13631488 | tf_op jit(solution)/shard_map/dot_general | solution.py:875
  697.9 20.8 %plane_swap.7 = (bf16[4,64,1536]{2,1,0:T(8,128)(2,1)}, bf16[4,64,1536]{2,1,0:T(8,128)(2,1)}) custom-call(bf16[4,64,1536]{2,1,0:T(8,128)(2,1)} %bitcast.349, bf16[4,64,1536]{2,1,0:T(8,128)(2,1)} %bitcast.350), custom_call_target="tpu_custom_call" | custom-call | tf_op jit(solution)/shard_map/plane_swap/pallas_call | solution.py:499
  729.3 6.8 add_convert_fusion.4
  744.6 4.1 reshape.580
  748.7 4.1 copy.174
  752.8 4.0 reshape.569
  756.8 3.9 reshape.579
  760.7 4.1 copy.173
  764.9 4.0 reshape.568
  770.5 9.9 %convolution_convert_fusion.1 = bf16[1024,2048]{1,0:T(8,128)(2,1)} fusion(bf16[2048,1280]{1,0:T(8,128)(2,1)} %all-gather.6.cloned.1.call-done, bf16[1024,640]{1,0:T(8,128)(2,1)S(1)} %bitcast.294, bf16[1024,640]{1,0:T(8,128)(2,1)} %get-tuple-element.119), kind=kOutput, calls=%fused_computation.15 | convolution fusion | flops 5376049152 | bytes 12058624 | tf_op jit(solution)/shard_map/tk,nk->tn/dot_general | solution.py:878
  782.6 36.1 %plane_sum.6 = f32[256,2048]{1,0:T(8,128)S(1)} custom-call(bf16[4,256,2048]{2,1,0:T(8,128)(2,1)S(1)} %bitcast.281), custom_call_target="tpu_custom_call" | custom-call | tf_op jit(solution)/shard_map/plane_sum/pallas_call | solution.py:577
  821.6 16.9 %small_sum.1 = f32[16,128]{1,0:T(8,128)} custom-call(f32[4,8,16,128]{3,2,1,0:T(8,128)} %select_maximum_fusion.x_ref), custom_call_target="tpu_custom_call" | custom-call | tf_op jit(solution)/shard_map/small_sum/pallas_call | solution.py:671
  841.9 37.2 %plane_sum.7 = f32[256,2048]{1,0:T(8,128)S(1)} custom-call(bf16[4,256,2048]{2,1,0:T(8,128)(2,1)S(1)} %bitcast.280), custom_call_target="tpu_custom_call" | custom-call | tf_op jit(solution)/shard_map/plane_sum/pallas_call | solution.py:577
  903.1 10.2 %plane_swap.6 = bf16[4,64,1280]{2,1,0:T(8,128)(2,1)} custom-call(bf16[4,64,1280]{2,1,0:T(8,128)(2,1)} %bitcast.351), custom_call_target="tpu_custom_call" | custom-call | tf_op jit(solution)/shard_map/plane_swap/pallas_call | solution.py:499
  (545 shorter events, 233.8 us)
Async XLA Ops:
  7.2 166.8 %all-gather.8.cloned.1.call-start = ((), (), s32[]{:S(2)}) async-start(), calls=%async_computation.6 | async-start | bytes 3502080 | tf_op jit(solution)/shard_map/all_gather | solution.py:842
  10.9 166.3 %all-gather.6.cloned.1.call-start = ((), (), s32[]{:S(2)}) async-start(), calls=%async_computation.5 | async-start | bytes 5898240 | tf_op jit(solution)/shard_map/all_gather | solution.py:842
  26.9 327.9 %all-gather.10.cloned.1.call-start = ((), (), s32[]{:S(2)}) async-start(), calls=%async_computation.7 | async-start | bytes 7077888 | tf_op jit(solution)/shard_map/all_gather | solution.py:842
  53.5 39.4 %copy-start.12 = (f32[256,2048]{1,0:T(8,128)}, f32[256,2048]{1,0:T(8,128)S(1)}, u32[]{:S(2)}) copy-start(f32[256,2048]{1,0:T(8,128)S(1)} %copy.134) | copy-start | bytes 6291460
  53.9 39.1 %copy-start.111 = (f32[256]{0:T(256)}, f32[256]{0:T(256)S(1)}, u32[]{:S(2)}) copy-start(f32[256]{0:T(256)S(1)} %multiply_reduce_fusion.12) | copy-start | bytes 3076
  53.9 39.0 %copy-start.103 = (f32[256]{0:T(256)}, f32[256]{0:T(256)S(1)}, u32[]{:S(2)}) copy-start(f32[256]{0:T(256)S(1)} %fusion.91) | copy-start | bytes 3076
  123.9 239.2 %all-gather.12.cloned.1.call-start = ((), (), s32[]{:S(2)}) async-start(), calls=%async_computation.8 | async-start | bytes 7077888 | tf_op jit(solution)/shard_map/all_gather | solution.py:842
  125.8 277.9 %all-gather.14.cloned.1.call-start = ((), (), s32[]{:S(2)}) async-start(), calls=%async_computation.9 | async-start | bytes 7077888 | tf_op jit(solution)/shard_map/all_gather | solution.py:842
  126.6 26.3 %collective-permute-start.2 = (bf16[256,2048]{0,1:T(8,128)(2,1)S(1)}, bf16[256,2048]{0,1:T(8,128)(2,1)}, u32[]{:S(2)}, u32[]{:S(2)}) collective-permute-start(bf16[256,2048]{0,1:T(8,128)(2,1)S(1)} %bitcast.303), channel_id=1, source_target_pairs={{0,2},{1,3},{2,0},{3,1},{4,6},{5,7},{6,4},{7,5},{8,10},{9,11},{10,... | collective-permute-start | bytes 3145736 | tf_op jit(solution)/shard_map/ppermute | solution.py:867
  127.7 44.2 %collective-permute-start.3 = (bf16[256,2048]{0,1:T(8,128)(2,1)S(1)}, bf16[256,2048]{0,1:T(8,128)(2,1)S(1)}, u32[]{:S(2)}, u32[]{:S(2)}) collective-permute-start(bf16[256,2048]{0,1:T(8,128)(2,1)S(1)} %bitcast.304), channel_id=1, source_target_pairs={{0,4},{1,5},{2,6},{3,7},{4,0},{5,1},{6,2},{7,3},{8,12},{9,13},{10,... | collective-permute-start | bytes 3145736 | tf_op jit(solution)/shard_map/ppermute | solution.py:867
  128.6 44.4 %collective-permute-start.4 = (bf16[256,2048]{0,1:T(8,128)(2,1)S(1)}, bf16[256,2048]{0,1:T(8,128)(2,1)S(1)}, u32[]{:S(2)}, u32[]{:S(2)}) collective-permute-start(bf16[256,2048]{0,1:T(8,128)(2,1)S(1)} %bitcast.305), channel_id=1, source_target_pairs={{0,6},{1,7},{2,4},{3,5},{4,2},{5,3},{6,0},{7,1},{8,14},{9,15},{10,... | collective-permute-start | bytes 3145736 | tf_op jit(solution)/shard_map/ppermute | solution.py:867
  130.1 435.2 %reduce-scatter.6.cloned.1.call-start = ((), (), s32[]{:S(2)}) async-start(), calls=%async_computation.10 | async-start | bytes 3932160 | tf_op jit(solution)/shard_map/reduce_scatter | solution.py:845
  133.5 57.7 %copy-start.91 = (f32[640]{0:T(1024)}, f32[640]{0:T(1024)S(1)}, u32[]{:S(2)}) copy-start(f32[640]{0:T(1024)S(1)} %mul.735) | copy-start | bytes 7684
  133.6 57.6 %copy-start.93 = (f32[640]{0:T(1024)}, f32[640]{0:T(1024)S(1)}, u32[]{:S(2)}) copy-start(f32[640]{0:T(1024)S(1)} %mul.750) | copy-start | bytes 7684
  133.7 57.6 %copy-start.95 = (f32[640]{0:T(1024)}, f32[640]{0:T(1024)S(1)}, u32[]{:S(2)}) copy-start(f32[640]{0:T(1024)S(1)} %mul.756) | copy-start | bytes 7684
  133.8 57.5 %copy-start.97 = (f32[640]{0:T(1024)}, f32[640]{0:T(1024)S(1)}, u32[]{:S(2)}) copy-start(f32[640]{0:T(1024)S(1)} %mul.762) | copy-start | bytes 7684
  133.8 57.5 %copy-start.77 = (f32[1,1,4,1,256]{4,2,3,1,0:T(4,128)}, f32[1,1,4,1,256]{4,2,3,1,0:T(4,128)S(1)}, u32[]{:S(2)}) copy-start(f32[1,1,4,1,256]{4,2,3,1,0:T(4,128)S(1)} %copy.217) | copy-start | bytes 12292
  133.8 57.5 %copy-start.79 = (f32[1,1,4,1,256]{4,2,3,1,0:T(4,128)}, f32[1,1,4,1,256]{4,2,3,1,0:T(4,128)S(1)}, u32[]{:S(2)}) copy-start(f32[1,1,4,1,256]{4,2,3,1,0:T(4,128)S(1)} %copy.218) | copy-start | bytes 12292
  133.9 57.4 %copy-start.81 = (f32[1,1,4,1,256]{4,2,3,1,0:T(4,128)}, f32[1,1,4,1,256]{4,2,3,1,0:T(4,128)S(1)}, u32[]{:S(2)}) copy-start(f32[1,1,4,1,256]{4,2,3,1,0:T(4,128)S(1)} %copy.219) | copy-start | bytes 12292
  133.9 57.4 %copy-start.83 = (f32[1,1,4,1,256]{4,2,3,1,0:T(4,128)}, f32[1,1,4,1,256]{4,2,3,1,0:T(4,128)S(1)}, u32[]{:S(2)}) copy-start(f32[1,1,4,1,256]{4,2,3,1,0:T(4,128)S(1)} %copy.220) | copy-start | bytes 12292
  135.4 59.4 %copy-start.75 = (f32[1,1,4,1,256]{4,3,2,1,0:T(1,128)}, f32[1,1,4,1,256]{4,3,2,1,0:T(1,128)S(1)}, u32[]{:S(2)}) copy-start(f32[1,1,4,1,256]{4,3,2,1,0:T(1,128)S(1)} %constant_dynamic-slice_fusion.11) | copy-start | bytes 12292
  135.4 59.4 %copy-start.89 = (f32[1024]{0:T(1024)}, f32[1024]{0:T(1024)S(1)}, u32[]{:S(2)}) copy-start(f32[1024]{0:T(1024)S(1)} %broadcast_subtract_fusion.1) | copy-start | bytes 12292
  136.1 58.8 %copy-start.87 = (f32[640]{0:T(1024)}, f32[640]{0:T(1024)S(1)}, u32[]{:S(2)}) copy-start(f32[640]{0:T(1024)S(1)} %get-tuple-element.168) | copy-start | bytes 7684
  184.4 5.8 collective-permute-start
  184.8 5.4 collective-permute-start.1
  242.3 71.9 %copy-start.13 = (f32[256,2048]{1,0:T(8,128)S(1)}, f32[256,2048]{1,0:T(8,128)}, u32[]{:S(2)}) copy-start(f32[256,2048]{1,0:T(8,128)} %copy-done.12) | copy-start | bytes 6291460
  314.5 198.4 %copy-start.100 = (f32[256]{0:T(256)}, f32[256]{0:T(256)S(1)}, u32[]{:S(2)}) copy-start(f32[256]{0:T(256)S(1)} %fusion.92) | copy-start | bytes 3076
  386.2 9.6 %collective-permute-start.6 = (bf16[1024,1536]{0,1:T(8,128)(2,1)}, bf16[1024,1536]{0,1:T(8,128)(2,1)}, u32[]{:S(2)}, u32[]{:S(2)}) collective-permute-start(bf16[1024,1536]{0,1:T(8,128)(2,1)} %pad_maximum_fusion), channel_id=1, source_target_pairs={{0,1},{1,0},{2,3},{3,2},{4,5},{5,4},{6,7},{7,6},{8,9},{9,8},{10,11... | collective-permute-start | bytes 9437192 | tf_op jit(solution)/shard_map/ppermute | solution.py:872
  389.3 6.5 collective-permute-start.5
  403.7 184.9 %reduce-scatter.8.cloned.1.call-start = ((), (), s32[]{:S(2)}) async-start(), calls=%async_computation.11 | async-start | bytes 3932160 | tf_op jit(solution)/shard_map/reduce_scatter | solution.py:845
  421.6 10.8 %collective-permute-start.7 = (bf16[1024,1536]{0,1:T(8,128)(2,1)}, bf16[1024,1536]{0,1:T(8,128)(2,1)}, u32[]{:S(2)}, u32[]{:S(2)}) collective-permute-start(bf16[1024,1536]{0,1:T(8,128)(2,1)} %pad_maximum_fusion.2), channel_id=1, source_target_pairs={{0,1},{1,0},{2,3},{3,2},{4,5},{5,4},{6,7},{7,6},{8,9},{9,8},{10,11... | collective-permute-start | bytes 9437192 | tf_op jit(solution)/shard_map/ppermute | solution.py:872
  424.1 90.6 %collective-permute-start.9 = (bf16[1024,2048]{0,1:T(8,128)(2,1)}, bf16[1024,2048]{0,1:T(8,128)(2,1)}, u32[]{:S(2)}, u32[]{:S(2)}) collective-permute-start(bf16[1024,2048]{0,1:T(8,128)(2,1)} %constant_dynamic-update-slice_fusion.8), channel_id=1, source_target_pairs={{0,1},{1,0},{2,3},{3,2},{4,5},{5,4},{6,7},{7,6},{8,9},{9,8},{10,11... | collective-permute-start | bytes 12582920 | tf_op jit(solution)/shard_map/ppermute | solution.py:872
  440.2 340.2 %reduce-scatter.10.cloned.1.call-start = ((), (), s32[]{:S(2)}) async-start(), calls=%async_computation.12 | async-start | bytes 3932160 | tf_op jit(solution)/shard_map/reduce_scatter | solution.py:845
  454.8 49.2 %copy-start.41 = (bf16[1024,1536]{0,1:T(8,128)(2,1)}, bf16[1024,1536]{0,1:T(8,128)(2,1)S(1)}, u32[]{:S(2)}) copy-start(bf16[1024,1536]{0,1:T(8,128)(2,1)S(1)} %pad_maximum_fusion.1) | copy-start | bytes 9437188
  505.3 9.4 %collective-permute-start.8 = (bf16[1024,768]{0,1:T(8,128)(2,1)}, bf16[1024,768]{0,1:T(8,128)(2,1)}, u32[]{:S(2)}, u32[]{:S(2)}) collective-permute-start(bf16[1024,768]{0,1:T(8,128)(2,1)} %constant_dynamic-slice_fusion.9), channel_id=1, source_target_pairs={{0,1},{1,0},{2,3},{3,2},{4,5},{5,4},{6,7},{7,6},{8,9},{9,8},{10,11... | collective-permute-start | bytes 4718600 | tf_op jit(solution)/shard_map/ppermute | solution.py:872
  565.3 332.7 %reduce-scatter.14.cloned.1.call-start = ((), (), s32[]{:S(2)}) async-start(), calls=%async_computation.14 | async-start | bytes 1945600 | tf_op jit(solution)/shard_map/reduce_scatter | solution.py:845
  649.9 31.5 %collective-permute-start.14 = (f32[320,2368]{1,0:T(8,128)}, f32[320,2368]{1,0:T(8,128)}, u32[]{:S(2)}, u32[]{:S(2)}) collective-permute-start(f32[320,2368]{1,0:T(8,128)} %constant_dynamic-slice_fusion.6), channel_id=1, source_target_pairs={{0,1},{1,0},{2,3},{3,2},{4,5},{5,4},{6,7},{7,6},{8,9},{9,8},{10,11... | collective-permute-start | bytes 9093128 | tf_op jit(solution)/shard_map/ppermute | solution.py:872
  652.9 76.4 %collective-permute-start.12 = (bf16[1024,1024]{1,0:T(8,128)(2,1)}, bf16[1024,1024]{1,0:T(8,128)(2,1)}, u32[]{:S(2)}, u32[]{:S(2)}) collective-permute-start(bf16[1024,1024]{1,0:T(8,128)(2,1)} %constant_dynamic-slice_fusion.7), channel_id=1, source_target_pairs={{0,1},{1,0},{2,3},{3,2},{4,5},{5,4},{6,7},{7,6},{8,9},{9,8},{10,11... | collective-permute-start | bytes 6291464 | tf_op jit(solution)/shard_map/ppermute | solution.py:872
  666.1 4.4 collective-permute-start.10
  666.6 4.0 collective-permute-start.11
  680.0 49.3 %collective-permute-start.13 = (bf16[1024,1280]{1,0:T(8,128)(2,1)}, bf16[1024,1280]{1,0:T(8,128)(2,1)}, u32[]{:S(2)}, u32[]{:S(2)}) collective-permute-start(bf16[1024,1280]{1,0:T(8,128)(2,1)} %pad_maximum_fusion.5), channel_id=1, source_target_pairs={{0,1},{1,0},{2,3},{3,2},{4,5},{5,4},{6,7},{7,6},{8,9},{9,8},{10,11... | collective-permute-start | bytes 7864328 | tf_op jit(solution)/shard_map/ppermute | solution.py:872
  685.7 217.4 %reduce-scatter.12.cloned.1.call-start = ((), (), s32[]{:S(2)}) async-start(), calls=%async_computation.13 | async-start | bytes 3276800 | tf_op jit(solution)/shard_map/reduce_scatter | solution.py:845
  782.6 37.5 %copy-start.14 = (f32[256,2048]{1,0:T(8,128)S(1)}, f32[256,2048]{1,0:T(8,128)}, u32[]{:S(2)}) copy-start(f32[256,2048]{1,0:T(8,128)} %copy-done.12) | copy-start | bytes 6291460
  782.6 37.5 %copy-start.70 = (f32[2048]{0:T(1024)S(1)}, f32[2048]{0:T(1024)}, u32[]{:S(2)}) copy-start(f32[2048]{0:T(1024)} %copy-done.69) | copy-start | bytes 24580
  782.6 37.5 %copy-start.104 = (f32[256]{0:T(256)S(1)}, f32[256]{0:T(256)}, u32[]{:S(2)}) copy-start(f32[256]{0:T(256)} %copy-done.103) | copy-start | bytes 3076
  782.6 96.5 %copy-start.112 = (f32[256]{0:T(256)S(1)}, f32[256]{0:T(256)}, u32[]{:S(2)}) copy-start(f32[256]{0:T(256)} %copy-done.111) | copy-start | bytes 3076
  820.1 59.0 %copy-start.40 = (bf16[256,2048]{1,0:T(8,128)(2,1)S(1)}, bf16[256,2048]{1,0:T(8,128)(2,1)}, u32[]{:S(2)}) copy-start(bf16[256,2048]{1,0:T(8,128)(2,1)} %copy.144) | copy-start | bytes 3145732
  841.9 37.3 %copy-start.110 = (f32[256]{0:T(256)S(1)}, f32[256]{0:T(256)}, u32[]{:S(2)}) copy-start(f32[256]{0:T(256)} %copy-done.109) | copy-start | bytes 3076
  (107 other events, 739.5 us)
Sparse Core Ops, SparseCore 0:
  11.1 46.2 all-gather.7
  59.0 54.8 all-gather.5
  124.0 70.2 all-gather.9
  196.3 66.7 all-gather.11
  264.6 63.2 all-gather.13
  403.8 62.4 reduce-scatter.5
  468.5 60.2 reduce-scatter.7
  565.4 64.6 reduce-scatter.9
  685.8 36.7 reduce-scatter.13
  736.3 53.9 reduce-scatter.11

commit v2 on v0

--- a/solution.py
+++ b/solution.py
@@ -1,6 +1,10 @@
+import functools
+
 import jax
 import jax.numpy as jnp
 from jax import lax
+from jax.experimental import pallas as pl
+from jax.experimental.pallas import tpu as pltpu
 from jax.sharding import PartitionSpec as P
 
 H = 16
@@ -117,7 +121,7 @@
     return gelu_tanh(gate_values) * up_values
 
 
-def body(
+def token_split_body(
     tokens,
     starts,
     cotangent,
@@ -377,6 +381,1537 @@
     )
 
 
+CHIPS = 4
+MESH = pl.DeviceIdType.MESH
+
+
+def place():
+    me = lax.axis_index("seq")
+    core = lax.rem(me, 2)
+    x = lax.rem(lax.div(me, 2), 2)
+    y = lax.rem(lax.div(me, 4), 2)
+    return me, lax.div(me, 8), 2 * y + x, core, x, y
+
+
+def column_groups(n):
+    return [[8 * z + 2 * p + c for c in range(2) for z in range(n // 8)] for p in range(CHIPS)]
+
+
+def line_groups(n):
+    return [[8 * z + r for z in range(n // 8)] for r in range(8)]
+
+
+def greet(devices):
+    barrier = pltpu.get_barrier_semaphore()
+    for device in devices:
+        pl.semaphore_signal(barrier, inc=1, device_id=(device,), device_id_type=MESH)
+    pl.semaphore_wait(barrier, len(devices))
+
+
+def remote(source, target, send_sem, recv_sem, device):
+    return pltpu.make_async_remote_copy(
+        src_ref=source,
+        dst_ref=target,
+        send_sem=send_sem,
+        recv_sem=recv_sem,
+        device_id=(device,),
+        device_id_type=MESH,
+    )
+
+
+def comm_params(collective_id, vmem_mib=None):
+    return pltpu.CompilerParams(
+        collective_id=collective_id,
+        has_side_effects=True,
+        vmem_limit_bytes=None if vmem_mib is None else vmem_mib * 2**20,
+    )
+
+
+ANY = pl.BlockSpec(memory_space=pl.ANY)
+VMEM = pl.BlockSpec(memory_space=pltpu.VMEM)
+
+
+def plane_neighbours():
+    me, z, p, c, x, y = place()
+    x_dev, y_dev = me + 2 - 4 * x, me + 4 - 8 * y
+    return (x_dev, y_dev, y_dev + 2 - 4 * x), (p + 1 - 2 * x, p + 2 - 4 * y, 3 - p)
+
+
+def gather_steps(source, whole, send, recv, local, first):
+    me, z, p, c, x, y = place()
+    (x_dev, y_dev, d_dev), (p_x, p_y, p_d) = plane_neighbours()
+    half = source.shape[0] // 2
+
+    def copy(k, source, target, device):
+        return remote(source, target, send.at[first + k], recv.at[first + k], device)
+
+    to_x, to_y = copy(0, source, whole.at[p], x_dev), copy(1, source, whole.at[p], y_dev)
+    low, high = whole.at[p_x, pl.ds(0, half)], whole.at[p_y, pl.ds(half, half)]
+    on_y, on_x = copy(2, low, low, y_dev), copy(3, high, high, x_dev)
+    own = pltpu.make_async_copy(source, whole.at[p], local)
+
+    def begin():
+        to_x.start()
+        to_y.start()
+        own.start()
+
+    def forward():
+        to_x.wait_recv()
+        on_y.start()
+        to_y.wait_recv()
+        on_x.start()
+
+    def end():
+        to_x.wait_send()
+        to_y.wait_send()
+        on_y.wait()
+        on_x.wait()
+        own.wait()
+
+    return begin, forward, end
+
+
+def sum_scratch(rows, columns, dtype):
+    whole, part = pltpu.VMEM((rows, columns), dtype), pltpu.VMEM((rows // 2, columns), dtype)
+    return [whole] * 3 + [part] * 4 + [pltpu.SemaphoreType.DMA((6,)), pltpu.SemaphoreType.DMA((6,)), pltpu.SemaphoreType.DMA((3,))]
+
+
+def sum_steps(part, own, from_x, from_y, diag_x, diag_y, on_x, on_y, send, recv, local):
+    me, z, p, c, x, y = place()
+    (x_dev, y_dev, d_dev), (p_x, p_y, p_d) = plane_neighbours()
+    half = part.shape[1] // 2
+    low, high = pl.ds(0, half), pl.ds(half, half)
+    copies = [
+        remote(part.at[p_d, low], diag_x, send.at[0], recv.at[0], x_dev),
+        remote(part.at[p_d, high], diag_y, send.at[1], recv.at[1], y_dev),
+        remote(part.at[p_x, low], from_x.at[low], send.at[2], recv.at[2], x_dev),
+        remote(part.at[p_y, high], from_y.at[high], send.at[3], recv.at[3], y_dev),
+    ]
+    locals_ = [
+        pltpu.make_async_copy(part.at[p_y, low], on_y, local.at[0]),
+        pltpu.make_async_copy(part.at[p_x, high], on_x, local.at[1]),
+        pltpu.make_async_copy(part.at[p], own, local.at[2]),
+    ]
+    to_y = remote(on_y, from_y.at[low], send.at[4], recv.at[4], y_dev)
+    to_x = remote(on_x, from_x.at[high], send.at[5], recv.at[5], x_dev)
+
+    def add_into(target, addend):
+        @pl.loop(0, half // 16)
+        def add_rows(i):
+            at = pl.ds(pl.multiple_of(i * 16, 16), 16)
+            target[at, :] = (
+                target[at, :].astype(jnp.float32) + addend[at, :].astype(jnp.float32)
+            ).astype(target.dtype)
+
+    def begin():
+        for copy in copies + locals_:
+            copy.start()
+
+    def forward():
+        locals_[0].wait()
+        copies[0].wait_recv()
+        add_into(on_y, diag_x)
+        to_y.start()
+        locals_[1].wait()
+        copies[1].wait_recv()
+        add_into(on_x, diag_y)
+        to_x.start()
+
+    def end():
+        locals_[2].wait()
+        copies[2].wait_recv()
+        copies[3].wait_recv()
+        to_y.wait()
+        to_x.wait()
+        for copy in copies:
+            copy.wait_send()
+
+    return begin, forward, end
+
+
+def sixteen(i):
+    return pl.ds(pl.multiple_of(i * 16, 16), 16)
+
+
+def middle_kernel(parts, tokens, gain, middle, whole, normed, *scratch):
+    sums, (send, recv, local) = scratch[:10], scratch[10:]
+    greet(plane_neighbours()[0][:2])
+    own, from_x, from_y = sums[:3]
+    for step in sum_steps(parts, *sums):
+        step()
+
+    @pl.loop(0, tokens.shape[0] // 16)
+    def norm_rows(i):
+        at = sixteen(i)
+        values = tokens[at, :].astype(jnp.float32) + (own[at, :] + from_x[at, :] + from_y[at, :])
+        middle[at, :] = values
+        inverse = lax.rsqrt(jnp.mean(values * values, axis=-1, keepdims=True) + epsilon)
+        normed[at, :] = (values * inverse * gain[...]).astype(jnp.bfloat16)
+
+    for step in gather_steps(normed, whole, send, recv, local, 0):
+        step()
+
+
+def middle_of(parts, tokens, gain, collective_id):
+    rows, width = tokens.shape
+    return pl.pallas_call(
+        middle_kernel,
+        out_shape=[
+            jax.ShapeDtypeStruct((rows, width), jnp.float32),
+            jax.ShapeDtypeStruct((CHIPS, rows, width), jnp.bfloat16),
+        ],
+        in_specs=[ANY, VMEM, VMEM],
+        out_specs=[VMEM, ANY],
+        scratch_shapes=[
+            pltpu.VMEM((rows, width), jnp.bfloat16),
+            *sum_scratch(rows, width, parts.dtype),
+            pltpu.SemaphoreType.DMA((4,)),
+            pltpu.SemaphoreType.DMA((4,)),
+            pltpu.SemaphoreType.DMA,
+        ],
+        compiler_params=comm_params(collective_id, 32),
+        name="middle",
+    )(parts, tokens, gain[None])
+
+
+def norm_back_rows(values, gain, grad, rest):
+    inverse = lax.rsqrt(jnp.mean(values * values, axis=-1, keepdims=True) + epsilon)
+    scaled = gain * grad
+    pull = jnp.mean(scaled * values, axis=-1, keepdims=True) * (inverse * inverse * inverse)
+    return rest + inverse * scaled - values * pull, grad * values * inverse
+
+
+def grads_of_middle_kernel(
+    parts,
+    middle,
+    cot,
+    gain,
+    hidden,
+    down,
+    cot_all,
+    cot_other,
+    grad_middle,
+    grad_gain,
+    whole,
+    down_grad,
+    down_parts,
+    branch,
+    hidden_here,
+    hidden_other,
+    down_here,
+    cot_here,
+    cot_there,
+    *scratch,
+):
+    sums, (send, recv, local, loads) = scratch[:10], scratch[10:]
+    me, z, p, c, x, y = place()
+    f32, bf16 = jnp.float32, jnp.bfloat16
+    sibling = me + 1 - 2 * c
+    greet((*plane_neighbours()[0][:2], sibling))
+    own, from_x, from_y = sums[:3]
+    begin, forward, end = sum_steps(parts, *sums)
+    begin()
+    units = hidden.shape[1]
+    half = units // 2
+    swap = remote(
+        hidden.at[:, pl.ds(pl.multiple_of((1 - c) * half, 128), half)], hidden_other, send.at[4], recv.at[4], sibling
+    )
+    swap.start()
+    fetched = [
+        pltpu.make_async_copy(source, target, loads.at[k])
+        for k, (source, target) in enumerate(
+            ((hidden, hidden_here), (cot_all, cot_here), (cot_other, cot_there), (down, down_here))
+        )
+    ]
+    for copy in fetched:
+        copy.start()
+    for copy in fetched[:3]:
+        copy.wait()
+    swap.wait()
+    tile = 256
+
+    def grad_tiles(m):
+        rows_here = pl.ds(pl.multiple_of(c * half + m * tile, 128), tile)
+        rows_there = pl.ds(pl.multiple_of(m * tile, 128), tile)
+
+        @pl.loop(0, cot_all.shape[1] // (2 * tile))
+        def grad_tile(k):
+            columns = pl.ds(pl.multiple_of(k * 2 * tile, 128), 2 * tile)
+
+            def dot_t(left, right):
+                return lax.dot_general(left, right, (((0,), (0,)), ((), ())), preferred_element_type=f32)
+
+            down_grad[rows_there, columns] = (
+                dot_t(hidden_here[:, rows_here], cot_here[:, columns])
+                + dot_t(hidden_other[:, rows_there], cot_there[:, columns])
+            ).astype(bf16)
+
+    pl.loop(0, 1)(grad_tiles)
+    forward()
+    pl.loop(1, half // tile)(grad_tiles)
+    end()
+    rows, width = middle.shape
+
+    def norm_rows(i, total):
+        at = sixteen(i)
+        grad = own[at, :].astype(f32) + from_x[at, :].astype(f32) + from_y[at, :].astype(f32)
+        given, terms = norm_back_rows(middle[at, :], gain[...], grad, cot[at, :].astype(f32))
+        grad_middle[at, :] = given
+        branch[at, :] = given.astype(bf16)
+        return total + terms[:8] + terms[8:]
+
+    total = lax.fori_loop(0, rows // 16, norm_rows, jnp.zeros((8, width), f32))
+    grad_gain[...] = jnp.sum(total, axis=0, keepdims=True)
+    begin, forward, end = gather_steps(branch, whole, send, recv, local, 0)
+    begin()
+    fetched[3].wait()
+
+    def down_tiles(j):
+        @pl.loop(0, width // (2 * tile))
+        def down_tile(k):
+            columns = pl.ds(pl.multiple_of(k * 2 * tile, 128), 2 * tile)
+            down_parts[j, :, columns] = jnp.dot(
+                hidden_here[pl.ds(pl.multiple_of(j * rows, 16), rows), :],
+                down_here[:, columns],
+                preferred_element_type=f32,
+            ).astype(bf16)
+
+    pl.loop(0, CHIPS)(down_tiles)
+    forward()
+    end()
+
+
+def grads_of_middle(parts, middle, cot, gain, hidden, down, cot_all, cot_other, collective_id):
+    rows, width = middle.shape
+    tokens, units = hidden.shape
+    f32, bf16 = jnp.float32, jnp.bfloat16
+    return pl.pallas_call(
+        grads_of_middle_kernel,
+        out_shape=[
+            jax.ShapeDtypeStruct((rows, width), f32),
+            jax.ShapeDtypeStruct((1, width), f32),
+            jax.ShapeDtypeStruct((CHIPS, rows, width), bf16),
+            jax.ShapeDtypeStruct((units // 2, width), bf16),
+            jax.ShapeDtypeStruct((CHIPS, rows, width), bf16),
+        ],
+        in_specs=[ANY, VMEM, VMEM, VMEM, ANY, ANY, ANY, ANY],
+        out_specs=[VMEM, VMEM, ANY, VMEM, VMEM],
+        scratch_shapes=[
+            pltpu.VMEM((rows, width), bf16),
+            pltpu.VMEM((tokens, units), bf16),
+            pltpu.VMEM((tokens, units // 2), bf16),
+            pltpu.VMEM((units, width), bf16),
+            pltpu.VMEM((tokens, width), bf16),
+            pltpu.VMEM((tokens, width), bf16),
+            *sum_scratch(rows, width, parts.dtype),
+            pltpu.SemaphoreType.DMA((5,)),
+            pltpu.SemaphoreType.DMA((5,)),
+            pltpu.SemaphoreType.DMA,
+            pltpu.SemaphoreType.DMA((4,)),
+        ],
+        compiler_params=comm_params(collective_id, 56),
+        name="grads_of_middle",
+    )(parts, middle, cot, gain[None], hidden, down, cot_all, cot_other)
+
+
+def closing_kernel(
+    planes,
+    parts,
+    tokens,
+    gain,
+    rest,
+    small,
+    conv_here,
+    conv_there,
+    decay_here,
+    decay_there,
+    input_here,
+    input_there,
+    piece,
+    grad_tokens,
+    small_out,
+    gates_out,
+    swapped,
+    conv_a,
+    conv_b,
+    low_a,
+    low_b,
+    low_c,
+    low_d,
+    gates,
+    gate_lines,
+    lines,
+    line,
+    near_parts,
+    gains,
+    gain_lines,
+    gain_line,
+    gain_near,
+    *scratch,
+):
+    sums, (send, recv, local, loads) = scratch[:10], scratch[10:]
+    me, z, p, c, x, y = place()
+    f32 = jnp.float32
+    r = lax.rem(me, 8)
+    near = [(lax.rem(r + d, 8), me - r + lax.rem(r + d, 8)) for d in range(1, 8)]
+    far = [(lax.rem(z + d, planes), 8 * lax.rem(z + d, planes) + r) for d in range(1, planes)]
+    greet([device for unused, device in near + far])
+    own, from_x, from_y = sums[:3]
+    begin, forward, end = sum_steps(parts, *sums)
+    begin()
+    devices, chips = plane_neighbours()
+
+    def copy(k, source, target, device):
+        return remote(source, target, send.at[k], recv.at[k], device)
+
+    swaps = [copy(k, piece.at[chips[k]], swapped.at[p], devices[k]) for k in range(3)]
+    for swap in swaps:
+        swap.start()
+    swap_own = pltpu.make_async_copy(piece.at[p], swapped.at[p], local)
+    swap_own.start()
+    at = 3
+    small_far = [copy(at + d, small.at[there], lines.at[d], device) for d, (there, device) in enumerate(far)]
+    at += len(far)
+    for sent in small_far:
+        sent.start()
+    fetched = [
+        pltpu.make_async_copy(source, target, loads.at[k])
+        for k, (source, target) in enumerate(
+            (
+                (conv_here, conv_a),
+                (conv_there, conv_b),
+                (decay_here, low_a),
+                (decay_there, low_b),
+                (input_here, low_c),
+                (input_there, low_d),
+            )
+        )
+    ]
+    for fetch in fetched:
+        fetch.start()
+    for fetch in fetched:
+        fetch.wait()
+
+    def dot_t(left, right):
+        return lax.dot_general(left, right, (((0,), (0,)), ((), ())), preferred_element_type=f32)
+
+    block = gates.shape[1]
+    count = conv_a.shape[1]
+    for k, (first, second) in enumerate(((low_a, low_b), (low_c, low_d))):
+        full = dot_t(conv_a[...], first[...]) + dot_t(conv_b[...], second[...])
+        for j in range(planes):
+            for e in range(2):
+                gates[j, :, (2 * k + e) * block : (2 * k + e + 1) * block] = full[
+                    j * block : (j + 1) * block, e * count + j * block : e * count + (j + 1) * block
+                ]
+    gate_far = [copy(at + d, gates.at[there], gate_lines.at[d], device) for d, (there, device) in enumerate(far)]
+    at += len(far)
+    for sent in gate_far:
+        sent.start()
+    forward()
+    for sent in small_far:
+        sent.wait()
+    line[...] = small[z] + sum(lines[d] for d in range(planes - 1))
+    small_near = [
+        copy(at + d, line.at[there], near_parts.at[d], device) for d, (there, device) in enumerate(near)
+    ]
+    at += len(near)
+    for sent in small_near:
+        sent.start()
+    end()
+    rows, width = tokens.shape
+    step = width // (8 * planes)
+
+    def norm_rows(i, total):
+        here = sixteen(i)
+        grad = own[here, :].astype(f32) + from_x[here, :].astype(f32) + from_y[here, :].astype(f32)
+        given, terms = norm_back_rows(tokens[here, :].astype(f32), gain[...], grad, rest[here, :])
+        for k in range(4 * planes):
+            for e in range(2):
+                grad_tokens[here, (2 * k + e) * step : (2 * k + e + 1) * step] = given[
+                    :, (4 * planes * e + k) * step : (4 * planes * e + k + 1) * step
+                ]
+        return total + terms[:8] + terms[8:]
+
+    total = lax.fori_loop(0, rows // 16, norm_rows, jnp.zeros((8, width), f32))
+    total = jnp.sum(total, axis=0, keepdims=True)
+    for j in range(planes):
+        for q in range(CHIPS):
+            for e in range(2):
+                start = ((e * planes + j) * CHIPS + q) * step
+                gains[j, 2 * q + e, 0:1, 0:step] = total[:, start : start + step]
+    gain_far = [copy(at + d, gains.at[there], gain_lines.at[d], device) for d, (there, device) in enumerate(far)]
+    at += len(far)
+    for sent in gain_far:
+        sent.start()
+    for sent in gain_far:
+        sent.wait()
+    gain_line[...] = gains[z] + sum(gain_lines[d] for d in range(planes - 1))
+    last = [
+        copy(at + d, gain_line.at[there], gain_near.at[d], device) for d, (there, device) in enumerate(near)
+    ]
+    for sent in last:
+        sent.start()
+    for sent in small_near + gate_far + swaps:
+        sent.wait()
+    swap_own.wait()
+    gates_out[...] = gates[z] + sum(gate_lines[d] for d in range(planes - 1))
+    for sent in last:
+        sent.wait()
+    rows_small = line.shape[1]
+    small_out[0:rows_small, :] = line[r] + sum(near_parts[d] for d in range(7))
+    small_out[rows_small : rows_small + 8, :] = gain_line[r] + sum(gain_near[d] for d in range(7))
+
+
+def closing(parts, tokens, gain, rest, small, convs, decays, inputs, piece, head, collective_id):
+    planes = lax.axis_size("seq") // 8
+    rows, width = tokens.shape
+    f32, bf16 = jnp.float32, jnp.bfloat16
+    rows_small, lanes = small.shape[2:]
+    block = convs[0].shape[1] // planes
+    count = 3 + 3 * (planes - 1) + 14
+    return pl.pallas_call(
+        functools.partial(closing_kernel, planes),
+        out_shape=[
+            jax.ShapeDtypeStruct((rows, width), f32),
+            jax.ShapeDtypeStruct((rows_small + 8, lanes), f32),
+            jax.ShapeDtypeStruct((block, 2 * head), f32),
+            jax.ShapeDtypeStruct(piece.shape, piece.dtype),
+        ],
+        in_specs=[ANY, VMEM, VMEM, VMEM, VMEM] + [ANY] * 7,
+        out_specs=[VMEM, VMEM, VMEM, ANY],
+        scratch_shapes=[
+            pltpu.VMEM(convs[0].shape, bf16),
+            pltpu.VMEM(convs[0].shape, bf16),
+            *[pltpu.VMEM(decays[0].shape, bf16)] * 4,
+            pltpu.VMEM((planes, block, 2 * head), f32),
+            pltpu.VMEM((planes - 1, block, 2 * head), f32),
+            pltpu.VMEM((planes - 1, 8, rows_small, lanes), f32),
+            pltpu.VMEM((8, rows_small, lanes), f32),
+            pltpu.VMEM((7, rows_small, lanes), f32),
+            pltpu.VMEM((planes, 8, 8, lanes), f32),
+            pltpu.VMEM((planes - 1, 8, 8, lanes), f32),
+            pltpu.VMEM((8, 8, lanes), f32),
+            pltpu.VMEM((7, 8, lanes), f32),
+            *sum_scratch(rows, width, parts.dtype),
+            pltpu.SemaphoreType.DMA((count,)),
+            pltpu.SemaphoreType.DMA((count,)),
+            pltpu.SemaphoreType.DMA,
+            pltpu.SemaphoreType.DMA((6,)),
+        ],
+        compiler_params=comm_params(collective_id, 40),
+        name="closing",
+    )(parts, tokens, gain[None], rest, small, *convs, *decays, *inputs, piece)
+
+
+def plane_gather_kernel(x_ref, o_ref, send, recv, local):
+    greet(plane_neighbours()[0][:2])
+    for step in gather_steps(x_ref, o_ref, send, recv, local, 0):
+        step()
+
+
+def plane_gather(block, collective_id):
+    return pl.pallas_call(
+        plane_gather_kernel,
+        out_shape=jax.ShapeDtypeStruct((CHIPS,) + block.shape, block.dtype),
+        in_specs=[ANY],
+        out_specs=ANY,
+        scratch_shapes=[
+            pltpu.SemaphoreType.DMA((4,)),
+            pltpu.SemaphoreType.DMA((4,)),
+            pltpu.SemaphoreType.DMA,
+        ],
+        compiler_params=comm_params(collective_id),
+        name="plane_gather",
+    )(block)
+
+
+def plane_swap_kernel(count, *refs):
+    ins, outs = refs[:count], refs[count : 2 * count]
+    send, recv, local = refs[2 * count :]
+    me, z, p, c, x, y = place()
+    x_dev, y_dev = me + 2 - 4 * x, me + 4 - 8 * y
+    d_dev = y_dev + 2 - 4 * x
+    p_x, p_y, p_d = p + 1 - 2 * x, p + 2 - 4 * y, 3 - p
+    peers = ((x_dev, p_x), (y_dev, p_y), (d_dev, p_d))
+    greet([device for device, unused in peers])
+    copies = []
+    for k in range(count):
+        for j, (device, chip) in enumerate(peers):
+            copies.append(remote(ins[k].at[chip], outs[k].at[p], send.at[k, j], recv.at[k, j], device))
+        copies.append(pltpu.make_async_copy(ins[k].at[p], outs[k].at[p], local.at[k]))
+    for copy in copies:
+        copy.start()
+    for copy in copies:
+        copy.wait()
+
+
+def plane_swap(arrays, collective_id):
+    count = len(arrays)
+    return pl.pallas_call(
+        functools.partial(plane_swap_kernel, count),
+        out_shape=[jax.ShapeDtypeStruct(a.shape, a.dtype) for a in arrays],
+        in_specs=[ANY] * count,
+        out_specs=[ANY] * count,
+        scratch_shapes=[
+            pltpu.SemaphoreType.DMA((count, 3)),
+            pltpu.SemaphoreType.DMA((count, 3)),
+            pltpu.SemaphoreType.DMA((count,)),
+        ],
+        compiler_params=comm_params(collective_id),
+        name="plane_swap",
+    )(*arrays)
+
+
+def opening_kernel(planes, weights_ref, x_ref, swapped_ref, o_ref, send, recv, local):
+    me, z, p, c, x, y = place()
+    r = lax.rem(me, 8)
+    base = me - r
+    near = [base + lax.rem(r + d, 8) for d in range(1, 8)]
+    far = [8 * lax.rem(z + d, planes) + r for d in range(1, planes)]
+    greet(near + far)
+    x_dev, y_dev = me + 2 - 4 * x, me + 4 - 8 * y
+    d_dev = y_dev + 2 - 4 * x
+    p_x, p_y, p_d = p + 1 - 2 * x, p + 2 - 4 * y, 3 - p
+    lines = [
+        remote(x_ref, o_ref.at[r, z], send.at[d], recv.at[d], device) for d, device in enumerate(far)
+    ]
+    swaps = [
+        remote(weights_ref.at[chip], swapped_ref.at[p], send.at[planes + j], recv.at[planes + j], device)
+        for j, (device, chip) in enumerate(((x_dev, p_x), (y_dev, p_y), (d_dev, p_d)))
+    ]
+    own = pltpu.make_async_copy(weights_ref.at[p], swapped_ref.at[p], local)
+    for copy in lines + swaps:
+        copy.start()
+    own.start()
+    o_ref[r, z] = x_ref[...]
+    for copy in lines:
+        copy.wait()
+    spreads = [
+        remote(o_ref.at[r], o_ref.at[r], send.at[planes + 3 + d], recv.at[planes + 3 + d], device)
+        for d, device in enumerate(near)
+    ]
+    for copy in spreads:
+        copy.start()
+    for copy in spreads + swaps:
+        copy.wait()
+    own.wait()
+
+
+def opening(weights, block, collective_id):
+    planes = lax.axis_size("seq") // 8
+    return pl.pallas_call(
+        functools.partial(opening_kernel, planes),
+        out_shape=[
+            jax.ShapeDtypeStruct(weights.shape, weights.dtype),
+            jax.ShapeDtypeStruct((8, planes) + block.shape, block.dtype),
+        ],
+        in_specs=[ANY, VMEM],
+        out_specs=[ANY, VMEM],
+        scratch_shapes=[
+            pltpu.SemaphoreType.DMA((planes + 10,)),
+            pltpu.SemaphoreType.DMA((planes + 10,)),
+            pltpu.SemaphoreType.DMA,
+        ],
+        compiler_params=comm_params(collective_id),
+        name="opening",
+    )(weights, block)
+
+
+def column_peers(planes, z, p, c):
+    count = 2 * planes
+    q = 2 * z + c
+    peers = []
+    for d in range(1, count):
+        other = lax.rem(q + d, count)
+        peers.append(8 * lax.div(other, 2) + 2 * p + lax.rem(other, 2))
+    return q, peers
+
+
+def carry_in(planes, reverse, z, c, q, peers, everyone, before, entering, send, recv):
+    own = everyone.at[q]
+    copies = [remote(own, own, send.at[d], recv.at[d], device) for d, device in enumerate(peers)]
+    for copy in copies:
+        copy.start()
+    for copy in copies:
+        copy.wait()
+    carried = jnp.zeros((1, everyone.shape[2]), jnp.float32)
+    order = [(k, j, e) for k in range(planes) for j in range(CHIPS) for e in range(2)]
+    for k, j, e in reversed(order) if reverse else order:
+        before[8 * k + 2 * j + e : 8 * k + 2 * j + e + 1, :] = carried
+        part = everyone.at[2 * k + e]
+        carried = part[j : j + 1, :] * carried + part[CHIPS + j : CHIPS + j + 1, :]
+    for j in range(CHIPS):
+        entering[j : j + 1, :] = before[pl.ds(8 * z + 2 * j + c, 1), :]
+
+
+def shift_down(earlier, values, step, row):
+    return jnp.where(row >= step, pltpu.roll(values, step, 0), pltpu.roll(earlier, step, 0))
+
+
+def shift_up(values, later, step, row):
+    return jnp.where(row < 8 - step, pltpu.roll(values, 8 - step, 0), pltpu.roll(later, 8 - step, 0))
+
+
+def tile_scan(a, b, row, reverse):
+    for step in (1, 2, 4):
+        if reverse:
+            keep = row < 8 - step
+            shifted_a, shifted_b = pltpu.roll(a, 8 - step, 0), pltpu.roll(b, 8 - step, 0)
+        else:
+            keep = row >= step
+            shifted_a, shifted_b = pltpu.roll(a, step, 0), pltpu.roll(b, step, 0)
+        b = a * jnp.where(keep, shifted_b, 0.0) + b
+        a = a * jnp.where(keep, shifted_a, 1.0)
+    return a, b
+
+
+def sigmoid(values):
+    return 1.0 / (1.0 + jnp.exp(-values))
+
+
+def gate_terms(decay_pre, rate, flag):
+    opened = sigmoid(decay_pre)
+    log_decay = rate * opened
+    decay = jnp.exp(log_decay)
+    keep = 1.0 - flag
+    squared = decay * decay
+    return opened, decay * keep, keep, squared, jnp.tanh(-log_decay) * (1.0 + squared)
+
+
+GELU_A, GELU_B = 0.7978845608028654, 0.044715
+
+
+def eight(i):
+    return pl.ds(pl.multiple_of(i * 8, 8), 8)
+
+
+def recurrence_kernel(
+    planes,
+    gate_pre,
+    conv_input,
+    masks,
+    vectors,
+    decay_blocks,
+    input_blocks,
+    cot,
+    conv_out,
+    conv_low,
+    decay_pre,
+    input_pre,
+    states,
+    mixed,
+    entering,
+    halo,
+    cot_all,
+    cumulative,
+    sibling_tails,
+    below_tail,
+    everyone,
+    before,
+    send,
+    recv,
+    local,
+):
+    me, z, p, c, x, y = place()
+    rows, channels = conv_input.shape[1:]
+    q, peers = column_peers(planes, z, p, c)
+    greet(peers + [*plane_neighbours()[0][:2]])
+    cot_begin, cot_forward, cot_end = gather_steps(cot, cot_all, send, recv, local, 9)
+    cot_begin()
+    f32 = jnp.float32
+    tail = pl.ds(rows - 16, 16)
+    to_sibling = remote(conv_input.at[:, tail], sibling_tails, send.at[7], recv.at[7], me + 1 - 2 * c)
+    to_above = remote(conv_input.at[CHIPS - 1, tail], below_tail, send.at[8], recv.at[8], me + 7)
+    from_below = remote(conv_input.at[CHIPS - 1, tail], below_tail, send.at[8], recv.at[8], me - 7)
+    to_sibling.start()
+
+    @pl.when((c == 1) & (z < planes - 1))
+    def send_above():
+        to_above.start()
+
+    to_sibling.wait()
+
+    @pl.when((c == 1) & (z < planes - 1))
+    def sent_above():
+        to_above.wait_send()
+
+    @pl.when((c == 0) & (z > 0))
+    def had_below():
+        from_below.wait_recv()
+
+    @pl.when(c == 1)
+    def halo_one():
+        for j in range(CHIPS):
+            halo[j] = sibling_tails[j].astype(f32)[8:]
+
+    @pl.when(c == 0)
+    def halo_zero():
+        for j in range(1, CHIPS):
+            halo[j] = sibling_tails[j - 1].astype(f32)[8:]
+
+        @pl.when(z > 0)
+        def halo_below():
+            halo[0] = below_tail[...].astype(f32)[8:]
+
+        @pl.when(z == 0)
+        def halo_none():
+            halo[0] = jnp.zeros((8, channels), f32)
+
+    row = lax.broadcasted_iota(jnp.int32, (8, channels), 0)
+
+    @pl.loop(0, CHIPS)
+    def block(j):
+        def conv_tile(i, earlier):
+            both = conv_input[j, sixteen(i), :].astype(f32)
+            outs = []
+            for h in range(2):
+                now = both[8 * h : 8 * h + 8]
+                keep = masks[j, eight(2 * i + h), :]
+                out = vectors[CW : CW + 1, :] + vectors[0:1, :] * now
+                for k in range(1, CW):
+                    out = out + vectors[k : k + 1, :] * (
+                        shift_down(earlier, now, k, row) * keep[:, k : k + 1]
+                    )
+                conv_out[j, eight(2 * i + h), :] = out
+                outs.append(out)
+                earlier = now
+            conv_low[j, sixteen(i), :] = jnp.concatenate(outs, axis=0).astype(jnp.bfloat16)
+            return earlier
+
+        lax.fori_loop(0, rows // 16, conv_tile, halo[j])
+        low = conv_low[j]
+        decay_pre[j] = jnp.dot(low, decay_blocks[...], preferred_element_type=f32) + vectors[CW + 1 : CW + 2, :]
+        input_pre[j] = jnp.dot(low, input_blocks[...], preferred_element_type=f32) + vectors[CW + 2 : CW + 3, :]
+
+        def scan_tile(i, carry):
+            at = eight(i)
+            flag = masks[j, at, :][:, 0:1]
+            opened, coef, keep, squared, gap = gate_terms(decay_pre[j, at, :], vectors[CW + 3 : CW + 4, :], flag)
+            drive = (flag + keep * jnp.sqrt(gap)) * sigmoid(input_pre[j, at, :]) * conv_out[j, at, :]
+            a, b = tile_scan(coef, drive, row, False)
+            before_a, before_b = carry
+            b = a * before_b + b
+            a = a * before_a
+            cumulative[j, at, :] = a
+            states[j, at, :] = b
+            return a[7:8], b[7:8]
+
+        last_a, last_b = lax.fori_loop(
+            0,
+            rows // 8,
+            scan_tile,
+            (jnp.ones((1, channels), f32), jnp.zeros((1, channels), f32)),
+        )
+        everyone[q, pl.ds(j, 1), :] = last_a
+        everyone[q, pl.ds(CHIPS + j, 1), :] = last_b
+
+    cot_forward()
+    carry_in(planes, False, z, c, q, peers, everyone, before, entering, send, recv)
+
+    @pl.loop(0, CHIPS)
+    def finish(j):
+        start = entering[pl.ds(j, 1), :]
+
+        def state_tile(i, unused):
+            at = sixteen(i)
+            state = states[j, at, :] + cumulative[j, at, :] * start
+            states[j, at, :] = state
+            v = gate_pre[j, at, :]
+            act = 0.5 * v * (1.0 + jnp.tanh(GELU_A * (v + GELU_B * (v * v * v))))
+            mixed[j, at, :] = (state * act).astype(jnp.bfloat16)
+            return unused
+
+        lax.fori_loop(0, rows // 16, state_tile, 0)
+
+    cot_end()
+
+
+def recurrence(gate_pre, conv_input, masks, vectors, decay_blocks, input_blocks, cot, collective_id):
+    planes = lax.axis_size("seq") // 8
+    blocks, rows, channels = conv_input.shape
+    f32, bf16 = jnp.float32, jnp.bfloat16
+    cube = conv_input.shape
+
+    def out(dtype, shape=cube):
+        return jax.ShapeDtypeStruct(shape, dtype)
+
+    return pl.pallas_call(
+        functools.partial(recurrence_kernel, planes),
+        out_shape=[
+            out(f32),
+            out(bf16),
+            out(f32),
+            out(f32),
+            out(f32),
+            out(bf16),
+            out(f32, (CHIPS, channels)),
+            out(f32, (CHIPS, 8, channels)),
+            out(cot.dtype, (CHIPS,) + cot.shape),
+        ],
+        in_specs=[VMEM] * 6 + [ANY],
+        out_specs=[VMEM] * 8 + [ANY],
+        scratch_shapes=[
+            pltpu.VMEM(cube, f32),
+            pltpu.VMEM((CHIPS, 16, channels), bf16),
+            pltpu.VMEM((16, channels), bf16),
+            pltpu.VMEM((2 * planes, 2 * CHIPS, channels), f32),
+            pltpu.VMEM((8 * planes, channels), f32),
+            pltpu.SemaphoreType.DMA((13,)),
+            pltpu.SemaphoreType.DMA((13,)),
+            pltpu.SemaphoreType.DMA,
+        ],
+        compiler_params=comm_params(collective_id, 48),
+        name="recurrence",
+    )(gate_pre, conv_input, masks, vectors, decay_blocks, input_blocks, cot)
+
+
+def recurrence_back_kernel(
+    planes,
+    grad_mixed,
+    gate_pre,
+    conv_input,
+    conv_out,
+    decay_pre,
+    input_pre,
+    states,
+    entering,
+    halo,
+    masks,
+    after_masks,
+    vectors,
+    decay_blocks,
+    input_blocks,
+    down_parts,
+    piece,
+    in_low,
+    decay_low,
+    input_low,
+    sums,
+    down_others,
+    swapped,
+    cumulative,
+    local,
+    grad_conv,
+    sibling_heads,
+    above_head,
+    ahead,
+    everyone,
+    before,
+    leaving,
+    send,
+    recv,
+    piece_sem,
+):
+    me, z, p, c, x, y = place()
+    rows, channels = conv_input.shape[1:]
+    q, peers = column_peers(planes, z, p, c)
+    devices, chips = plane_neighbours()
+    greet(peers + [*devices])
+    downs = [
+        remote(down_parts.at[chips[k]], down_others.at[k], send.at[9 + k], recv.at[9 + k], devices[k])
+        for k in range(3)
+    ] + [
+        remote(piece.at[chips[k]], swapped.at[p], send.at[12 + k], recv.at[12 + k], devices[k]) for k in range(3)
+    ]
+    downs.append(pltpu.make_async_copy(piece.at[p], swapped.at[p], piece_sem))
+    for copy in downs:
+        copy.start()
+    f32, bf16 = jnp.float32, jnp.bfloat16
+    row = lax.broadcasted_iota(jnp.int32, (8, channels), 0)
+    rate = vectors[CW + 3 : CW + 4, :]
+    nothing = jnp.zeros((8, channels), f32)
+
+    @pl.loop(0, CHIPS)
+    def scan_block(j):
+        def scan_tile(i, carry):
+            i = rows // 16 - 1 - i
+            at = sixteen(i)
+            v = gate_pre[j, at, :]
+            grad = grad_mixed[j, at, :]
+            t = jnp.tanh(GELU_A * (v + GELU_B * (v * v * v)))
+            act = 0.5 * v * (1.0 + t)
+            slope = 0.5 * (1.0 + t) + 0.5 * v * (1.0 - t * t) * (GELU_A * (1.0 + 3.0 * GELU_B * (v * v)))
+            in_low[j, at, 0:channels] = (grad * states[j, at, :] * slope).astype(bf16)
+            drive = grad * act
+            later_a, later_b, later_coef = carry
+            for h in (1, 0):
+                here = eight(2 * i + h)
+                flag = masks[j, here, :][:, 0:1]
+                coef = gate_terms(decay_pre[j, here, :], rate, flag)[1]
+                shifted = jnp.where(row < 7, pltpu.roll(coef, 7, 0), later_coef)
+                a, b = tile_scan(shifted, drive[8 * h : 8 * h + 8], row, True)
+                b = a * later_b + b
+                a = a * later_a
+                cumulative[j, here, :] = a
+                local[j, here, :] = b
+                later_a, later_b, later_coef = a[0:1], b[0:1], coef[0:1]
+            return later_a, later_b, later_coef
+
+        ones = jnp.ones((1, channels), f32)
+        first_a, first_b, first_coef = lax.fori_loop(
+            0, rows // 16, scan_tile, (ones, jnp.zeros((1, channels), f32), ones)
+        )
+        everyone[q, pl.ds(j, 1), :] = first_coef * first_a
+        everyone[q, pl.ds(CHIPS + j, 1), :] = first_coef * first_b
+
+    carry_in(planes, True, z, c, q, peers, everyone, before, leaving, send, recv)
+
+    def terms_block(j, totals):
+        behind_all = leaving[pl.ds(j, 1), :]
+
+        def terms_tile(i, carry):
+            previous, decay_sum, input_sum, param_sum = carry
+            lows = []
+            for h in range(2):
+                at = eight(2 * i + h)
+                adjoint = local[j, at, :] + cumulative[j, at, :] * behind_all
+                state = states[j, at, :]
+                earlier = jnp.where(row >= 1, pltpu.roll(state, 1, 0), previous)
+                previous = state[7:8]
+                flag = masks[j, at, :][:, 0:1]
+                opened, coef, keep, squared, gap = gate_terms(decay_pre[j, at, :], rate, flag)
+                passed = sigmoid(input_pre[j, at, :])
+                conv = conv_out[j, at, :]
+                inverse = lax.rsqrt(gap)
+                scale = flag + keep * (gap * inverse)
+                grad_log = adjoint * (earlier * coef - keep * passed * conv * squared * inverse)
+                log_open = grad_log * opened
+                decay_full = log_open * rate * (1.0 - opened)
+                direct = adjoint * scale * passed
+                input_full = direct * (1.0 - passed) * conv
+                grad_conv[j, at, :] = direct
+                lows.append((decay_full, input_full))
+                decay_sum = decay_sum + decay_full
+                input_sum = input_sum + input_full
+                param_sum = param_sum + log_open
+            decay_low[j, sixteen(i), :] = jnp.concatenate([low[0] for low in lows], axis=0).astype(bf16)
+            input_low[j, sixteen(i), :] = jnp.concatenate([low[1] for low in lows], axis=0).astype(bf16)
+            return previous, decay_sum, input_sum, param_sum
+
+        totals = lax.fori_loop(
+            0, rows // 16, terms_tile, (entering[pl.ds(j, 1), :], *totals)
+        )[1:]
+
+        def dot_t(left, right):
+            return lax.dot_general(left, right, (((1,), (1,)), ((), ())), preferred_element_type=f32)
+
+        grad_conv[j] = (
+            grad_conv[j] + dot_t(decay_low[j], decay_blocks[...]) + dot_t(input_low[j], input_blocks[...])
+        )
+        return totals
+
+    decay_sum, input_sum, param_sum = lax.fori_loop(0, CHIPS, terms_block, (nothing,) * 3)
+
+    to_sibling = remote(grad_conv.at[:, pl.ds(0, 8)], sibling_heads, send.at[7], recv.at[7], me + 1 - 2 * c)
+    to_below = remote(grad_conv.at[0, pl.ds(0, 8)], above_head, send.at[8], recv.at[8], me - 7)
+    from_above = remote(grad_conv.at[0, pl.ds(0, 8)], above_head, send.at[8], recv.at[8], me + 7)
+    to_sibling.start()
+
+    @pl.when((c == 0) & (z > 0))
+    def send_below():
+        to_below.start()
+
+    to_sibling.wait()
+
+    @pl.when((c == 0) & (z > 0))
+    def sent_below():
+        to_below.wait_send()
+
+    @pl.when((c == 1) & (z < planes - 1))
+    def had_above():
+        from_above.wait_recv()
+
+    @pl.when(c == 0)
+    def ahead_zero():
+        for j in range(CHIPS):
+            ahead[j] = sibling_heads[j]
+
+    @pl.when(c == 1)
+    def ahead_one():
+        for j in range(CHIPS - 1):
+            ahead[j] = sibling_heads[j + 1]
+
+        @pl.when(z < planes - 1)
+        def ahead_above():
+            ahead[CHIPS - 1] = above_head[...]
+
+        @pl.when(z == planes - 1)
+        def ahead_none():
+            ahead[CHIPS - 1] = nothing
+
+    def conv_block(j, totals):
+        def conv_pair(i, now, later, keep, later_keep, outs, earlier, given, totals):
+            out = vectors[0:1, :] * now
+            new_totals = [totals[0] + now * given]
+            for k in range(1, CW):
+                masked = now * keep[:, k : k + 1]
+                out = out + vectors[k : k + 1, :] * shift_up(
+                    masked, later * later_keep[:, k : k + 1], k, row
+                )
+                new_totals.append(totals[k] + masked * shift_down(earlier, given, k, row))
+            new_totals.append(totals[CW] + now)
+            outs.append(out)
+            return tuple(new_totals)
+
+        def conv_tile(i, carry, last):
+            earlier, totals = carry
+            inputs = conv_input[j, sixteen(i), :].astype(f32)
+            first, second = grad_conv[j, eight(2 * i), :], grad_conv[j, eight(2 * i + 1), :]
+            first_keep, second_keep = masks[j, eight(2 * i), :], masks[j, eight(2 * i + 1), :]
+            if last:
+                third, third_keep = ahead[j], after_masks[j]
+            else:
+                third, third_keep = grad_conv[j, eight(2 * i + 2), :], masks[j, eight(2 * i + 2), :]
+            outs = []
+            totals = conv_pair(i, first, second, first_keep, second_keep, outs, earlier, inputs[:8], totals)
+            totals = conv_pair(i, second, third, second_keep, third_keep, outs, inputs[:8], inputs[8:], totals)
+            in_low[j, sixteen(i), channels : 2 * channels] = jnp.concatenate(outs, axis=0).astype(bf16)
+            return inputs[8:], totals
+
+        carry = lax.fori_loop(
+            0, rows // 16 - 1, lambda i, carry: conv_tile(i, carry, False), (halo[j], totals)
+        )
+        return conv_tile(rows // 16 - 1, carry, True)[1]
+
+    totals = lax.fori_loop(0, CHIPS, conv_block, (nothing,) * (CW + 1))
+    for k, total in enumerate((*totals, decay_sum, input_sum, param_sum)):
+        sums[k : k + 1, :] = jnp.sum(total, axis=0, keepdims=True)
+    for copy in downs:
+        copy.wait()
+
+
+def recurrence_back(
+    grad_mixed,
+    gate_pre,
+    conv_input,
+    conv_out,
+    decay_pre,
+    input_pre,
+    states,
+    entering,
+    halo,
+    masks,
+    after_masks,
+    vectors,
+    decay_blocks,
+    input_blocks,
+    down_parts,
+    piece,
+    collective_id,
+):
+    planes = lax.axis_size("seq") // 8
+    cube = conv_input.shape
+    blocks, rows, channels = cube
+    f32, bf16 = jnp.float32, jnp.bfloat16
+    return pl.pallas_call(
+        functools.partial(recurrence_back_kernel, planes),
+        out_shape=[
+            jax.ShapeDtypeStruct((CHIPS, rows, 2 * channels), bf16),
+            jax.ShapeDtypeStruct(cube, bf16),
+            jax.ShapeDtypeStruct(cube, bf16),
+            jax.ShapeDtypeStruct((CW + 4, channels), f32),
+            jax.ShapeDtypeStruct((CHIPS - 1,) + down_parts.shape[1:], bf16),
+            jax.ShapeDtypeStruct(piece.shape, bf16),
+        ],
+        in_specs=[VMEM] * 14 + [ANY] * 2,
+        out_specs=[VMEM] * 4 + [ANY] * 2,
+        scratch_shapes=[
+            pltpu.VMEM(cube, f32),
+            pltpu.VMEM(cube, f32),
+            pltpu.VMEM(cube, f32),
+            pltpu.VMEM((CHIPS, 8, channels), f32),
+            pltpu.VMEM((8, channels), f32),
+            pltpu.VMEM((CHIPS, 8, channels), f32),
+            pltpu.VMEM((2 * planes, 2 * CHIPS, channels), f32),
+            pltpu.VMEM((8 * planes, channels), f32),
+            pltpu.VMEM((CHIPS, channels), f32),
+            pltpu.SemaphoreType.DMA((15,)),
+            pltpu.SemaphoreType.DMA((15,)),
+            pltpu.SemaphoreType.DMA,
+        ],
+        compiler_params=comm_params(collective_id, 52),
+        name="recurrence_back",
+    )(
+        grad_mixed,
+        gate_pre,
+        conv_input,
+        conv_out,
+        decay_pre,
+        input_pre,
+        states,
+        entering,
+        halo,
+        masks,
+        after_masks,
+        vectors,
+        decay_blocks,
+        input_blocks,
+        down_parts,
+        piece,
+    )
+
+
+def regrouped_kernel(back, devices, *refs):
+    count = len(refs) // 2
+    for source, target in zip(refs[:count], refs[count:]):
+        step = source.shape[1] // devices
+        for k in range(devices // 2):
+            for e in range(2):
+                split, joined = (2 * k + e) * step, (devices // 2 * e + k) * step
+                start, end = (joined, split) if back else (split, joined)
+                target[:, end : end + step] = source[:, start : start + step].astype(target.dtype)
+
+
+def regrouped_columns(arrays, dtypes, back):
+    devices = lax.axis_size("seq")
+    return pl.pallas_call(
+        functools.partial(regrouped_kernel, back, devices),
+        out_shape=[jax.ShapeDtypeStruct(a.shape, dtype) for a, dtype in zip(arrays, dtypes)],
+        in_specs=[VMEM] * len(arrays),
+        out_specs=[VMEM] * len(arrays),
+        compiler_params=pltpu.CompilerParams(vmem_limit_bytes=24 * 2**20),
+        name="regrouped_columns",
+    )(*arrays)
+
+
+def to_chips_kernel(planes, pairs, *refs):
+    ins, outs = refs[: len(pairs)], refs[len(pairs) :]
+    for source, targets in zip(ins, pairs):
+        width = source.shape[1] // (planes * 8)
+        for z in range(planes):
+            for p in range(CHIPS):
+                for c in range(2):
+                    k, at = targets[c]
+                    start = ((z * CHIPS + p) * 2 + c) * width
+                    outs[k][p, :, at + z * width : at + (z + 1) * width] = source[:, start : start + width]
+
+
+def to_chips(weights, pairs, widths):
+    planes = lax.axis_size("seq") // 8
+    return pl.pallas_call(
+        functools.partial(to_chips_kernel, planes, pairs),
+        out_shape=[
+            jax.ShapeDtypeStruct((CHIPS, weights[0].shape[0], width), weights[0].dtype) for width in widths
+        ],
+        in_specs=[VMEM] * len(weights),
+        out_specs=[VMEM] * len(widths),
+        name="to_chips",
+    )(*weights)
+
+
+def from_chips_kernel(planes, pairs, *refs):
+    outs, ins = refs[-len(pairs) :], refs[: -len(pairs)]
+    for target, sources in zip(outs, pairs):
+        width = target.shape[1] // (planes * 8)
+        for z in range(planes):
+            for p in range(CHIPS):
+                for c in range(2):
+                    k, at = sources[c]
+                    start = ((z * CHIPS + p) * 2 + c) * width
+                    target[:, start : start + width] = ins[k][
+                        p, :, at + z * width : at + (z + 1) * width
+                    ].astype(jnp.float32)
+
+
+def from_chips(parts, pairs, widths):
+    planes = lax.axis_size("seq") // 8
+    return pl.pallas_call(
+        functools.partial(from_chips_kernel, planes, pairs),
+        out_shape=[jax.ShapeDtypeStruct((parts[0].shape[1], width), jnp.float32) for width in widths],
+        in_specs=[VMEM] * len(parts),
+        out_specs=[VMEM] * len(widths),
+        compiler_params=pltpu.CompilerParams(vmem_limit_bytes=32 * 2**20),
+        name="from_chips",
+    )(*parts)
+
+
+def regrouped(values, axis, n):
+    shape = values.shape
+    split = shape[:axis] + (n // 2, 2, shape[axis] // n) + shape[axis + 1 :]
+    return jnp.moveaxis(values.reshape(split), axis + 1, axis).reshape(shape)
+
+
+def behind(value, *earlier):
+    return lax.optimization_barrier((value, *earlier))[0]
+
+
+def plane_body(
+    tokens,
+    starts,
+    cotangent,
+    norm_gain,
+    gate_branch,
+    input_branch,
+    conv_weight,
+    conv_bias,
+    decay_gate,
+    decay_bias,
+    input_gate,
+    input_bias,
+    decay_param,
+    out_proj,
+    mlp_gain,
+    mlp_gate,
+    mlp_up,
+    mlp_down,
+):
+    f32, bf16 = jnp.float32, jnp.bfloat16
+    n = lax.axis_size("seq")
+    planes = n // 8
+    me, z, p, c, x, y = place()
+    groups = column_groups(n)
+    rows, width = tokens.shape
+    rows_d, lru_width = gate_branch.shape
+    head = decay_gate.shape[1]
+    rows_r, rows_f = out_proj.shape[0], mlp_down.shape[0]
+    channels = lru_width // CHIPS
+    units = mlp_gate.shape[1] // CHIPS
+    half_units = units // 2
+
+    def column_gather(block):
+        return lax.all_gather(block, "seq", axis=0, tiled=True, axis_index_groups=groups)
+
+    def line_sum(parts):
+        return lax.psum_scatter(
+            parts, "seq", scatter_dimension=0, tiled=True, axis_index_groups=line_groups(n)
+        )
+
+    sibling = [(d, d + 1 - 2 * (d % 2)) for d in range(n)]
+
+    def halves(values, axis):
+        half = values.shape[axis] // 2
+        return (
+            lax.dynamic_slice_in_dim(values, c * half, half, axis),
+            lax.dynamic_slice_in_dim(values, (1 - c) * half, half, axis),
+        )
+
+    def exchanged(values):
+        return lax.ppermute(values, "seq", sibling)
+
+    def product(left, right):
+        return jnp.dot(left, right, preferred_element_type=f32)
+
+    def product_t(left, right):
+        return jnp.einsum("tk,nk->tn", left, right, preferred_element_type=f32)
+
+    def weight_grad(left, right):
+        return jnp.einsum("ta,tb->ab", left, right, preferred_element_type=f32)
+
+    lanes = 128
+
+    def row(values):
+        return jnp.pad(values.astype(f32), (0, lanes - values.shape[0]))[None]
+
+    small = jnp.concatenate(
+        [
+            row(norm_gain),
+            row(mlp_gain),
+            starts.astype(f32).reshape(rows // lanes, lanes),
+            *[row(conv_weight[k]) for k in range(CW)],
+            row(conv_bias),
+            row(decay_bias),
+            row(input_bias),
+            row(decay_param),
+            jnp.zeros((4, lanes), f32),
+        ],
+        axis=0,
+    )
+    half = channels // 2
+    in_pairs = (((0, 0), (0, half)), ((0, channels), (0, channels + half)))
+    (weights_in,) = to_chips([gate_branch, input_branch], in_pairs, [2 * channels])
+    swapped_in, small = opening(weights_in, small, 1)
+    small = small.transpose(1, 0, 2, 3)
+    flags = 2 + rows // lanes
+    gain_one = regrouped(small[:, :, 0, :rows_d].reshape(width), 0, n)
+    gain_two = regrouped(small[:, :, 1, :rows_d].reshape(width), 0, n)
+    all_flags = small[:, :, 2:flags].reshape(n * rows)
+    vectors = lax.dynamic_slice_in_dim(
+        small.reshape(planes, CHIPS, 2, 16, lanes), p, 1, axis=1
+    )[:, 0, :, flags : flags + CW + 4, :rows_r]
+    vectors = vectors.transpose(2, 1, 0, 3).reshape(CW + 4, channels)
+    param = vectors[CW + 3]
+    vectors = vectors.at[CW + 3].set(-rate_scale * jax.nn.softplus(param))
+
+    running = jnp.ones((n * rows,), f32)
+    masks_all = [running]
+    for offset in range(1, CW):
+        earlier = jnp.concatenate([jnp.zeros((offset - 1,), f32), all_flags[: n * rows - (offset - 1)]])
+        running = running * (1.0 - earlier)
+        masks_all.append(running)
+    masks_all = jnp.stack(masks_all).reshape(CW, planes, CHIPS, 2, rows)
+
+    def own_blocks(values):
+        return lax.dynamic_slice(
+            values,
+            (0, z, 0, c, 0),
+            (values.shape[0], 1, CHIPS, 1, values.shape[4]),
+        )[:, 0, :, 0]
+
+    after_masks = masks_all[..., :8].reshape(CW, n, 8)
+    after_masks = jnp.concatenate([after_masks[:, 1:], jnp.zeros((CW, 1, 8), f32)], axis=1)
+    after_masks = own_blocks(after_masks.reshape(CW, planes, CHIPS, 2, 8)).transpose(1, 2, 0)
+    masks_all = jnp.concatenate([all_flags.reshape(1, planes, CHIPS, 2, rows), masks_all[1:]], axis=0)
+    masks = own_blocks(masks_all).transpose(1, 2, 0)
+
+    mlp_pairs = (((0, 0), (1, 0)), ((0, half_units), (1, half_units)))
+    mlp_pieces = to_chips([mlp_gate, mlp_up], mlp_pairs, [2 * half_units] * 2)
+    whole_in = column_gather(swapped_in.reshape(CHIPS * rows_d, 2 * channels))
+    tokens, cot, out_proj, mlp_down = regrouped_columns(
+        [tokens, cotangent, out_proj, mlp_down], [bf16] * 4, False
+    )
+    rec_rows = column_gather(jnp.concatenate([out_proj, decay_gate, input_gate], axis=1))
+    whole_out, gates = rec_rows[:, :width], rec_rows[:, width:]
+    gates = gates.reshape(2, planes, rows_r, 2, 2, rows_r)
+    diagonal = jnp.eye(planes, dtype=bf16)[None, :, None, None, :, None]
+    decay_blocks, input_blocks = (
+        (gates[:, :, :, k, :, None, :] * diagonal).reshape(channels, channels) for k in range(2)
+    )
+
+    normed = rms_norm(tokens.astype(f32), gain_one).astype(bf16)
+    normed_all = plane_gather(normed, 3).reshape(CHIPS * rows, width)
+    swapped_mlp = plane_swap(behind(tuple(mlp_pieces), normed_all, decay_blocks, input_blocks), 4)
+    whole_down = column_gather(mlp_down)
+    whole_mlp = [column_gather(part.reshape(CHIPS * rows_d, 2 * half_units)) for part in swapped_mlp]
+
+    gate_pre = product(normed_all, whole_in[:, :channels])
+    cube = (CHIPS, rows, channels)
+    gate_pre = gate_pre.reshape(cube)
+    conv_input = product(normed_all, whole_in[:, channels:]).astype(bf16).reshape(cube)
+    conv_out, conv_low, decay_pre, input_pre, states, mixed, entering, halo, cot_all = recurrence(
+        gate_pre, conv_input, masks, vectors, decay_blocks, input_blocks, cot, 6
+    )
+    cot_all = cot_all.reshape(CHIPS * rows, width)
+    mixed = mixed.reshape(CHIPS * rows, channels)
+    branch_parts = product(mixed, whole_out).reshape(CHIPS, rows, width)
+    middle, two_all = middle_of(branch_parts, tokens, gain_two, 7)
+    two_all = two_all.reshape(CHIPS * rows, width)
+
+    cot_other = exchanged(cot_all)
+    two_own, two_other = halves(two_all, 1)
+    two_other = exchanged(two_other)
+    grad_hidden = product_t(cot_all, whole_down)
+    hiddens, grads_low, piece_grads = [], [], []
+    two_now = two_all
+    for k in range(2):
+        weights = whole_mlp[k]
+        gate_mlp = product(two_now, weights[:, :half_units])
+        up_mlp = product(two_now, weights[:, half_units:])
+        hidden, pull_act = jax.vjp(mlp_act, gate_mlp, up_mlp)
+        hiddens.append(hidden.astype(bf16))
+        grad_gate, grad_up = pull_act(grad_hidden[:, k * half_units : (k + 1) * half_units])
+        low = jnp.concatenate([grad_gate.astype(bf16), grad_up.astype(bf16)], axis=1)
+        grads_low.append(low)
+        piece_grads.append((weight_grad(two_own, low) + weight_grad(two_other, exchanged(low))).astype(bf16))
+        two_now = behind(two_now, piece_grads[-1])
+    hidden = jnp.concatenate(hiddens, axis=1)
+    two_parts = product_t(grads_low[0], whole_mlp[0]) + product_t(grads_low[1], whole_mlp[1])
+    two_parts = behind(two_parts.astype(bf16), piece_grads[1])
+    piece_grads = [line_sum(part) for part in piece_grads]
+    grad_middle, grad_mlp_gain, grad_branch, down_grad, down_parts = grads_of_middle(
+        two_parts.reshape(CHIPS, rows, width), middle, cot, gain_two, hidden, whole_down, cot_all, cot_other, 9
+    )
+    grad_mlp_down = line_sum(down_grad)
+    grad_branch = grad_branch.reshape(CHIPS * rows, width)
+
+    mixed_own, mixed_other = halves(mixed, 1)
+    out_grad = weight_grad(mixed_own, grad_branch) + weight_grad(
+        exchanged(mixed_other), exchanged(grad_branch)
+    )
+    out_grad = out_grad.astype(bf16)
+    grad_out_proj = line_sum(out_grad)
+    grad_mixed = behind(product_t(grad_branch, whole_out), out_grad)
+    in_low, grad_decay_low, grad_input_low, sums, down_others, swapped_grads = recurrence_back(
+        grad_mixed.reshape(cube),
+        gate_pre,
+        conv_input,
+        conv_out,
+        decay_pre,
+        input_pre,
+        states,
+        entering,
+        halo,
+        masks,
+        after_masks,
+        vectors,
+        decay_blocks,
+        input_blocks,
+        down_parts,
+        piece_grads[0].reshape(CHIPS, rows_d, 2 * half_units),
+        12,
+    )
+    down_sum = lax.dynamic_index_in_dim(down_parts, p, 0, False).astype(f32) + jnp.sum(
+        down_others.astype(f32), axis=0
+    )
+    block_out = middle + down_sum
+    sums = sums.at[CW + 3].multiply(-rate_scale * jax.nn.sigmoid(param))
+    in_low = in_low.reshape(CHIPS * rows, 2 * channels)
+    flat = (CHIPS * rows, channels)
+    conv_low, grad_decay_low, grad_input_low = (
+        a.reshape(flat) for a in (conv_low, grad_decay_low, grad_input_low)
+    )
+
+    normed_own, normed_other = halves(normed_all, 1)
+    in_grads = weight_grad(normed_own, in_low) + weight_grad(exchanged(normed_other), exchanged(in_low))
+    in_total = in_grads.astype(bf16)
+    in_grads = line_sum(in_total)
+    normed_parts = product_t(in_low, whole_in).astype(bf16).reshape(CHIPS, rows, width)
+    normed_parts = behind(normed_parts, in_total)
+    convs, decays, inputs = (
+        (own, exchanged(other))
+        for own, other in (halves(conv_low, 1), (grad_decay_low, grad_decay_low), (grad_input_low, grad_input_low))
+    )
+    vector_parts = sums.reshape(CW + 4, 2, planes, rows_r).transpose(2, 1, 0, 3)
+    vector_parts = jnp.pad(vector_parts, ((0, 0), (0, 0), (0, 0), (0, lanes - rows_r)))
+    here = (jnp.arange(CHIPS) == p).astype(f32)[None, :, None, None, None]
+    vector_parts = (vector_parts[:, None] * here).reshape(planes, 8, CW + 4, lanes)
+    gain_parts = grad_mlp_gain.reshape(2, planes, CHIPS, 1, rows_d).transpose(1, 2, 0, 3, 4)
+    gain_parts = jnp.pad(
+        gain_parts.reshape(planes, 8, 1, rows_d), ((0, 0), (0, 0), (0, 7), (0, lanes - rows_d))
+    )
+    grad_tokens, small_grads, gate_grads, swapped_late = closing(
+        normed_parts,
+        tokens,
+        gain_one,
+        grad_middle,
+        jnp.concatenate([vector_parts, gain_parts], axis=2),
+        convs,
+        decays,
+        inputs,
+        piece_grads[1].reshape(CHIPS, rows_d, 2 * half_units),
+        head,
+        13,
+    )
+    grad_mlp_gate, grad_mlp_up = from_chips(
+        [swapped_grads, swapped_late], mlp_pairs, [mlp_gate.shape[1]] * 2
+    )
+    block_out, grad_out_proj, grad_mlp_down = regrouped_columns(
+        behind((block_out, grad_out_proj, grad_mlp_down), grad_tokens), [bf16, f32, f32], True
+    )
+    in_out = plane_swap([in_grads.reshape(CHIPS, rows_d, 2 * channels)], 16)
+    grad_gate_branch, grad_input_branch = from_chips(in_out, in_pairs, [lru_width] * 2)
+    vector_grads = small_grads[: CW + 4, :rows_r]
+    return (
+        block_out,
+        grad_tokens,
+        small_grads[CW + 12, :rows_d],
+        grad_gate_branch,
+        grad_input_branch,
+        vector_grads[:CW],
+        vector_grads[CW],
+        gate_grads[:, :head],
+        vector_grads[CW + 1],
+        gate_grads[:, head:],
+        vector_grads[CW + 2],
+        vector_grads[CW + 3],
+        grad_out_proj,
+        small_grads[CW + 4, :rows_d],
+        grad_mlp_gate,
+        grad_mlp_up,
+        grad_mlp_down,
+    )
+
+
 def solution(mesh):
     in_specs = (
         P("seq", None),
@@ -417,4 +1952,5 @@
         P("seq", None),
         P("seq", None),
     )
+    body = plane_body if mesh.shape["seq"] == 2 * H else token_split_body
     return jax.shard_map(body, mesh=mesh, in_specs=in_specs, out_specs=out_specs, check_vma=False)

time: 3600 us -> 722 us (0.20)
  waiting for transfers between devices: 2430 us -> 4.99 us
  Pallas kernels: 0 us -> 466 us
  blocking collectives: 372 us -> 0 us
  local copies, waits for them, and re-layouts: 402 us -> 71.1 us
  matrix products: 253 us -> 140 us
  other arithmetic: 111 us -> 16.1 us
    reduce_scatter x8 -> x5, waiting for transfers between devices: 2230 us -> 0.01 us  [line_sum(): lax.psum_scatter(parts, 'seq', scatter_dimension=0, tiled=True, axis_inde...]
    pallas_call x0 -> x15, Pallas kernels: none -> 466 us  [the longest x1 105 us: middle_of(): pl.pallas_call(middle_kernel, out_shape=[jax.ShapeDtypeStruct((rows, widt...]
    all_gather x7 -> x0, blocking collectives: 289 us -> none  [the longest x4 157 us: prefix(): everything = jax.tree.map(lambda part: lax.all_gather(part, axis), value)]
    slice x114 -> x12, local copies, waits for them, and re-layouts: 233 us -> 5.45 us  [the longest x2 1.32 us: plane_body(): whole_out, gates = (rec_rows[:, :width], rec_rows[:, width:])]
    all_gather x6 -> x5, waiting for transfers between devices: 192 us -> 0.05 us  [column_gather(): lax.all_gather(block, 'seq', axis=0, tiled=True, axis_index_groups=groups)]
    dot_general x24 -> x20, matrix products: 253 us -> 140 us  [the longest x5 51.9 us: product_t(): return jnp.einsum('tk,nk->tn', left, right, preferred_element_type=f32)]
    pad x56 -> x1, local copies, waits for them, and re-layouts: 86.2 us -> 0.01 us  [plane_body(): jnp.pad(vector_parts, ((0, 0), (0, 0), (0, 0), (0, lanes - rows_r)))]
    unnamed x2 -> x0, blocking collectives: 83.6 us -> none
  transfers between devices with their start and end apart: 17 -> 21, of which waited for: 12 -> 3; matrix products, arithmetic and copies ran while one was open for 12% -> 26% of each run, Pallas kernels for 0% -> 63%
where the time goes in v2:
time: 722 us; the launch traced here: 717 us
  Pallas kernels  466 us (65%)
  matrix products  140 us (19%)
  local copies, waits for them, and re-layouts  71.1 us (10%)
  other arithmetic  16.1 us (2%)
  between operations  15.6 us (2%)
    pallas_call x1, Pallas kernels, middle_of(): pl.pallas_call(middle_kernel, out_shape=[jax.ShapeDtypeStruct((rows, widt...  105 us
    pallas_call x1, Pallas kernels, grads_of_middle(): pl.pallas_call(grads_of_middle_kernel, out_shape=[jax.ShapeDtypeStruct((r...  82.1 us
    pallas_call x1, Pallas kernels, recurrence_back(): pl.pallas_call(functools.partial(recurrence_back_kernel, planes), out_sha...  72.3 us
    pallas_call x1, Pallas kernels, closing(): pl.pallas_call(functools.partial(closing_kernel, planes), out_shape=[jax....  57.9 us
    dot_general x5, matrix products, product_t(): return jnp.einsum('tk,nk->tn', left, right, preferred_element_type=f32)  51.9 us
    unnamed x144, local copies, waits for them, and re-layouts  45.8 us
    pallas_call x1, Pallas kernels, recurrence(): pl.pallas_call(functools.partial(recurrence_kernel, planes), out_shape=[o...  45.5 us
    dot_general x7, matrix products, product(): return jnp.dot(left, right, preferred_element_type=f32)  45.3 us
  transfers between devices with their start and end apart: 21, of which 3 were waited for; matrix products, arithmetic and copies ran while one was open for 26% of the time, Pallas kernels for 63%

profile of v2, /device:TPU:0, one launch (start us, length us, event | category | flops | bytes accessed | tf_op | source)
XLA Modules:
  0.0 717.0 jit_solution(2912320616890695271)
XLA Ops:
  11.9 2.8 regrouped_columns.2
  16.6 2.4 to_chips.2.weights_ref
  20.4 18.6 %opening.1 = (bf16[4,64,1280]{2,1,0:T(8,128)(2,1)}, f32[8,4,16,128]{3,2,1,0:T(8,128)}) custom-call(bf16[4,64,1280]{2,1,0:T(8,128)(2,1)} %to_chips.2.weights_ref, f32[16,128]{1,0:T(8,128)} %concatenate.45.x_ref), custom_call_target="tpu_custom_call" | custom-call | tf_op jit(solution)/shard_map/opening/pallas_call | solution.py:1003
  42.6 39.5 %plane_gather.1 = bf16[4,256,2048]{2,1,0:T(8,128)(2,1)} custom-call(bf16[256,2048]{1,0:T(8,128)(2,1)} %fusion.33.x_ref), custom_call_target="tpu_custom_call" | custom-call | tf_op jit(solution)/shard_map/plane_gather/pallas_call | solution.py:914
  82.1 2.8 to_chips.3
  88.1 2.9 broadcast_multiply_fusion
  91.0 2.2 mul.251.decay_blocks
  93.2 2.5 mul.255.input_blocks
  95.7 20.1 %plane_swap.2 = (bf16[4,64,1536]{2,1,0:T(8,128)(2,1)}, bf16[4,64,1536]{2,1,0:T(8,128)(2,1)}) custom-call(bf16[4,64,1536]{2,1,0:T(8,128)(2,1)} %get-tuple-element.105.refs_0_, bf16[4,64,1536]{2,1,0:T(8,128)(2,1)} %get-tuple-element.106.refs_1_), custom_call_target="tpu_custom_call" | custom-call | tf_op jit(solution)/shard_map/plane_swap/pallas_call | solution.py:951
  120.0 8.2 %fusion.41 = bf16[1024,640]{1,0:T(8,128)(2,1)} fusion(bf16[1024,2048]{1,0:T(8,128)(2,1)} %bitcast.160, bf16[2048,1280]{1,0:T(8,128)(2,1)} %all-gather.6.cloned.1.call-done), kind=kOutput, calls=%fused_computation.65 | convolution fusion | flops 2685009920 | bytes 8126464 | tf_op jit(solution)/shard_map/dot_general | solution.py:1693
  128.2 4.9 fusion.25.gate_pre
  133.1 45.5 %recurrence.1 = (f32[4,256,640]{2,1,0:T(8,128)}, bf16[4,256,640]{2,1,0:T(8,128)(2,1)S(1)}, f32[4,256,640]{2,1,0:T(8,128)}, f32[4,256,640]{2,1,0:T(8,128)}, f32[4...) custom-call(f32[4,256,640]{2,1,0:T(8,128)} %fusion.25.gate_pre, ...), custom_call_target="tpu_custom_call" | custom-call | tf_op jit(solution)/shard_map/recurrence/pallas_call | solution.py:1239
  179.7 5.2 fusion.26.parts
  184.9 105.4 %middle.1 = (f32[256,2048]{1,0:T(8,128)S(1)}, bf16[4,256,2048]{2,1,0:T(8,128)(2,1)S(1)}) custom-call(f32[4,256,2048]{2,1,0:T(8,128)S(1)} %fusion.26.parts, bf16[256,2048]{1,0:T(8,128)(2,1)S(1)} %get-tuple-element.93.tokens, f32[1,2048]{1,0:T(1,128)S(1)} %broadcast_in_dim_reshape.8.gain), custom_call_target="tpu_custom_call" | custom-call | tf_op jit(solution)/shard_map/middle/pallas_call | solution.py:557
  291.7 2.0 copy-done.22
  293.7 11.9 %fusion.62 = f32[1024,1536]{1,0:T(8,128)} fusion(bf16[1024,2048]{1,0:T(8,128)(2,1)} %bitcast.166, bf16[1536,2048]{1,0:T(8,128)(2,1)} %all-gather.10.cloned.1.call-done.down), kind=kOutput, calls=%fused_computation.135 | convolution fusion | flops 6442450944 | bytes 16777216 | tf_op jit(solution)/shard_map/tk,nk->tn/dot_general | solution.py:1696
  305.6 6.3 fusion.20
  311.9 1.8 copy-done.67
  313.7 6.1 fusion.6
  319.9 2.1 pad_maximum_fusion
  322.5 3.1 constant_dynamic-slice_fusion.5
  326.1 6.0 fusion.39
  332.2 7.8 %add_convert_fusion.2 = bf16[1024,1536]{1,0:T(8,128)(2,1)} fusion(f32[1024,1536]{1,0:T(8,128)S(1)} %fusion.39, bf16[1024,1024]{1,0:T(8,128)(2,1)} %collective-permute-done, bf16[1024,1536]{1,0:T(8,128)(2,1)} %collective-permute-done.1), kind=kOutput, calls=%fused_computation.3 | convolution fusion | flops 3224371200 | bytes 14680064 | tf_op jit(solution)/shard_map/ta,tb->ab/dot_general | solution.py:1699
  340.1 6.5 fusion.16
  346.7 8.0 %fusion.13 = (bf16[1024,768]{1,0:T(8,128)(2,1)S(1)}, bf16[1024,768]{1,0:T(8,128)(2,1)S(1)}, bf16[1024,768]{1,0:T(8,128)(2,1)}) fusion(f32[1024,768]{1,0:T(8,128)S(1)} %fusion.16, f32[1024,1536]{1,0:T(8,128)} %fusion.62, bf16[1024,2048]{1,0:T(8,128)(2,1)S(1)} %bitcast.154, bf16[2048,1536]{1,0:T(8,128)(2,1)S(1)} %copy-done.63), kind=kOutput, calls=%fused_computation.23 | convolution fusion | flops 3241672704 | bytes 18350080 | tf_op jit(solution)/shard_map/dot_general | solution.py:1693
  356.3 3.5 fusion.37
  360.6 6.8 add_convert_fusion.1
  367.7 12.3 %fusion.58 = f32[1024,2048]{1,0:T(8,128)} fusion(bf16[2048,1536]{1,0:T(8,128)(2,1)} %all-gather.12.cloned.1.call-done, bf16[1024,768]{1,0:T(8,128)(2,1)} %copy-done.41, bf16[1024,768]{1,0:T(8,128)(2,1)} %copy-done.40), kind=kOutput, calls=%fused_computation.131 | convolution fusion | flops 6448742400 | bytes 17825792 | tf_op jit(solution)/shard_map/tk,nk->tn/dot_general | solution.py:1696
  379.9 1.9 pad_maximum_fusion.2.hidden
  383.0 12.5 %add_convert_fusion = bf16[1024,2048]{1,0:T(8,128)(2,1)} fusion(f32[1024,2048]{1,0:T(8,128)} %fusion.58, bf16[2048,1536]{1,0:T(8,128)(2,1)} %all-gather.14.cloned.1.call-done, bf16[1024,768]{1,0:T(8,128)(2,1)S(1)} %copy-done.45, bf16[1024,768]{1,0:T(8,128)(2,1)S(1)} %copy-done.43), kind=kOutput, calls=%fused_computation | convolution fusion | flops 6452936704 | bytes 22020096 | tf_op jit(solution)/shard_map/tk,nk->tn/dot_general | solution.py:1696
  395.5 1.9 copy-done.39
  397.4 82.1 %grads_of_middle.1 = (f32[256,2048]{1,0:T(8,128)}, f32[1,2048]{1,0:T(1,128)}, bf16[4,256,2048]{2,1,0:T(8,128)(2,1)}, bf16[768,2048]{1,0:T(8,128)(2,1)}, bf16[4,256,2048]{2,1,0:T(8,128)(2,1)}) custom-call(bf16[4,256,2048]{2,1,0:T(8,128)(2,1)} %bitcast.169, f32[256,2048]{1,0:T(8,128)} %copy-done, bf16[256,2048]{1,0:T(8,128)(2,1)} %copy-done.5, ...), custom_call_target="tpu_custom_call" | custom-call | tf_op jit(solution)/shard_map/grads_of_middle/pallas_call | solution.py:688
  482.0 2.2 copy.161
  484.3 8.0 %fusion.28 = f32[1024,640]{1,0:T(8,128)} fusion(bf16[1024,2048]{1,0:T(8,128)(2,1)} %bitcast.196, bf16[640,2368]{1,0:T(8,128)(2,1)} %all-gather.8.cloned.1.call-done), kind=kOutput, calls=%fused_computation.51 | convolution fusion | flops 2684354560 | bytes 9437184 | tf_op jit(solution)/shard_map/tk,nk->tn/dot_general | solution.py:1696
  492.3 3.9 fusion.63
  496.2 2.8 fusion.22
  499.0 72.3 %recurrence_back.1 = (bf16[4,256,1280]{2,1,0:T(8,128)(2,1)}, bf16[4,256,640]{2,1,0:T(8,128)(2,1)}, bf16[4,256,640]{2,1,0:T(8,128)(2,1)}, f32[8,640]{1,0:T(8,128)...) custom-call(f32[4,256,640]{2,1,0:T(8,128)} %bitcast.170, f32[4,256,640]{2,1,0:T(8,128)} %fusion.25.gate_pre, ...), custom_call_target="tpu_custom_call" | custom-call | tf_op jit(solution)/shard_map/recurrence_back/pallas_call | solution.py:1507
  573.3 5.3 fusion.35
  580.2 6.8 add_convert_fusion.3
  590.7 1.7 collective-permute-done.8
  596.2 2.9 convert_reduce_fusion
  599.1 3.2 fusion.34.refs_0_
  602.4 7.2 %convolution_convert_fusion = bf16[1024,2048]{1,0:T(8,128)(2,1)} fusion(bf16[1024,1280]{1,0:T(8,128)(2,1)S(1)} %bitcast.200, bf16[2048,1280]{1,0:T(8,128)(2,1)S(1)} %bitcast.194), kind=kOutput, calls=%fused_computation.9 | convolution fusion | flops 5370806272 | bytes 12058624 | tf_op jit(solution)/shard_map/tk,nk->tn/dot_general | solution.py:1696
  622.1 57.9 %closing.1 = (f32[256,2048]{1,0:T(8,128)S(1)}, f32[24,128]{1,0:T(8,128)S(1)}, f32[80,320]{1,0:T(8,128)S(1)}, bf16[4,64,1536]{2,1,0:T(8,128)(2,1)S(1)}) custom-call(bf16[4,256,2048]{2,1,0:T(8,128)(2,1)} %bitcast.165, bf16[256,2048]{1,0:T(8,128)(2,1)S(1)} %get-tuple-element.93.tokens, f32[1,2048]{1,0:T(1,128)S(1)} %broadcast_in_dim_reshape.9.gain, ...), custom_call_target="tpu_custom_call" | custom-call | tf_op jit(solution)/shard_map/closing/pallas_call | solution.py:873
  685.0 1.9 from_chips.3
  689.1 2.4 regrouped_columns.3
  693.2 11.0 %plane_swap.3.refs_0_ = bf16[4,64,1280]{2,1,0:T(8,128)(2,1)} custom-call(bf16[4,64,1280]{2,1,0:T(8,128)(2,1)} %bitcast.179), custom_call_target="tpu_custom_call" | custom-call | tf_op jit(solution)/shard_map/plane_swap/pallas_call | solution.py:951
  706.8 3.1 copy.171
  (266 shorter events, 63.1 us)
Async XLA Ops:
  7.2 77.8 %all-gather.8.cloned.1.call-start = ((), (), s32[]{:S(2)}) async-start(), calls=%async_computation.6 | async-start | bytes 3502080 | tf_op jit(solution)/shard_map/all_gather | solution.py:1673
  11.8 7.2 %copy-start.54 = (bf16[4,80]{1,0:T(4,128)(2,1)S(1)}, bf16[4,80]{1,0:T(4,128)(2,1)}, u32[]{:S(2)}) copy-start(bf16[4,80]{1,0:T(4,128)(2,1)} %param.28) | copy-start | bytes 1924
  11.8 7.3 %copy-start.56 = (bf16[80]{0:T(256)(128)(2,1)S(1)}, bf16[80]{0:T(256)(128)(2,1)}, u32[]{:S(2)}) copy-start(bf16[80]{0:T(256)(128)(2,1)} %param.34) | copy-start | bytes 484
  11.8 7.3 %copy-start.57 = (bf16[80]{0:T(256)(128)(2,1)S(1)}, bf16[80]{0:T(256)(128)(2,1)}, u32[]{:S(2)}) copy-start(bf16[80]{0:T(256)(128)(2,1)} %param.33) | copy-start | bytes 484
  11.8 7.3 %copy-start.58 = (bf16[80]{0:T(256)(128)(2,1)S(1)}, bf16[80]{0:T(256)(128)(2,1)}, u32[]{:S(2)}) copy-start(bf16[80]{0:T(256)(128)(2,1)} %param.31) | copy-start | bytes 484
  11.8 7.3 %copy-start.59 = (bf16[80]{0:T(256)(128)(2,1)S(1)}, bf16[80]{0:T(256)(128)(2,1)}, u32[]{:S(2)}) copy-start(bf16[80]{0:T(256)(128)(2,1)} %param.29) | copy-start | bytes 484
  11.8 7.3 %copy-start.60 = (bf16[64]{0:T(256)(128)(2,1)S(1)}, bf16[64]{0:T(256)(128)(2,1)}, u32[]{:S(2)}) copy-start(bf16[64]{0:T(256)(128)(2,1)} %param.36) | copy-start | bytes 388
  11.8 7.3 %copy-start.61 = (bf16[64]{0:T(256)(128)(2,1)S(1)}, bf16[64]{0:T(256)(128)(2,1)}, u32[]{:S(2)}) copy-start(bf16[64]{0:T(256)(128)(2,1)} %param.25) | copy-start | bytes 388
  11.9 7.3 %copy-start.55 = (s32[256]{0:T(256)S(1)}, s32[256]{0:T(256)}, u32[]{:S(2)}) copy-start(s32[256]{0:T(256)} %param.23) | copy-start | bytes 3076
  16.5 103.5 %all-gather.6.cloned.1.call-start = ((), (), s32[]{:S(2)}) async-start(), calls=%async_computation.5 | async-start | bytes 5898240 | tf_op jit(solution)/shard_map/all_gather | solution.py:1673
  39.1 254.6 %all-gather.10.cloned.1.call-start = ((), (), s32[]{:S(2)}) async-start(), calls=%async_computation.7 | async-start | bytes 7077888 | tf_op jit(solution)/shard_map/all_gather | solution.py:1673
  39.8 265.8 %all-gather.12.cloned.1.call-start = ((), (), s32[]{:S(2)}) async-start(), calls=%async_computation.8 | async-start | bytes 7077888 | tf_op jit(solution)/shard_map/all_gather | solution.py:1673
  40.9 41.2 %copy-start.47 = (f32[2,16,64]{2,1,0:T(8,128)}, f32[2,16,64]{2,1,0:T(8,128)S(1)}, u32[]{:S(2)}) copy-start(f32[2,16,64]{2,1,0:T(8,128)S(1)} %copy.121) | copy-start | bytes 24580
  93.2 40.0 %copy-start.3 = (bf16[640,640]{1,0:T(8,128)(2,1)}, bf16[640,640]{1,0:T(8,128)(2,1)S(1)}, u32[]{:S(2)}) copy-start(bf16[640,640]{1,0:T(8,128)(2,1)S(1)} %mul.251.decay_blocks) | copy-start | bytes 2457604
  95.7 37.5 %copy-start.4 = (bf16[640,640]{1,0:T(8,128)(2,1)}, bf16[640,640]{1,0:T(8,128)(2,1)S(1)}, u32[]{:S(2)}) copy-start(bf16[640,640]{1,0:T(8,128)(2,1)S(1)} %mul.255.input_blocks) | copy-start | bytes 2457604
  115.8 224.3 %all-gather.14.cloned.1.call-start = ((), (), s32[]{:S(2)}) async-start(), calls=%async_computation.9 | async-start | bytes 7077888 | tf_op jit(solution)/shard_map/all_gather | solution.py:1673
  119.0 380.1 %reduce-scatter.6.cloned.1.call-start = ((), (), s32[]{:S(2)}) async-start(), calls=%async_computation.10 | async-start | bytes 3932160 | tf_op jit(solution)/shard_map/reduce_scatter | solution.py:1676
  119.4 65.6 %copy-start.36 = (f32[1,2048]{1,0:T(1,128)}, f32[1,2048]{1,0:T(1,128)S(1)}, u32[]{:S(2)}) copy-start(f32[1,2048]{1,0:T(1,128)S(1)} %broadcast_in_dim_reshape.8.gain) | copy-start | bytes 24580
  120.0 8.2 %copy-start.37 = (bf16[4,256,2048]{2,1,0:T(8,128)(2,1)S(1)}, bf16[4,256,2048]{2,1,0:T(8,128)(2,1)}, u32[]{:S(2)}) copy-start(bf16[4,256,2048]{2,1,0:T(8,128)(2,1)} %plane_gather.1) | copy-start | bytes 12582916
  120.0 8.2 %copy-start.64 = (bf16[2048,1280]{1,0:T(8,128)(2,1)S(1)}, bf16[2048,1280]{1,0:T(8,128)(2,1)}, u32[]{:S(2)}) copy-start(bf16[2048,1280]{1,0:T(8,128)(2,1)} %all-gather.6.cloned.1.call-done) | copy-start | bytes 15728644
  178.7 6.3 copy-start.12
  305.6 6.3 copy-start.23
  305.6 6.3 copy-start.62
  305.6 8.1 %copy-start.67 = (f32[1024,1536]{1,0:T(8,128)S(1)}, f32[1024,1536]{1,0:T(8,128)}, u32[]{:S(2)}) copy-start(f32[1024,1536]{1,0:T(8,128)} %fusion.62) | copy-start | bytes 18874372
  322.5 9.6 %collective-permute-start.1 = (bf16[1024,1536]{1,0:T(8,128)(2,1)}, bf16[1024,1536]{1,0:T(8,128)(2,1)}, u32[]{:S(2)}, u32[]{:S(2)}) collective-permute-start(bf16[1024,1536]{1,0:T(8,128)(2,1)} %pad_maximum_fusion), channel_id=1, source_target_pairs={{0,1},{1,0},{2,3},{3,2},{4,5},{5,4},{6,7},{7,6},{8,9},{9,8},{10,11... | collective-permute-start | bytes 9437192 | tf_op jit(solution)/shard_map/ppermute | solution.py:1690
  325.6 6.6 collective-permute-start
  340.0 271.7 %reduce-scatter.12.cloned.1.call-start = ((), (), s32[]{:S(2)}) async-start(), calls=%async_computation.13 | async-start | bytes 3932160 | tf_op jit(solution)/shard_map/reduce_scatter | solution.py:1676
  340.1 6.6 copy-start.24
  340.1 6.6 copy-start.63
  354.9 5.7 collective-permute-start.2
  367.4 314.8 %reduce-scatter.10.cloned.1.call-start = ((), (), s32[]{:S(2)}) async-start(), calls=%async_computation.12 | async-start | bytes 3932160 | tf_op jit(solution)/shard_map/reduce_scatter | solution.py:1676
  367.5 12.5 %copy-start.46 = (bf16[1024,768]{1,0:T(8,128)(2,1)S(1)}, bf16[1024,768]{1,0:T(8,128)(2,1)}, u32[]{:S(2)}) copy-start(bf16[1024,768]{1,0:T(8,128)(2,1)} %get-tuple-element.150) | copy-start | bytes 4718596
  367.5 28.0 %collective-permute-start.3 = (bf16[1024,2048]{1,0:T(8,128)(2,1)}, bf16[1024,2048]{1,0:T(8,128)(2,1)S(1)}, u32[]{:S(2)}, u32[]{:S(2)}) collective-permute-start(bf16[1024,2048]{1,0:T(8,128)(2,1)} %bitcast.167), channel_id=1, source_target_pairs={{0,1},{1,0},{2,3},{3,2},{4,5},{5,4},{6,7},{7,6},{8,9},{9,8},{10,11... | collective-permute-start | bytes 12582920 | tf_op jit(solution)/shard_map/ppermute | solution.py:1690
  479.5 202.7 %reduce-scatter.8.cloned.1.call-start = ((), (), s32[]{:S(2)}) async-start(), calls=%async_computation.11 | async-start | bytes 1638400 | tf_op jit(solution)/shard_map/reduce_scatter | solution.py:1676
  479.8 12.5 %collective-permute-start.5 = (bf16[1024,2048]{1,0:T(8,128)(2,1)}, bf16[1024,2048]{1,0:T(8,128)(2,1)}, u32[]{:S(2)}, u32[]{:S(2)}) collective-permute-start(bf16[1024,2048]{1,0:T(8,128)(2,1)} %bitcast.195), channel_id=1, source_target_pairs={{0,1},{1,0},{2,3},{3,2},{4,5},{5,4},{6,7},{7,6},{8,9},{9,8},{10,11... | collective-permute-start | bytes 12582920 | tf_op jit(solution)/shard_map/ppermute | solution.py:1690
  484.3 8.0 %collective-permute-start.4 = (bf16[1024,320]{0,1:T(8,128)(2,1)}, bf16[1024,320]{0,1:T(8,128)(2,1)S(1)}, u32[]{:S(2)}, u32[]{:S(2)}) collective-permute-start(bf16[1024,320]{0,1:T(8,128)(2,1)} %copy.161), channel_id=1, source_target_pairs={{0,1},{1,0},{2,3},{3,2},{4,5},{5,4},{6,7},{7,6},{8,9},{9,8},{10,11... | collective-permute-start | bytes 1966088 | tf_op jit(solution)/shard_map/ppermute | solution.py:1690
  499.0 73.2 %copy-start.38 = (bf16[4,256,2048]{2,1,0:T(8,128)(2,1)S(1)}, bf16[4,256,2048]{2,1,0:T(8,128)(2,1)}, u32[]{:S(2)}) copy-start(bf16[4,256,2048]{2,1,0:T(8,128)(2,1)} %plane_gather.1) | copy-start | bytes 12582916
  572.2 8.0 %collective-permute-start.7 = (bf16[1024,1280]{1,0:T(8,128)(2,1)}, bf16[1024,1280]{1,0:T(8,128)(2,1)}, u32[]{:S(2)}, u32[]{:S(2)}) collective-permute-start(bf16[1024,1280]{1,0:T(8,128)(2,1)} %bitcast.198), channel_id=1, source_target_pairs={{0,1},{1,0},{2,3},{3,2},{4,5},{5,4},{6,7},{7,6},{8,9},{9,8},{10,11... | collective-permute-start | bytes 7864328 | tf_op jit(solution)/shard_map/ppermute | solution.py:1690
  572.4 7.8 %collective-permute-start.6 = (bf16[1024,1024]{1,0:T(8,128)(2,1)S(1)}, bf16[1024,1024]{1,0:T(8,128)(2,1)}, u32[]{:S(2)}, u32[]{:S(2)}) collective-permute-start(bf16[1024,1024]{1,0:T(8,128)(2,1)S(1)} %constant_dynamic-slice_fusion.2), channel_id=1, source_target_pairs={{0,1},{1,0},{2,3},{3,2},{4,5},{5,4},{6,7},{7,6},{8,9},{9,8},{10,11... | collective-permute-start | bytes 6291464 | tf_op jit(solution)/shard_map/ppermute | solution.py:1690
  573.0 120.2 %reduce-scatter.14.cloned.1.call-start = ((), (), s32[]{:S(2)}) async-start(), calls=%async_computation.14 | async-start | bytes 3276800 | tf_op jit(solution)/shard_map/reduce_scatter | solution.py:1676
  587.0 7.1 copy-start.53
  587.0 8.0 %copy-start.52 = (f32[1,640]{1,0:T(1,128)S(1)}, f32[1,640]{1,0:T(1,128)}, u32[]{:S(2)}) copy-start(f32[1,640]{1,0:T(1,128)} %copy-done.51) | copy-start | bytes 7684
  590.2 2.2 collective-permute-start.8
  593.6 5.5 copy-start.1
  595.5 14.1 %collective-permute-start.10 = (bf16[1024,640]{1,0:T(8,128)(2,1)}, bf16[1024,640]{1,0:T(8,128)(2,1)S(1)}, u32[]{:S(2)}, u32[]{:S(2)}) collective-permute-start(bf16[1024,640]{1,0:T(8,128)(2,1)} %bitcast.147), channel_id=1, source_target_pairs={{0,1},{1,0},{2,3},{3,2},{4,5},{5,4},{6,7},{7,6},{8,9},{9,8},{10,11... | collective-permute-start | bytes 3932168 | tf_op jit(solution)/shard_map/ppermute | solution.py:1690
  595.7 15.0 %collective-permute-start.9 = (bf16[1024,640]{1,0:T(8,128)(2,1)}, bf16[1024,640]{1,0:T(8,128)(2,1)S(1)}, u32[]{:S(2)}, u32[]{:S(2)}) collective-permute-start(bf16[1024,640]{1,0:T(8,128)(2,1)} %bitcast.145), channel_id=1, source_target_pairs={{0,1},{1,0},{2,3},{3,2},{4,5},{5,4},{6,7},{7,6},{8,9},{9,8},{10,11... | collective-permute-start | bytes 3932168 | tf_op jit(solution)/shard_map/ppermute | solution.py:1690
  596.2 6.2 slice-start
  622.0 64.9 %copy-start.2 = (f32[256,2048]{1,0:T(8,128)S(1)}, f32[256,2048]{1,0:T(8,128)}, u32[]{:S(2)}) copy-start(f32[256,2048]{1,0:T(8,128)} %fusion.34.refs_0_) | copy-start | bytes 6291460
  (43 other events, 75.3 us)
Sparse Core Ops, SparseCore 0:
  16.7 40.7 all-gather.7
  59.0 54.8 all-gather.5
  116.1 66.8 all-gather.9
  184.5 63.5 all-gather.11
  249.5 63.3 all-gather.13
  340.1 63.4 reduce-scatter.5
  406.0 60.2 reduce-scatter.11
  479.7 66.1 reduce-scatter.9
  573.2 29.2 reduce-scatter.7
  604.6 62.8 reduce-scatter.13

commit v3 on v2

--- a/solution.py
+++ b/solution.py
@@ -427,6 +427,12 @@
     )
 
 
+def lasting(microseconds):
+    return pl.CostEstimate(
+        flops=int(microseconds * 1e9), bytes_accessed=int(microseconds * 3e6), transcendentals=0
+    )
+
+
 ANY = pl.BlockSpec(memory_space=pl.ANY)
 VMEM = pl.BlockSpec(memory_space=pltpu.VMEM)
 
@@ -533,45 +539,299 @@
     return pl.ds(pl.multiple_of(i * 16, 16), 16)
 
 
-def middle_kernel(parts, tokens, gain, middle, whole, normed, *scratch):
-    sums, (send, recv, local) = scratch[:10], scratch[10:]
+def fetch_rows(rows_all, first, start, target, sems):
+    count = sems.shape[0]
+    rows = target.shape[0] // count
+    return [
+        pltpu.make_async_copy(
+            rows_all.at[first + k, pl.ds(start, rows)], target.at[pl.ds(k * rows, rows)], sems.at[k]
+        )
+        for k in range(count)
+    ]
+
+
+def computed_scratch(rows, columns):
+    f32, bf16 = jnp.float32, jnp.bfloat16
+    whole, half = (rows, columns), (rows // 2, columns)
+    shapes = [(whole, bf16)] * 3 + [(whole, f32)] + [(half, f32)] * 2 + [(whole, bf16)] * 2 + [(half, bf16)] * 2
+    return [pltpu.VMEM(*shape) for shape in shapes] + [pltpu.SemaphoreType.DMA((6,))] * 2
+
+
+def computed_sum(product, sent_d, sent_x, sent_y, own, kept_x, kept_y, from_x, from_y, diag_x, diag_y, send, recv):
+    (x_dev, y_dev, d_dev), (p_x, p_y, p_d) = plane_neighbours()
+    p = place()[2]
+    rows, width = own.shape
+    half = rows // 2
+    low, high = pl.ds(0, half), pl.ds(half, half)
+    tile = 512
+
+    def into(chip, at, target, target_at):
+        @pl.loop(0, width // tile)
+        def product_tile(k):
+            columns = pl.ds(pl.multiple_of(k * tile, tile), tile)
+            target[target_at, columns] = product(chip, at, columns).astype(target.dtype)
+
+    def copy(k, source, target, device):
+        return remote(source, target, send.at[k], recv.at[k], device)
+
+    first = [copy(0, sent_d.at[low], diag_x, x_dev), copy(1, sent_d.at[high], diag_y, y_dev)]
+    second = [
+        copy(2, sent_x.at[low], from_x.at[low], x_dev),
+        copy(3, sent_y.at[high], from_y.at[high], y_dev),
+    ]
+    third = [
+        copy(4, sent_y.at[low], from_y.at[low], y_dev),
+        copy(5, sent_x.at[high], from_x.at[high], x_dev),
+    ]
+    everything = slice(None)
+
+    def begin():
+        into(p_d, everything, sent_d, everything)
+        for sent in first:
+            sent.start()
+        into(p_x, low, sent_x, low)
+        into(p_y, high, sent_y, high)
+        for sent in second:
+            sent.start()
+        into(p_y, low, kept_y, everything)
+        into(p_x, high, kept_x, everything)
+        into(p, everything, own, everything)
+
+    def add(target, start, kept, addend):
+        @pl.loop(0, half // 16)
+        def add_rows(i):
+            here = sixteen(i)
+            there = pl.ds(pl.multiple_of(start + i * 16, 16), 16)
+            target[there, :] = (kept[here, :] + addend[here, :].astype(jnp.float32)).astype(target.dtype)
+
+    def forward():
+        first[0].wait_recv()
+        add(sent_y, 0, kept_y, diag_x)
+        third[0].start()
+        first[1].wait_recv()
+        add(sent_x, half, kept_x, diag_y)
+        third[1].start()
+
+    def end():
+        for sent in first:
+            sent.wait_send()
+        for sent in second + third:
+            sent.wait()
+
+    return begin, forward, end
+
+
+def middle_kernel(
+    mixed, rows_all, tokens, gain, middle, whole, normed, out_here, send, recv, local, loads, *sums
+):
     greet(plane_neighbours()[0][:2])
-    own, from_x, from_y = sums[:3]
-    for step in sum_steps(parts, *sums):
+    f32, bf16 = jnp.float32, jnp.bfloat16
+    fetched = fetch_rows(rows_all, 0, 0, out_here, loads)
+    for copy in fetched:
+        copy.start()
+    for copy in fetched:
+        copy.wait()
+
+    def product(chip, at, columns):
+        return jnp.dot(mixed[chip, at, :], out_here[:, columns], preferred_element_type=f32)
+
+    for step in computed_sum(product, *sums):
         step()
+    own, from_x, from_y = sums[3], sums[6], sums[7]
 
     @pl.loop(0, tokens.shape[0] // 16)
     def norm_rows(i):
         at = sixteen(i)
-        values = tokens[at, :].astype(jnp.float32) + (own[at, :] + from_x[at, :] + from_y[at, :])
+        values = tokens[at, :].astype(f32) + (
+            own[at, :] + from_x[at, :].astype(f32) + from_y[at, :].astype(f32)
+        )
         middle[at, :] = values
         inverse = lax.rsqrt(jnp.mean(values * values, axis=-1, keepdims=True) + epsilon)
-        normed[at, :] = (values * inverse * gain[...]).astype(jnp.bfloat16)
+        normed[at, :] = (values * inverse * gain[...]).astype(bf16)
 
     for step in gather_steps(normed, whole, send, recv, local, 0):
         step()
 
 
-def middle_of(parts, tokens, gain, collective_id):
+def middle_of(mixed, rows_all, tokens, gain, collective_id):
     rows, width = tokens.shape
+    channels = mixed.shape[2]
+    f32, bf16 = jnp.float32, jnp.bfloat16
     return pl.pallas_call(
         middle_kernel,
         out_shape=[
-            jax.ShapeDtypeStruct((rows, width), jnp.float32),
-            jax.ShapeDtypeStruct((CHIPS, rows, width), jnp.bfloat16),
+            jax.ShapeDtypeStruct((rows, width), f32),
+            jax.ShapeDtypeStruct((CHIPS, rows, width), bf16),
         ],
-        in_specs=[ANY, VMEM, VMEM],
+        in_specs=[VMEM, ANY, VMEM, VMEM],
         out_specs=[VMEM, ANY],
         scratch_shapes=[
-            pltpu.VMEM((rows, width), jnp.bfloat16),
-            *sum_scratch(rows, width, parts.dtype),
+            pltpu.VMEM((rows, width), bf16),
+            pltpu.VMEM((channels, width), bf16),
             pltpu.SemaphoreType.DMA((4,)),
             pltpu.SemaphoreType.DMA((4,)),
             pltpu.SemaphoreType.DMA,
+            pltpu.SemaphoreType.DMA((rows_all.shape[0],)),
+            *computed_scratch(rows, width),
         ],
-        compiler_params=comm_params(collective_id, 32),
+        compiler_params=comm_params(collective_id, 60),
+        cost_estimate=lasting(75),
         name="middle",
-    )(parts, tokens, gain[None])
+    )(mixed, rows_all, tokens, gain[None])
+
+
+def feed_forward_kernel(
+    piece,
+    two,
+    cot,
+    weights,
+    down,
+    *refs,
+):
+    last = piece == 1
+    if last:
+        (
+            earlier_weights,
+            earlier_low,
+            hidden,
+            grad,
+            parts,
+            low,
+            earlier_here,
+            earlier_low_here,
+            *refs,
+        ) = refs
+    else:
+        hidden, grad, low, *refs = refs
+    two_here, two_there, cot_here, weights_here, down_here, low_there, send, recv, loads, down_loads = refs
+    me, z, p, c, x, y = place()
+    sibling = me + 1 - 2 * c
+    greet((sibling,))
+    f32, bf16 = jnp.float32, jnp.bfloat16
+    tokens, width = two.shape
+    units = hidden.shape[1]
+    half = width // 2
+    pairs = [
+        (two, two_here),
+        (weights, weights_here),
+        (cot, cot_here),
+    ]
+    if last:
+        pairs += [(earlier_weights, earlier_here), (earlier_low, earlier_low_here)]
+    fetched = [pltpu.make_async_copy(a, b, loads.at[k]) for k, (a, b) in enumerate(pairs)]
+    count = down_loads.shape[0]
+    fetched[3:3] = fetch_rows(down, count * piece, down.shape[1] - units // count, down_here, down_loads)
+    for copy in fetched:
+        copy.start()
+    other_half = two.at[:, pl.ds(pl.multiple_of((1 - c) * half, 128), half)]
+    two_swap = remote(other_half, two_there, send.at[0], recv.at[0], sibling)
+    two_swap.start()
+    for copy in fetched[: 3 + count]:
+        copy.wait()
+    tile, block = 256, 512
+
+    def dot_t(left, right):
+        return lax.dot_general(left, right, (((1,), (1,)), ((), ())), preferred_element_type=f32)
+
+    def dot_first(left, right):
+        return lax.dot_general(left, right, (((0,), (0,)), ((), ())), preferred_element_type=f32)
+
+    low_swaps = []
+    for t in range(units // tile):
+        gate_at, up_at = pl.ds(t * tile, tile), pl.ds(units + t * tile, tile)
+
+        @pl.loop(0, tokens // block)
+        def rows_block(j):
+            at = pl.ds(pl.multiple_of(j * block, block), block)
+            v = jnp.dot(two_here[at, :], weights_here[:, gate_at], preferred_element_type=f32)
+            up = jnp.dot(two_here[at, :], weights_here[:, up_at], preferred_element_type=f32)
+            grad_hidden = dot_t(cot_here[at, :], down_here[gate_at, :])
+            square = v * v
+            bent = jnp.tanh(v * (GELU_A + GELU_A * GELU_B * square))
+            rising = 0.5 + 0.5 * bent
+            act = v * rising
+            slope = rising + 0.5 * v * (1.0 - bent * bent) * (GELU_A + 3.0 * GELU_A * GELU_B * square)
+            hidden[at, gate_at] = (act * up).astype(bf16)
+            low[at, gate_at] = (grad_hidden * up * slope).astype(bf16)
+            low[at, up_at] = (grad_hidden * act).astype(bf16)
+
+        for k, columns in enumerate((gate_at, up_at)):
+            sems = 1 + 2 * t + k
+            low_swaps.append(
+                remote(low.at[:, columns], low_there.at[:, columns], send.at[sems], recv.at[sems], sibling)
+            )
+            low_swaps[-1].start()
+    if last:
+        for copy in fetched[3 + count :]:
+            copy.wait()
+
+        @pl.loop(0, tokens // block)
+        def parts_block(j):
+            at = pl.ds(pl.multiple_of(j * block, block), block)
+
+            @pl.loop(0, width // block)
+            def parts_tile(k):
+                columns = pl.ds(pl.multiple_of(k * block, block), block)
+                parts[at, columns] = (
+                    dot_t(earlier_low_here[at, :], earlier_here[columns, :])
+                    + dot_t(low[at, :], weights_here[columns, :])
+                ).astype(bf16)
+
+    two_swap.wait()
+    for copy in low_swaps:
+        copy.wait()
+
+    @pl.loop(0, half // block)
+    def grad_block(m):
+        here = pl.ds(pl.multiple_of(c * half + m * block, 128), block)
+        there = pl.ds(pl.multiple_of(m * block, block), block)
+
+        @pl.loop(0, 2 * units // block)
+        def grad_tile(k):
+            columns = pl.ds(pl.multiple_of(k * block, block), block)
+            grad[there, columns] = (
+                dot_first(two_here[:, here], low[:, columns]) + dot_first(two_there[:, there], low_there[:, columns])
+            ).astype(bf16)
+
+
+def feed_forward(piece, two, cot, weights, down, earlier, collective_id):
+    tokens, width = two.shape
+    units = weights.shape[1] // 2
+    bf16 = jnp.bfloat16
+    out_shape = [
+        jax.ShapeDtypeStruct((tokens, units), bf16),
+        jax.ShapeDtypeStruct((width // 2, 2 * units), bf16),
+    ]
+    low = pltpu.VMEM((tokens, 2 * units), bf16)
+    scratch = []
+    if earlier:
+        out_shape.append(jax.ShapeDtypeStruct((tokens, width), bf16))
+        scratch = [low, pltpu.VMEM(weights.shape, bf16), low]
+    else:
+        out_shape.append(jax.ShapeDtypeStruct((tokens, 2 * units), bf16))
+    swaps = 1 + 2 * (units // 256)
+    return pl.pallas_call(
+        functools.partial(feed_forward_kernel, piece),
+        out_shape=out_shape,
+        in_specs=[ANY] * (4 + len(earlier)),
+        out_specs=[VMEM] * 3,
+        scratch_shapes=[
+            *scratch,
+            pltpu.VMEM((tokens, width), bf16),
+            pltpu.VMEM((tokens, width // 2), bf16),
+            pltpu.VMEM((tokens, width), bf16),
+            pltpu.VMEM(weights.shape, bf16),
+            pltpu.VMEM((units, width), bf16),
+            low,
+            pltpu.SemaphoreType.DMA((swaps,)),
+            pltpu.SemaphoreType.DMA((swaps,)),
+            pltpu.SemaphoreType.DMA((3 + len(earlier),)),
+            pltpu.SemaphoreType.DMA((down.shape[0] // 2,)),
+        ],
+        compiler_params=comm_params(collective_id, 60),
+        cost_estimate=lasting(35),
+        name="feed_forward",
+    )(two, cot, weights, down, *earlier)
 
 
 def norm_back_rows(values, gain, grad, rest):
@@ -586,7 +846,8 @@
     middle,
     cot,
     gain,
-    hidden,
+    hidden_zero,
+    hidden_one,
     down,
     cot_all,
     cot_other,
@@ -603,7 +864,7 @@
     cot_there,
     *scratch,
 ):
-    sums, (send, recv, local, loads) = scratch[:10], scratch[10:]
+    sums, (send, recv, local, loads, down_loads) = scratch[:10], scratch[10:]
     me, z, p, c, x, y = place()
     f32, bf16 = jnp.float32, jnp.bfloat16
     sibling = me + 1 - 2 * c
@@ -611,28 +872,41 @@
     own, from_x, from_y = sums[:3]
     begin, forward, end = sum_steps(parts, *sums)
     begin()
-    units = hidden.shape[1]
-    half = units // 2
-    swap = remote(
-        hidden.at[:, pl.ds(pl.multiple_of((1 - c) * half, 128), half)], hidden_other, send.at[4], recv.at[4], sibling
-    )
-    swap.start()
+    half = hidden_zero.shape[1]
+    swaps = [remote(hidden, hidden_other, send.at[4], recv.at[4], sibling) for hidden in (hidden_one, hidden_zero)]
+
+    @pl.when(c == 0)
+    def send_one():
+        swaps[0].start()
+
+    @pl.when(c == 1)
+    def send_zero():
+        swaps[1].start()
+
     fetched = [
         pltpu.make_async_copy(source, target, loads.at[k])
         for k, (source, target) in enumerate(
-            ((hidden, hidden_here), (cot_all, cot_here), (cot_other, cot_there), (down, down_here))
+            (
+                (hidden_zero, hidden_here.at[:, pl.ds(0, half)]),
+                (hidden_one, hidden_here.at[:, pl.ds(half, half)]),
+                (cot_all, cot_here),
+                (cot_other, cot_there),
+            )
         )
     ]
-    for copy in fetched:
+    count = down_loads.shape[0]
+    down_fetched = fetch_rows(down, 0, down.shape[1] - down_here.shape[0] // count, down_here, down_loads)
+    for copy in fetched + down_fetched:
         copy.start()
-    for copy in fetched[:3]:
+    for copy in fetched[:4]:
         copy.wait()
-    swap.wait()
+    swaps[0].wait()
     tile = 256
+
+    planes, units = down_grad.shape[:2]
 
     def grad_tiles(m):
         rows_here = pl.ds(pl.multiple_of(c * half + m * tile, 128), tile)
-        rows_there = pl.ds(pl.multiple_of(m * tile, 128), tile)
 
         @pl.loop(0, cot_all.shape[1] // (2 * tile))
         def grad_tile(k):
@@ -641,14 +915,21 @@
             def dot_t(left, right):
                 return lax.dot_general(left, right, (((0,), (0,)), ((), ())), preferred_element_type=f32)
 
-            down_grad[rows_there, columns] = (
+            values = (
                 dot_t(hidden_here[:, rows_here], cot_here[:, columns])
-                + dot_t(hidden_other[:, rows_there], cot_there[:, columns])
+                + dot_t(hidden_other[:, m * tile : (m + 1) * tile], cot_there[:, columns])
             ).astype(bf16)
-
-    pl.loop(0, 1)(grad_tiles)
+            for j in range(planes):
+                start, stop = max(j * units, m * tile), min((j + 1) * units, (m + 1) * tile)
+                if start < stop:
+                    down_grad[j, start - j * units : stop - j * units, columns] = values[
+                        start - m * tile : stop - m * tile
+                    ]
+
+    grad_tiles(0)
     forward()
-    pl.loop(1, half // tile)(grad_tiles)
+    for m in range(1, half // tile):
+        grad_tiles(m)
     end()
     rows, width = middle.shape
 
@@ -664,7 +945,8 @@
     grad_gain[...] = jnp.sum(total, axis=0, keepdims=True)
     begin, forward, end = gather_steps(branch, whole, send, recv, local, 0)
     begin()
-    fetched[3].wait()
+    for copy in down_fetched:
+        copy.wait()
 
     def down_tiles(j):
         @pl.loop(0, width // (2 * tile))
@@ -681,9 +963,9 @@
     end()
 
 
-def grads_of_middle(parts, middle, cot, gain, hidden, down, cot_all, cot_other, collective_id):
+def grads_of_middle(parts, middle, cot, gain, hiddens, down, cot_all, cot_other, collective_id):
     rows, width = middle.shape
-    tokens, units = hidden.shape
+    tokens, units = hiddens[0].shape[0], 2 * hiddens[0].shape[1]
     f32, bf16 = jnp.float32, jnp.bfloat16
     return pl.pallas_call(
         grads_of_middle_kernel,
@@ -691,10 +973,10 @@
             jax.ShapeDtypeStruct((rows, width), f32),
             jax.ShapeDtypeStruct((1, width), f32),
             jax.ShapeDtypeStruct((CHIPS, rows, width), bf16),
-            jax.ShapeDtypeStruct((units // 2, width), bf16),
+            jax.ShapeDtypeStruct((down.shape[0] // 2, 2 * hiddens[0].shape[1] // down.shape[0], width), bf16),
             jax.ShapeDtypeStruct((CHIPS, rows, width), bf16),
         ],
-        in_specs=[ANY, VMEM, VMEM, VMEM, ANY, ANY, ANY, ANY],
+        in_specs=[ANY, VMEM, VMEM, VMEM] + [ANY] * 5,
         out_specs=[VMEM, VMEM, ANY, VMEM, VMEM],
         scratch_shapes=[
             pltpu.VMEM((rows, width), bf16),
@@ -708,25 +990,25 @@
             pltpu.SemaphoreType.DMA((5,)),
             pltpu.SemaphoreType.DMA,
             pltpu.SemaphoreType.DMA((4,)),
+            pltpu.SemaphoreType.DMA((down.shape[0],)),
         ],
-        compiler_params=comm_params(collective_id, 56),
+        compiler_params=comm_params(collective_id, 60),
+        cost_estimate=lasting(80),
         name="grads_of_middle",
-    )(parts, middle, cot, gain[None], hidden, down, cot_all, cot_other)
+    )(parts, middle, cot, gain[None], *hiddens, down, cot_all, cot_other)
 
 
 def closing_kernel(
     planes,
-    parts,
+    in_low,
+    whole_in,
     tokens,
     gain,
     rest,
     small,
-    conv_here,
-    conv_there,
-    decay_here,
-    decay_there,
-    input_here,
-    input_there,
+    conv_low,
+    decay_low,
+    input_low,
     piece,
     grad_tokens,
     small_out,
@@ -734,10 +1016,11 @@
     swapped,
     conv_a,
     conv_b,
-    low_a,
-    low_b,
-    low_c,
-    low_d,
+    decay_a,
+    decay_b,
+    input_a,
+    input_b,
+    full,
     gates,
     gate_lines,
     lines,
@@ -747,68 +1030,64 @@
     gain_lines,
     gain_line,
     gain_near,
-    *scratch,
+    send,
+    recv,
+    loads,
+    swap_send,
+    swap_recv,
+    *sums,
 ):
-    sums, (send, recv, local, loads) = scratch[:10], scratch[10:]
     me, z, p, c, x, y = place()
     f32 = jnp.float32
     r = lax.rem(me, 8)
     near = [(lax.rem(r + d, 8), me - r + lax.rem(r + d, 8)) for d in range(1, 8)]
     far = [(lax.rem(z + d, planes), 8 * lax.rem(z + d, planes) + r) for d in range(1, planes)]
     greet([device for unused, device in near + far])
-    own, from_x, from_y = sums[:3]
-    begin, forward, end = sum_steps(parts, *sums)
-    begin()
-    devices, chips = plane_neighbours()
 
     def copy(k, source, target, device):
         return remote(source, target, send.at[k], recv.at[k], device)
 
-    swaps = [copy(k, piece.at[chips[k]], swapped.at[p], devices[k]) for k in range(3)]
-    for swap in swaps:
-        swap.start()
-    swap_own = pltpu.make_async_copy(piece.at[p], swapped.at[p], local)
-    swap_own.start()
+    lows = ((conv_low, conv_a, conv_b), (decay_low, decay_a, decay_b), (input_low, input_a, input_b))
+    fetched = [pltpu.make_async_copy(source, here, loads.at[k]) for k, (source, here, there) in enumerate(lows)]
+    exchanges = [copy(k, source, there, me + 1 - 2 * c) for k, (source, here, there) in enumerate(lows)]
     at = 3
     small_far = [copy(at + d, small.at[there], lines.at[d], device) for d, (there, device) in enumerate(far)]
     at += len(far)
-    for sent in small_far:
-        sent.start()
-    fetched = [
-        pltpu.make_async_copy(source, target, loads.at[k])
-        for k, (source, target) in enumerate(
-            (
-                (conv_here, conv_a),
-                (conv_there, conv_b),
-                (decay_here, low_a),
-                (decay_there, low_b),
-                (input_here, low_c),
-                (input_there, low_d),
-            )
+    for started in small_far + fetched + exchanges:
+        started.start()
+
+    def product(chip, rows_at, columns):
+        return lax.dot_general(
+            in_low[chip, rows_at, :], whole_in[columns, :], (((1,), (1,)), ((), ())), preferred_element_type=f32
         )
-    ]
-    for fetch in fetched:
-        fetch.start()
-    for fetch in fetched:
-        fetch.wait()
-
-    def dot_t(left, right):
+
+    begin, forward, end = computed_sum(product, *sums)
+    own, from_x, from_y = sums[3], sums[6], sums[7]
+    begin()
+    for ended in fetched + exchanges:
+        ended.wait()
+    swaps = swap_copies(piece, swapped, swap_send, swap_recv, loads.at[3])
+
+    def dot_first(left, right):
         return lax.dot_general(left, right, (((0,), (0,)), ((), ())), preferred_element_type=f32)
 
     block = gates.shape[1]
-    count = conv_a.shape[1]
-    for k, (first, second) in enumerate(((low_a, low_b), (low_c, low_d))):
-        full = dot_t(conv_a[...], first[...]) + dot_t(conv_b[...], second[...])
+    count = planes * block
+    for k, (first, second) in enumerate(((decay_a, decay_b), (input_a, input_b))):
+        full[...] = dot_first(conv_a[...], first[...]) + dot_first(conv_b[...], second[...])
         for j in range(planes):
+            rows_at = pl.ds(pl.multiple_of(c * count + j * block, 8), block)
             for e in range(2):
                 gates[j, :, (2 * k + e) * block : (2 * k + e + 1) * block] = full[
-                    j * block : (j + 1) * block, e * count + j * block : e * count + (j + 1) * block
+                    rows_at, e * count + j * block : e * count + (j + 1) * block
                 ]
     gate_far = [copy(at + d, gates.at[there], gate_lines.at[d], device) for d, (there, device) in enumerate(far)]
     at += len(far)
     for sent in gate_far:
         sent.start()
     forward()
+    for sent in swaps:
+        sent.start()
     for sent in small_far:
         sent.wait()
     line[...] = small[z] + sum(lines[d] for d in range(planes - 1))
@@ -824,7 +1103,7 @@
 
     def norm_rows(i, total):
         here = sixteen(i)
-        grad = own[here, :].astype(f32) + from_x[here, :].astype(f32) + from_y[here, :].astype(f32)
+        grad = own[here, :] + from_x[here, :].astype(f32) + from_y[here, :].astype(f32)
         given, terms = norm_back_rows(tokens[here, :].astype(f32), gain[...], grad, rest[here, :])
         for k in range(4 * planes):
             for e in range(2):
@@ -854,7 +1133,6 @@
         sent.start()
     for sent in small_near + gate_far + swaps:
         sent.wait()
-    swap_own.wait()
     gates_out[...] = gates[z] + sum(gate_lines[d] for d in range(planes - 1))
     for sent in last:
         sent.wait()
@@ -863,12 +1141,13 @@
     small_out[rows_small : rows_small + 8, :] = gain_line[r] + sum(gain_near[d] for d in range(7))
 
 
-def closing(parts, tokens, gain, rest, small, convs, decays, inputs, piece, head, collective_id):
+def closing(in_low, whole_in, tokens, gain, rest, small, lows, piece, head, collective_id):
     planes = lax.axis_size("seq") // 8
     rows, width = tokens.shape
     f32, bf16 = jnp.float32, jnp.bfloat16
     rows_small, lanes = small.shape[2:]
-    block = convs[0].shape[1] // planes
+    channels = lows[0].shape[1]
+    block = channels // (2 * planes)
     count = 3 + 3 * (planes - 1) + 14
     return pl.pallas_call(
         functools.partial(closing_kernel, planes),
@@ -876,14 +1155,13 @@
             jax.ShapeDtypeStruct((rows, width), f32),
             jax.ShapeDtypeStruct((rows_small + 8, lanes), f32),
             jax.ShapeDtypeStruct((block, 2 * head), f32),
-            jax.ShapeDtypeStruct(piece.shape, piece.dtype),
+            jax.ShapeDtypeStruct(piece.shape, bf16),
         ],
-        in_specs=[ANY, VMEM, VMEM, VMEM, VMEM] + [ANY] * 7,
-        out_specs=[VMEM, VMEM, VMEM, ANY],
+        in_specs=[VMEM] * 6 + [ANY] * 4,
+        out_specs=[VMEM] * 3 + [ANY],
         scratch_shapes=[
-            pltpu.VMEM(convs[0].shape, bf16),
-            pltpu.VMEM(convs[0].shape, bf16),
-            *[pltpu.VMEM(decays[0].shape, bf16)] * 4,
+            *[pltpu.VMEM(lows[0].shape, bf16)] * 6,
+            pltpu.VMEM((channels, channels), f32),
             pltpu.VMEM((planes, block, 2 * head), f32),
             pltpu.VMEM((planes - 1, block, 2 * head), f32),
             pltpu.VMEM((planes - 1, 8, rows_small, lanes), f32),
@@ -893,37 +1171,17 @@
             pltpu.VMEM((planes - 1, 8, 8, lanes), f32),
             pltpu.VMEM((8, 8, lanes), f32),
             pltpu.VMEM((7, 8, lanes), f32),
-            *sum_scratch(rows, width, parts.dtype),
             pltpu.SemaphoreType.DMA((count,)),
             pltpu.SemaphoreType.DMA((count,)),
-            pltpu.SemaphoreType.DMA,
-            pltpu.SemaphoreType.DMA((6,)),
+            pltpu.SemaphoreType.DMA((4,)),
+            pltpu.SemaphoreType.DMA((3,)),
+            pltpu.SemaphoreType.DMA((3,)),
+            *computed_scratch(rows, width),
         ],
-        compiler_params=comm_params(collective_id, 40),
+        compiler_params=comm_params(collective_id, 60),
+        cost_estimate=lasting(50),
         name="closing",
-    )(parts, tokens, gain[None], rest, small, *convs, *decays, *inputs, piece)
-
-
-def plane_gather_kernel(x_ref, o_ref, send, recv, local):
-    greet(plane_neighbours()[0][:2])
-    for step in gather_steps(x_ref, o_ref, send, recv, local, 0):
-        step()
-
-
-def plane_gather(block, collective_id):
-    return pl.pallas_call(
-        plane_gather_kernel,
-        out_shape=jax.ShapeDtypeStruct((CHIPS,) + block.shape, block.dtype),
-        in_specs=[ANY],
-        out_specs=ANY,
-        scratch_shapes=[
-            pltpu.SemaphoreType.DMA((4,)),
-            pltpu.SemaphoreType.DMA((4,)),
-            pltpu.SemaphoreType.DMA,
-        ],
-        compiler_params=comm_params(collective_id),
-        name="plane_gather",
-    )(block)
+    )(in_low, whole_in, tokens, gain[None], rest, small, *lows, piece)
 
 
 def plane_swap_kernel(count, *refs):
@@ -959,63 +1217,139 @@
             pltpu.SemaphoreType.DMA((count,)),
         ],
         compiler_params=comm_params(collective_id),
+        cost_estimate=lasting(10),
         name="plane_swap",
     )(*arrays)
 
 
-def opening_kernel(planes, weights_ref, x_ref, swapped_ref, o_ref, send, recv, local):
+def swap_copies(source, target, send, recv, local):
+    devices, chips = plane_neighbours()
+    p = place()[2]
+    return [
+        *[remote(source.at[chips[j]], target.at[p], send.at[j], recv.at[j], devices[j]) for j in range(3)],
+        pltpu.make_async_copy(source.at[p], target.at[p], local),
+    ]
+
+
+def opening_kernel(
+    planes,
+    small,
+    gates,
+    tokens,
+    piece,
+    gathered,
+    decay_blocks,
+    input_blocks,
+    whole,
+    swapped,
+    gates_all,
+    gain,
+    normed,
+    *sems,
+):
+    send, recv, gate_send, gate_recv, swap_send, swap_recv, swap_local, gather_send, gather_recv, gather_local = sems
     me, z, p, c, x, y = place()
     r = lax.rem(me, 8)
-    base = me - r
-    near = [base + lax.rem(r + d, 8) for d in range(1, 8)]
+    near = [me - r + lax.rem(r + d, 8) for d in range(1, 8)]
     far = [8 * lax.rem(z + d, planes) + r for d in range(1, planes)]
     greet(near + far)
-    x_dev, y_dev = me + 2 - 4 * x, me + 4 - 8 * y
-    d_dev = y_dev + 2 - 4 * x
-    p_x, p_y, p_d = p + 1 - 2 * x, p + 2 - 4 * y, 3 - p
     lines = [
-        remote(x_ref, o_ref.at[r, z], send.at[d], recv.at[d], device) for d, device in enumerate(far)
+        remote(small, gathered.at[r, z], send.at[d], recv.at[d], device) for d, device in enumerate(far)
     ]
-    swaps = [
-        remote(weights_ref.at[chip], swapped_ref.at[p], send.at[planes + j], recv.at[planes + j], device)
-        for j, (device, chip) in enumerate(((x_dev, p_x), (y_dev, p_y), (d_dev, p_d)))
+    gate_lines = [
+        remote(gates, gates_all.at[c, z], gate_send.at[d], gate_recv.at[d], device) for d, device in enumerate(far)
     ]
-    own = pltpu.make_async_copy(weights_ref.at[p], swapped_ref.at[p], local)
-    for copy in lines + swaps:
+    for copy in lines + gate_lines:
         copy.start()
-    own.start()
-    o_ref[r, z] = x_ref[...]
+    gathered[r, z] = small[...]
+    gates_all[c, z] = gates[...]
     for copy in lines:
         copy.wait()
     spreads = [
-        remote(o_ref.at[r], o_ref.at[r], send.at[planes + 3 + d], recv.at[planes + 3 + d], device)
+        remote(gathered.at[r], gathered.at[r], send.at[planes + d], recv.at[planes + d], device)
         for d, device in enumerate(near)
     ]
     for copy in spreads:
         copy.start()
-    for copy in spreads + swaps:
+    for copy in gate_lines:
         copy.wait()
-    own.wait()
-
-
-def opening(weights, block, collective_id):
+    gate_swap = remote(
+        gates_all.at[c], gates_all.at[c], gate_send.at[planes], gate_recv.at[planes], me + 1 - 2 * c
+    )
+    gate_swap.start()
+    for copy in spreads:
+        copy.wait()
+    swaps = swap_copies(piece, swapped, swap_send, swap_recv, swap_local)
+    rows, width = tokens.shape
+    step = width // (8 * planes)
+    for j in range(planes):
+        for q in range(CHIPS):
+            for e in range(2):
+                start = ((e * planes + j) * CHIPS + q) * step
+                gain[0:1, start : start + step] = gathered[2 * q + e, j, 0:1, 0:step]
+
+    @pl.loop(0, rows // 16)
+    def norm_rows(i):
+        at = sixteen(i)
+        values = tokens[at, :].astype(jnp.float32)
+        inverse = lax.rsqrt(jnp.mean(values * values, axis=-1, keepdims=True) + epsilon)
+        normed[at, :] = (values * inverse * gain[0:1, :]).astype(jnp.bfloat16)
+
+    begin, forward, end = gather_steps(normed, whole, gather_send, gather_recv, gather_local, 0)
+    begin()
+    for copy in swaps:
+        copy.start()
+    gate_swap.wait()
+    block = gates.shape[0]
+    for k, target in enumerate((decay_blocks, input_blocks)):
+        target[...] = jnp.zeros_like(target)
+        for e in range(2):
+            for j in range(planes):
+                for h in range(2):
+                    row, column = (e * planes + j) * block, (h * planes + j) * block
+                    target[row : row + block, column : column + block] = gates_all[
+                        e, j, :, (2 * k + h) * block : (2 * k + h + 1) * block
+                    ]
+    forward()
+    end()
+    for copy in swaps:
+        copy.wait()
+
+
+def opening(small, gates, tokens, piece, collective_id):
     planes = lax.axis_size("seq") // 8
+    rows, width = tokens.shape
+    channels = 2 * planes * gates.shape[0]
     return pl.pallas_call(
         functools.partial(opening_kernel, planes),
         out_shape=[
-            jax.ShapeDtypeStruct(weights.shape, weights.dtype),
-            jax.ShapeDtypeStruct((8, planes) + block.shape, block.dtype),
+            jax.ShapeDtypeStruct((8, planes) + small.shape, small.dtype),
+            jax.ShapeDtypeStruct((channels, channels), gates.dtype),
+            jax.ShapeDtypeStruct((channels, channels), gates.dtype),
+            jax.ShapeDtypeStruct((CHIPS, rows, width), jnp.bfloat16),
+            jax.ShapeDtypeStruct(piece.shape, piece.dtype),
         ],
-        in_specs=[ANY, VMEM],
-        out_specs=[ANY, VMEM],
+        in_specs=[VMEM, VMEM, VMEM, ANY],
+        out_specs=[VMEM, VMEM, VMEM, ANY, ANY],
         scratch_shapes=[
-            pltpu.SemaphoreType.DMA((planes + 10,)),
-            pltpu.SemaphoreType.DMA((planes + 10,)),
+            pltpu.VMEM((2, planes) + gates.shape, gates.dtype),
+            pltpu.VMEM((8, width), jnp.float32),
+            pltpu.VMEM((rows, width), jnp.bfloat16),
+            pltpu.SemaphoreType.DMA((planes + 7,)),
+            pltpu.SemaphoreType.DMA((planes + 7,)),
+            pltpu.SemaphoreType.DMA((planes + 1,)),
+            pltpu.SemaphoreType.DMA((planes + 1,)),
+            pltpu.SemaphoreType.DMA((3,)),
+            pltpu.SemaphoreType.DMA((3,)),
+            pltpu.SemaphoreType.DMA,
+            pltpu.SemaphoreType.DMA((4,)),
+            pltpu.SemaphoreType.DMA((4,)),
             pltpu.SemaphoreType.DMA,
         ],
-        compiler_params=comm_params(collective_id),
+        compiler_params=comm_params(collective_id, 60),
+        cost_estimate=lasting(65),
         name="opening",
-    )(weights, block)
+    )(small, gates, tokens, piece)
 
 
 def column_peers(planes, z, p, c):
@@ -1095,6 +1429,7 @@
     decay_blocks,
     input_blocks,
     cot,
+    piece,
     conv_out,
     conv_low,
     decay_pre,
@@ -1104,6 +1439,7 @@
     entering,
     halo,
     cot_all,
+    swapped,
     cumulative,
     sibling_tails,
     below_tail,
@@ -1112,13 +1448,16 @@
     send,
     recv,
     local,
+    swap_send,
+    swap_recv,
 ):
     me, z, p, c, x, y = place()
     rows, channels = conv_input.shape[1:]
     q, peers = column_peers(planes, z, p, c)
-    greet(peers + [*plane_neighbours()[0][:2]])
-    cot_begin, cot_forward, cot_end = gather_steps(cot, cot_all, send, recv, local, 9)
+    greet(peers + [*plane_neighbours()[0]])
+    cot_begin, cot_forward, cot_end = gather_steps(cot, cot_all, send, recv, local.at[0], 9)
     cot_begin()
+    swaps = swap_copies(piece, swapped, swap_send, swap_recv, local.at[1])
     f32 = jnp.float32
     tail = pl.ds(rows - 16, 16)
     to_sibling = remote(conv_input.at[:, tail], sibling_tails, send.at[7], recv.at[7], me + 1 - 2 * c)
@@ -1179,7 +1518,7 @@
             conv_low[j, sixteen(i), :] = jnp.concatenate(outs, axis=0).astype(jnp.bfloat16)
             return earlier
 
-        lax.fori_loop(0, rows // 16, conv_tile, halo[j])
+        lax.fori_loop(0, rows // 16, conv_tile, halo[j], unroll=2)
         low = conv_low[j]
         decay_pre[j] = jnp.dot(low, decay_blocks[...], preferred_element_type=f32) + vectors[CW + 1 : CW + 2, :]
         input_pre[j] = jnp.dot(low, input_blocks[...], preferred_element_type=f32) + vectors[CW + 2 : CW + 3, :]
@@ -1202,11 +1541,14 @@
             rows // 8,
             scan_tile,
             (jnp.ones((1, channels), f32), jnp.zeros((1, channels), f32)),
+            unroll=4,
         )
         everyone[q, pl.ds(j, 1), :] = last_a
         everyone[q, pl.ds(CHIPS + j, 1), :] = last_b
 
     cot_forward()
+    for copy in swaps:
+        copy.start()
     carry_in(planes, False, z, c, q, peers, everyone, before, entering, send, recv)
 
     @pl.loop(0, CHIPS)
@@ -1222,12 +1564,14 @@
             mixed[j, at, :] = (state * act).astype(jnp.bfloat16)
             return unused
 
-        lax.fori_loop(0, rows // 16, state_tile, 0)
+        lax.fori_loop(0, rows // 16, state_tile, 0, unroll=2)
 
     cot_end()
-
-
-def recurrence(gate_pre, conv_input, masks, vectors, decay_blocks, input_blocks, cot, collective_id):
+    for copy in swaps:
+        copy.wait()
+
+
+def recurrence(gate_pre, conv_input, masks, vectors, decay_blocks, input_blocks, cot, piece, collective_id):
     planes = lax.axis_size("seq") // 8
     blocks, rows, channels = conv_input.shape
     f32, bf16 = jnp.float32, jnp.bfloat16
@@ -1248,9 +1592,10 @@
             out(f32, (CHIPS, channels)),
             out(f32, (CHIPS, 8, channels)),
             out(cot.dtype, (CHIPS,) + cot.shape),
+            out(piece.dtype, piece.shape),
         ],
-        in_specs=[VMEM] * 6 + [ANY],
-        out_specs=[VMEM] * 8 + [ANY],
+        in_specs=[VMEM] * 6 + [ANY] * 2,
+        out_specs=[VMEM] * 8 + [ANY] * 2,
         scratch_shapes=[
             pltpu.VMEM(cube, f32),
             pltpu.VMEM((CHIPS, 16, channels), bf16),
@@ -1259,16 +1604,20 @@
             pltpu.VMEM((8 * planes, channels), f32),
             pltpu.SemaphoreType.DMA((13,)),
             pltpu.SemaphoreType.DMA((13,)),
-            pltpu.SemaphoreType.DMA,
+            pltpu.SemaphoreType.DMA((2,)),
+            pltpu.SemaphoreType.DMA((3,)),
+            pltpu.SemaphoreType.DMA((3,)),
         ],
-        compiler_params=comm_params(collective_id, 48),
+        compiler_params=comm_params(collective_id, 60),
+        cost_estimate=lasting(46),
         name="recurrence",
-    )(gate_pre, conv_input, masks, vectors, decay_blocks, input_blocks, cot)
+    )(gate_pre, conv_input, masks, vectors, decay_blocks, input_blocks, cot, piece)
 
 
 def recurrence_back_kernel(
     planes,
-    grad_mixed,
+    grad_branch,
+    rows_all,
     gate_pre,
     conv_input,
     conv_out,
@@ -1288,8 +1637,11 @@
     decay_low,
     input_low,
     sums,
-    down_others,
+    down_sum,
     swapped,
+    grad_mixed,
+    branch_here,
+    out_here,
     cumulative,
     local,
     grad_conv,
@@ -1302,21 +1654,23 @@
     send,
     recv,
     piece_sem,
+    loads,
+    *down_scratch,
 ):
     me, z, p, c, x, y = place()
     rows, channels = conv_input.shape[1:]
     q, peers = column_peers(planes, z, p, c)
     devices, chips = plane_neighbours()
     greet(peers + [*devices])
-    downs = [
-        remote(down_parts.at[chips[k]], down_others.at[k], send.at[9 + k], recv.at[9 + k], devices[k])
-        for k in range(3)
-    ] + [
-        remote(piece.at[chips[k]], swapped.at[p], send.at[12 + k], recv.at[12 + k], devices[k]) for k in range(3)
-    ]
-    downs.append(pltpu.make_async_copy(piece.at[p], swapped.at[p], piece_sem))
-    for copy in downs:
+    down_begin, down_forward, down_end = sum_steps(down_parts, *down_scratch)
+    down_begin()
+    swaps = swap_copies(piece, swapped, send.at[pl.ds(9, 3)], recv.at[pl.ds(9, 3)], piece_sem.at[0])
+    fetched = fetch_rows(rows_all, 0, 0, out_here, loads)
+    fetched.append(pltpu.make_async_copy(grad_branch, branch_here, piece_sem.at[1]))
+    for copy in fetched:
         copy.start()
+    for copy in fetched:
+        copy.wait()
     f32, bf16 = jnp.float32, jnp.bfloat16
     row = lax.broadcasted_iota(jnp.int32, (8, channels), 0)
     rate = vectors[CW + 3 : CW + 4, :]
@@ -1324,6 +1678,10 @@
 
     @pl.loop(0, CHIPS)
     def scan_block(j):
+        grad_mixed[j] = lax.dot_general(
+            branch_here[j], out_here[...], (((1,), (1,)), ((), ())), preferred_element_type=f32
+        )
+
         def scan_tile(i, carry):
             i = rows // 16 - 1 - i
             at = sixteen(i)
@@ -1350,12 +1708,15 @@
 
         ones = jnp.ones((1, channels), f32)
         first_a, first_b, first_coef = lax.fori_loop(
-            0, rows // 16, scan_tile, (ones, jnp.zeros((1, channels), f32), ones)
+            0, rows // 16, scan_tile, (ones, jnp.zeros((1, channels), f32), ones), unroll=2
         )
         everyone[q, pl.ds(j, 1), :] = first_coef * first_a
         everyone[q, pl.ds(CHIPS + j, 1), :] = first_coef * first_b
 
     carry_in(planes, True, z, c, q, peers, everyone, before, leaving, send, recv)
+    down_forward()
+    for copy in swaps:
+        copy.start()
 
     def terms_block(j, totals):
         behind_all = leaving[pl.ds(j, 1), :]
@@ -1390,7 +1751,7 @@
             return previous, decay_sum, input_sum, param_sum
 
         totals = lax.fori_loop(
-            0, rows // 16, terms_tile, (entering[pl.ds(j, 1), :], *totals)
+            0, rows // 16, terms_tile, (entering[pl.ds(j, 1), :], *totals), unroll=2
         )[1:]
 
         def dot_t(left, right):
@@ -1477,12 +1838,21 @@
     totals = lax.fori_loop(0, CHIPS, conv_block, (nothing,) * (CW + 1))
     for k, total in enumerate((*totals, decay_sum, input_sum, param_sum)):
         sums[k : k + 1, :] = jnp.sum(total, axis=0, keepdims=True)
-    for copy in downs:
+    down_end()
+    own, from_x, from_y = down_scratch[:3]
+
+    @pl.loop(0, own.shape[0] // 16)
+    def sum_rows(i):
+        at = sixteen(i)
+        down_sum[at, :] = own[at, :].astype(f32) + from_x[at, :].astype(f32) + from_y[at, :].astype(f32)
+
+    for copy in swaps:
         copy.wait()
 
 
 def recurrence_back(
-    grad_mixed,
+    grad_branch,
+    rows_all,
     gate_pre,
     conv_input,
     conv_out,
@@ -1511,12 +1881,15 @@
             jax.ShapeDtypeStruct(cube, bf16),
             jax.ShapeDtypeStruct(cube, bf16),
             jax.ShapeDtypeStruct((CW + 4, channels), f32),
-            jax.ShapeDtypeStruct((CHIPS - 1,) + down_parts.shape[1:], bf16),
+            jax.ShapeDtypeStruct(down_parts.shape[1:], f32),
             jax.ShapeDtypeStruct(piece.shape, bf16),
         ],
-        in_specs=[VMEM] * 14 + [ANY] * 2,
-        out_specs=[VMEM] * 4 + [ANY] * 2,
+        in_specs=[ANY] * 2 + [VMEM] * 13 + [ANY] * 2,
+        out_specs=[VMEM] * 5 + [ANY],
         scratch_shapes=[
+            pltpu.VMEM(cube, f32),
+            pltpu.VMEM(grad_branch.shape, bf16),
+            pltpu.VMEM((channels, grad_branch.shape[2]), bf16),
             pltpu.VMEM(cube, f32),
             pltpu.VMEM(cube, f32),
             pltpu.VMEM(cube, f32),
@@ -1526,14 +1899,18 @@
             pltpu.VMEM((2 * planes, 2 * CHIPS, channels), f32),
             pltpu.VMEM((8 * planes, channels), f32),
             pltpu.VMEM((CHIPS, channels), f32),
-            pltpu.SemaphoreType.DMA((15,)),
-            pltpu.SemaphoreType.DMA((15,)),
-            pltpu.SemaphoreType.DMA,
+            pltpu.SemaphoreType.DMA((12,)),
+            pltpu.SemaphoreType.DMA((12,)),
+            pltpu.SemaphoreType.DMA((2,)),
+            pltpu.SemaphoreType.DMA((rows_all.shape[0],)),
+            *sum_scratch(*down_parts.shape[1:], bf16),
         ],
-        compiler_params=comm_params(collective_id, 52),
+        compiler_params=comm_params(collective_id, 60),
+        cost_estimate=lasting(58),
         name="recurrence_back",
     )(
-        grad_mixed,
+        grad_branch,
+        rows_all,
         gate_pre,
         conv_input,
         conv_out,
@@ -1720,7 +2097,18 @@
     half = channels // 2
     in_pairs = (((0, 0), (0, half)), ((0, channels), (0, channels + half)))
     (weights_in,) = to_chips([gate_branch, input_branch], in_pairs, [2 * channels])
-    swapped_in, small = opening(weights_in, small, 1)
+    (swapped_in,) = plane_swap([weights_in], 2)
+    whole_in = column_gather(swapped_in.reshape(CHIPS * rows_d, 2 * channels))
+    tokens, cot, out_proj, mlp_down = regrouped_columns(
+        [tokens, cotangent, out_proj, mlp_down], [bf16] * 4, False
+    )
+    mlp_pairs = (((0, 0), (1, 0)), ((0, half_units), (1, half_units)))
+    mlp_pieces = to_chips([mlp_gate, mlp_up], mlp_pairs, [2 * half_units] * 2)
+    gates = jnp.concatenate([decay_gate, input_gate], axis=1)
+    small, decay_blocks, input_blocks, normed_all, first_piece = opening(
+        behind(small, swapped_in), gates, tokens, mlp_pieces[0], 1
+    )
+    normed_all = normed_all.reshape(CHIPS * rows, width)
     small = small.transpose(1, 0, 2, 3)
     flags = 2 + rows // lanes
     gain_one = regrouped(small[:, :, 0, :rows_d].reshape(width), 0, n)
@@ -1754,65 +2142,50 @@
     masks_all = jnp.concatenate([all_flags.reshape(1, planes, CHIPS, 2, rows), masks_all[1:]], axis=0)
     masks = own_blocks(masks_all).transpose(1, 2, 0)
 
-    mlp_pairs = (((0, 0), (1, 0)), ((0, half_units), (1, half_units)))
-    mlp_pieces = to_chips([mlp_gate, mlp_up], mlp_pairs, [2 * half_units] * 2)
-    whole_in = column_gather(swapped_in.reshape(CHIPS * rows_d, 2 * channels))
-    tokens, cot, out_proj, mlp_down = regrouped_columns(
-        [tokens, cotangent, out_proj, mlp_down], [bf16] * 4, False
-    )
-    rec_rows = column_gather(jnp.concatenate([out_proj, decay_gate, input_gate], axis=1))
-    whole_out, gates = rec_rows[:, :width], rec_rows[:, width:]
-    gates = gates.reshape(2, planes, rows_r, 2, 2, rows_r)
-    diagonal = jnp.eye(planes, dtype=bf16)[None, :, None, None, :, None]
-    decay_blocks, input_blocks = (
-        (gates[:, :, :, k, :, None, :] * diagonal).reshape(channels, channels) for k in range(2)
-    )
-
-    normed = rms_norm(tokens.astype(f32), gain_one).astype(bf16)
-    normed_all = plane_gather(normed, 3).reshape(CHIPS * rows, width)
-    swapped_mlp = plane_swap(behind(tuple(mlp_pieces), normed_all, decay_blocks, input_blocks), 4)
-    whole_down = column_gather(mlp_down)
-    whole_mlp = [column_gather(part.reshape(CHIPS * rows_d, 2 * half_units)) for part in swapped_mlp]
+    rows_all = column_gather(behind(jnp.concatenate([out_proj, mlp_down], axis=0), swapped_in))
+    rows_all = rows_all.reshape(2 * planes, rows_r + rows_f, width)
 
     gate_pre = product(normed_all, whole_in[:, :channels])
     cube = (CHIPS, rows, channels)
     gate_pre = gate_pre.reshape(cube)
     conv_input = product(normed_all, whole_in[:, channels:]).astype(bf16).reshape(cube)
-    conv_out, conv_low, decay_pre, input_pre, states, mixed, entering, halo, cot_all = recurrence(
-        gate_pre, conv_input, masks, vectors, decay_blocks, input_blocks, cot, 6
-    )
+    conv_out, conv_low, decay_pre, input_pre, states, mixed, entering, halo, cot_all, second_piece = recurrence(
+        gate_pre,
+        conv_input,
+        masks,
+        vectors,
+        decay_blocks,
+        input_blocks,
+        cot,
+        mlp_pieces[1],
+        6,
+    )
+    whole_mlp = [
+        column_gather(part.reshape(CHIPS * rows_d, 2 * half_units)) for part in (first_piece, second_piece)
+    ]
     cot_all = cot_all.reshape(CHIPS * rows, width)
+    middle, two_all = middle_of(mixed, rows_all, tokens, gain_two, 7)
     mixed = mixed.reshape(CHIPS * rows, channels)
-    branch_parts = product(mixed, whole_out).reshape(CHIPS, rows, width)
-    middle, two_all = middle_of(branch_parts, tokens, gain_two, 7)
     two_all = two_all.reshape(CHIPS * rows, width)
 
     cot_other = exchanged(cot_all)
-    two_own, two_other = halves(two_all, 1)
-    two_other = exchanged(two_other)
-    grad_hidden = product_t(cot_all, whole_down)
-    hiddens, grads_low, piece_grads = [], [], []
-    two_now = two_all
-    for k in range(2):
-        weights = whole_mlp[k]
-        gate_mlp = product(two_now, weights[:, :half_units])
-        up_mlp = product(two_now, weights[:, half_units:])
-        hidden, pull_act = jax.vjp(mlp_act, gate_mlp, up_mlp)
-        hiddens.append(hidden.astype(bf16))
-        grad_gate, grad_up = pull_act(grad_hidden[:, k * half_units : (k + 1) * half_units])
-        low = jnp.concatenate([grad_gate.astype(bf16), grad_up.astype(bf16)], axis=1)
-        grads_low.append(low)
-        piece_grads.append((weight_grad(two_own, low) + weight_grad(two_other, exchanged(low))).astype(bf16))
-        two_now = behind(two_now, piece_grads[-1])
-    hidden = jnp.concatenate(hiddens, axis=1)
-    two_parts = product_t(grads_low[0], whole_mlp[0]) + product_t(grads_low[1], whole_mlp[1])
-    two_parts = behind(two_parts.astype(bf16), piece_grads[1])
-    piece_grads = [line_sum(part) for part in piece_grads]
+    hidden_zero, first_grad, first_low = feed_forward(0, two_all, cot_all, whole_mlp[0], rows_all, (), 8)
+    hidden_one, second_grad, two_parts = feed_forward(
+        1, two_all, cot_all, whole_mlp[1], rows_all, (whole_mlp[0], first_low), 14
+    )
+    piece_grads = [line_sum(first_grad), line_sum(second_grad)]
     grad_middle, grad_mlp_gain, grad_branch, down_grad, down_parts = grads_of_middle(
-        two_parts.reshape(CHIPS, rows, width), middle, cot, gain_two, hidden, whole_down, cot_all, cot_other, 9
-    )
-    grad_mlp_down = line_sum(down_grad)
-    grad_branch = grad_branch.reshape(CHIPS * rows, width)
+        two_parts.reshape(CHIPS, rows, width),
+        middle,
+        cot,
+        gain_two,
+        (hidden_zero, hidden_one),
+        rows_all,
+        cot_all,
+        cot_other,
+        9,
+    )
+    branch_cube, grad_branch = grad_branch, grad_branch.reshape(CHIPS * rows, width)
 
     mixed_own, mixed_other = halves(mixed, 1)
     out_grad = weight_grad(mixed_own, grad_branch) + weight_grad(
@@ -1820,9 +2193,11 @@
     )
     out_grad = out_grad.astype(bf16)
     grad_out_proj = line_sum(out_grad)
-    grad_mixed = behind(product_t(grad_branch, whole_out), out_grad)
-    in_low, grad_decay_low, grad_input_low, sums, down_others, swapped_grads = recurrence_back(
-        grad_mixed.reshape(cube),
+    grad_mlp_down = line_sum(down_grad.reshape(planes * rows_f, width))
+    branch_cube = behind(branch_cube, out_grad)
+    in_low, grad_decay_low, grad_input_low, sums, down_sum, first_swapped = recurrence_back(
+        branch_cube,
+        rows_all,
         gate_pre,
         conv_input,
         conv_out,
@@ -1840,12 +2215,9 @@
         piece_grads[0].reshape(CHIPS, rows_d, 2 * half_units),
         12,
     )
-    down_sum = lax.dynamic_index_in_dim(down_parts, p, 0, False).astype(f32) + jnp.sum(
-        down_others.astype(f32), axis=0
-    )
-    block_out = middle + down_sum
     sums = sums.at[CW + 3].multiply(-rate_scale * jax.nn.sigmoid(param))
-    in_low = in_low.reshape(CHIPS * rows, 2 * channels)
+    low_cube = in_low
+    in_low = low_cube.reshape(CHIPS * rows, 2 * channels)
     flat = (CHIPS * rows, channels)
     conv_low, grad_decay_low, grad_input_low = (
         a.reshape(flat) for a in (conv_low, grad_decay_low, grad_input_low)
@@ -1855,12 +2227,7 @@
     in_grads = weight_grad(normed_own, in_low) + weight_grad(exchanged(normed_other), exchanged(in_low))
     in_total = in_grads.astype(bf16)
     in_grads = line_sum(in_total)
-    normed_parts = product_t(in_low, whole_in).astype(bf16).reshape(CHIPS, rows, width)
-    normed_parts = behind(normed_parts, in_total)
-    convs, decays, inputs = (
-        (own, exchanged(other))
-        for own, other in (halves(conv_low, 1), (grad_decay_low, grad_decay_low), (grad_input_low, grad_input_low))
-    )
+    low_cube = behind(low_cube, in_total)
     vector_parts = sums.reshape(CW + 4, 2, planes, rows_r).transpose(2, 1, 0, 3)
     vector_parts = jnp.pad(vector_parts, ((0, 0), (0, 0), (0, 0), (0, lanes - rows_r)))
     here = (jnp.arange(CHIPS) == p).astype(f32)[None, :, None, None, None]
@@ -1869,24 +2236,24 @@
     gain_parts = jnp.pad(
         gain_parts.reshape(planes, 8, 1, rows_d), ((0, 0), (0, 0), (0, 7), (0, lanes - rows_d))
     )
-    grad_tokens, small_grads, gate_grads, swapped_late = closing(
-        normed_parts,
+    grad_tokens, small_grads, gate_grads, second_swapped = closing(
+        low_cube,
+        whole_in,
         tokens,
         gain_one,
         grad_middle,
         jnp.concatenate([vector_parts, gain_parts], axis=2),
-        convs,
-        decays,
-        inputs,
+        (conv_low, grad_decay_low, grad_input_low),
         piece_grads[1].reshape(CHIPS, rows_d, 2 * half_units),
         head,
         13,
     )
     grad_mlp_gate, grad_mlp_up = from_chips(
-        [swapped_grads, swapped_late], mlp_pairs, [mlp_gate.shape[1]] * 2
-    )
+        [first_swapped, second_swapped], mlp_pairs, [mlp_gate.shape[1]] * 2
+    )
+    block_out = middle + behind(down_sum, grad_tokens)
     block_out, grad_out_proj, grad_mlp_down = regrouped_columns(
-        behind((block_out, grad_out_proj, grad_mlp_down), grad_tokens), [bf16, f32, f32], True
+        (block_out, *behind((grad_out_proj, grad_mlp_down), grad_tokens)), [bf16, f32, f32], True
     )
     in_out = plane_swap([in_grads.reshape(CHIPS, rows_d, 2 * channels)], 16)
     grad_gate_branch, grad_input_branch = from_chips(in_out, in_pairs, [lru_width] * 2)

time: 722 us -> 634 us (0.88)
  matrix products: 140 us -> 31.4 us
  Pallas kernels: 466 us -> 516 us
  local copies, waits for them, and re-layouts: 71.1 us -> 24.4 us
  waiting for transfers between devices: 4.99 us -> 27.9 us
  other arithmetic: 16.1 us -> 6.32 us
    dot_general x5 -> x0, matrix products: 51.9 us -> none  [product_t(): return jnp.einsum('tk,nk->tn', left, right, preferred_element_type=f32)]
    pallas_call x1, Pallas kernels: 18.6 us -> 63.4 us  [opening(): pl.pallas_call(functools.partial(opening_kernel, planes), out_shape=[jax....]
    unnamed x144 -> x82, local copies, waits for them, and re-layouts: 45.8 us -> 8.65 us
    pallas_call x1 -> x2, Pallas kernels: 39.5 us -> 76.2 us  [feed_forward(): pl.pallas_call(functools.partial(feed_forward_kernel, piece), out_shape=o...]
    dot_general x7 -> x2, matrix products: 45.3 us -> 12.6 us  [product(): return jnp.dot(left, right, preferred_element_type=f32)]
    dot_general x8 -> x4, matrix products: 42.9 us -> 18.8 us  [weight_grad(): return jnp.einsum('ta,tb->ab', left, right, preferred_element_type=f32)]
    pallas_call x1, Pallas kernels: 105 us -> 81.5 us  [middle_of(): pl.pallas_call(middle_kernel, out_shape=[jax.ShapeDtypeStruct((rows, widt...]
    pallas_call x1, Pallas kernels: 72.3 us -> 55.5 us  [recurrence_back(): pl.pallas_call(functools.partial(recurrence_back_kernel, planes), out_sha...]
  transfers between devices with their start and end apart: 21 -> 14, of which waited for: 3 -> 3; matrix products, arithmetic and copies ran while one was open for 26% -> 9% of each run, Pallas kernels for 63% -> 78%
where the time goes in v3:
time: 634 us; the launch traced here: 624 us
  Pallas kernels  516 us (81%)
  matrix products  31.4 us (5%)
  waiting for transfers between devices  27.9 us (4%)
  local copies, waits for them, and re-layouts  24.4 us (4%)
  between operations  15 us (2%)
    pallas_call x1, Pallas kernels, grads_of_middle(): pl.pallas_call(grads_of_middle_kernel, out_shape=[jax.ShapeDtypeStruct((r...  82.2 us
    pallas_call x1, Pallas kernels, middle_of(): pl.pallas_call(middle_kernel, out_shape=[jax.ShapeDtypeStruct((rows, widt...  81.5 us
    pallas_call x2, Pallas kernels, feed_forward(): pl.pallas_call(functools.partial(feed_forward_kernel, piece), out_shape=o...  76.2 us
    pallas_call x1, Pallas kernels, opening(): pl.pallas_call(functools.partial(opening_kernel, planes), out_shape=[jax....  63.4 us
    pallas_call x1, Pallas kernels, recurrence(): pl.pallas_call(functools.partial(recurrence_kernel, planes), out_shape=[o...  61.4 us
    pallas_call x1, Pallas kernels, closing(): pl.pallas_call(functools.partial(closing_kernel, planes), out_shape=[jax....  59.5 us
    pallas_call x1, Pallas kernels, recurrence_back(): pl.pallas_call(functools.partial(recurrence_back_kernel, planes), out_sha...  55.5 us
    pallas_call x2, Pallas kernels, plane_swap(): pl.pallas_call(functools.partial(plane_swap_kernel, count), out_shape=[ja...  23.2 us
  transfers between devices with their start and end apart: 14, of which 3 were waited for; matrix products, arithmetic and copies ran while one was open for 9% of the time, Pallas kernels for 78%

profile of v3, /device:TPU:0, one launch (start us, length us, event | category | flops | bytes accessed | tf_op | source)
XLA Modules:
  0.0 623.6 jit_solution(8835885068300266165)
XLA Ops:
  7.2 2.4 to_chips.2.refs_0_
  9.7 12.3 %plane_swap.2 = bf16[4,64,1280]{2,1,0:T(8,128)(2,1)} custom-call(bf16[4,64,1280]{2,1,0:T(8,128)(2,1)} %to_chips.2.refs_0_), custom_call_target="tpu_custom_call" | custom-call | flops 10000000000 | bytes 30000000 | tf_op jit(solution)/shard_map/plane_swap/pallas_call | solution.py:1209
  22.2 1.9 regrouped_columns.2
  24.1 1.0 copy-done.9
  25.1 1.0 copy-done.10
  26.0 1.1 pad_maximum_fusion
  27.4 1.2 concatenate.39.small
  28.6 2.9 to_chips.3
  31.5 0.7 pad_maximum_fusion.4.gates
  32.2 63.4 %opening.1 = (f32[8,4,16,128]{3,2,1,0:T(8,128)}, bf16[640,640]{1,0:T(8,128)(2,1)}, bf16[640,640]{1,0:T(8,128)(2,1)}, bf16[4,256,2048]{2,1,0:T(8,128)(2,1)}, bf16[4,64,1536]{2,1,0:T(8,128)(2,1)}) custom-call(f32[16,128]{1,0:T(8,128)} %concatenate.39.small, bf16[80,320]{1,0:T(8,128)(2,1)} %pad_maximum_fusion.4.gates, bf16[256,2048]{1,0:T(8,128)(2,1)} %copy-done.9, ...), custom_call_target="tpu_custom_call" | custom-call | flops 65000001536 | bytes 195000000 | tf_op jit(solution)/shard_map/opening/pallas_call | solution.py:1323
  95.8 0.9 slice.141
  96.8 0.9 constant_dynamic-slice_fusion.3
  98.8 1.0 copy.56
  100.1 8.2 %fusion.3.gate_pre = f32[4,256,640]{2,1,0:T(8,128)} fusion(bf16[4,256,2048]{2,1,0:T(8,128)(2,1)} %get-tuple-element.102, bf16[2048,1280]{1,0:T(8,128)(2,1)} %all-gather.5.cloned.1.call-done.whole_in), kind=kOutput, calls=%fused_computation.6 | convolution fusion | flops 2684354560 | bytes 9437184 | tf_op jit(solution)/shard_map/dot_general | solution.py:2070
  108.3 4.5 fusion.6
  112.8 61.4 %recurrence.1 = (f32[4,256,640]{2,1,0:T(8,128)}, bf16[4,256,640]{2,1,0:T(8,128)(2,1)}, f32[4,256,640]{2,1,0:T(8,128)}, f32[4,256,640]{2,1,0:T(8,128)}, f32[4,256...) custom-call(f32[4,256,640]{2,1,0:T(8,128)} %fusion.3.gate_pre, ...), custom_call_target="tpu_custom_call" | custom-call | flops 46000001024 | bytes 138000000 | tf_op jit(solution)/shard_map/recurrence/pallas_call | solution.py:1583
  174.5 1.6 fusion.20
  176.8 81.5 %middle.1 = (f32[256,2048]{1,0:T(8,128)}, bf16[4,256,2048]{2,1,0:T(8,128)(2,1)}) custom-call(bf16[4,256,640]{2,1,0:T(8,128)(2,1)} %get-tuple-element.108.mixed, bf16[8,272,2048]{2,1,0:T(8,128)(2,1)} %bitcast.143, bf16[256,2048]{1,0:T(8,128)(2,1)} %copy-done.9, f32[1,2048]{1,0:T(1,128)} %broadcast_in_dim_reshape.7.gain), custom_call_target="tpu_custom_call" | custom-call | flops 74999996416 | bytes 225000000 | tf_op jit(solution)/shard_map/middle/pallas_call | solution.py:660
  258.3 30.8 %feed_forward.2 = (bf16[1024,768]{1,0:T(8,128)(2,1)}, bf16[1024,1536]{1,0:T(8,128)(2,1)}, bf16[1024,1536]{1,0:T(8,128)(2,1)}) custom-call(bf16[1024,2048]{1,0:T(8,128)(2,1)} %bitcast.159, bf16[1024,2048]{1,0:T(8,128)(2,1)} %bitcast.150, bf16[2048,1536]{1,0:T(8,128)(2,1)} %all-gather.11.cloned.1.call-done.weights.refs_0_, bf16[8,272,2048]{2,1,0:T(8,128)(2,1)} %bitcast.144), custom_call_target="tpu_custom_call" | custom-call | flops 35000000512 | bytes 105000000 | tf_op jit(solution)/shard_map/feed_forward/pallas_call | solution.py:813
  289.8 16.0 %all-gather.9.cloned.1.call-done.weights = bf16[2048,1536]{1,0:T(8,128)(2,1)} async-done(((bf16[256,1536]{1,0:T(8,128)(2,1)}), bf16[2048,1536]{1,0:T(8,128)(2,1)}) %all-gather.9.cloned.1.call-update) | async-done | bytes 6291472 | tf_op jit(solution)/shard_map/all_gather | solution.py:2050
  305.8 45.5 %feed_forward.3 = (bf16[1024,768]{1,0:T(8,128)(2,1)}, bf16[1024,1536]{1,0:T(8,128)(2,1)}, bf16[1024,2048]{1,0:T(8,128)(2,1)}) custom-call(bf16[1024,2048]{1,0:T(8,128)(2,1)} %bitcast.160, bf16[1024,2048]{1,0:T(8,128)(2,1)} %bitcast.152, bf16[2048,1536]{1,0:T(8,128)(2,1)} %all-gather.9.cloned.1.call-done.weights, bf16[8,272,2048]{2,1,0:T(8,128)(2,1)} %bitcast.145, ...), custom_call_target="tpu_custom_call" | custom-call | flops 35000000512 | bytes 105000000 | tf_op jit(solution)/shard_map/feed_forward/pallas_call | solution.py:813
  351.4 82.2 %grads_of_middle.1 = (f32[256,2048]{1,0:T(8,128)}, f32[1,2048]{1,0:T(1,128)}, bf16[4,256,2048]{2,1,0:T(8,128)(2,1)}, bf16[4,192,2048]{2,1,0:T(8,128)(2,1)}, bf16[4,256,2048]{2,1,0:T(8,128)(2,1)}) custom-call(bf16[4,256,2048]{2,1,0:T(8,128)(2,1)} %bitcast.161, f32[256,2048]{1,0:T(8,128)} %get-tuple-element.112.middle, bf16[256,2048]{1,0:T(8,128)(2,1)} %copy-done.10, ...), custom_call_target="tpu_custom_call" | custom-call | flops 80000000000 | bytes 240000000 | tf_op jit(solution)/shard_map/grads_of_middle/pallas_call | solution.py:970
  435.1 0.7 copy.61
  436.0 5.8 collective-permute-done.1
  441.8 3.7 fusion.23
  445.6 2.8 fusion
  448.4 55.5 %recurrence_back.1 = (bf16[4,256,1280]{2,1,0:T(8,128)(2,1)}, bf16[4,256,640]{2,1,0:T(8,128)(2,1)}, bf16[4,256,640]{2,1,0:T(8,128)(2,1)}, f32[8,640]{1,0:T(8,128)...) custom-call(bf16[4,256,2048]{2,1,0:T(8,128)(2,1)} %get-tuple-element.122.grad_branch, ...), custom_call_target="tpu_custom_call" | custom-call | flops 57999998976 | bytes 174000000 | tf_op jit(solution)/shard_map/recurrence_back/pallas_call | solution.py:1877
  504.1 1.8 constant_dynamic-slice_fusion
  506.4 0.7 broadcast_in_dim_reshape.8.gain
  508.9 0.7 select_maximum_fusion.small
  509.6 5.3 fusion.4
  515.0 6.9 %add_convert_fusion = bf16[1024,1280]{1,0:T(8,128)(2,1)} fusion(f32[1024,1280]{1,0:T(8,128)S(1)} %fusion.4, bf16[1024,1024]{1,0:T(8,128)(2,1)} %collective-permute-done.3, bf16[1024,1280]{1,0:T(8,128)(2,1)} %collective-permute-done.4), kind=kOutput, calls=%fused_computation | convolution fusion | flops 2686976000 | bytes 12582912 | tf_op jit(solution)/shard_map/ta,tb->ab/dot_general | solution.py:2076
  522.0 59.5 %closing.1 = (f32[256,2048]{1,0:T(8,128)}, f32[24,128]{1,0:T(8,128)}, f32[80,320]{1,0:T(8,128)}, bf16[4,64,1536]{2,1,0:T(8,128)(2,1)}) custom-call(bf16[4,256,1280]{2,1,0:T(8,128)(2,1)} %get-tuple-element.133.in_low, bf16[2048,1280]{1,0:T(8,128)(2,1)} %all-gather.5.cloned.1.call-done.whole_in, bf16[256,2048]{1,0:T(8,128)(2,1)} %copy-done.9, ...), custom_call_target="tpu_custom_call" | custom-call | flops 49999998976 | bytes 150000000 | tf_op jit(solution)/shard_map/closing/pallas_call | solution.py:1152
  581.5 2.6 add.106.refs_0_
  584.2 1.3 slice.131
  585.4 1.1 copy-done.3
  586.6 2.0 from_chips.3
  588.5 1.1 copy-done.5
  589.7 1.0 copy-done.8
  590.6 2.4 regrouped_columns.3
  593.0 1.2 slice_bitcast_fusion.2
  594.2 1.3 slice_bitcast_fusion.3
  595.6 0.7 fusion.21
  596.3 5.8 reduce-scatter.14.cloned.1.call-done
  602.1 10.9 %plane_swap.3.refs_0_ = bf16[4,64,1280]{2,1,0:T(8,128)(2,1)} custom-call(bf16[4,64,1280]{2,1,0:T(8,128)(2,1)} %bitcast.158), custom_call_target="tpu_custom_call" | custom-call | flops 10000000000 | bytes 30000000 | tf_op jit(solution)/shard_map/plane_swap/pallas_call | solution.py:1209
  613.0 1.1 copy-done.6
  614.1 1.4 from_chips.2
  615.6 1.3 copy.78
  (154 shorter events, 7.6 us)
Async XLA Ops:
  7.2 92.9 %all-gather.5.cloned.1.call-start = ((), (), s32[]{:S(2)}) async-start(), calls=%async_computation.5 | async-start | bytes 5898240 | tf_op jit(solution)/shard_map/all_gather | solution.py:2050
  9.7 12.5 %copy-start = (bf16[256,2048]{1,0:T(8,128)(2,1)S(1)}, bf16[256,2048]{1,0:T(8,128)(2,1)}, u32[]{:S(2)}) copy-start(bf16[256,2048]{1,0:T(8,128)(2,1)} %refs_0_.4) | copy-start | bytes 3145732
  9.7 12.5 %copy-start.1 = (bf16[256,2048]{1,0:T(8,128)(2,1)S(1)}, bf16[256,2048]{1,0:T(8,128)(2,1)}, u32[]{:S(2)}) copy-start(bf16[256,2048]{1,0:T(8,128)(2,1)} %refs_1_.4) | copy-start | bytes 3145732
  9.7 12.5 %copy-start.4 = (bf16[192,2048]{1,0:T(8,128)(2,1)S(1)}, bf16[192,2048]{1,0:T(8,128)(2,1)}, u32[]{:S(2)}) copy-start(bf16[192,2048]{1,0:T(8,128)(2,1)} %refs_3_.1) | copy-start | bytes 2359300
  9.7 12.5 %copy-start.7 = (bf16[80,2048]{1,0:T(8,128)(2,1)S(1)}, bf16[80,2048]{1,0:T(8,128)(2,1)}, u32[]{:S(2)}) copy-start(bf16[80,2048]{1,0:T(8,128)(2,1)} %refs_2_.1) | copy-start | bytes 983044
  22.0 5.2 copy-start.31
  22.0 5.2 copy-start.32
  22.0 5.2 copy-start.29
  22.0 5.3 copy-start.33
  22.1 5.3 copy-start.34
  22.1 5.3 copy-start.35
  22.1 5.3 copy-start.36
  22.1 5.3 copy-start.30
  22.1 154.7 %all-gather.7.cloned.1.call-start = ((), (), s32[]{:S(2)}) async-start(), calls=%async_computation.6 | async-start | bytes 10027008 | tf_op jit(solution)/shard_map/all_gather | solution.py:2050
  26.0 5.5 copy-start.22
  26.0 5.5 copy-start.23
  27.2 231.1 %all-gather.11.cloned.1.call-start = ((), (), s32[]{:S(2)}) async-start(), calls=%async_computation.8 | async-start | bytes 7077888 | tf_op jit(solution)/shard_map/all_gather | solution.py:2050
  95.7 210.1 %all-gather.9.cloned.1.call-start = ((), (), s32[]{:S(2)}) async-start(), calls=%async_computation.7 | async-start | bytes 7077888 | tf_op jit(solution)/shard_map/all_gather | solution.py:2050
  97.9 10.4 %copy-start.18 = (f32[1,4,4,2,256]{4,3,2,1,0:T(2,128)}, f32[1,4,4,2,256]{4,3,2,1,0:T(2,128)S(1)}, u32[]{:S(2)}) copy-start(f32[1,4,4,2,256]{4,3,2,1,0:T(2,128)S(1)} %stack.8) | copy-start | bytes 98308
  99.9 8.4 %copy-start.25 = (f32[1,640]{1,0:T(1,128)}, f32[1,640]{1,0:T(1,128)S(1)}, u32[]{:S(2)}) copy-start(f32[1,640]{1,0:T(1,128)S(1)} %squeeze.36) | copy-start | bytes 7684
  100.0 8.2 %copy-start.27 = (f32[8,640]{1,0:T(8,128)}, f32[8,640]{1,0:T(8,128)S(1)}, u32[]{:S(2)}) copy-start(f32[8,640]{1,0:T(8,128)S(1)} %scatter.4.vectors) | copy-start | bytes 61444
  100.1 8.2 %copy-start.12 = (bf16[4,256,2048]{2,1,0:T(8,128)(2,1)S(1)}, bf16[4,256,2048]{2,1,0:T(8,128)(2,1)}, u32[]{:S(2)}) copy-start(bf16[4,256,2048]{2,1,0:T(8,128)(2,1)} %get-tuple-element.102) | copy-start | bytes 12582916
  100.1 8.2 %copy-start.37 = (bf16[2048,1280]{1,0:T(8,128)(2,1)S(1)}, bf16[2048,1280]{1,0:T(8,128)(2,1)}, u32[]{:S(2)}) copy-start(bf16[2048,1280]{1,0:T(8,128)(2,1)} %all-gather.5.cloned.1.call-done.whole_in) | copy-start | bytes 15728644
  174.2 274.2 %reduce-scatter.6.cloned.1.call-start = ((), (), s32[]{:S(2)}) async-start(), calls=%async_computation.9 | async-start | bytes 3932160 | tf_op jit(solution)/shard_map/reduce_scatter | solution.py:2053
  289.1 232.9 %reduce-scatter.8.cloned.1.call-start = ((), (), s32[]{:S(2)}) async-start(), calls=%async_computation.10 | async-start | bytes 3932160 | tf_op jit(solution)/shard_map/reduce_scatter | solution.py:2053
  289.5 61.8 %collective-permute-start = (bf16[1024,2048]{1,0:T(8,128)(2,1)}, bf16[1024,2048]{1,0:T(8,128)(2,1)}, u32[]{:S(2)}, u32[]{:S(2)}) collective-permute-start(bf16[1024,2048]{1,0:T(8,128)(2,1)} %bitcast.151), channel_id=1, source_target_pairs={{0,1},{1,0},{2,3},{3,2},{4,5},{5,4},{6,7},{7,6},{8,9},{9,8},{10,11... | collective-permute-start | bytes 12582920 | tf_op jit(solution)/shard_map/ppermute | solution.py:2067
  351.3 232.8 %reduce-scatter.12.cloned.1.call-start = ((), (), s32[]{:S(2)}) async-start(), calls=%async_computation.12 | async-start | bytes 3932160 | tf_op jit(solution)/shard_map/reduce_scatter | solution.py:2053
  351.4 82.4 %copy-start.13 = (bf16[4,256,640]{2,1,0:T(8,128)(2,1)S(1)}, bf16[4,256,640]{2,1,0:T(8,128)(2,1)}, u32[]{:S(2)}) copy-start(bf16[4,256,640]{2,1,0:T(8,128)(2,1)} %get-tuple-element.108.mixed) | copy-start | bytes 3932164
  433.6 1.3 copy-start.15
  433.6 1.3 copy-start.17
  433.7 1.3 copy-start.19
  433.7 8.2 %collective-permute-start.2 = (bf16[1024,2048]{1,0:T(8,128)(2,1)}, bf16[1024,2048]{1,0:T(8,128)(2,1)}, u32[]{:S(2)}, u32[]{:S(2)}) collective-permute-start(bf16[1024,2048]{1,0:T(8,128)(2,1)} %bitcast.148), channel_id=1, source_target_pairs={{0,1},{1,0},{2,3},{3,2},{4,5},{5,4},{6,7},{7,6},{8,9},{9,8},{10,11... | collective-permute-start | bytes 12582920 | tf_op jit(solution)/shard_map/ppermute | solution.py:2067
  434.4 7.4 %collective-permute-start.1 = (bf16[1024,320]{0,1:T(8,128)(2,1)S(1)}, bf16[1024,320]{0,1:T(8,128)(2,1)S(1)}, u32[]{:S(2)}, u32[]{:S(2)}) collective-permute-start(bf16[1024,320]{0,1:T(8,128)(2,1)S(1)} %copy.68), channel_id=1, source_target_pairs={{0,1},{1,0},{2,3},{3,2},{4,5},{5,4},{6,7},{7,6},{8,9},{9,8},{10,11... | collective-permute-start | bytes 1966088 | tf_op jit(solution)/shard_map/ppermute | solution.py:2067
  435.8 148.4 %reduce-scatter.10.cloned.1.call-start = ((), (), s32[]{:S(2)}) async-start(), calls=%async_computation.11 | async-start | bytes 1638400 | tf_op jit(solution)/shard_map/reduce_scatter | solution.py:2053
  436.0 9.5 %copy-start.38 = (bf16[4,256,2048]{2,1,0:T(8,128)(2,1)S(1)}, bf16[4,256,2048]{2,1,0:T(8,128)(2,1)}, u32[]{:S(2)}) copy-start(bf16[4,256,2048]{2,1,0:T(8,128)(2,1)} %get-tuple-element.122.grad_branch) | copy-start | bytes 12582916
  503.9 11.1 %collective-permute-start.4 = (bf16[1024,1280]{1,0:T(8,128)(2,1)}, bf16[1024,1280]{1,0:T(8,128)(2,1)}, u32[]{:S(2)}, u32[]{:S(2)}) collective-permute-start(bf16[1024,1280]{1,0:T(8,128)(2,1)} %bitcast.154), channel_id=1, source_target_pairs={{0,1},{1,0},{2,3},{3,2},{4,5},{5,4},{6,7},{7,6},{8,9},{9,8},{10,11... | collective-permute-start | bytes 7864328 | tf_op jit(solution)/shard_map/ppermute | solution.py:2067
  504.1 2.4 copy-start.21
  504.1 3.7 copy-start.28
  504.1 4.5 copy-start.24
  504.1 4.5 copy-start.26
  505.9 9.1 %collective-permute-start.3 = (bf16[1024,1024]{1,0:T(8,128)(2,1)S(1)}, bf16[1024,1024]{1,0:T(8,128)(2,1)}, u32[]{:S(2)}, u32[]{:S(2)}) collective-permute-start(bf16[1024,1024]{1,0:T(8,128)(2,1)S(1)} %constant_dynamic-slice_fusion), channel_id=1, source_target_pairs={{0,1},{1,0},{2,3},{3,2},{4,5},{5,4},{6,7},{7,6},{8,9},{9,8},{10,11... | collective-permute-start | bytes 6291464 | tf_op jit(solution)/shard_map/ppermute | solution.py:2067
  506.4 95.7 %reduce-scatter.14.cloned.1.call-start = ((), (), s32[]{:S(2)}) async-start(), calls=%async_computation.13 | async-start | bytes 3276800 | tf_op jit(solution)/shard_map/reduce_scatter | solution.py:2053
  581.5 4.0 copy-start.2
  581.5 14.1 %copy-start.20 = (f32[80,320]{1,0:T(8,128)S(1)}, f32[80,320]{1,0:T(8,128)}, u32[]{:S(2)}) copy-start(f32[80,320]{1,0:T(8,128)} %get-tuple-element.150) | copy-start | bytes 307204
  585.4 1.1 copy-start.3
  588.5 1.1 copy-start.5
  602.1 13.5 %copy-start.11 = (f32[256,2048]{1,0:T(8,128)S(1)}, f32[256,2048]{1,0:T(8,128)}, u32[]{:S(2)}) copy-start(f32[256,2048]{1,0:T(8,128)} %get-tuple-element.202) | copy-start | bytes 6291460
  613.0 1.1 copy-start.6
  (5 other events, 4.2 us)
Sparse Core Ops, SparseCore 0:
  22.1 63.0 all-gather.4
  87.4 88.5 all-gather.6
  177.5 63.3 all-gather.10
  242.4 63.3 all-gather.8
  308.0 58.8 reduce-scatter.5
  369.1 60.3 reduce-scatter.7
  435.9 60.5 reduce-scatter.11
  506.5 35.2 reduce-scatter.9
  544.1 57.9 reduce-scatter.13

commit v4 on v3

--- a/solution.py
+++ b/solution.py
@@ -550,14 +550,15 @@
     ]
 
 
-def computed_scratch(rows, columns):
+def computed_scratch(rows, columns, dtype):
     f32, bf16 = jnp.float32, jnp.bfloat16
     whole, half = (rows, columns), (rows // 2, columns)
-    shapes = [(whole, bf16)] * 3 + [(whole, f32)] + [(half, f32)] * 2 + [(whole, bf16)] * 2 + [(half, bf16)] * 2
+    shapes = [(whole, bf16), (whole, f32)] + [(half, f32)] * 2 + [(half, bf16)] * 6 + [(half, dtype)] * 4
     return [pltpu.VMEM(*shape) for shape in shapes] + [pltpu.SemaphoreType.DMA((6,))] * 2
 
 
-def computed_sum(product, sent_d, sent_x, sent_y, own, kept_x, kept_y, from_x, from_y, diag_x, diag_y, send, recv):
+def computed_sum(product, sent_d, own, kept_x, kept_y, *refs):
+    sent_x, sent_y, from_x, from_y, diag_x, diag_y, joint_x, joint_y, also_x, also_y, send, recv = refs
     (x_dev, y_dev, d_dev), (p_x, p_y, p_d) = plane_neighbours()
     p = place()[2]
     rows, width = own.shape
@@ -565,51 +566,43 @@
     low, high = pl.ds(0, half), pl.ds(half, half)
     tile = 512
 
-    def into(chip, at, target, target_at):
+    def into(chip, at, target):
         @pl.loop(0, width // tile)
         def product_tile(k):
             columns = pl.ds(pl.multiple_of(k * tile, tile), tile)
-            target[target_at, columns] = product(chip, at, columns).astype(target.dtype)
+            target[:, columns] = product(chip, at, columns).astype(target.dtype)
 
     def copy(k, source, target, device):
         return remote(source, target, send.at[k], recv.at[k], device)
 
     first = [copy(0, sent_d.at[low], diag_x, x_dev), copy(1, sent_d.at[high], diag_y, y_dev)]
-    second = [
-        copy(2, sent_x.at[low], from_x.at[low], x_dev),
-        copy(3, sent_y.at[high], from_y.at[high], y_dev),
-    ]
-    third = [
-        copy(4, sent_y.at[low], from_y.at[low], y_dev),
-        copy(5, sent_x.at[high], from_x.at[high], x_dev),
-    ]
-    everything = slice(None)
+    second = [copy(2, sent_x, from_x, x_dev), copy(3, sent_y, from_y, y_dev)]
+    third = [copy(4, joint_y, also_y, y_dev), copy(5, joint_x, also_x, x_dev)]
 
     def begin():
-        into(p_d, everything, sent_d, everything)
+        into(p_d, slice(None), sent_d)
         for sent in first:
             sent.start()
-        into(p_x, low, sent_x, low)
-        into(p_y, high, sent_y, high)
+        into(p_x, low, sent_x)
+        into(p_y, high, sent_y)
         for sent in second:
             sent.start()
-        into(p_y, low, kept_y, everything)
-        into(p_x, high, kept_x, everything)
-        into(p, everything, own, everything)
-
-    def add(target, start, kept, addend):
+        into(p_y, low, kept_y)
+        into(p_x, high, kept_x)
+        into(p, slice(None), own)
+
+    def add(target, kept, addend):
         @pl.loop(0, half // 16)
         def add_rows(i):
-            here = sixteen(i)
-            there = pl.ds(pl.multiple_of(start + i * 16, 16), 16)
-            target[there, :] = (kept[here, :] + addend[here, :].astype(jnp.float32)).astype(target.dtype)
+            at = sixteen(i)
+            target[at, :] = (kept[at, :] + addend[at, :].astype(jnp.float32)).astype(target.dtype)
 
     def forward():
         first[0].wait_recv()
-        add(sent_y, 0, kept_y, diag_x)
+        add(joint_y, kept_y, diag_x)
         third[0].start()
         first[1].wait_recv()
-        add(sent_x, half, kept_x, diag_y)
+        add(joint_x, kept_x, diag_y)
         third[1].start()
 
     def end():
@@ -618,13 +611,23 @@
         for sent in second + third:
             sent.wait()
 
-    return begin, forward, end
+    def total(i, j):
+        at = sixteen(j)
+        parts = (from_x, also_y) if i == 0 else (also_x, from_y)
+        here = pl.ds(pl.multiple_of(i * half + j * 16, 16), 16)
+        return here, own[here, :] + parts[0][at, :].astype(jnp.float32) + parts[1][at, :].astype(jnp.float32)
+
+    return begin, forward, end, total
 
 
 def middle_kernel(
-    mixed, rows_all, tokens, gain, middle, whole, normed, out_here, send, recv, local, loads, *sums
+    mixed, rows_all, tokens, gain, cot, middle, whole, cot_other, normed, out_here, send, recv, local, loads, *sums
 ):
-    greet(plane_neighbours()[0][:2])
+    me, z, p, c, x, y = place()
+    sibling = me + 1 - 2 * c
+    greet((*plane_neighbours()[0][:2], sibling))
+    to_sibling = remote(cot, cot_other, send.at[4], recv.at[4], sibling)
+    to_sibling.start()
     f32, bf16 = jnp.float32, jnp.bfloat16
     fetched = fetch_rows(rows_all, 0, 0, out_here, loads)
     for copy in fetched:
@@ -635,25 +638,25 @@
     def product(chip, at, columns):
         return jnp.dot(mixed[chip, at, :], out_here[:, columns], preferred_element_type=f32)
 
-    for step in computed_sum(product, *sums):
+    *steps, total = computed_sum(product, *sums)
+    for step in steps:
         step()
-    own, from_x, from_y = sums[3], sums[6], sums[7]
-
-    @pl.loop(0, tokens.shape[0] // 16)
-    def norm_rows(i):
-        at = sixteen(i)
-        values = tokens[at, :].astype(f32) + (
-            own[at, :] + from_x[at, :].astype(f32) + from_y[at, :].astype(f32)
-        )
-        middle[at, :] = values
-        inverse = lax.rsqrt(jnp.mean(values * values, axis=-1, keepdims=True) + epsilon)
-        normed[at, :] = (values * inverse * gain[...]).astype(bf16)
+    for i in range(2):
+
+        @pl.loop(0, tokens.shape[0] // 32)
+        def norm_rows(j):
+            at, values = total(i, j)
+            values = tokens[at, :].astype(f32) + values
+            middle[at, :] = values
+            inverse = lax.rsqrt(jnp.mean(values * values, axis=-1, keepdims=True) + epsilon)
+            normed[at, :] = (values * inverse * gain[...]).astype(bf16)
 
     for step in gather_steps(normed, whole, send, recv, local, 0):
         step()
-
-
-def middle_of(mixed, rows_all, tokens, gain, collective_id):
+    to_sibling.wait()
+
+
+def middle_of(mixed, rows_all, tokens, gain, cot, collective_id):
     rows, width = tokens.shape
     channels = mixed.shape[2]
     f32, bf16 = jnp.float32, jnp.bfloat16
@@ -662,22 +665,23 @@
         out_shape=[
             jax.ShapeDtypeStruct((rows, width), f32),
             jax.ShapeDtypeStruct((CHIPS, rows, width), bf16),
+            jax.ShapeDtypeStruct(cot.shape, cot.dtype),
         ],
-        in_specs=[VMEM, ANY, VMEM, VMEM],
-        out_specs=[VMEM, ANY],
+        in_specs=[VMEM, ANY, VMEM, VMEM, ANY],
+        out_specs=[VMEM, ANY, ANY],
         scratch_shapes=[
             pltpu.VMEM((rows, width), bf16),
             pltpu.VMEM((channels, width), bf16),
-            pltpu.SemaphoreType.DMA((4,)),
-            pltpu.SemaphoreType.DMA((4,)),
+            pltpu.SemaphoreType.DMA((5,)),
+            pltpu.SemaphoreType.DMA((5,)),
             pltpu.SemaphoreType.DMA,
             pltpu.SemaphoreType.DMA((rows_all.shape[0],)),
-            *computed_scratch(rows, width),
+            *computed_scratch(rows, width, f32),
         ],
         compiler_params=comm_params(collective_id, 60),
         cost_estimate=lasting(75),
         name="middle",
-    )(mixed, rows_all, tokens, gain[None])
+    )(mixed, rows_all, tokens, gain[None], cot)
 
 
 def feed_forward_kernel(
@@ -690,20 +694,10 @@
 ):
     last = piece == 1
     if last:
-        (
-            earlier_weights,
-            earlier_low,
-            hidden,
-            grad,
-            parts,
-            low,
-            earlier_here,
-            earlier_low_here,
-            *refs,
-        ) = refs
+        earlier, hidden, grad, parts, earlier_here, *refs = refs
     else:
-        hidden, grad, low, *refs = refs
-    two_here, two_there, cot_here, weights_here, down_here, low_there, send, recv, loads, down_loads = refs
+        hidden, grad, parts, *refs = refs
+    low, two_here, two_there, cot_here, weights_here, down_here, low_there, send, recv, loads, down_loads = refs
     me, z, p, c, x, y = place()
     sibling = me + 1 - 2 * c
     greet((sibling,))
@@ -717,7 +711,7 @@
         (cot, cot_here),
     ]
     if last:
-        pairs += [(earlier_weights, earlier_here), (earlier_low, earlier_low_here)]
+        pairs.append((earlier, earlier_here))
     fetched = [pltpu.make_async_copy(a, b, loads.at[k]) for k, (a, b) in enumerate(pairs)]
     count = down_loads.shape[0]
     fetched[3:3] = fetch_rows(down, count * piece, down.shape[1] - units // count, down_here, down_loads)
@@ -761,21 +755,20 @@
                 remote(low.at[:, columns], low_there.at[:, columns], send.at[sems], recv.at[sems], sibling)
             )
             low_swaps[-1].start()
-    if last:
-        for copy in fetched[3 + count :]:
-            copy.wait()
-
-        @pl.loop(0, tokens // block)
-        def parts_block(j):
-            at = pl.ds(pl.multiple_of(j * block, block), block)
-
-            @pl.loop(0, width // block)
-            def parts_tile(k):
-                columns = pl.ds(pl.multiple_of(k * block, block), block)
-                parts[at, columns] = (
-                    dot_t(earlier_low_here[at, :], earlier_here[columns, :])
-                    + dot_t(low[at, :], weights_here[columns, :])
-                ).astype(bf16)
+    for copy in fetched[3 + count :]:
+        copy.wait()
+
+    @pl.loop(0, tokens // block)
+    def parts_block(j):
+        at = pl.ds(pl.multiple_of(j * block, block), block)
+
+        @pl.loop(0, width // block)
+        def parts_tile(k):
+            columns = pl.ds(pl.multiple_of(k * block, block), block)
+            values = dot_t(low[at, :], weights_here[columns, :])
+            if last:
+                values = values + earlier_here[at, columns]
+            parts[at, columns] = values.astype(parts.dtype)
 
     two_swap.wait()
     for copy in low_swaps:
@@ -806,9 +799,9 @@
     scratch = []
     if earlier:
         out_shape.append(jax.ShapeDtypeStruct((tokens, width), bf16))
-        scratch = [low, pltpu.VMEM(weights.shape, bf16), low]
+        scratch = [pltpu.VMEM((tokens, width), jnp.float32)]
     else:
-        out_shape.append(jax.ShapeDtypeStruct((tokens, 2 * units), bf16))
+        out_shape.append(jax.ShapeDtypeStruct((tokens, width), jnp.float32))
     swaps = 1 + 2 * (units // 256)
     return pl.pallas_call(
         functools.partial(feed_forward_kernel, piece),
@@ -817,6 +810,7 @@
         out_specs=[VMEM] * 3,
         scratch_shapes=[
             *scratch,
+            low,
             pltpu.VMEM((tokens, width), bf16),
             pltpu.VMEM((tokens, width // 2), bf16),
             pltpu.VMEM((tokens, width), bf16),
@@ -851,12 +845,19 @@
     down,
     cot_all,
     cot_other,
+    mixed_zero,
+    mixed_one,
     grad_middle,
     grad_gain,
     whole,
-    down_grad,
+    row_grads,
     down_parts,
     branch,
+    branch_all,
+    branch_other,
+    mixed_here,
+    mixed_there,
+    out_sum,
     hidden_here,
     hidden_other,
     down_here,
@@ -874,14 +875,20 @@
     begin()
     half = hidden_zero.shape[1]
     swaps = [remote(hidden, hidden_other, send.at[4], recv.at[4], sibling) for hidden in (hidden_one, hidden_zero)]
+    mixed_swaps = [remote(mixed, mixed_there, send.at[9], recv.at[9], sibling) for mixed in (mixed_one, mixed_zero)]
+    mixed_loads = [pltpu.make_async_copy(mixed, mixed_here, loads.at[4]) for mixed in (mixed_zero, mixed_one)]
 
     @pl.when(c == 0)
     def send_one():
         swaps[0].start()
+        mixed_swaps[0].start()
+        mixed_loads[0].start()
 
     @pl.when(c == 1)
     def send_zero():
         swaps[1].start()
+        mixed_swaps[1].start()
+        mixed_loads[1].start()
 
     fetched = [
         pltpu.make_async_copy(source, target, loads.at[k])
@@ -903,7 +910,9 @@
     swaps[0].wait()
     tile = 256
 
-    planes, units = down_grad.shape[:2]
+    planes = row_grads.shape[0]
+    units = half // planes
+    above = row_grads.shape[1] - units
 
     def grad_tiles(m):
         rows_here = pl.ds(pl.multiple_of(c * half + m * tile, 128), tile)
@@ -922,7 +931,7 @@
             for j in range(planes):
                 start, stop = max(j * units, m * tile), min((j + 1) * units, (m + 1) * tile)
                 if start < stop:
-                    down_grad[j, start - j * units : stop - j * units, columns] = values[
+                    row_grads[j, above + start - j * units : above + stop - j * units, columns] = values[
                         start - m * tile : stop - m * tile
                     ]
 
@@ -943,9 +952,18 @@
 
     total = lax.fori_loop(0, rows // 16, norm_rows, jnp.zeros((8, width), f32))
     grad_gain[...] = jnp.sum(total, axis=0, keepdims=True)
-    begin, forward, end = gather_steps(branch, whole, send, recv, local, 0)
+    begin, forward, end = gather_steps(branch, branch_all, send, recv, local, 0)
+    (p_x, p_y, p_d) = plane_neighbours()[1]
+
+    def to_sibling(k, chip, source):
+        return remote(source, branch_other.at[chip], send.at[5 + k], recv.at[5 + k], sibling)
+
+    shares = [to_sibling(0, p, branch)] + [
+        to_sibling(1 + k, chip, branch_all.at[chip]) for k, chip in enumerate((p_x, p_y, p_d))
+    ]
     begin()
-    for copy in down_fetched:
+    shares[0].start()
+    for copy in down_fetched + [mixed_loads[0], mixed_swaps[0]]:
         copy.wait()
 
     def down_tiles(j):
@@ -959,11 +977,42 @@
             ).astype(bf16)
 
     pl.loop(0, CHIPS)(down_tiles)
+
+    def out_tiles(mixed, branches, chips, finish):
+        @pl.loop(0, width // (2 * tile))
+        def out_tile(k):
+            columns = pl.ds(pl.multiple_of(k * 2 * tile, 128), 2 * tile)
+            values = out_sum[:, columns]
+            for chip in chips:
+                values = values + lax.dot_general(
+                    mixed[pl.ds(pl.multiple_of(chip * rows, 16), rows), :],
+                    branches[chip, :, columns],
+                    (((0,), (0,)), ((), ())),
+                    preferred_element_type=f32,
+                )
+            if finish:
+                for j in range(planes):
+                    row_grads[j, 0:above, columns] = values[j * above : (j + 1) * above].astype(bf16)
+            else:
+                out_sum[:, columns] = values
+
     forward()
+    shares[1].start()
+    shares[2].start()
+    out_sum[...] = jnp.zeros_like(out_sum)
+    out_tiles(mixed_here, branch_all, (p_x, p_y), False)
     end()
-
-
-def grads_of_middle(parts, middle, cot, gain, hiddens, down, cot_all, cot_other, collective_id):
+    shares[3].start()
+    to_whole = pltpu.make_async_copy(branch_all, whole, local)
+    to_whole.start()
+    out_tiles(mixed_here, branch_all, (p, p_d), False)
+    for copy in shares:
+        copy.wait()
+    out_tiles(mixed_there, branch_other, range(CHIPS), True)
+    to_whole.wait()
+
+
+def grads_of_middle(parts, middle, cot, gain, hiddens, down, cots, mixeds, collective_id):
     rows, width = middle.shape
     tokens, units = hiddens[0].shape[0], 2 * hiddens[0].shape[1]
     f32, bf16 = jnp.float32, jnp.bfloat16
@@ -973,29 +1022,34 @@
             jax.ShapeDtypeStruct((rows, width), f32),
             jax.ShapeDtypeStruct((1, width), f32),
             jax.ShapeDtypeStruct((CHIPS, rows, width), bf16),
-            jax.ShapeDtypeStruct((down.shape[0] // 2, 2 * hiddens[0].shape[1] // down.shape[0], width), bf16),
+            jax.ShapeDtypeStruct((down.shape[0] // 2, down.shape[1], width), bf16),
             jax.ShapeDtypeStruct((CHIPS, rows, width), bf16),
         ],
-        in_specs=[ANY, VMEM, VMEM, VMEM] + [ANY] * 5,
+        in_specs=[ANY, VMEM, VMEM, VMEM] + [ANY] * 7,
         out_specs=[VMEM, VMEM, ANY, VMEM, VMEM],
         scratch_shapes=[
             pltpu.VMEM((rows, width), bf16),
+            pltpu.VMEM((CHIPS, rows, width), bf16),
+            pltpu.VMEM((CHIPS, rows, width), bf16),
+            pltpu.VMEM(mixeds[0].shape, bf16),
+            pltpu.VMEM(mixeds[0].shape, bf16),
+            pltpu.VMEM((mixeds[0].shape[1], width), f32),
             pltpu.VMEM((tokens, units), bf16),
             pltpu.VMEM((tokens, units // 2), bf16),
             pltpu.VMEM((units, width), bf16),
             pltpu.VMEM((tokens, width), bf16),
             pltpu.VMEM((tokens, width), bf16),
             *sum_scratch(rows, width, parts.dtype),
+            pltpu.SemaphoreType.DMA((10,)),
+            pltpu.SemaphoreType.DMA((10,)),
+            pltpu.SemaphoreType.DMA,
             pltpu.SemaphoreType.DMA((5,)),
-            pltpu.SemaphoreType.DMA((5,)),
-            pltpu.SemaphoreType.DMA,
-            pltpu.SemaphoreType.DMA((4,)),
             pltpu.SemaphoreType.DMA((down.shape[0],)),
         ],
         compiler_params=comm_params(collective_id, 60),
         cost_estimate=lasting(80),
         name="grads_of_middle",
-    )(parts, middle, cot, gain[None], *hiddens, down, cot_all, cot_other)
+    )(parts, middle, cot, gain[None], *hiddens, down, *cots, *mixeds)
 
 
 def closing_kernel(
@@ -1061,8 +1115,7 @@
             in_low[chip, rows_at, :], whole_in[columns, :], (((1,), (1,)), ((), ())), preferred_element_type=f32
         )
 
-    begin, forward, end = computed_sum(product, *sums)
-    own, from_x, from_y = sums[3], sums[6], sums[7]
+    begin, forward, end, part_of = computed_sum(product, *sums)
     begin()
     for ended in fetched + exchanges:
         ended.wait()
@@ -1101,9 +1154,8 @@
     rows, width = tokens.shape
     step = width // (8 * planes)
 
-    def norm_rows(i, total):
-        here = sixteen(i)
-        grad = own[here, :] + from_x[here, :].astype(f32) + from_y[here, :].astype(f32)
+    def norm_rows(i, j, total):
+        here, grad = part_of(i, j)
         given, terms = norm_back_rows(tokens[here, :].astype(f32), gain[...], grad, rest[here, :])
         for k in range(4 * planes):
             for e in range(2):
@@ -1112,7 +1164,9 @@
                 ]
         return total + terms[:8] + terms[8:]
 
-    total = lax.fori_loop(0, rows // 16, norm_rows, jnp.zeros((8, width), f32))
+    total = jnp.zeros((8, width), f32)
+    for i in range(2):
+        total = lax.fori_loop(0, rows // 32, functools.partial(norm_rows, i), total)
     total = jnp.sum(total, axis=0, keepdims=True)
     for j in range(planes):
         for q in range(CHIPS):
@@ -1176,7 +1230,7 @@
             pltpu.SemaphoreType.DMA((4,)),
             pltpu.SemaphoreType.DMA((3,)),
             pltpu.SemaphoreType.DMA((3,)),
-            *computed_scratch(rows, width),
+            *computed_scratch(rows, width, bf16),
         ],
         compiler_params=comm_params(collective_id, 60),
         cost_estimate=lasting(50),
@@ -1430,16 +1484,20 @@
     input_blocks,
     cot,
     piece,
+    normed,
     conv_out,
     conv_low,
     decay_pre,
     input_pre,
     states,
     mixed,
+    mixed_zero,
+    mixed_one,
     entering,
     halo,
     cot_all,
     swapped,
+    normed_other,
     cumulative,
     sibling_tails,
     below_tail,
@@ -1450,6 +1508,8 @@
     local,
     swap_send,
     swap_recv,
+    other_send,
+    other_recv,
 ):
     me, z, p, c, x, y = place()
     rows, channels = conv_input.shape[1:]
@@ -1457,6 +1517,15 @@
     greet(peers + [*plane_neighbours()[0]])
     cot_begin, cot_forward, cot_end = gather_steps(cot, cot_all, send, recv, local.at[0], 9)
     cot_begin()
+    half = normed.shape[1] // 2
+    other = remote(
+        normed.at[:, pl.ds(pl.multiple_of((1 - c) * half, 128), half)],
+        normed_other,
+        other_send,
+        other_recv,
+        me + 1 - 2 * c,
+    )
+    other.start()
     swaps = swap_copies(piece, swapped, swap_send, swap_recv, local.at[1])
     f32 = jnp.float32
     tail = pl.ds(rows - 16, 16)
@@ -1561,17 +1630,21 @@
             states[j, at, :] = state
             v = gate_pre[j, at, :]
             act = 0.5 * v * (1.0 + jnp.tanh(GELU_A * (v + GELU_B * (v * v * v))))
-            mixed[j, at, :] = (state * act).astype(jnp.bfloat16)
+            product = (state * act).astype(jnp.bfloat16)
+            mixed[j, at, :] = product
+            mixed_zero[j, at, :] = product[:, : channels // 2]
+            mixed_one[j, at, :] = product[:, channels // 2 :]
             return unused
 
         lax.fori_loop(0, rows // 16, state_tile, 0, unroll=2)
 
     cot_end()
+    other.wait()
     for copy in swaps:
         copy.wait()
 
 
-def recurrence(gate_pre, conv_input, masks, vectors, decay_blocks, input_blocks, cot, piece, collective_id):
+def recurrence(gate_pre, conv_input, masks, vectors, decay_blocks, input_blocks, cot, piece, normed, collective_id):
     planes = lax.axis_size("seq") // 8
     blocks, rows, channels = conv_input.shape
     f32, bf16 = jnp.float32, jnp.bfloat16
@@ -1589,13 +1662,15 @@
             out(f32),
             out(f32),
             out(bf16),
+            *[out(bf16, (CHIPS, rows, channels // 2))] * 2,
             out(f32, (CHIPS, channels)),
             out(f32, (CHIPS, 8, channels)),
             out(cot.dtype, (CHIPS,) + cot.shape),
             out(piece.dtype, piece.shape),
+            out(normed.dtype, (normed.shape[0], normed.shape[1] // 2)),
         ],
-        in_specs=[VMEM] * 6 + [ANY] * 2,
-        out_specs=[VMEM] * 8 + [ANY] * 2,
+        in_specs=[VMEM] * 6 + [ANY] * 3,
+        out_specs=[VMEM] * 10 + [ANY] * 3,
         scratch_shapes=[
             pltpu.VMEM(cube, f32),
             pltpu.VMEM((CHIPS, 16, channels), bf16),
@@ -1607,11 +1682,13 @@
             pltpu.SemaphoreType.DMA((2,)),
             pltpu.SemaphoreType.DMA((3,)),
             pltpu.SemaphoreType.DMA((3,)),
+            pltpu.SemaphoreType.DMA,
+            pltpu.SemaphoreType.DMA,
         ],
         compiler_params=comm_params(collective_id, 60),
         cost_estimate=lasting(46),
         name="recurrence",
-    )(gate_pre, conv_input, masks, vectors, decay_blocks, input_blocks, cot, piece)
+    )(gate_pre, conv_input, masks, vectors, decay_blocks, input_blocks, cot, piece, normed)
 
 
 def recurrence_back_kernel(
@@ -1929,6 +2006,83 @@
     )
 
 
+def input_grads_kernel(
+    normed, normed_other, low, grad, here, there, low_here, low_there, kept, send, recv, loads
+):
+    me, z, p, c, x, y = place()
+    sibling = me + 1 - 2 * c
+    greet((sibling,))
+    swap = remote(low, low_there, send, recv, sibling)
+    swap.start()
+    half, columns = grad.shape
+    fetched = [
+        pltpu.make_async_copy(source, target, loads.at[k])
+        for k, (source, target) in enumerate(
+            (
+                (normed.at[:, pl.ds(pl.multiple_of(c * half, 128), half)], here),
+                (low, low_here),
+                (normed_other, there),
+            )
+        )
+    ]
+    for copy in fetched:
+        copy.start()
+    for copy in fetched[:2]:
+        copy.wait()
+    block, tile = 512, 256
+
+    def products(left, right, keep):
+        @pl.loop(0, half // block)
+        def product_block(m):
+            at = pl.ds(pl.multiple_of(m * block, block), block)
+
+            @pl.loop(0, columns // tile)
+            def product_tile(k):
+                across = pl.ds(pl.multiple_of(k * tile, tile), tile)
+                keep(
+                    at,
+                    across,
+                    lax.dot_general(
+                        left[:, at], right[:, across], (((0,), (0,)), ((), ())), preferred_element_type=jnp.float32
+                    ),
+                )
+
+    def keep_first(at, across, values):
+        kept[at, across] = values
+
+    def keep_sum(at, across, values):
+        grad[at, across] = (kept[at, across] + values).astype(grad.dtype)
+
+    products(here, low_here, keep_first)
+    fetched[2].wait()
+    swap.wait()
+    products(there, low_there, keep_sum)
+
+
+def input_grads(normed, normed_other, low, collective_id):
+    tokens, width = normed.shape
+    columns = low.shape[1]
+    bf16 = low.dtype
+    return pl.pallas_call(
+        input_grads_kernel,
+        out_shape=jax.ShapeDtypeStruct((width // 2, columns), bf16),
+        in_specs=[ANY] * 3,
+        out_specs=VMEM,
+        scratch_shapes=[
+            pltpu.VMEM((tokens, width // 2), bf16),
+            pltpu.VMEM((tokens, width // 2), bf16),
+            pltpu.VMEM((tokens, columns), bf16),
+            pltpu.VMEM((tokens, columns), bf16),
+            pltpu.VMEM((width // 2, columns), jnp.float32),
+            pltpu.SemaphoreType.DMA,
+            pltpu.SemaphoreType.DMA,
+            pltpu.SemaphoreType.DMA((3,)),
+        ],
+        compiler_params=comm_params(collective_id, 60),
+        name="input_grads",
+    )(normed, normed_other, low)
+
+
 def regrouped_kernel(back, devices, *refs):
     count = len(refs) // 2
     for source, target in zip(refs[:count], refs[count:]):
@@ -2054,18 +2208,6 @@
             parts, "seq", scatter_dimension=0, tiled=True, axis_index_groups=line_groups(n)
         )
 
-    sibling = [(d, d + 1 - 2 * (d % 2)) for d in range(n)]
-
-    def halves(values, axis):
-        half = values.shape[axis] // 2
-        return (
-            lax.dynamic_slice_in_dim(values, c * half, half, axis),
-            lax.dynamic_slice_in_dim(values, (1 - c) * half, half, axis),
-        )
-
-    def exchanged(values):
-        return lax.ppermute(values, "seq", sibling)
-
     def product(left, right):
         return jnp.dot(left, right, preferred_element_type=f32)
 
@@ -2149,7 +2291,7 @@
     cube = (CHIPS, rows, channels)
     gate_pre = gate_pre.reshape(cube)
     conv_input = product(normed_all, whole_in[:, channels:]).astype(bf16).reshape(cube)
-    conv_out, conv_low, decay_pre, input_pre, states, mixed, entering, halo, cot_all, second_piece = recurrence(
+    conv_out, conv_low, decay_pre, input_pre, states, mixed, *mixeds, entering, halo, cot_all, second_piece, normed_other = recurrence(
         gate_pre,
         conv_input,
         masks,
@@ -2158,45 +2300,37 @@
         input_blocks,
         cot,
         mlp_pieces[1],
+        normed_all,
         6,
     )
     whole_mlp = [
         column_gather(part.reshape(CHIPS * rows_d, 2 * half_units)) for part in (first_piece, second_piece)
     ]
     cot_all = cot_all.reshape(CHIPS * rows, width)
-    middle, two_all = middle_of(mixed, rows_all, tokens, gain_two, 7)
-    mixed = mixed.reshape(CHIPS * rows, channels)
+    middle, two_all, cot_other = middle_of(mixed, rows_all, tokens, gain_two, cot_all, 7)
+    mixeds = [part.reshape(CHIPS * rows, channels // 2) for part in mixeds]
     two_all = two_all.reshape(CHIPS * rows, width)
 
-    cot_other = exchanged(cot_all)
-    hidden_zero, first_grad, first_low = feed_forward(0, two_all, cot_all, whole_mlp[0], rows_all, (), 8)
+    hidden_zero, first_grad, first_parts = feed_forward(0, two_all, cot_all, whole_mlp[0], rows_all, (), 8)
     hidden_one, second_grad, two_parts = feed_forward(
-        1, two_all, cot_all, whole_mlp[1], rows_all, (whole_mlp[0], first_low), 14
+        1, two_all, cot_all, whole_mlp[1], rows_all, (first_parts,), 14
     )
     piece_grads = [line_sum(first_grad), line_sum(second_grad)]
-    grad_middle, grad_mlp_gain, grad_branch, down_grad, down_parts = grads_of_middle(
+    grad_middle, grad_mlp_gain, grad_branch, row_grads, down_parts = grads_of_middle(
         two_parts.reshape(CHIPS, rows, width),
         middle,
         cot,
         gain_two,
         (hidden_zero, hidden_one),
         rows_all,
-        cot_all,
-        cot_other,
+        (cot_all, cot_other),
+        mixeds,
         9,
     )
-    branch_cube, grad_branch = grad_branch, grad_branch.reshape(CHIPS * rows, width)
-
-    mixed_own, mixed_other = halves(mixed, 1)
-    out_grad = weight_grad(mixed_own, grad_branch) + weight_grad(
-        exchanged(mixed_other), exchanged(grad_branch)
-    )
-    out_grad = out_grad.astype(bf16)
-    grad_out_proj = line_sum(out_grad)
-    grad_mlp_down = line_sum(down_grad.reshape(planes * rows_f, width))
-    branch_cube = behind(branch_cube, out_grad)
+    grad_rows = line_sum(row_grads.reshape(planes * (rows_r + rows_f), width))
+
     in_low, grad_decay_low, grad_input_low, sums, down_sum, first_swapped = recurrence_back(
-        branch_cube,
+        grad_branch,
         rows_all,
         gate_pre,
         conv_input,
@@ -2223,9 +2357,7 @@
         a.reshape(flat) for a in (conv_low, grad_decay_low, grad_input_low)
     )
 
-    normed_own, normed_other = halves(normed_all, 1)
-    in_grads = weight_grad(normed_own, in_low) + weight_grad(exchanged(normed_other), exchanged(in_low))
-    in_total = in_grads.astype(bf16)
+    in_total = input_grads(normed_all, normed_other, in_low, 15)
     in_grads = line_sum(in_total)
     low_cube = behind(low_cube, in_total)
     vector_parts = sums.reshape(CW + 4, 2, planes, rows_r).transpose(2, 1, 0, 3)
@@ -2253,8 +2385,9 @@
     )
     block_out = middle + behind(down_sum, grad_tokens)
     block_out, grad_out_proj, grad_mlp_down = regrouped_columns(
-        (block_out, *behind((grad_out_proj, grad_mlp_down), grad_tokens)), [bf16, f32, f32], True
-    )
+        (block_out, *behind((grad_rows[:rows_r], grad_rows[rows_r:]), grad_tokens)), [bf16, f32, f32], True
+    )
+    in_grads = behind(in_grads, grad_out_proj)
     in_out = plane_swap([in_grads.reshape(CHIPS, rows_d, 2 * channels)], 16)
     grad_gate_branch, grad_input_branch = from_chips(in_out, in_pairs, [lru_width] * 2)
     vector_grads = small_grads[: CW + 4, :rows_r]

time: 634 us -> 616 us (0.972)
  Pallas kernels: 516 us -> 547 us
  waiting for transfers between devices: 27.9 us -> 2.44 us
  matrix products: 31.4 us -> 12.6 us
    dot_general x4 -> x0, matrix products: 18.8 us -> none  [weight_grad(): return jnp.einsum('ta,tb->ab', left, right, preferred_element_type=f32)]
    all_gather x4, waiting for transfers between devices: 16 us -> 0.06 us  [column_gather(): lax.all_gather(block, 'seq', axis=0, tiled=True, axis_index_groups=groups)]
    pallas_call x0 -> x1, Pallas kernels: none -> 14.5 us  [input_grads(): pl.pallas_call(input_grads_kernel, out_shape=jax.ShapeDtypeStruct((width...]
    pallas_call x1, Pallas kernels: 81.5 us -> 91.9 us  [middle_of(): pl.pallas_call(middle_kernel, out_shape=[jax.ShapeDtypeStruct((rows, widt...]
  transfers between devices with their start and end apart: 14 -> 8, of which waited for: 3 -> 1; matrix products, arithmetic and copies ran while one was open for 9% -> 6% of each run, Pallas kernels for 78% -> 86%
where the time goes in v4:
time: 616 us; the launch traced here: 605 us
  Pallas kernels  547 us (89%)
  local copies, waits for them, and re-layouts  21.3 us (3%)
  between operations  15.4 us (2%)
  matrix products  12.6 us (2%)
  other arithmetic  6.3 us (1%)
    pallas_call x1, Pallas kernels, middle_of(): pl.pallas_call(middle_kernel, out_shape=[jax.ShapeDtypeStruct((rows, widt...  91.9 us
    pallas_call x1, Pallas kernels, grads_of_middle(): pl.pallas_call(grads_of_middle_kernel, out_shape=[jax.ShapeDtypeStruct((r...  85.1 us
    pallas_call x2, Pallas kernels, feed_forward(): pl.pallas_call(functools.partial(feed_forward_kernel, piece), out_shape=o...  75.4 us
    pallas_call x1, Pallas kernels, opening(): pl.pallas_call(functools.partial(opening_kernel, planes), out_shape=[jax....  63.4 us
    pallas_call x1, Pallas kernels, recurrence(): pl.pallas_call(functools.partial(recurrence_kernel, planes), out_shape=[o...  61.9 us
    pallas_call x1, Pallas kernels, closing(): pl.pallas_call(functools.partial(closing_kernel, planes), out_shape=[jax....  61 us
    pallas_call x1, Pallas kernels, recurrence_back(): pl.pallas_call(functools.partial(recurrence_back_kernel, planes), out_sha...  57.5 us
    pallas_call x2, Pallas kernels, plane_swap(): pl.pallas_call(functools.partial(plane_swap_kernel, count), out_shape=[ja...  22.9 us
  transfers between devices with their start and end apart: 8, of which 1 were waited for; matrix products, arithmetic and copies ran while one was open for 6% of the time, Pallas kernels for 86%

profile of v4, /device:TPU:0, one launch (start us, length us, event | category | flops | bytes accessed | tf_op | source)
XLA Modules:
  0.0 605.4 jit_solution(12864260919802978911)
XLA Ops:
  7.2 2.4 to_chips.2.refs_0_
  9.7 12.3 %plane_swap.2 = bf16[4,64,1280]{2,1,0:T(8,128)(2,1)} custom-call(bf16[4,64,1280]{2,1,0:T(8,128)(2,1)} %to_chips.2.refs_0_), custom_call_target="tpu_custom_call" | custom-call | flops 10000000000 | bytes 30000000 | tf_op jit(solution)/shard_map/plane_swap/pallas_call | solution.py:1263
  22.2 1.8 regrouped_columns.2
  24.0 1.0 copy-done.7
  25.0 1.0 copy-done.8
  26.0 1.1 pad_maximum_fusion
  27.3 1.2 concatenate.39.small
  28.5 2.9 to_chips.3
  31.4 0.7 pad_maximum_fusion.4.gates
  32.1 63.4 %opening.1 = (f32[8,4,16,128]{3,2,1,0:T(8,128)}, bf16[640,640]{1,0:T(8,128)(2,1)}, bf16[640,640]{1,0:T(8,128)(2,1)}, bf16[4,256,2048]{2,1,0:T(8,128)(2,1)}, bf16[4,64,1536]{2,1,0:T(8,128)(2,1)}) custom-call(f32[16,128]{1,0:T(8,128)} %concatenate.39.small, bf16[80,320]{1,0:T(8,128)(2,1)} %pad_maximum_fusion.4.gates, bf16[256,2048]{1,0:T(8,128)(2,1)} %copy-done.7, ...), custom_call_target="tpu_custom_call" | custom-call | flops 65000001536 | bytes 195000000 | tf_op jit(solution)/shard_map/opening/pallas_call | solution.py:1377
  95.7 0.9 constant_dynamic-slice_fusion.1
  96.6 0.9 slice.149
  98.1 0.6 copy-done.11
  98.8 1.0 copy.44
  100.0 8.1 %fusion.2.gate_pre = f32[4,256,640]{2,1,0:T(8,128)} fusion(bf16[4,256,2048]{2,1,0:T(8,128)(2,1)} %get-tuple-element.106, bf16[2048,1280]{1,0:T(8,128)(2,1)} %all-gather.5.cloned.1.call-done.whole_in), kind=kOutput, calls=%fused_computation.3 | convolution fusion | flops 2684354560 | bytes 9437184 | tf_op jit(solution)/shard_map/dot_general | solution.py:2212
  108.1 4.5 fusion.3
  112.6 61.9 %recurrence.1 = (f32[4,256,640]{2,1,0:T(8,128)}, bf16[4,256,640]{2,1,0:T(8,128)(2,1)}, f32[4,256,640]{2,1,0:T(8,128)}, f32[4,256,640]{2,1,0:T(8,128)}, f32[4,256...) custom-call(f32[4,256,640]{2,1,0:T(8,128)} %fusion.2.gate_pre, ...), custom_call_target="tpu_custom_call" | custom-call | flops 46000001024 | bytes 138000000 | tf_op jit(solution)/shard_map/recurrence/pallas_call | solution.py:1656
  174.5 0.2 reduce-scatter.5.cloned.1.call-start
  174.7 1.6 fusion.14
  176.4 0.7 broadcast_in_dim_reshape.7.gain
  177.1 91.9 %middle.1 = (f32[256,2048]{1,0:T(8,128)}, bf16[4,256,2048]{2,1,0:T(8,128)(2,1)}, bf16[1024,2048]{1,0:T(8,128)(2,1)}) custom-call(bf16[4,256,640]{2,1,0:T(8,128)(2,1)} %get-tuple-element.112.mixed, bf16[8,272,2048]{2,1,0:T(8,128)(2,1)} %bitcast.136, bf16[256,2048]{1,0:T(8,128)(2,1)} %copy-done.7, f32[1,2048]{1,0:T(1,128)} %broadcast_in_dim_reshape.7.gain, ...), custom_call_target="tpu_custom_call" | custom-call | flops 74999996416 | bytes 225000000 | tf_op jit(solution)/shard_map/middle/pallas_call | solution.py:663
  269.0 37.8 %feed_forward.2 = (bf16[1024,768]{1,0:T(8,128)(2,1)}, bf16[1024,1536]{1,0:T(8,128)(2,1)}, f32[1024,2048]{1,0:T(8,128)}) custom-call(bf16[1024,2048]{1,0:T(8,128)(2,1)} %bitcast.148, bf16[1024,2048]{1,0:T(8,128)(2,1)} %bitcast.145, bf16[2048,1536]{1,0:T(8,128)(2,1)} %all-gather.11.cloned.1.call-done.weights, bf16[8,272,2048]{2,1,0:T(8,128)(2,1)} %bitcast.137), custom_call_target="tpu_custom_call" | custom-call | flops 35000000512 | bytes 105000000 | tf_op jit(solution)/shard_map/feed_forward/pallas_call | solution.py:806
  306.9 0.3 reduce-scatter.7.cloned.1.call-start
  307.2 37.6 %feed_forward.3 = (bf16[1024,768]{1,0:T(8,128)(2,1)}, bf16[1024,1536]{1,0:T(8,128)(2,1)}, bf16[1024,2048]{1,0:T(8,128)(2,1)}) custom-call(bf16[1024,2048]{1,0:T(8,128)(2,1)} %bitcast.149, bf16[1024,2048]{1,0:T(8,128)(2,1)} %bitcast.146, bf16[2048,1536]{1,0:T(8,128)(2,1)} %all-gather.9.cloned.1.call-done.weights, bf16[8,272,2048]{2,1,0:T(8,128)(2,1)} %bitcast.138, ...), custom_call_target="tpu_custom_call" | custom-call | flops 35000000512 | bytes 105000000 | tf_op jit(solution)/shard_map/feed_forward/pallas_call | solution.py:806
  344.8 85.1 %grads_of_middle.1 = (f32[256,2048]{1,0:T(8,128)}, f32[1,2048]{1,0:T(1,128)}, bf16[4,256,2048]{2,1,0:T(8,128)(2,1)}, bf16[4,272,2048]{2,1,0:T(8,128)(2,1)}, bf16[4,256,2048]{2,1,0:T(8,128)(2,1)}) custom-call(bf16[4,256,2048]{2,1,0:T(8,128)(2,1)} %bitcast.150, f32[256,2048]{1,0:T(8,128)} %get-tuple-element.117.middle, bf16[256,2048]{1,0:T(8,128)(2,1)} %copy-done.8, ...), custom_call_target="tpu_custom_call" | custom-call | flops 80000000000 | bytes 240000000 | tf_op jit(solution)/shard_map/grads_of_middle/pallas_call | solution.py:1019
  430.2 0.4 copy-done.18
  430.7 0.7 broadcast_in_dim_reshape.8.gain
  431.5 0.7 copy.48
  432.2 0.5 broadcast.157
  432.7 0.7 reduce.11
  433.5 57.5 %recurrence_back.1 = (bf16[4,256,1280]{2,1,0:T(8,128)(2,1)}, bf16[4,256,640]{2,1,0:T(8,128)(2,1)}, bf16[4,256,640]{2,1,0:T(8,128)(2,1)}, f32[8,640]{1,0:T(8,128)...) custom-call(bf16[4,256,2048]{2,1,0:T(8,128)(2,1)} %get-tuple-element.128.grad_branch, ...), custom_call_target="tpu_custom_call" | custom-call | flops 57999998976 | bytes 174000000 | tf_op jit(solution)/shard_map/recurrence_back/pallas_call | solution.py:1954
  491.1 14.5 %input_grads.1 = bf16[1024,1280]{1,0:T(8,128)(2,1)} custom-call(bf16[1024,2048]{1,0:T(8,128)(2,1)} %bitcast.110, bf16[1024,1024]{1,0:T(8,128)(2,1)} %get-tuple-element.139.normed_other, bf16[1024,1280]{1,0:T(8,128)(2,1)} %bitcast.112), custom_call_target="tpu_custom_call" | custom-call | tf_op jit(solution)/shard_map/input_grads/pallas_call | solution.py:2066
  506.0 0.7 select_maximum_fusion.small
  506.7 61.0 %closing.1 = (f32[256,2048]{1,0:T(8,128)}, f32[24,128]{1,0:T(8,128)}, f32[80,320]{1,0:T(8,128)}, bf16[4,64,1536]{2,1,0:T(8,128)(2,1)}) custom-call(bf16[4,256,1280]{2,1,0:T(8,128)(2,1)} %get-tuple-element.140.in_low, bf16[2048,1280]{1,0:T(8,128)(2,1)} %all-gather.5.cloned.1.call-done.whole_in, bf16[256,2048]{1,0:T(8,128)(2,1)} %copy-done.7, ...), custom_call_target="tpu_custom_call" | custom-call | flops 49999998976 | bytes 150000000 | tf_op jit(solution)/shard_map/closing/pallas_call | solution.py:1206
  567.7 2.6 add.80.refs_0_
  570.3 1.3 slice.139
  571.6 1.9 from_chips.3
  573.5 1.2 slice_bitcast_fusion.2
  574.7 1.3 slice_bitcast_fusion.3
  576.1 0.7 fusion.15
  576.8 1.0 slice.156.refs_1_
  577.8 1.2 slice.157.refs_2_
  579.0 2.4 regrouped_columns.3
  581.4 2.2 reduce-scatter.11.cloned.1.call-done
  583.6 10.6 %plane_swap.3.refs_0_ = bf16[4,64,1280]{2,1,0:T(8,128)(2,1)} custom-call(bf16[4,64,1280]{2,1,0:T(8,128)(2,1)} %bitcast.143), custom_call_target="tpu_custom_call" | custom-call | flops 10000000000 | bytes 30000000 | tf_op jit(solution)/shard_map/plane_swap/pallas_call | solution.py:1263
  594.3 1.1 copy-done.5
  595.3 1.4 from_chips.2
  596.8 1.3 copy.64
  (129 shorter events, 2.0 us)
Async XLA Ops:
  7.2 92.8 %all-gather.5.cloned.1.call-start = ((), (), s32[]{:S(2)}) async-start(), calls=%async_computation.4 | async-start | bytes 5898240 | tf_op jit(solution)/shard_map/all_gather | solution.py:2204
  9.7 12.5 %copy-start = (bf16[256,2048]{1,0:T(8,128)(2,1)S(1)}, bf16[256,2048]{1,0:T(8,128)(2,1)}, u32[]{:S(2)}) copy-start(bf16[256,2048]{1,0:T(8,128)(2,1)} %refs_0_.4) | copy-start | bytes 3145732
  9.7 12.5 %copy-start.1 = (bf16[256,2048]{1,0:T(8,128)(2,1)S(1)}, bf16[256,2048]{1,0:T(8,128)(2,1)}, u32[]{:S(2)}) copy-start(bf16[256,2048]{1,0:T(8,128)(2,1)} %refs_1_.4) | copy-start | bytes 3145732
  9.7 12.5 %copy-start.4 = (bf16[192,2048]{1,0:T(8,128)(2,1)S(1)}, bf16[192,2048]{1,0:T(8,128)(2,1)}, u32[]{:S(2)}) copy-start(bf16[192,2048]{1,0:T(8,128)(2,1)} %refs_3_.1) | copy-start | bytes 2359300
  9.7 12.5 %copy-start.6 = (bf16[80,2048]{1,0:T(8,128)(2,1)S(1)}, bf16[80,2048]{1,0:T(8,128)(2,1)}, u32[]{:S(2)}) copy-start(bf16[80,2048]{1,0:T(8,128)(2,1)} %refs_2_.1) | copy-start | bytes 983044
  22.0 5.1 copy-start.28
  22.0 5.1 copy-start.29
  22.0 5.1 copy-start.30
  22.0 5.1 copy-start.31
  22.1 5.2 copy-start.32
  22.1 5.1 copy-start.33
  22.1 5.2 copy-start.26
  22.1 5.2 copy-start.27
  22.1 154.9 %all-gather.7.cloned.1.call-start = ((), (), s32[]{:S(2)}) async-start(), calls=%async_computation.5 | async-start | bytes 10027008 | tf_op jit(solution)/shard_map/all_gather | solution.py:2204
  24.0 1.0 copy-start.7
  25.0 1.0 copy-start.8
  25.9 5.5 copy-start.19
  26.0 5.5 copy-start.20
  27.1 241.9 %all-gather.11.cloned.1.call-start = ((), (), s32[]{:S(2)}) async-start(), calls=%async_computation.7 | async-start | bytes 7077888 | tf_op jit(solution)/shard_map/all_gather | solution.py:2204
  95.6 211.6 %all-gather.9.cloned.1.call-start = ((), (), s32[]{:S(2)}) async-start(), calls=%async_computation.6 | async-start | bytes 7077888 | tf_op jit(solution)/shard_map/all_gather | solution.py:2204
  97.7 10.4 %copy-start.22 = (f32[1,640]{1,0:T(1,128)}, f32[1,640]{1,0:T(1,128)S(1)}, u32[]{:S(2)}) copy-start(f32[1,640]{1,0:T(1,128)S(1)} %squeeze.36) | copy-start | bytes 7684
  97.9 10.2 %copy-start.15 = (f32[1,4,4,2,256]{4,3,2,1,0:T(2,128)}, f32[1,4,4,2,256]{4,3,2,1,0:T(2,128)S(1)}, u32[]{:S(2)}) copy-start(f32[1,4,4,2,256]{4,3,2,1,0:T(2,128)S(1)} %stack.8) | copy-start | bytes 98308
  98.1 0.6 copy-start.11
  98.1 0.6 copy-start.13
  99.9 8.2 %copy-start.24 = (f32[8,640]{1,0:T(8,128)}, f32[8,640]{1,0:T(8,128)S(1)}, u32[]{:S(2)}) copy-start(f32[8,640]{1,0:T(8,128)S(1)} %scatter.4.vectors) | copy-start | bytes 61444
  100.0 8.2 %copy-start.9 = (bf16[4,256,2048]{2,1,0:T(8,128)(2,1)S(1)}, bf16[4,256,2048]{2,1,0:T(8,128)(2,1)}, u32[]{:S(2)}) copy-start(bf16[4,256,2048]{2,1,0:T(8,128)(2,1)} %get-tuple-element.106) | copy-start | bytes 12582916
  100.0 8.2 %copy-start.34 = (bf16[2048,1280]{1,0:T(8,128)(2,1)S(1)}, bf16[2048,1280]{1,0:T(8,128)(2,1)}, u32[]{:S(2)}) copy-start(bf16[2048,1280]{1,0:T(8,128)(2,1)} %all-gather.5.cloned.1.call-done.whole_in) | copy-start | bytes 15728644
  174.5 259.0 %reduce-scatter.5.cloned.1.call-start = ((), (), s32[]{:S(2)}) async-start(), calls=%async_computation.8 | async-start | bytes 3932160 | tf_op jit(solution)/shard_map/reduce_scatter | solution.py:2207
  306.9 199.8 %reduce-scatter.7.cloned.1.call-start = ((), (), s32[]{:S(2)}) async-start(), calls=%async_computation.9 | async-start | bytes 3932160 | tf_op jit(solution)/shard_map/reduce_scatter | solution.py:2207
  344.8 232.0 %reduce-scatter.9.cloned.1.call-start = ((), (), s32[]{:S(2)}) async-start(), calls=%async_computation.10 | async-start | bytes 5570560 | tf_op jit(solution)/shard_map/reduce_scatter | solution.py:2207
  429.9 0.7 copy-start.18
  429.9 1.4 copy-start.12
  429.9 1.4 copy-start.14
  430.0 1.4 copy-start.16
  430.0 2.7 copy-start.25
  430.0 153.6 %reduce-scatter.11.cloned.1.call-start = ((), (), s32[]{:S(2)}) async-start(), calls=%async_computation.11 | async-start | bytes 3276800 | tf_op jit(solution)/shard_map/reduce_scatter | solution.py:2207
  491.0 14.6 %copy-start.21 = (f32[8,640]{1,0:T(8,128)S(1)}, f32[8,640]{1,0:T(8,128)}, u32[]{:S(2)}) copy-start(f32[8,640]{1,0:T(8,128)} %get-tuple-element.142) | copy-start | bytes 61444
  491.1 14.6 %copy-start.23 = (f32[1,640]{1,0:T(1,128)S(1)}, f32[1,640]{1,0:T(1,128)}, u32[]{:S(2)}) copy-start(f32[1,640]{1,0:T(1,128)} %copy-done.22) | copy-start | bytes 7684
  567.7 3.9 copy-start.2
  567.7 3.9 copy-start.3
  567.7 8.4 %copy-start.17 = (f32[80,320]{1,0:T(8,128)S(1)}, f32[80,320]{1,0:T(8,128)}, u32[]{:S(2)}) copy-start(f32[80,320]{1,0:T(8,128)} %get-tuple-element.159) | copy-start | bytes 307204
  583.6 13.2 %copy-start.10 = (f32[256,2048]{1,0:T(8,128)S(1)}, f32[256,2048]{1,0:T(8,128)}, u32[]{:S(2)}) copy-start(f32[256,2048]{1,0:T(8,128)} %get-tuple-element.210) | copy-start | bytes 6291460
  594.2 1.1 copy-start.5
Sparse Core Ops, SparseCore 0:
  22.1 63.0 all-gather.4
  87.4 88.5 all-gather.6
  177.5 63.4 all-gather.10
  242.4 63.2 all-gather.8
  307.9 58.8 reduce-scatter.4
  369.0 60.2 reduce-scatter.6
  431.6 83.9 reduce-scatter.8
  517.9 65.6 reduce-scatter.10

commit v5 on v4

--- a/solution.py
+++ b/solution.py
@@ -1022,7 +1022,9 @@
             jax.ShapeDtypeStruct((rows, width), f32),
             jax.ShapeDtypeStruct((1, width), f32),
             jax.ShapeDtypeStruct((CHIPS, rows, width), bf16),
-            jax.ShapeDtypeStruct((down.shape[0] // 2, down.shape[1], width), bf16),
+            jax.ShapeDtypeStruct(
+                (down.shape[0] // 2, down.shape[1], width), bf16
+            ),
             jax.ShapeDtypeStruct((CHIPS, rows, width), bf16),
         ],
         in_specs=[ANY, VMEM, VMEM, VMEM] + [ANY] * 7,
@@ -1060,6 +1062,7 @@
     gain,
     rest,
     small,
+    mlp_gain,
     conv_low,
     decay_low,
     input_low,
@@ -1079,11 +1082,12 @@
     gate_lines,
     lines,
     line,
-    near_parts,
+    near_part,
     gains,
     gain_lines,
     gain_line,
     gain_near,
+    gain_sum,
     send,
     recv,
     loads,
@@ -1133,7 +1137,7 @@
             for e in range(2):
                 gates[j, :, (2 * k + e) * block : (2 * k + e + 1) * block] = full[
                     rows_at, e * count + j * block : e * count + (j + 1) * block
-                ]
+                ].astype(gates.dtype)
     gate_far = [copy(at + d, gates.at[there], gate_lines.at[d], device) for d, (there, device) in enumerate(far)]
     at += len(far)
     for sent in gate_far:
@@ -1144,12 +1148,9 @@
     for sent in small_far:
         sent.wait()
     line[...] = small[z] + sum(lines[d] for d in range(planes - 1))
-    small_near = [
-        copy(at + d, line.at[there], near_parts.at[d], device) for d, (there, device) in enumerate(near)
-    ]
-    at += len(near)
-    for sent in small_near:
-        sent.start()
+    small_near = copy(at, line.at[1 - c], near_part, me + 1 - 2 * c)
+    small_near.start()
+    at += 1
     end()
     rows, width = tokens.shape
     step = width // (8 * planes)
@@ -1172,7 +1173,8 @@
         for q in range(CHIPS):
             for e in range(2):
                 start = ((e * planes + j) * CHIPS + q) * step
-                gains[j, 2 * q + e, 0:1, 0:step] = total[:, start : start + step]
+                gains[j, 2 * q + e : 2 * q + e + 1, 0:step] = total[:, start : start + step]
+                gains[j, 2 * q + e : 2 * q + e + 1, step : 2 * step] = mlp_gain[:, start : start + step]
     gain_far = [copy(at + d, gains.at[there], gain_lines.at[d], device) for d, (there, device) in enumerate(far)]
     at += len(far)
     for sent in gain_far:
@@ -1180,51 +1182,51 @@
     for sent in gain_far:
         sent.wait()
     gain_line[...] = gains[z] + sum(gain_lines[d] for d in range(planes - 1))
-    last = [
-        copy(at + d, gain_line.at[there], gain_near.at[d], device) for d, (there, device) in enumerate(near)
-    ]
+    last = [copy(at + d, gain_line, gain_near.at[d], device) for d, (there, device) in enumerate(near)]
     for sent in last:
         sent.start()
-    for sent in small_near + gate_far + swaps:
+    for sent in gate_far + swaps + [small_near]:
         sent.wait()
-    gates_out[...] = gates[z] + sum(gate_lines[d] for d in range(planes - 1))
+    gates_out[...] = gates[z].astype(f32) + sum(gate_lines[d].astype(f32) for d in range(planes - 1))
     for sent in last:
         sent.wait()
     rows_small = line.shape[1]
-    small_out[0:rows_small, :] = line[r] + sum(near_parts[d] for d in range(7))
-    small_out[rows_small : rows_small + 8, :] = gain_line[r] + sum(gain_near[d] for d in range(7))
-
-
-def closing(in_low, whole_in, tokens, gain, rest, small, lows, piece, head, collective_id):
+    small_out[0:rows_small, :] = line[c] + near_part[...]
+    gain_sum[...] = gain_line[...] + sum(gain_near[d] for d in range(7))
+    small_out[rows_small : rows_small + 1, :] = gain_sum[pl.ds(r, 1), :]
+
+
+def closing(in_low, whole_in, tokens, gain, rest, small, mlp_gain, lows, piece, head, collective_id):
     planes = lax.axis_size("seq") // 8
     rows, width = tokens.shape
     f32, bf16 = jnp.float32, jnp.bfloat16
     rows_small, lanes = small.shape[2:]
     channels = lows[0].shape[1]
     block = channels // (2 * planes)
-    count = 3 + 3 * (planes - 1) + 14
+    count = 3 + 3 * (planes - 1) + 8
     return pl.pallas_call(
         functools.partial(closing_kernel, planes),
         out_shape=[
             jax.ShapeDtypeStruct((rows, width), f32),
-            jax.ShapeDtypeStruct((rows_small + 8, lanes), f32),
+            jax.ShapeDtypeStruct((rows_small + 1, lanes), f32),
             jax.ShapeDtypeStruct((block, 2 * head), f32),
             jax.ShapeDtypeStruct(piece.shape, bf16),
         ],
-        in_specs=[VMEM] * 6 + [ANY] * 4,
+        in_specs=[VMEM] * 7 + [ANY] * 4,
         out_specs=[VMEM] * 3 + [ANY],
         scratch_shapes=[
             *[pltpu.VMEM(lows[0].shape, bf16)] * 6,
             pltpu.VMEM((channels, channels), f32),
-            pltpu.VMEM((planes, block, 2 * head), f32),
-            pltpu.VMEM((planes - 1, block, 2 * head), f32),
-            pltpu.VMEM((planes - 1, 8, rows_small, lanes), f32),
-            pltpu.VMEM((8, rows_small, lanes), f32),
-            pltpu.VMEM((7, rows_small, lanes), f32),
-            pltpu.VMEM((planes, 8, 8, lanes), f32),
-            pltpu.VMEM((planes - 1, 8, 8, lanes), f32),
-            pltpu.VMEM((8, 8, lanes), f32),
+            pltpu.VMEM((planes, block, 2 * head), bf16),
+            pltpu.VMEM((planes - 1, block, 2 * head), bf16),
+            pltpu.VMEM((planes - 1, 2, rows_small, lanes), f32),
+            pltpu.VMEM((2, rows_small, lanes), f32),
+            pltpu.VMEM((rows_small, lanes), f32),
+            pltpu.VMEM((planes, 8, lanes), f32),
+            pltpu.VMEM((planes - 1, 8, lanes), f32),
+            pltpu.VMEM((8, lanes), f32),
             pltpu.VMEM((7, 8, lanes), f32),
+            pltpu.VMEM((8, lanes), f32),
             pltpu.SemaphoreType.DMA((count,)),
             pltpu.SemaphoreType.DMA((count,)),
             pltpu.SemaphoreType.DMA((4,)),
@@ -1235,7 +1237,38 @@
         compiler_params=comm_params(collective_id, 60),
         cost_estimate=lasting(50),
         name="closing",
-    )(in_low, whole_in, tokens, gain[None], rest, small, *lows, piece)
+    )(in_low, whole_in, tokens, gain[None], rest, small, mlp_gain, *lows, piece)
+
+
+def first_swap_kernel(planes, pairs, *refs):
+    count = len(pairs)
+    ins, (out, parts, send, recv, local) = refs[:count], refs[count:]
+    to_chips_kernel(planes, pairs, *ins, parts)
+    greet(plane_neighbours()[0])
+    copies = swap_copies(parts, out, send, recv, local)
+    for copy in copies:
+        copy.start()
+    for copy in copies:
+        copy.wait()
+
+
+def first_swap(weights, pairs, width, collective_id):
+    planes = lax.axis_size("seq") // 8
+    shape = (CHIPS, weights[0].shape[0], width)
+    return pl.pallas_call(
+        functools.partial(first_swap_kernel, planes, pairs),
+        out_shape=jax.ShapeDtypeStruct(shape, weights[0].dtype),
+        in_specs=[VMEM] * len(weights),
+        out_specs=ANY,
+        scratch_shapes=[
+            pltpu.VMEM(shape, weights[0].dtype),
+            pltpu.SemaphoreType.DMA((3,)),
+            pltpu.SemaphoreType.DMA((3,)),
+            pltpu.SemaphoreType.DMA,
+        ],
+        compiler_params=comm_params(collective_id, 60),
+        name="first_swap",
+    )(*weights)
 
 
 def plane_swap_kernel(count, *refs):
@@ -1270,7 +1303,7 @@
             pltpu.SemaphoreType.DMA((count, 3)),
             pltpu.SemaphoreType.DMA((count,)),
         ],
-        compiler_params=comm_params(collective_id),
+        compiler_params=comm_params(collective_id, 60),
         cost_estimate=lasting(10),
         name="plane_swap",
     )(*arrays)
@@ -1287,15 +1320,19 @@
 
 def opening_kernel(
     planes,
+    pairs,
     small,
     gates,
     tokens,
-    piece,
+    mlp_gate,
+    mlp_up,
     gathered,
     decay_blocks,
     input_blocks,
+    second_piece,
     whole,
     swapped,
+    piece,
     gates_all,
     gain,
     normed,
@@ -1317,6 +1354,7 @@
         copy.start()
     gathered[r, z] = small[...]
     gates_all[c, z] = gates[...]
+    to_chips_kernel(planes, pairs, mlp_gate, mlp_up, piece, second_piece)
     for copy in lines:
         copy.wait()
     spreads = [
@@ -1370,22 +1408,25 @@
         copy.wait()
 
 
-def opening(small, gates, tokens, piece, collective_id):
+def opening(small, gates, tokens, mlp_gate, mlp_up, pairs, collective_id):
     planes = lax.axis_size("seq") // 8
     rows, width = tokens.shape
     channels = 2 * planes * gates.shape[0]
+    piece = (CHIPS, mlp_gate.shape[0], mlp_gate.shape[1] // CHIPS)
     return pl.pallas_call(
-        functools.partial(opening_kernel, planes),
+        functools.partial(opening_kernel, planes, pairs),
         out_shape=[
             jax.ShapeDtypeStruct((8, planes) + small.shape, small.dtype),
             jax.ShapeDtypeStruct((channels, channels), gates.dtype),
             jax.ShapeDtypeStruct((channels, channels), gates.dtype),
+            jax.ShapeDtypeStruct(piece, mlp_gate.dtype),
             jax.ShapeDtypeStruct((CHIPS, rows, width), jnp.bfloat16),
-            jax.ShapeDtypeStruct(piece.shape, piece.dtype),
+            jax.ShapeDtypeStruct(piece, mlp_gate.dtype),
         ],
-        in_specs=[VMEM, VMEM, VMEM, ANY],
-        out_specs=[VMEM, VMEM, VMEM, ANY, ANY],
+        in_specs=[VMEM] * 5,
+        out_specs=[VMEM] * 4 + [ANY, ANY],
         scratch_shapes=[
+            pltpu.VMEM(piece, mlp_gate.dtype),
             pltpu.VMEM((2, planes) + gates.shape, gates.dtype),
             pltpu.VMEM((8, width), jnp.float32),
             pltpu.VMEM((rows, width), jnp.bfloat16),
@@ -1403,7 +1444,7 @@
         compiler_params=comm_params(collective_id, 60),
         cost_estimate=lasting(65),
         name="opening",
-    )(small, gates, tokens, piece)
+    )(small, gates, tokens, mlp_gate, mlp_up)
 
 
 def column_peers(planes, z, p, c):
@@ -1708,13 +1749,14 @@
     vectors,
     decay_blocks,
     input_blocks,
+    middle,
     down_parts,
     piece,
     in_low,
     decay_low,
     input_low,
     sums,
-    down_sum,
+    block_out,
     swapped,
     grad_mixed,
     branch_here,
@@ -1921,7 +1963,9 @@
     @pl.loop(0, own.shape[0] // 16)
     def sum_rows(i):
         at = sixteen(i)
-        down_sum[at, :] = own[at, :].astype(f32) + from_x[at, :].astype(f32) + from_y[at, :].astype(f32)
+        block_out[at, :] = middle[at, :] + (
+            own[at, :].astype(f32) + from_x[at, :].astype(f32) + from_y[at, :].astype(f32)
+        )
 
     for copy in swaps:
         copy.wait()
@@ -1943,6 +1987,7 @@
     vectors,
     decay_blocks,
     input_blocks,
+    middle,
     down_parts,
     piece,
     collective_id,
@@ -1961,7 +2006,7 @@
             jax.ShapeDtypeStruct(down_parts.shape[1:], f32),
             jax.ShapeDtypeStruct(piece.shape, bf16),
         ],
-        in_specs=[ANY] * 2 + [VMEM] * 13 + [ANY] * 2,
+        in_specs=[ANY] * 2 + [VMEM] * 14 + [ANY] * 2,
         out_specs=[VMEM] * 5 + [ANY],
         scratch_shapes=[
             pltpu.VMEM(cube, f32),
@@ -2001,6 +2046,7 @@
         vectors,
         decay_blocks,
         input_blocks,
+        middle,
         down_parts,
         piece,
     )
@@ -2083,25 +2129,29 @@
     )(normed, normed_other, low)
 
 
-def regrouped_kernel(back, devices, *refs):
-    count = len(refs) // 2
-    for source, target in zip(refs[:count], refs[count:]):
+def regrouped_kernel(back, devices, places, *refs):
+    count = 1 + max(place[0] for place in places)
+    for source, first, rows, target, row in places:
+        source, target = refs[source], refs[count + target]
         step = source.shape[1] // devices
         for k in range(devices // 2):
             for e in range(2):
                 split, joined = (2 * k + e) * step, (devices // 2 * e + k) * step
                 start, end = (joined, split) if back else (split, joined)
-                target[:, end : end + step] = source[:, start : start + step].astype(target.dtype)
-
-
-def regrouped_columns(arrays, dtypes, back):
+                target[row : row + rows, end : end + step] = source[
+                    first : first + rows, start : start + step
+                ].astype(target.dtype)
+
+
+def regrouped_columns(arrays, places, dtypes, back, vmem_mib):
     devices = lax.axis_size("seq")
+    sizes = [max(row + rows for unused, unused, rows, m, row in places if m == k) for k in range(len(dtypes))]
     return pl.pallas_call(
-        functools.partial(regrouped_kernel, back, devices),
-        out_shape=[jax.ShapeDtypeStruct(a.shape, dtype) for a, dtype in zip(arrays, dtypes)],
+        functools.partial(regrouped_kernel, back, devices, places),
+        out_shape=[jax.ShapeDtypeStruct((r, arrays[0].shape[1]), dtype) for r, dtype in zip(sizes, dtypes)],
         in_specs=[VMEM] * len(arrays),
-        out_specs=[VMEM] * len(arrays),
-        compiler_params=pltpu.CompilerParams(vmem_limit_bytes=24 * 2**20),
+        out_specs=[VMEM] * len(dtypes),
+        compiler_params=pltpu.CompilerParams(vmem_limit_bytes=vmem_mib * 2**20),
         name="regrouped_columns",
     )(*arrays)
 
@@ -2116,19 +2166,6 @@
                     k, at = targets[c]
                     start = ((z * CHIPS + p) * 2 + c) * width
                     outs[k][p, :, at + z * width : at + (z + 1) * width] = source[:, start : start + width]
-
-
-def to_chips(weights, pairs, widths):
-    planes = lax.axis_size("seq") // 8
-    return pl.pallas_call(
-        functools.partial(to_chips_kernel, planes, pairs),
-        out_shape=[
-            jax.ShapeDtypeStruct((CHIPS, weights[0].shape[0], width), weights[0].dtype) for width in widths
-        ],
-        in_specs=[VMEM] * len(weights),
-        out_specs=[VMEM] * len(widths),
-        name="to_chips",
-    )(*weights)
 
 
 def from_chips_kernel(planes, pairs, *refs):
@@ -2238,17 +2275,19 @@
     )
     half = channels // 2
     in_pairs = (((0, 0), (0, half)), ((0, channels), (0, channels + half)))
-    (weights_in,) = to_chips([gate_branch, input_branch], in_pairs, [2 * channels])
-    (swapped_in,) = plane_swap([weights_in], 2)
+    swapped_in = first_swap([gate_branch, input_branch], in_pairs, 2 * channels, 2)
     whole_in = column_gather(swapped_in.reshape(CHIPS * rows_d, 2 * channels))
-    tokens, cot, out_proj, mlp_down = regrouped_columns(
-        [tokens, cotangent, out_proj, mlp_down], [bf16] * 4, False
+    tokens, cot, row_shards = regrouped_columns(
+        [tokens, cotangent, out_proj, mlp_down],
+        [(0, 0, rows, 0, 0), (1, 0, rows, 1, 0), (2, 0, rows_r, 2, 0), (3, 0, rows_f, 2, rows_r)],
+        [bf16] * 3,
+        False,
+        60,
     )
     mlp_pairs = (((0, 0), (1, 0)), ((0, half_units), (1, half_units)))
-    mlp_pieces = to_chips([mlp_gate, mlp_up], mlp_pairs, [2 * half_units] * 2)
     gates = jnp.concatenate([decay_gate, input_gate], axis=1)
-    small, decay_blocks, input_blocks, normed_all, first_piece = opening(
-        behind(small, swapped_in), gates, tokens, mlp_pieces[0], 1
+    small, decay_blocks, input_blocks, second_part, normed_all, first_piece = opening(
+        behind(small, swapped_in), gates, tokens, mlp_gate, mlp_up, mlp_pairs, 1
     )
     normed_all = normed_all.reshape(CHIPS * rows, width)
     small = small.transpose(1, 0, 2, 3)
@@ -2284,8 +2323,7 @@
     masks_all = jnp.concatenate([all_flags.reshape(1, planes, CHIPS, 2, rows), masks_all[1:]], axis=0)
     masks = own_blocks(masks_all).transpose(1, 2, 0)
 
-    rows_all = column_gather(behind(jnp.concatenate([out_proj, mlp_down], axis=0), swapped_in))
-    rows_all = rows_all.reshape(2 * planes, rows_r + rows_f, width)
+    rows_all = column_gather(behind(row_shards, swapped_in)).reshape(2 * planes, rows_r + rows_f, width)
 
     gate_pre = product(normed_all, whole_in[:, :channels])
     cube = (CHIPS, rows, channels)
@@ -2299,7 +2337,7 @@
         decay_blocks,
         input_blocks,
         cot,
-        mlp_pieces[1],
+        second_part,
         normed_all,
         6,
     )
@@ -2329,7 +2367,7 @@
     )
     grad_rows = line_sum(row_grads.reshape(planes * (rows_r + rows_f), width))
 
-    in_low, grad_decay_low, grad_input_low, sums, down_sum, first_swapped = recurrence_back(
+    in_low, grad_decay_low, grad_input_low, sums, block_out, first_swapped = recurrence_back(
         grad_branch,
         rows_all,
         gate_pre,
@@ -2345,6 +2383,7 @@
         vectors,
         decay_blocks,
         input_blocks,
+        middle,
         down_parts,
         piece_grads[0].reshape(CHIPS, rows_d, 2 * half_units),
         12,
@@ -2362,19 +2401,14 @@
     low_cube = behind(low_cube, in_total)
     vector_parts = sums.reshape(CW + 4, 2, planes, rows_r).transpose(2, 1, 0, 3)
     vector_parts = jnp.pad(vector_parts, ((0, 0), (0, 0), (0, 0), (0, lanes - rows_r)))
-    here = (jnp.arange(CHIPS) == p).astype(f32)[None, :, None, None, None]
-    vector_parts = (vector_parts[:, None] * here).reshape(planes, 8, CW + 4, lanes)
-    gain_parts = grad_mlp_gain.reshape(2, planes, CHIPS, 1, rows_d).transpose(1, 2, 0, 3, 4)
-    gain_parts = jnp.pad(
-        gain_parts.reshape(planes, 8, 1, rows_d), ((0, 0), (0, 0), (0, 7), (0, lanes - rows_d))
-    )
     grad_tokens, small_grads, gate_grads, second_swapped = closing(
         low_cube,
         whole_in,
         tokens,
         gain_one,
         grad_middle,
-        jnp.concatenate([vector_parts, gain_parts], axis=2),
+        vector_parts,
+        grad_mlp_gain,
         (conv_low, grad_decay_low, grad_input_low),
         piece_grads[1].reshape(CHIPS, rows_d, 2 * half_units),
         head,
@@ -2383,9 +2417,12 @@
     grad_mlp_gate, grad_mlp_up = from_chips(
         [first_swapped, second_swapped], mlp_pairs, [mlp_gate.shape[1]] * 2
     )
-    block_out = middle + behind(down_sum, grad_tokens)
     block_out, grad_out_proj, grad_mlp_down = regrouped_columns(
-        (block_out, *behind((grad_rows[:rows_r], grad_rows[rows_r:]), grad_tokens)), [bf16, f32, f32], True
+        [block_out, behind(grad_rows, grad_tokens)],
+        [(0, 0, rows, 0, 0), (1, 0, rows_r, 1, 0), (1, rows_r, rows_f, 2, 0)],
+        [bf16, f32, f32],
+        True,
+        24,
     )
     in_grads = behind(in_grads, grad_out_proj)
     in_out = plane_swap([in_grads.reshape(CHIPS, rows_d, 2 * channels)], 16)
@@ -2394,7 +2431,7 @@
     return (
         block_out,
         grad_tokens,
-        small_grads[CW + 12, :rows_d],
+        small_grads[CW + 4, :rows_d],
         grad_gate_branch,
         grad_input_branch,
         vector_grads[:CW],
@@ -2405,7 +2442,7 @@
         vector_grads[CW + 2],
         vector_grads[CW + 3],
         grad_out_proj,
-        small_grads[CW + 4, :rows_d],
+        small_grads[CW + 4, rows_d : 2 * rows_d],
         grad_mlp_gate,
         grad_mlp_up,
         grad_mlp_down,

time: 616 us -> 608 us (0.987)
    pallas_call x5 -> x4, Pallas kernels: 72.9 us -> 85.7 us  [the longest x1 64.9 us: opening(): pl.pallas_call(functools.partial(opening_kernel, planes, pairs), out_shap...]
    pallas_call x2 -> x1, Pallas kernels: 22.9 us -> 11.1 us  [plane_swap(): pl.pallas_call(functools.partial(plane_swap_kernel, count), out_shape=[ja...]
  transfers between devices with their start and end apart: 8 -> 8, of which waited for: 1 -> 1; matrix products, arithmetic and copies ran while one was open for 6% -> 5% of each run, Pallas kernels for 86% -> 87%
where the time goes in v5:
time: 608 us; the launch traced here: 599 us
  Pallas kernels  546 us (90%)
  local copies, waits for them, and re-layouts  20.7 us (3%)
  between operations  15.3 us (3%)
  matrix products  12.5 us (2%)
    pallas_call x1, Pallas kernels, middle_of(): pl.pallas_call(middle_kernel, out_shape=[jax.ShapeDtypeStruct((rows, widt...  93.6 us
    pallas_call x1, Pallas kernels, grads_of_middle(): pl.pallas_call(grads_of_middle_kernel, out_shape=[jax.ShapeDtypeStruct((r...  85.1 us
    pallas_call x2, Pallas kernels, feed_forward(): pl.pallas_call(functools.partial(feed_forward_kernel, piece), out_shape=o...  75.4 us
    pallas_call x1, Pallas kernels, opening(): pl.pallas_call(functools.partial(opening_kernel, planes, pairs), out_shap...  64.9 us
    pallas_call x1, Pallas kernels, recurrence(): pl.pallas_call(functools.partial(recurrence_kernel, planes), out_shape=[o...  60.4 us
    pallas_call x1, Pallas kernels, closing(): pl.pallas_call(functools.partial(closing_kernel, planes), out_shape=[jax....  60 us
    pallas_call x1, Pallas kernels, recurrence_back(): pl.pallas_call(functools.partial(recurrence_back_kernel, planes), out_sha...  57.4 us
    pallas_call x1, Pallas kernels, input_grads(): pl.pallas_call(input_grads_kernel, out_shape=jax.ShapeDtypeStruct((width...  14.2 us
  transfers between devices with their start and end apart: 8, of which 1 were waited for; matrix products, arithmetic and copies ran while one was open for 5% of the time, Pallas kernels for 87%

profile of v5, /device:TPU:0, one launch (start us, length us, event | category | flops | bytes accessed | tf_op | source)
XLA Modules:
  0.0 598.9 jit_solution(6687675233863369540)
XLA Ops:
  7.2 13.7 %first_swap.1 = bf16[4,64,1280]{2,1,0:T(8,128)(2,1)} custom-call(bf16[64,2560]{1,0:T(8,128)(2,1)} %refs_0_.2, bf16[64,2560]{1,0:T(8,128)(2,1)} %refs_1_.2), custom_call_target="tpu_custom_call" | custom-call | tf_op jit(solution)/shard_map/first_swap/pallas_call | solution.py:1258
  21.1 4.7 regrouped_columns.2
  26.1 1.2 concatenate.33.small
  27.3 0.7 pad_maximum_fusion.3.gates
  28.0 64.9 %opening.1 = (f32[8,4,16,128]{3,2,1,0:T(8,128)}, bf16[640,640]{1,0:T(8,128)(2,1)}, bf16[640,640]{1,0:T(8,128)(2,1)}, bf16[4,64,1536]{2,1,0:T(8,128)(2,1)}, bf16[...) custom-call(f32[16,128]{1,0:T(8,128)} %concatenate.33.small, bf16[80,320]{1,0:T(8,128)(2,1)} %pad_maximum_fusion.3.gates, ...), custom_call_target="tpu_custom_call" | custom-call | flops 65000001536 | bytes 195000000 | tf_op jit(solution)/shard_map/opening/pallas_call | solution.py:1416
  93.1 0.9 constant_dynamic-slice_fusion.1
  94.0 0.1 reshape.288
  94.1 1.0 slice.141
  95.1 0.1 squeeze.36
  95.2 0.1 fusion.8
  95.3 0.2 fusion.6
  95.6 0.6 copy-done.7
  96.3 1.0 copy.42
  97.3 0.1 scatter.4.vectors
  97.4 8.1 %fusion.2.gate_pre = f32[4,256,640]{2,1,0:T(8,128)} fusion(bf16[4,256,2048]{2,1,0:T(8,128)(2,1)} %get-tuple-element.101, bf16[2048,1280]{1,0:T(8,128)(2,1)} %all-gather.5.cloned.1.call-done.whole_in), kind=kOutput, calls=%fused_computation.3 | convolution fusion | flops 2684354560 | bytes 9437184 | tf_op jit(solution)/shard_map/dot_general | solution.py:2249
  105.5 4.5 fusion.3
  110.0 60.4 %recurrence.1 = (f32[4,256,640]{2,1,0:T(8,128)}, bf16[4,256,640]{2,1,0:T(8,128)(2,1)}, f32[4,256,640]{2,1,0:T(8,128)}, f32[4,256,640]{2,1,0:T(8,128)}, f32[4,256...) custom-call(f32[4,256,640]{2,1,0:T(8,128)} %fusion.2.gate_pre, ...), custom_call_target="tpu_custom_call" | custom-call | flops 46000001024 | bytes 138000000 | tf_op jit(solution)/shard_map/recurrence/pallas_call | solution.py:1697
  170.5 0.2 reduce-scatter.5.cloned.1.call-start
  170.7 1.6 fusion.14
  172.3 0.7 broadcast_in_dim_reshape.7.gain
  173.0 2.0 all-gather.7.cloned.1.call-done
  175.0 93.6 %middle.1 = (f32[256,2048]{1,0:T(8,128)}, bf16[4,256,2048]{2,1,0:T(8,128)(2,1)}, bf16[1024,2048]{1,0:T(8,128)(2,1)}) custom-call(bf16[4,256,640]{2,1,0:T(8,128)(2,1)} %get-tuple-element.107.mixed, bf16[8,272,2048]{2,1,0:T(8,128)(2,1)} %bitcast.132, bf16[256,2048]{1,0:T(8,128)(2,1)} %get-tuple-element.100.tokens, f32[1,2048]{1,0:T(1,128)} %broadcast_in_dim_reshape.7.gain, ...), custom_call_target="tpu_custom_call" | custom-call | flops 74999996416 | bytes 225000000 | tf_op jit(solution)/shard_map/middle/pallas_call | solution.py:663
  268.6 37.8 %feed_forward.2 = (bf16[1024,768]{1,0:T(8,128)(2,1)}, bf16[1024,1536]{1,0:T(8,128)(2,1)}, f32[1024,2048]{1,0:T(8,128)}) custom-call(bf16[1024,2048]{1,0:T(8,128)(2,1)} %bitcast.144, bf16[1024,2048]{1,0:T(8,128)(2,1)} %bitcast.141, bf16[2048,1536]{1,0:T(8,128)(2,1)} %all-gather.11.cloned.1.call-done.weights, bf16[8,272,2048]{2,1,0:T(8,128)(2,1)} %bitcast.133), custom_call_target="tpu_custom_call" | custom-call | flops 35000000512 | bytes 105000000 | tf_op jit(solution)/shard_map/feed_forward/pallas_call | solution.py:806
  306.5 0.3 reduce-scatter.9.cloned.1.call-start
  306.8 37.6 %feed_forward.3 = (bf16[1024,768]{1,0:T(8,128)(2,1)}, bf16[1024,1536]{1,0:T(8,128)(2,1)}, bf16[1024,2048]{1,0:T(8,128)(2,1)}) custom-call(bf16[1024,2048]{1,0:T(8,128)(2,1)} %bitcast.145, bf16[1024,2048]{1,0:T(8,128)(2,1)} %bitcast.142, bf16[2048,1536]{1,0:T(8,128)(2,1)} %all-gather.9.cloned.1.call-done.weights, bf16[8,272,2048]{2,1,0:T(8,128)(2,1)} %bitcast.134, ...), custom_call_target="tpu_custom_call" | custom-call | flops 35000000512 | bytes 105000000 | tf_op jit(solution)/shard_map/feed_forward/pallas_call | solution.py:806
  344.4 0.0 reduce-scatter.7.cloned.1.call-start
  344.5 85.1 %grads_of_middle.1 = (f32[256,2048]{1,0:T(8,128)}, f32[1,2048]{1,0:T(1,128)}, bf16[4,256,2048]{2,1,0:T(8,128)(2,1)}, bf16[4,272,2048]{2,1,0:T(8,128)(2,1)}, bf16[4,256,2048]{2,1,0:T(8,128)(2,1)}) custom-call(bf16[4,256,2048]{2,1,0:T(8,128)(2,1)} %bitcast.146, f32[256,2048]{1,0:T(8,128)} %get-tuple-element.116.middle, ...), custom_call_target="tpu_custom_call" | custom-call | flops 80000000000 | bytes 240000000 | tf_op jit(solution)/shard_map/grads_of_middle/pallas_call | solution.py:1019
  429.7 0.6 copy-done.13
  430.3 0.7 broadcast_in_dim_reshape.8.gain
  431.1 0.7 copy.46
  431.8 57.4 %recurrence_back.1 = (bf16[4,256,1280]{2,1,0:T(8,128)(2,1)}, bf16[4,256,640]{2,1,0:T(8,128)(2,1)}, bf16[4,256,640]{2,1,0:T(8,128)(2,1)}, f32[8,640]{1,0:T(8,128)...) custom-call(bf16[4,256,2048]{2,1,0:T(8,128)(2,1)} %get-tuple-element.122.grad_branch, ...), custom_call_target="tpu_custom_call" | custom-call | flops 57999998976 | bytes 174000000 | tf_op jit(solution)/shard_map/recurrence_back/pallas_call | solution.py:1999
  489.3 14.2 %input_grads.1 = bf16[1024,1280]{1,0:T(8,128)(2,1)} custom-call(bf16[1024,2048]{1,0:T(8,128)(2,1)} %bitcast.108, bf16[1024,1024]{1,0:T(8,128)(2,1)} %get-tuple-element.134.normed_other, bf16[1024,1280]{1,0:T(8,128)(2,1)} %bitcast.111), custom_call_target="tpu_custom_call" | custom-call | tf_op jit(solution)/shard_map/input_grads/pallas_call | solution.py:2112
  503.6 0.1 scatter-mul.4
  503.7 0.1 reshape.302
  503.8 0.6 pad.62.small
  504.4 60.0 %closing.1 = (f32[256,2048]{1,0:T(8,128)}, f32[9,128]{1,0:T(8,128)}, f32[80,320]{1,0:T(8,128)}, bf16[4,64,1536]{2,1,0:T(8,128)(2,1)}) custom-call(bf16[4,256,1280]{2,1,0:T(8,128)(2,1)} %get-tuple-element.135.in_low, bf16[2048,1280]{1,0:T(8,128)(2,1)} %all-gather.5.cloned.1.call-done.whole_in, bf16[256,2048]{1,0:T(8,128)(2,1)} %get-tuple-element.100.tokens, ...), custom_call_target="tpu_custom_call" | custom-call | flops 49999998976 | bytes 150000000 | tf_op jit(solution)/shard_map/closing/pallas_call | solution.py:1207
  564.4 1.2 slice.131
  565.7 1.1 copy-done.3
  566.8 1.9 from_chips.3
  568.8 1.3 slice_bitcast_fusion.2
  570.1 1.3 slice_bitcast_fusion.3
  571.4 1.7 fusion.15
  573.1 1.3 copy-done.1
  574.4 2.4 regrouped_columns.3
  576.8 11.1 %plane_swap.1.refs_0_ = bf16[4,64,1280]{2,1,0:T(8,128)(2,1)} custom-call(bf16[4,64,1280]{2,1,0:T(8,128)(2,1)} %bitcast.139), custom_call_target="tpu_custom_call" | custom-call | flops 10000000000 | bytes 30000000 | tf_op jit(solution)/shard_map/plane_swap/pallas_call | solution.py:1296
  587.8 1.1 copy-done.4
  588.9 1.4 from_chips.2
  590.3 1.3 copy.62
  (101 shorter events, 0.9 us)
Async XLA Ops:
  7.2 90.2 %all-gather.5.cloned.1.call-start = ((), (), s32[]{:S(2)}) async-start(), calls=%async_computation.4 | async-start | bytes 5898240 | tf_op jit(solution)/shard_map/all_gather | solution.py:2241
  20.9 5.0 copy-start.22
  20.9 5.0 copy-start.23
  20.9 5.0 copy-start.24
  20.9 5.0 copy-start.25
  20.9 5.0 copy-start.26
  21.0 5.0 copy-start.27
  21.0 5.0 copy-start.20
  21.0 5.1 copy-start.21
  21.0 6.3 %copy-start.14 = (bf16[80,160]{1,0:T(8,128)(2,1)S(1)}, bf16[80,160]{1,0:T(8,128)(2,1)}, u32[]{:S(2)}) copy-start(bf16[80,160]{1,0:T(8,128)(2,1)} %param.32) | copy-start | bytes 76804
  21.0 6.3 %copy-start.15 = (bf16[80,160]{1,0:T(8,128)(2,1)S(1)}, bf16[80,160]{1,0:T(8,128)(2,1)}, u32[]{:S(2)}) copy-start(bf16[80,160]{1,0:T(8,128)(2,1)} %param.30) | copy-start | bytes 76804
  21.0 153.9 %all-gather.7.cloned.1.call-start = ((), (), s32[]{:S(2)}) async-start(), calls=%async_computation.5 | async-start | bytes 10027008 | tf_op jit(solution)/shard_map/all_gather | solution.py:2241
  25.9 242.8 %all-gather.11.cloned.1.call-start = ((), (), s32[]{:S(2)}) async-start(), calls=%async_computation.7 | async-start | bytes 7077888 | tf_op jit(solution)/shard_map/all_gather | solution.py:2241
  93.0 213.8 %all-gather.9.cloned.1.call-start = ((), (), s32[]{:S(2)}) async-start(), calls=%async_computation.6 | async-start | bytes 7077888 | tf_op jit(solution)/shard_map/all_gather | solution.py:2241
  95.2 10.3 %copy-start.17 = (f32[1,640]{1,0:T(1,128)}, f32[1,640]{1,0:T(1,128)S(1)}, u32[]{:S(2)}) copy-start(f32[1,640]{1,0:T(1,128)S(1)} %squeeze.36) | copy-start | bytes 7684
  95.3 10.2 %copy-start.11 = (f32[1,4,4,2,256]{4,3,2,1,0:T(2,128)}, f32[1,4,4,2,256]{4,3,2,1,0:T(2,128)S(1)}, u32[]{:S(2)}) copy-start(f32[1,4,4,2,256]{4,3,2,1,0:T(2,128)S(1)} %stack.8) | copy-start | bytes 98308
  95.6 0.6 copy-start.7
  95.6 0.6 copy-start.9
  97.4 8.1 %copy-start.19 = (f32[8,640]{1,0:T(8,128)}, f32[8,640]{1,0:T(8,128)S(1)}, u32[]{:S(2)}) copy-start(f32[8,640]{1,0:T(8,128)S(1)} %scatter.4.vectors) | copy-start | bytes 61444
  97.4 8.1 %copy-start.5 = (bf16[4,256,2048]{2,1,0:T(8,128)(2,1)S(1)}, bf16[4,256,2048]{2,1,0:T(8,128)(2,1)}, u32[]{:S(2)}) copy-start(bf16[4,256,2048]{2,1,0:T(8,128)(2,1)} %get-tuple-element.101) | copy-start | bytes 12582916
  97.4 8.1 %copy-start.28 = (bf16[2048,1280]{1,0:T(8,128)(2,1)S(1)}, bf16[2048,1280]{1,0:T(8,128)(2,1)}, u32[]{:S(2)}) copy-start(bf16[2048,1280]{1,0:T(8,128)(2,1)} %all-gather.5.cloned.1.call-done.whole_in) | copy-start | bytes 15728644
  170.5 261.4 %reduce-scatter.5.cloned.1.call-start = ((), (), s32[]{:S(2)}) async-start(), calls=%async_computation.8 | async-start | bytes 3932160 | tf_op jit(solution)/shard_map/reduce_scatter | solution.py:2244
  306.5 197.9 %reduce-scatter.9.cloned.1.call-start = ((), (), s32[]{:S(2)}) async-start(), calls=%async_computation.10 | async-start | bytes 3932160 | tf_op jit(solution)/shard_map/reduce_scatter | solution.py:2244
  344.4 228.7 %reduce-scatter.7.cloned.1.call-start = ((), (), s32[]{:S(2)}) async-start(), calls=%async_computation.9 | async-start | bytes 5570560 | tf_op jit(solution)/shard_map/reduce_scatter | solution.py:2244
  429.6 0.7 copy-start.13
  429.6 1.4 copy-start.8
  429.6 1.4 copy-start.10
  429.6 1.4 copy-start.12
  429.6 147.1 %reduce-scatter.11.cloned.1.call-start = ((), (), s32[]{:S(2)}) async-start(), calls=%async_computation.11 | async-start | bytes 3276800 | tf_op jit(solution)/shard_map/reduce_scatter | solution.py:2244
  489.3 14.3 %copy-start.16 = (f32[8,640]{1,0:T(8,128)S(1)}, f32[8,640]{1,0:T(8,128)}, u32[]{:S(2)}) copy-start(f32[8,640]{1,0:T(8,128)} %get-tuple-element.137) | copy-start | bytes 61444
  489.3 14.3 %copy-start.18 = (f32[1,640]{1,0:T(1,128)S(1)}, f32[1,640]{1,0:T(1,128)}, u32[]{:S(2)}) copy-start(f32[1,640]{1,0:T(1,128)} %copy-done.17) | copy-start | bytes 7684
  504.4 61.3 %copy-start.2 = (bf16[4,64,1536]{2,1,0:T(8,128)(2,1)S(1)}, bf16[4,64,1536]{2,1,0:T(8,128)(2,1)}, u32[]{:S(2)}) copy-start(bf16[4,64,1536]{2,1,0:T(8,128)(2,1)} %get-tuple-element.152.refs_0_) | copy-start | bytes 2359300
  504.4 68.7 %copy-start = (f32[256,2048]{1,0:T(8,128)S(1)}, f32[256,2048]{1,0:T(8,128)}, u32[]{:S(2)}) copy-start(f32[256,2048]{1,0:T(8,128)} %get-tuple-element.131.refs_0_) | copy-start | bytes 6291460
  565.7 1.1 copy-start.3
  573.1 1.3 copy-start.1
  576.8 13.6 %copy-start.6 = (f32[256,2048]{1,0:T(8,128)S(1)}, f32[256,2048]{1,0:T(8,128)}, u32[]{:S(2)}) copy-start(f32[256,2048]{1,0:T(8,128)} %get-tuple-element.202) | copy-start | bytes 6291460
  587.8 1.1 copy-start.4
Sparse Core Ops, SparseCore 0:
  21.2 63.0 all-gather.4
  86.4 88.5 all-gather.6
  176.6 63.3 all-gather.10
  241.4 63.3 all-gather.8
  307.0 58.9 reduce-scatter.4
  368.1 60.2 reduce-scatter.8
  430.7 83.8 reduce-scatter.6
  516.9 57.2 reduce-scatter.10

commit v6 on v5

--- a/solution.py
+++ b/solution.py
@@ -1242,33 +1242,49 @@
 
 def first_swap_kernel(planes, pairs, *refs):
     count = len(pairs)
-    ins, (out, parts, send, recv, local) = refs[:count], refs[count:]
+    ins, refs = refs[:count], refs[count:]
+    decay_gate, input_gate, out, line, gates, parts, send, recv, local, line_send, line_recv = refs
+    me, z, p, c, x, y = place()
+    far = [8 * lax.rem(z + d, planes) + lax.rem(me, 8) for d in range(1, planes)]
+    head = decay_gate.shape[1]
+    gates[:, :head] = decay_gate[...]
+    gates[:, head:] = input_gate[...]
     to_chips_kernel(planes, pairs, *ins, parts)
-    greet(plane_neighbours()[0])
-    copies = swap_copies(parts, out, send, recv, local)
+    greet([*plane_neighbours()[0], *far])
+    copies = swap_copies(parts, out, send, recv, local) + [
+        remote(gates, line.at[z], line_send.at[d], line_recv.at[d], device) for d, device in enumerate(far)
+    ]
     for copy in copies:
         copy.start()
+    line[z] = gates[...]
     for copy in copies:
         copy.wait()
 
 
-def first_swap(weights, pairs, width, collective_id):
+def first_swap(weights, pairs, width, gates, collective_id):
     planes = lax.axis_size("seq") // 8
+    rows, head = gates[0].shape
     shape = (CHIPS, weights[0].shape[0], width)
     return pl.pallas_call(
         functools.partial(first_swap_kernel, planes, pairs),
-        out_shape=jax.ShapeDtypeStruct(shape, weights[0].dtype),
-        in_specs=[VMEM] * len(weights),
-        out_specs=ANY,
+        out_shape=[
+            jax.ShapeDtypeStruct(shape, weights[0].dtype),
+            jax.ShapeDtypeStruct((planes, rows, 2 * head), gates[0].dtype),
+        ],
+        in_specs=[VMEM] * (len(weights) + 2),
+        out_specs=[ANY, VMEM],
         scratch_shapes=[
+            pltpu.VMEM((rows, 2 * head), gates[0].dtype),
             pltpu.VMEM(shape, weights[0].dtype),
             pltpu.SemaphoreType.DMA((3,)),
             pltpu.SemaphoreType.DMA((3,)),
             pltpu.SemaphoreType.DMA,
+            pltpu.SemaphoreType.DMA((planes - 1,)),
+            pltpu.SemaphoreType.DMA((planes - 1,)),
         ],
         compiler_params=comm_params(collective_id, 60),
         name="first_swap",
-    )(*weights)
+    )(*weights, *gates)
 
 
 def plane_swap_kernel(count, *refs):
@@ -1347,14 +1363,15 @@
     lines = [
         remote(small, gathered.at[r, z], send.at[d], recv.at[d], device) for d, device in enumerate(far)
     ]
-    gate_lines = [
-        remote(gates, gates_all.at[c, z], gate_send.at[d], gate_recv.at[d], device) for d, device in enumerate(far)
-    ]
-    for copy in lines + gate_lines:
+    gate_swap = remote(gates, gates_all.at[c], gate_send, gate_recv, me + 1 - 2 * c)
+    for copy in lines + [gate_swap]:
         copy.start()
     gathered[r, z] = small[...]
-    gates_all[c, z] = gates[...]
+    gates_all[c] = gates[...]
     to_chips_kernel(planes, pairs, mlp_gate, mlp_up, piece, second_piece)
+    swaps = swap_copies(piece, swapped, swap_send, swap_recv, swap_local)
+    for copy in swaps:
+        copy.start()
     for copy in lines:
         copy.wait()
     spreads = [
@@ -1363,15 +1380,8 @@
     ]
     for copy in spreads:
         copy.start()
-    for copy in gate_lines:
-        copy.wait()
-    gate_swap = remote(
-        gates_all.at[c], gates_all.at[c], gate_send.at[planes], gate_recv.at[planes], me + 1 - 2 * c
-    )
-    gate_swap.start()
     for copy in spreads:
         copy.wait()
-    swaps = swap_copies(piece, swapped, swap_send, swap_recv, swap_local)
     rows, width = tokens.shape
     step = width // (8 * planes)
     for j in range(planes):
@@ -1389,10 +1399,8 @@
 
     begin, forward, end = gather_steps(normed, whole, gather_send, gather_recv, gather_local, 0)
     begin()
-    for copy in swaps:
-        copy.start()
     gate_swap.wait()
-    block = gates.shape[0]
+    block = gates.shape[1]
     for k, target in enumerate((decay_blocks, input_blocks)):
         target[...] = jnp.zeros_like(target)
         for e in range(2):
@@ -1411,7 +1419,7 @@
 def opening(small, gates, tokens, mlp_gate, mlp_up, pairs, collective_id):
     planes = lax.axis_size("seq") // 8
     rows, width = tokens.shape
-    channels = 2 * planes * gates.shape[0]
+    channels = 2 * planes * gates.shape[1]
     piece = (CHIPS, mlp_gate.shape[0], mlp_gate.shape[1] // CHIPS)
     return pl.pallas_call(
         functools.partial(opening_kernel, planes, pairs),
@@ -1427,13 +1435,13 @@
         out_specs=[VMEM] * 4 + [ANY, ANY],
         scratch_shapes=[
             pltpu.VMEM(piece, mlp_gate.dtype),
-            pltpu.VMEM((2, planes) + gates.shape, gates.dtype),
+            pltpu.VMEM((2,) + gates.shape, gates.dtype),
             pltpu.VMEM((8, width), jnp.float32),
             pltpu.VMEM((rows, width), jnp.bfloat16),
             pltpu.SemaphoreType.DMA((planes + 7,)),
             pltpu.SemaphoreType.DMA((planes + 7,)),
-            pltpu.SemaphoreType.DMA((planes + 1,)),
-            pltpu.SemaphoreType.DMA((planes + 1,)),
+            pltpu.SemaphoreType.DMA,
+            pltpu.SemaphoreType.DMA,
             pltpu.SemaphoreType.DMA((3,)),
             pltpu.SemaphoreType.DMA((3,)),
             pltpu.SemaphoreType.DMA,
@@ -2275,7 +2283,9 @@
     )
     half = channels // 2
     in_pairs = (((0, 0), (0, half)), ((0, channels), (0, channels + half)))
-    swapped_in = first_swap([gate_branch, input_branch], in_pairs, 2 * channels, 2)
+    swapped_in, gates = first_swap(
+        [gate_branch, input_branch], in_pairs, 2 * channels, [decay_gate, input_gate], 2
+    )
     whole_in = column_gather(swapped_in.reshape(CHIPS * rows_d, 2 * channels))
     tokens, cot, row_shards = regrouped_columns(
         [tokens, cotangent, out_proj, mlp_down],
@@ -2285,7 +2295,6 @@
         60,
     )
     mlp_pairs = (((0, 0), (1, 0)), ((0, half_units), (1, half_units)))
-    gates = jnp.concatenate([decay_gate, input_gate], axis=1)
     small, decay_blocks, input_blocks, second_part, normed_all, first_piece = opening(
         behind(small, swapped_in), gates, tokens, mlp_gate, mlp_up, mlp_pairs, 1
     )

time: 608 us -> 603 us (level)
    pallas_call x1, Pallas kernels: 64.9 us -> 58.8 us  [opening(): pl.pallas_call(functools.partial(opening_kernel, planes, pairs), out_shap...]
  transfers between devices with their start and end apart: 8 -> 8, of which waited for: 1 -> 1; matrix products, arithmetic and copies ran while one was open for 5% -> 5% of each run, Pallas kernels for 87% -> 86%
where the time goes in v6:
time: 603 us; the launch traced here: 595 us
  Pallas kernels  540 us (90%)
  local copies, waits for them, and re-layouts  20.7 us (3%)
  between operations  15.3 us (3%)
  matrix products  12.6 us (2%)
    pallas_call x1, Pallas kernels, middle_of(): pl.pallas_call(middle_kernel, out_shape=[jax.ShapeDtypeStruct((rows, widt...  93.6 us
    pallas_call x1, Pallas kernels, grads_of_middle(): pl.pallas_call(grads_of_middle_kernel, out_shape=[jax.ShapeDtypeStruct((r...  85.1 us
    pallas_call x2, Pallas kernels, feed_forward(): pl.pallas_call(functools.partial(feed_forward_kernel, piece), out_shape=o...  75.4 us
    pallas_call x1, Pallas kernels, closing(): pl.pallas_call(functools.partial(closing_kernel, planes), out_shape=[jax....  60.1 us
    pallas_call x1, Pallas kernels, opening(): pl.pallas_call(functools.partial(opening_kernel, planes, pairs), out_shap...  58.8 us
    pallas_call x1, Pallas kernels, recurrence_back(): pl.pallas_call(functools.partial(recurrence_back_kernel, planes), out_sha...  57.5 us
    pallas_call x1, Pallas kernels, recurrence(): pl.pallas_call(functools.partial(recurrence_kernel, planes), out_shape=[o...  56.5 us
    pallas_call x1, Pallas kernels, first_swap(): pl.pallas_call(functools.partial(first_swap_kernel, planes, pairs), out_s...  17.5 us
  transfers between devices with their start and end apart: 8, of which 1 were waited for; matrix products, arithmetic and copies ran while one was open for 5% of the time, Pallas kernels for 86%

profile of v6, /device:TPU:0, one launch (start us, length us, event | category | flops | bytes accessed | tf_op | source)
XLA Modules:
  0.0 594.7 jit_solution(14414854232166129142)
XLA Ops:
  7.2 17.5 %first_swap.1 = (bf16[4,64,1280]{2,1,0:T(8,128)(2,1)}, bf16[4,80,320]{2,1,0:T(8,128)(2,1)}) custom-call(bf16[64,2560]{1,0:T(8,128)(2,1)} %refs_0_.2, bf16[64,2560]{1,0:T(8,128)(2,1)} %refs_1_.2, bf16[80,160]{1,0:T(8,128)(2,1)} %refs_2_.2, bf16[80,160]{1,0:T(8,128)(2,1)} %refs_3_.2), custom_call_target="tpu_custom_call" | custom-call | tf_op jit(solution)/shard_map/first_swap/pallas_call | solution.py:1268
  24.9 0.0 all-gather.7.cloned.1.call-start
  24.9 4.7 regrouped_columns.2
  29.9 1.2 concatenate.30.small
  31.1 58.8 %opening.1 = (f32[8,4,16,128]{3,2,1,0:T(8,128)}, bf16[640,640]{1,0:T(8,128)(2,1)}, bf16[640,640]{1,0:T(8,128)(2,1)}, bf16[4,64,1536]{2,1,0:T(8,128)(2,1)}, bf16[...) custom-call(f32[16,128]{1,0:T(8,128)} %concatenate.30.small, bf16[4,80,320]{2,1,0:T(8,128)(2,1)} %get-tuple-element.103.gates, ...), custom_call_target="tpu_custom_call" | custom-call | flops 65000001536 | bytes 195000000 | tf_op jit(solution)/shard_map/opening/pallas_call | solution.py:1424
  90.0 0.0 all-gather.9.cloned.1.call-start
  90.1 0.9 constant_dynamic-slice_fusion.1
  91.0 0.1 reshape.288
  91.0 0.9 slice.141
  92.0 0.1 squeeze.36
  92.1 0.1 fusion.8
  92.3 0.2 fusion.6
  92.5 0.6 copy-done.7
  93.2 1.0 copy.42
  94.2 0.1 scatter.4.vectors
  94.4 8.1 %fusion.2.gate_pre = f32[4,256,640]{2,1,0:T(8,128)} fusion(bf16[4,256,2048]{2,1,0:T(8,128)(2,1)} %get-tuple-element.105, bf16[2048,1280]{1,0:T(8,128)(2,1)} %all-gather.5.cloned.1.call-done.whole_in), kind=kOutput, calls=%fused_computation.3 | convolution fusion | flops 2684354560 | bytes 9437184 | tf_op jit(solution)/shard_map/dot_general | solution.py:2257
  102.5 4.5 fusion.3
  107.0 56.5 %recurrence.1 = (f32[4,256,640]{2,1,0:T(8,128)}, bf16[4,256,640]{2,1,0:T(8,128)(2,1)}, f32[4,256,640]{2,1,0:T(8,128)}, f32[4,256,640]{2,1,0:T(8,128)}, f32[4,256...) custom-call(f32[4,256,640]{2,1,0:T(8,128)} %fusion.2.gate_pre, ...), custom_call_target="tpu_custom_call" | custom-call | flops 46000001024 | bytes 138000000 | tf_op jit(solution)/shard_map/recurrence/pallas_call | solution.py:1705
  163.5 0.2 reduce-scatter.5.cloned.1.call-start
  163.8 1.6 fusion.14
  165.4 0.7 broadcast_in_dim_reshape.7.gain
  166.1 4.5 all-gather.7.cloned.1.call-done
  170.6 93.6 %middle.1 = (f32[256,2048]{1,0:T(8,128)}, bf16[4,256,2048]{2,1,0:T(8,128)(2,1)}, bf16[1024,2048]{1,0:T(8,128)(2,1)}) custom-call(bf16[4,256,640]{2,1,0:T(8,128)(2,1)} %get-tuple-element.111.mixed, bf16[8,272,2048]{2,1,0:T(8,128)(2,1)} %bitcast.132, bf16[256,2048]{1,0:T(8,128)(2,1)} %get-tuple-element.104.tokens, f32[1,2048]{1,0:T(1,128)} %broadcast_in_dim_reshape.7.gain, ...), custom_call_target="tpu_custom_call" | custom-call | flops 74999996416 | bytes 225000000 | tf_op jit(solution)/shard_map/middle/pallas_call | solution.py:663
  264.2 37.8 %feed_forward.2 = (bf16[1024,768]{1,0:T(8,128)(2,1)}, bf16[1024,1536]{1,0:T(8,128)(2,1)}, f32[1024,2048]{1,0:T(8,128)}) custom-call(bf16[1024,2048]{1,0:T(8,128)(2,1)} %bitcast.144, bf16[1024,2048]{1,0:T(8,128)(2,1)} %bitcast.141, bf16[2048,1536]{1,0:T(8,128)(2,1)} %all-gather.11.cloned.1.call-done.weights, bf16[8,272,2048]{2,1,0:T(8,128)(2,1)} %bitcast.133), custom_call_target="tpu_custom_call" | custom-call | flops 35000000512 | bytes 105000000 | tf_op jit(solution)/shard_map/feed_forward/pallas_call | solution.py:806
  302.1 0.3 reduce-scatter.9.cloned.1.call-start
  302.4 37.6 %feed_forward.3 = (bf16[1024,768]{1,0:T(8,128)(2,1)}, bf16[1024,1536]{1,0:T(8,128)(2,1)}, bf16[1024,2048]{1,0:T(8,128)(2,1)}) custom-call(bf16[1024,2048]{1,0:T(8,128)(2,1)} %bitcast.145, bf16[1024,2048]{1,0:T(8,128)(2,1)} %bitcast.142, bf16[2048,1536]{1,0:T(8,128)(2,1)} %all-gather.9.cloned.1.call-done.weights, bf16[8,272,2048]{2,1,0:T(8,128)(2,1)} %bitcast.134, ...), custom_call_target="tpu_custom_call" | custom-call | flops 35000000512 | bytes 105000000 | tf_op jit(solution)/shard_map/feed_forward/pallas_call | solution.py:806
  340.0 85.1 %grads_of_middle.1 = (f32[256,2048]{1,0:T(8,128)}, f32[1,2048]{1,0:T(1,128)}, bf16[4,256,2048]{2,1,0:T(8,128)(2,1)}, bf16[4,272,2048]{2,1,0:T(8,128)(2,1)}, bf16[4,256,2048]{2,1,0:T(8,128)(2,1)}) custom-call(bf16[4,256,2048]{2,1,0:T(8,128)(2,1)} %bitcast.146, f32[256,2048]{1,0:T(8,128)} %get-tuple-element.120.middle, ...), custom_call_target="tpu_custom_call" | custom-call | flops 80000000000 | bytes 240000000 | tf_op jit(solution)/shard_map/grads_of_middle/pallas_call | solution.py:1019
  425.3 0.6 copy-done.13
  425.9 0.7 broadcast_in_dim_reshape.8.gain
  426.7 0.7 copy.46
  427.4 57.5 %recurrence_back.1 = (bf16[4,256,1280]{2,1,0:T(8,128)(2,1)}, bf16[4,256,640]{2,1,0:T(8,128)(2,1)}, bf16[4,256,640]{2,1,0:T(8,128)(2,1)}, f32[8,640]{1,0:T(8,128)...) custom-call(bf16[4,256,2048]{2,1,0:T(8,128)(2,1)} %get-tuple-element.126.grad_branch, ...), custom_call_target="tpu_custom_call" | custom-call | flops 57999998976 | bytes 174000000 | tf_op jit(solution)/shard_map/recurrence_back/pallas_call | solution.py:2007
  484.9 14.2 %input_grads.1 = bf16[1024,1280]{1,0:T(8,128)(2,1)} custom-call(bf16[1024,2048]{1,0:T(8,128)(2,1)} %bitcast.108, bf16[1024,1024]{1,0:T(8,128)(2,1)} %get-tuple-element.138.normed_other, bf16[1024,1280]{1,0:T(8,128)(2,1)} %bitcast.110), custom_call_target="tpu_custom_call" | custom-call | tf_op jit(solution)/shard_map/input_grads/pallas_call | solution.py:2120
  499.2 0.1 scatter-mul.4
  499.3 0.1 reshape.302
  499.4 0.6 pad.62.small
  500.0 60.1 %closing.1 = (f32[256,2048]{1,0:T(8,128)}, f32[9,128]{1,0:T(8,128)}, f32[80,320]{1,0:T(8,128)}, bf16[4,64,1536]{2,1,0:T(8,128)(2,1)}) custom-call(bf16[4,256,1280]{2,1,0:T(8,128)(2,1)} %get-tuple-element.139.in_low, bf16[2048,1280]{1,0:T(8,128)(2,1)} %all-gather.5.cloned.1.call-done.whole_in, bf16[256,2048]{1,0:T(8,128)(2,1)} %get-tuple-element.104.tokens, ...), custom_call_target="tpu_custom_call" | custom-call | flops 49999998976 | bytes 150000000 | tf_op jit(solution)/shard_map/closing/pallas_call | solution.py:1207
  560.1 1.3 slice.131
  561.4 1.1 copy-done.3
  562.5 1.9 from_chips.3
  564.5 1.3 slice_bitcast_fusion.2
  565.8 1.3 slice_bitcast_fusion.3
  567.2 1.7 fusion.15
  568.9 1.3 copy-done.1
  570.1 2.4 regrouped_columns.3
  572.5 11.0 %plane_swap.1.refs_0_ = bf16[4,64,1280]{2,1,0:T(8,128)(2,1)} custom-call(bf16[4,64,1280]{2,1,0:T(8,128)(2,1)} %bitcast.139), custom_call_target="tpu_custom_call" | custom-call | flops 10000000000 | bytes 30000000 | tf_op jit(solution)/shard_map/plane_swap/pallas_call | solution.py:1312
  583.5 1.1 copy-done.4
  584.6 1.4 from_chips.2
  586.1 1.3 copy.62
  (96 shorter events, 0.9 us)
Async XLA Ops:
  7.2 87.2 %all-gather.5.cloned.1.call-start = ((), (), s32[]{:S(2)}) async-start(), calls=%async_computation.4 | async-start | bytes 5898240 | tf_op jit(solution)/shard_map/all_gather | solution.py:2249
  24.7 5.0 copy-start.20
  24.7 5.0 copy-start.21
  24.8 5.0 copy-start.22
  24.8 5.0 copy-start.23
  24.8 5.0 copy-start.24
  24.8 5.0 copy-start.25
  24.8 5.0 copy-start.18
  24.8 5.1 copy-start.19
  24.9 145.7 %all-gather.7.cloned.1.call-start = ((), (), s32[]{:S(2)}) async-start(), calls=%async_computation.5 | async-start | bytes 10027008 | tf_op jit(solution)/shard_map/all_gather | solution.py:2249
  29.7 234.5 %all-gather.11.cloned.1.call-start = ((), (), s32[]{:S(2)}) async-start(), calls=%async_computation.7 | async-start | bytes 7077888 | tf_op jit(solution)/shard_map/all_gather | solution.py:2249
  90.0 212.4 %all-gather.9.cloned.1.call-start = ((), (), s32[]{:S(2)}) async-start(), calls=%async_computation.6 | async-start | bytes 7077888 | tf_op jit(solution)/shard_map/all_gather | solution.py:2249
  92.1 10.4 %copy-start.15 = (f32[1,640]{1,0:T(1,128)}, f32[1,640]{1,0:T(1,128)S(1)}, u32[]{:S(2)}) copy-start(f32[1,640]{1,0:T(1,128)S(1)} %squeeze.36) | copy-start | bytes 7684
  92.3 10.3 %copy-start.11 = (f32[1,4,4,2,256]{4,3,2,1,0:T(2,128)}, f32[1,4,4,2,256]{4,3,2,1,0:T(2,128)S(1)}, u32[]{:S(2)}) copy-start(f32[1,4,4,2,256]{4,3,2,1,0:T(2,128)S(1)} %stack.8) | copy-start | bytes 98308
  92.5 0.6 copy-start.7
  92.5 0.6 copy-start.9
  94.3 8.2 %copy-start.17 = (f32[8,640]{1,0:T(8,128)}, f32[8,640]{1,0:T(8,128)S(1)}, u32[]{:S(2)}) copy-start(f32[8,640]{1,0:T(8,128)S(1)} %scatter.4.vectors) | copy-start | bytes 61444
  94.4 8.2 %copy-start.5 = (bf16[4,256,2048]{2,1,0:T(8,128)(2,1)S(1)}, bf16[4,256,2048]{2,1,0:T(8,128)(2,1)}, u32[]{:S(2)}) copy-start(bf16[4,256,2048]{2,1,0:T(8,128)(2,1)} %get-tuple-element.105) | copy-start | bytes 12582916
  94.4 8.2 %copy-start.26 = (bf16[2048,1280]{1,0:T(8,128)(2,1)S(1)}, bf16[2048,1280]{1,0:T(8,128)(2,1)}, u32[]{:S(2)}) copy-start(bf16[2048,1280]{1,0:T(8,128)(2,1)} %all-gather.5.cloned.1.call-done.whole_in) | copy-start | bytes 15728644
  163.5 263.9 %reduce-scatter.5.cloned.1.call-start = ((), (), s32[]{:S(2)}) async-start(), calls=%async_computation.8 | async-start | bytes 3932160 | tf_op jit(solution)/shard_map/reduce_scatter | solution.py:2252
  302.1 197.9 %reduce-scatter.9.cloned.1.call-start = ((), (), s32[]{:S(2)}) async-start(), calls=%async_computation.10 | async-start | bytes 3932160 | tf_op jit(solution)/shard_map/reduce_scatter | solution.py:2252
  340.0 228.9 %reduce-scatter.7.cloned.1.call-start = ((), (), s32[]{:S(2)}) async-start(), calls=%async_computation.9 | async-start | bytes 5570560 | tf_op jit(solution)/shard_map/reduce_scatter | solution.py:2252
  425.2 0.7 copy-start.13
  425.2 1.4 copy-start.8
  425.2 1.4 copy-start.10
  425.2 1.4 copy-start.12
  425.2 147.3 %reduce-scatter.11.cloned.1.call-start = ((), (), s32[]{:S(2)}) async-start(), calls=%async_computation.11 | async-start | bytes 3276800 | tf_op jit(solution)/shard_map/reduce_scatter | solution.py:2252
  484.9 14.2 %copy-start.14 = (f32[8,640]{1,0:T(8,128)S(1)}, f32[8,640]{1,0:T(8,128)}, u32[]{:S(2)}) copy-start(f32[8,640]{1,0:T(8,128)} %get-tuple-element.141) | copy-start | bytes 61444
  484.9 14.2 %copy-start.16 = (f32[1,640]{1,0:T(1,128)S(1)}, f32[1,640]{1,0:T(1,128)}, u32[]{:S(2)}) copy-start(f32[1,640]{1,0:T(1,128)} %copy-done.15) | copy-start | bytes 7684
  500.0 61.4 %copy-start.2 = (bf16[4,64,1536]{2,1,0:T(8,128)(2,1)S(1)}, bf16[4,64,1536]{2,1,0:T(8,128)(2,1)}, u32[]{:S(2)}) copy-start(bf16[4,64,1536]{2,1,0:T(8,128)(2,1)} %get-tuple-element.156.refs_0_) | copy-start | bytes 2359300
  500.0 68.8 %copy-start = (f32[256,2048]{1,0:T(8,128)S(1)}, f32[256,2048]{1,0:T(8,128)}, u32[]{:S(2)}) copy-start(f32[256,2048]{1,0:T(8,128)} %get-tuple-element.135.refs_0_) | copy-start | bytes 6291460
  561.4 1.1 copy-start.3
  568.9 1.3 copy-start.1
  572.5 13.6 %copy-start.6 = (f32[256,2048]{1,0:T(8,128)S(1)}, f32[256,2048]{1,0:T(8,128)}, u32[]{:S(2)}) copy-start(f32[256,2048]{1,0:T(8,128)} %get-tuple-element.206) | copy-start | bytes 6291460
  583.5 1.1 copy-start.4
Sparse Core Ops, SparseCore 0:
  25.0 54.8 all-gather.4
  82.0 88.5 all-gather.6
  172.2 63.2 all-gather.10
  237.0 63.3 all-gather.8
  302.5 58.9 reduce-scatter.4
  363.7 60.2 reduce-scatter.8
  426.3 83.8 reduce-scatter.6
  512.5 57.2 reduce-scatter.10

commit v7 on v6

--- a/solution.py
+++ b/solution.py
@@ -1465,18 +1465,24 @@
     return q, peers
 
 
-def carry_in(planes, reverse, z, c, q, peers, everyone, before, entering, send, recv):
-    own = everyone.at[q]
-    copies = [remote(own, own, send.at[d], recv.at[d], device) for d, device in enumerate(peers)]
-    for copy in copies:
+def carry_in(planes, reverse, z, c, me, everyone, before, entering, send, recv):
+    own = everyone.at[c, z]
+    r = lax.rem(me, 8)
+    lines = [
+        remote(own, own, send.at[d], recv.at[d], 8 * lax.rem(z + d, planes) + r) for d in range(1, planes)
+    ]
+    for copy in lines:
         copy.start()
-    for copy in copies:
+    for copy in lines:
         copy.wait()
-    carried = jnp.zeros((1, everyone.shape[2]), jnp.float32)
+    share = remote(everyone.at[c], everyone.at[c], send.at[0], recv.at[0], me + 1 - 2 * c)
+    share.start()
+    share.wait()
+    carried = jnp.zeros((1, everyone.shape[3]), jnp.float32)
     order = [(k, j, e) for k in range(planes) for j in range(CHIPS) for e in range(2)]
     for k, j, e in reversed(order) if reverse else order:
         before[8 * k + 2 * j + e : 8 * k + 2 * j + e + 1, :] = carried
-        part = everyone.at[2 * k + e]
+        part = everyone.at[e, k]
         carried = part[j : j + 1, :] * carried + part[CHIPS + j : CHIPS + j + 1, :]
     for j in range(CHIPS):
         entering[j : j + 1, :] = before[pl.ds(8 * z + 2 * j + c, 1), :]
@@ -1661,13 +1667,13 @@
             (jnp.ones((1, channels), f32), jnp.zeros((1, channels), f32)),
             unroll=4,
         )
-        everyone[q, pl.ds(j, 1), :] = last_a
-        everyone[q, pl.ds(CHIPS + j, 1), :] = last_b
+        everyone[c, z, pl.ds(j, 1), :] = last_a
+        everyone[c, z, pl.ds(CHIPS + j, 1), :] = last_b
 
     cot_forward()
     for copy in swaps:
         copy.start()
-    carry_in(planes, False, z, c, q, peers, everyone, before, entering, send, recv)
+    carry_in(planes, False, z, c, me, everyone, before, entering, send, recv)
 
     @pl.loop(0, CHIPS)
     def finish(j):
@@ -1724,7 +1730,7 @@
             pltpu.VMEM(cube, f32),
             pltpu.VMEM((CHIPS, 16, channels), bf16),
             pltpu.VMEM((16, channels), bf16),
-            pltpu.VMEM((2 * planes, 2 * CHIPS, channels), f32),
+            pltpu.VMEM((2, planes, 2 * CHIPS, channels), f32),
             pltpu.VMEM((8 * planes, channels), f32),
             pltpu.SemaphoreType.DMA((13,)),
             pltpu.SemaphoreType.DMA((13,)),
@@ -1837,10 +1843,10 @@
         first_a, first_b, first_coef = lax.fori_loop(
             0, rows // 16, scan_tile, (ones, jnp.zeros((1, channels), f32), ones), unroll=2
         )
-        everyone[q, pl.ds(j, 1), :] = first_coef * first_a
-        everyone[q, pl.ds(CHIPS + j, 1), :] = first_coef * first_b
-
-    carry_in(planes, True, z, c, q, peers, everyone, before, leaving, send, recv)
+        everyone[c, z, pl.ds(j, 1), :] = first_coef * first_a
+        everyone[c, z, pl.ds(CHIPS + j, 1), :] = first_coef * first_b
+
+    carry_in(planes, True, z, c, me, everyone, before, leaving, send, recv)
     down_forward()
     for copy in swaps:
         copy.start()
@@ -2026,7 +2032,7 @@
             pltpu.VMEM((CHIPS, 8, channels), f32),
             pltpu.VMEM((8, channels), f32),
             pltpu.VMEM((CHIPS, 8, channels), f32),
-            pltpu.VMEM((2 * planes, 2 * CHIPS, channels), f32),
+            pltpu.VMEM((2, planes, 2 * CHIPS, channels), f32),
             pltpu.VMEM((8 * planes, channels), f32),
             pltpu.VMEM((CHIPS, channels), f32),
             pltpu.SemaphoreType.DMA((12,)),

time: 603 us -> 600 us (level)
  no operation moved by 1% of the time
where the time goes in v7:
time: 600 us; the launch traced here: 592 us
  Pallas kernels  539 us (90%)
  local copies, waits for them, and re-layouts  20.7 us (3%)
  between operations  15.3 us (3%)
  matrix products  12.6 us (2%)
    pallas_call x1, Pallas kernels, middle_of(): pl.pallas_call(middle_kernel, out_shape=[jax.ShapeDtypeStruct((rows, widt...  93.6 us
    pallas_call x1, Pallas kernels, grads_of_middle(): pl.pallas_call(grads_of_middle_kernel, out_shape=[jax.ShapeDtypeStruct((r...  85.1 us
    pallas_call x2, Pallas kernels, feed_forward(): pl.pallas_call(functools.partial(feed_forward_kernel, piece), out_shape=o...  75.4 us
    pallas_call x1, Pallas kernels, closing(): pl.pallas_call(functools.partial(closing_kernel, planes), out_shape=[jax....  58.9 us
    pallas_call x1, Pallas kernels, opening(): pl.pallas_call(functools.partial(opening_kernel, planes, pairs), out_shap...  58.8 us
    pallas_call x1, Pallas kernels, recurrence_back(): pl.pallas_call(functools.partial(recurrence_back_kernel, planes), out_sha...  57.4 us
    pallas_call x1, Pallas kernels, recurrence(): pl.pallas_call(functools.partial(recurrence_kernel, planes), out_shape=[o...  56.5 us
    pallas_call x1, Pallas kernels, first_swap(): pl.pallas_call(functools.partial(first_swap_kernel, planes, pairs), out_s...  17.5 us
  transfers between devices with their start and end apart: 8, of which 1 were waited for; matrix products, arithmetic and copies ran while one was open for 5% of the time, Pallas kernels for 86%

profile of v7, /device:TPU:0, one launch (start us, length us, event | category | flops | bytes accessed | tf_op | source)
XLA Modules:
  0.0 591.6 jit_solution(15249235301343328365)
XLA Ops:
  7.2 17.5 %first_swap.1 = (bf16[4,64,1280]{2,1,0:T(8,128)(2,1)}, bf16[4,80,320]{2,1,0:T(8,128)(2,1)}) custom-call(bf16[64,2560]{1,0:T(8,128)(2,1)} %refs_0_.2, bf16[64,2560]{1,0:T(8,128)(2,1)} %refs_1_.2, bf16[80,160]{1,0:T(8,128)(2,1)} %refs_2_.2, bf16[80,160]{1,0:T(8,128)(2,1)} %refs_3_.2), custom_call_target="tpu_custom_call" | custom-call | tf_op jit(solution)/shard_map/first_swap/pallas_call | solution.py:1268
  24.9 0.0 all-gather.7.cloned.1.call-start
  24.9 4.7 regrouped_columns.2
  29.9 1.2 concatenate.30.small
  31.1 58.8 %opening.1 = (f32[8,4,16,128]{3,2,1,0:T(8,128)}, bf16[640,640]{1,0:T(8,128)(2,1)}, bf16[640,640]{1,0:T(8,128)(2,1)}, bf16[4,64,1536]{2,1,0:T(8,128)(2,1)}, bf16[...) custom-call(f32[16,128]{1,0:T(8,128)} %concatenate.30.small, bf16[4,80,320]{2,1,0:T(8,128)(2,1)} %get-tuple-element.103.gates, ...), custom_call_target="tpu_custom_call" | custom-call | flops 65000001536 | bytes 195000000 | tf_op jit(solution)/shard_map/opening/pallas_call | solution.py:1424
  90.0 0.0 all-gather.9.cloned.1.call-start
  90.1 0.9 constant_dynamic-slice_fusion.1
  91.0 0.1 reshape.288
  91.0 0.9 slice.141
  92.0 0.1 squeeze.36
  92.1 0.1 fusion.8
  92.3 0.2 fusion.6
  92.5 0.6 copy-done.7
  93.2 1.0 copy.42
  94.2 0.1 scatter.4.vectors
  94.4 8.1 %fusion.2.gate_pre = f32[4,256,640]{2,1,0:T(8,128)} fusion(bf16[4,256,2048]{2,1,0:T(8,128)(2,1)} %get-tuple-element.105, bf16[2048,1280]{1,0:T(8,128)(2,1)} %all-gather.5.cloned.1.call-done.whole_in), kind=kOutput, calls=%fused_computation.3 | convolution fusion | flops 2684354560 | bytes 9437184 | tf_op jit(solution)/shard_map/dot_general | solution.py:2263
  102.5 4.5 fusion.3
  107.0 56.5 %recurrence.1 = (f32[4,256,640]{2,1,0:T(8,128)}, bf16[4,256,640]{2,1,0:T(8,128)(2,1)}, f32[4,256,640]{2,1,0:T(8,128)}, f32[4,256,640]{2,1,0:T(8,128)}, f32[4,256...) custom-call(f32[4,256,640]{2,1,0:T(8,128)} %fusion.2.gate_pre, ...), custom_call_target="tpu_custom_call" | custom-call | flops 46000001024 | bytes 138000000 | tf_op jit(solution)/shard_map/recurrence/pallas_call | solution.py:1711
  163.5 0.2 reduce-scatter.5.cloned.1.call-start
  163.8 1.6 fusion.14
  165.4 0.7 broadcast_in_dim_reshape.7.gain
  166.1 2.8 all-gather.7.cloned.1.call-done
  168.8 93.6 %middle.1 = (f32[256,2048]{1,0:T(8,128)}, bf16[4,256,2048]{2,1,0:T(8,128)(2,1)}, bf16[1024,2048]{1,0:T(8,128)(2,1)}) custom-call(bf16[4,256,640]{2,1,0:T(8,128)(2,1)} %get-tuple-element.111.mixed, bf16[8,272,2048]{2,1,0:T(8,128)(2,1)} %bitcast.132, bf16[256,2048]{1,0:T(8,128)(2,1)} %get-tuple-element.104.tokens, f32[1,2048]{1,0:T(1,128)} %broadcast_in_dim_reshape.7.gain, ...), custom_call_target="tpu_custom_call" | custom-call | flops 74999996416 | bytes 225000000 | tf_op jit(solution)/shard_map/middle/pallas_call | solution.py:663
  262.5 37.8 %feed_forward.2 = (bf16[1024,768]{1,0:T(8,128)(2,1)}, bf16[1024,1536]{1,0:T(8,128)(2,1)}, f32[1024,2048]{1,0:T(8,128)}) custom-call(bf16[1024,2048]{1,0:T(8,128)(2,1)} %bitcast.144, bf16[1024,2048]{1,0:T(8,128)(2,1)} %bitcast.141, bf16[2048,1536]{1,0:T(8,128)(2,1)} %all-gather.11.cloned.1.call-done.weights, bf16[8,272,2048]{2,1,0:T(8,128)(2,1)} %bitcast.133), custom_call_target="tpu_custom_call" | custom-call | flops 35000000512 | bytes 105000000 | tf_op jit(solution)/shard_map/feed_forward/pallas_call | solution.py:806
  300.3 0.3 reduce-scatter.9.cloned.1.call-start
  300.6 37.6 %feed_forward.3 = (bf16[1024,768]{1,0:T(8,128)(2,1)}, bf16[1024,1536]{1,0:T(8,128)(2,1)}, bf16[1024,2048]{1,0:T(8,128)(2,1)}) custom-call(bf16[1024,2048]{1,0:T(8,128)(2,1)} %bitcast.145, bf16[1024,2048]{1,0:T(8,128)(2,1)} %bitcast.142, bf16[2048,1536]{1,0:T(8,128)(2,1)} %all-gather.9.cloned.1.call-done.weights, bf16[8,272,2048]{2,1,0:T(8,128)(2,1)} %bitcast.134, ...), custom_call_target="tpu_custom_call" | custom-call | flops 35000000512 | bytes 105000000 | tf_op jit(solution)/shard_map/feed_forward/pallas_call | solution.py:806
  338.3 85.1 %grads_of_middle.1 = (f32[256,2048]{1,0:T(8,128)}, f32[1,2048]{1,0:T(1,128)}, bf16[4,256,2048]{2,1,0:T(8,128)(2,1)}, bf16[4,272,2048]{2,1,0:T(8,128)(2,1)}, bf16[4,256,2048]{2,1,0:T(8,128)(2,1)}) custom-call(bf16[4,256,2048]{2,1,0:T(8,128)(2,1)} %bitcast.146, f32[256,2048]{1,0:T(8,128)} %get-tuple-element.120.middle, ...), custom_call_target="tpu_custom_call" | custom-call | flops 80000000000 | bytes 240000000 | tf_op jit(solution)/shard_map/grads_of_middle/pallas_call | solution.py:1019
  423.5 0.6 copy-done.13
  424.1 0.7 broadcast_in_dim_reshape.8.gain
  424.9 0.7 copy.46
  425.6 57.4 %recurrence_back.1 = (bf16[4,256,1280]{2,1,0:T(8,128)(2,1)}, bf16[4,256,640]{2,1,0:T(8,128)(2,1)}, bf16[4,256,640]{2,1,0:T(8,128)(2,1)}, f32[8,640]{1,0:T(8,128)...) custom-call(bf16[4,256,2048]{2,1,0:T(8,128)(2,1)} %get-tuple-element.126.grad_branch, ...), custom_call_target="tpu_custom_call" | custom-call | flops 57999998976 | bytes 174000000 | tf_op jit(solution)/shard_map/recurrence_back/pallas_call | solution.py:2013
  483.1 14.2 %input_grads.1 = bf16[1024,1280]{1,0:T(8,128)(2,1)} custom-call(bf16[1024,2048]{1,0:T(8,128)(2,1)} %bitcast.108, bf16[1024,1024]{1,0:T(8,128)(2,1)} %get-tuple-element.138.normed_other, bf16[1024,1280]{1,0:T(8,128)(2,1)} %bitcast.110), custom_call_target="tpu_custom_call" | custom-call | tf_op jit(solution)/shard_map/input_grads/pallas_call | solution.py:2126
  497.4 0.1 scatter-mul.4
  497.5 0.1 reshape.302
  497.6 0.6 pad.62.small
  498.2 58.9 %closing.1 = (f32[256,2048]{1,0:T(8,128)}, f32[9,128]{1,0:T(8,128)}, f32[80,320]{1,0:T(8,128)}, bf16[4,64,1536]{2,1,0:T(8,128)(2,1)}) custom-call(bf16[4,256,1280]{2,1,0:T(8,128)(2,1)} %get-tuple-element.139.in_low, bf16[2048,1280]{1,0:T(8,128)(2,1)} %all-gather.5.cloned.1.call-done.whole_in, bf16[256,2048]{1,0:T(8,128)(2,1)} %get-tuple-element.104.tokens, ...), custom_call_target="tpu_custom_call" | custom-call | flops 49999998976 | bytes 150000000 | tf_op jit(solution)/shard_map/closing/pallas_call | solution.py:1207
  557.1 1.3 slice.131
  558.4 1.1 copy-done.3
  559.5 1.9 from_chips.3
  561.4 1.3 slice_bitcast_fusion.2
  562.8 1.3 slice_bitcast_fusion.3
  564.1 1.7 fusion.15
  565.8 1.3 copy-done.1
  567.1 2.4 regrouped_columns.3
  569.5 11.0 %plane_swap.1.refs_0_ = bf16[4,64,1280]{2,1,0:T(8,128)(2,1)} custom-call(bf16[4,64,1280]{2,1,0:T(8,128)(2,1)} %bitcast.139), custom_call_target="tpu_custom_call" | custom-call | flops 10000000000 | bytes 30000000 | tf_op jit(solution)/shard_map/plane_swap/pallas_call | solution.py:1312
  580.5 1.1 copy-done.4
  581.6 1.4 from_chips.2
  583.0 1.3 copy.62
  (96 shorter events, 0.9 us)
Async XLA Ops:
  7.2 87.2 %all-gather.5.cloned.1.call-start = ((), (), s32[]{:S(2)}) async-start(), calls=%async_computation.4 | async-start | bytes 5898240 | tf_op jit(solution)/shard_map/all_gather | solution.py:2255
  24.7 5.0 copy-start.20
  24.7 5.0 copy-start.21
  24.8 5.0 copy-start.22
  24.8 5.0 copy-start.23
  24.8 5.0 copy-start.24
  24.8 5.0 copy-start.25
  24.8 5.0 copy-start.18
  24.8 5.1 copy-start.19
  24.9 144.0 %all-gather.7.cloned.1.call-start = ((), (), s32[]{:S(2)}) async-start(), calls=%async_computation.5 | async-start | bytes 10027008 | tf_op jit(solution)/shard_map/all_gather | solution.py:2255
  29.7 232.8 %all-gather.11.cloned.1.call-start = ((), (), s32[]{:S(2)}) async-start(), calls=%async_computation.7 | async-start | bytes 7077888 | tf_op jit(solution)/shard_map/all_gather | solution.py:2255
  90.0 210.6 %all-gather.9.cloned.1.call-start = ((), (), s32[]{:S(2)}) async-start(), calls=%async_computation.6 | async-start | bytes 7077888 | tf_op jit(solution)/shard_map/all_gather | solution.py:2255
  92.1 10.4 %copy-start.15 = (f32[1,640]{1,0:T(1,128)}, f32[1,640]{1,0:T(1,128)S(1)}, u32[]{:S(2)}) copy-start(f32[1,640]{1,0:T(1,128)S(1)} %squeeze.36) | copy-start | bytes 7684
  92.3 10.3 %copy-start.11 = (f32[1,4,4,2,256]{4,3,2,1,0:T(2,128)}, f32[1,4,4,2,256]{4,3,2,1,0:T(2,128)S(1)}, u32[]{:S(2)}) copy-start(f32[1,4,4,2,256]{4,3,2,1,0:T(2,128)S(1)} %stack.8) | copy-start | bytes 98308
  92.5 0.6 copy-start.7
  92.5 0.6 copy-start.9
  94.3 8.2 %copy-start.17 = (f32[8,640]{1,0:T(8,128)}, f32[8,640]{1,0:T(8,128)S(1)}, u32[]{:S(2)}) copy-start(f32[8,640]{1,0:T(8,128)S(1)} %scatter.4.vectors) | copy-start | bytes 61444
  94.4 8.2 %copy-start.5 = (bf16[4,256,2048]{2,1,0:T(8,128)(2,1)S(1)}, bf16[4,256,2048]{2,1,0:T(8,128)(2,1)}, u32[]{:S(2)}) copy-start(bf16[4,256,2048]{2,1,0:T(8,128)(2,1)} %get-tuple-element.105) | copy-start | bytes 12582916
  94.4 8.2 %copy-start.26 = (bf16[2048,1280]{1,0:T(8,128)(2,1)S(1)}, bf16[2048,1280]{1,0:T(8,128)(2,1)}, u32[]{:S(2)}) copy-start(bf16[2048,1280]{1,0:T(8,128)(2,1)} %all-gather.5.cloned.1.call-done.whole_in) | copy-start | bytes 15728644
  163.5 262.1 %reduce-scatter.5.cloned.1.call-start = ((), (), s32[]{:S(2)}) async-start(), calls=%async_computation.8 | async-start | bytes 3932160 | tf_op jit(solution)/shard_map/reduce_scatter | solution.py:2258
  300.3 197.9 %reduce-scatter.9.cloned.1.call-start = ((), (), s32[]{:S(2)}) async-start(), calls=%async_computation.10 | async-start | bytes 3932160 | tf_op jit(solution)/shard_map/reduce_scatter | solution.py:2258
  338.2 227.6 %reduce-scatter.7.cloned.1.call-start = ((), (), s32[]{:S(2)}) async-start(), calls=%async_computation.9 | async-start | bytes 5570560 | tf_op jit(solution)/shard_map/reduce_scatter | solution.py:2258
  423.4 0.7 copy-start.13
  423.4 1.4 copy-start.8
  423.4 1.4 copy-start.10
  423.4 1.4 copy-start.12
  423.5 146.0 %reduce-scatter.11.cloned.1.call-start = ((), (), s32[]{:S(2)}) async-start(), calls=%async_computation.11 | async-start | bytes 3276800 | tf_op jit(solution)/shard_map/reduce_scatter | solution.py:2258
  483.1 14.3 %copy-start.14 = (f32[8,640]{1,0:T(8,128)S(1)}, f32[8,640]{1,0:T(8,128)}, u32[]{:S(2)}) copy-start(f32[8,640]{1,0:T(8,128)} %get-tuple-element.141) | copy-start | bytes 61444
  483.1 14.3 %copy-start.16 = (f32[1,640]{1,0:T(1,128)S(1)}, f32[1,640]{1,0:T(1,128)}, u32[]{:S(2)}) copy-start(f32[1,640]{1,0:T(1,128)} %copy-done.15) | copy-start | bytes 7684
  498.2 60.1 %copy-start.2 = (bf16[4,64,1536]{2,1,0:T(8,128)(2,1)S(1)}, bf16[4,64,1536]{2,1,0:T(8,128)(2,1)}, u32[]{:S(2)}) copy-start(bf16[4,64,1536]{2,1,0:T(8,128)(2,1)} %get-tuple-element.156.refs_0_) | copy-start | bytes 2359300
  498.2 67.6 %copy-start = (f32[256,2048]{1,0:T(8,128)S(1)}, f32[256,2048]{1,0:T(8,128)}, u32[]{:S(2)}) copy-start(f32[256,2048]{1,0:T(8,128)} %get-tuple-element.135.refs_0_) | copy-start | bytes 6291460
  558.4 1.1 copy-start.3
  565.8 1.3 copy-start.1
  569.5 13.6 %copy-start.6 = (f32[256,2048]{1,0:T(8,128)S(1)}, f32[256,2048]{1,0:T(8,128)}, u32[]{:S(2)}) copy-start(f32[256,2048]{1,0:T(8,128)} %get-tuple-element.206) | copy-start | bytes 6291460
  580.5 1.1 copy-start.4
Sparse Core Ops, SparseCore 0:
  25.0 54.8 all-gather.4
  82.0 86.7 all-gather.6
  170.4 63.3 all-gather.10
  235.3 63.3 all-gather.8
  300.8 58.9 reduce-scatter.4
  361.9 60.2 reduce-scatter.8
  424.5 82.5 reduce-scatter.6
  509.4 57.2 reduce-scatter.10
